TPU v7x, 32 devices: a whole 2x2x4 slice. The times are simulated.
32 devices in a mesh: rep: 2 (over x), shard: 16 (over z, y, core).
Axes of the slice: x: 2, y: 2, z: 4, core: 2. Of those that a mesh axis runs over, the one named last changes fastest.
Arguments:
- tokens: bfloat16 [5632, 1024], P(('rep', 'shard')), may hold values from -6 to 6
- cotangent: bfloat16 [5632, 1024], P(('rep', 'shard')), may hold values from -6 to 6
- lengths: int32 [64], replicated, may hold values from 1 to 176, as said below
- owners: int32 [64], replicated, may hold values from 0 to 31, as said below
- first_gain: bfloat16 [1024], P('shard'), may hold values from 0.099609375 to 1.8984375
- first_bias: bfloat16 [1024], P('shard'), may hold values from -2 to 2
- joint_weight: bfloat16 [1024, 3072], P('shard'), may hold values from -0.1875 to 0.1875
- joint_bias: bfloat16 [3072], P('shard'), may hold values from -3 to 3
- output_weight: bfloat16 [1024, 1024], P('shard'), may hold values from -0.875 to 0.875
- output_bias: bfloat16 [1024], P('shard'), may hold values from -2 to 2
- second_gain: bfloat16 [1024], P('shard'), may hold values from 0.099609375 to 1.8984375
- second_bias: bfloat16 [1024], P('shard'), may hold values from -2 to 2
- up_weight: bfloat16 [1024, 4096], P('shard'), may hold values from -0.1875 to 0.1875
- up_bias: bfloat16 [4096], P('shard'), may hold values from -3 to 3
- down_weight: bfloat16 [4096, 1024], P('shard'), may hold values from -0.09375 to 0.09375
- down_bias: bfloat16 [1024], P('shard'), may hold values from -2 to 2
Outputs:
- result: bfloat16 [5632, 1024], P(('rep', 'shard'))
- grad_tokens: float32 [5632, 1024], P(('rep', 'shard'))
- first_gain_grad: float32 [1024], P('shard')
- first_bias_grad: float32 [1024], P('shard')
- joint_weight_grad: float32 [1024, 3072], P('shard')
- joint_bias_grad: float32 [3072], P('shard')
- output_weight_grad: float32 [1024, 1024], P('shard')
- output_bias_grad: float32 [1024], P('shard')
- second_gain_grad: float32 [1024], P('shard')
- second_bias_grad: float32 [1024], P('shard')
- up_weight_grad: float32 [1024, 4096], P('shard')
- up_bias_grad: float32 [4096], P('shard')
- down_weight_grad: float32 [4096, 1024], P('shard')
- down_bias_grad: float32 [1024], P('shard')
Inputs may be any that keep to these rules, and one draw needn't show every extreme that they name: `lengths`: the sequences of one device, in increasing number, lie end to end from its first row of tokens and cotangent and total at most 176 tokens; in every draw one device holds a single sequence of exactly 176 tokens. `owners`: A device is numbered rep index * size of shard + shard index; every device holds one sequence or more.
All inputs are finite; a program needn't handle non-finite values.
Results may differ from a plain program's by a relative error of at most 0.0083.
Values may be sent and summed in bfloat16 or wider, within the bound.
No kernel may reach another device: no remote copies, remote signals or barrier semaphores. Data moves between devices by JAX's collectives and lax.ppermute only.
A program may use at most 192 MiB of HBM per device.

v0:
```python
from functools import partial

import jax
import jax.numpy as jnp
from jax import lax
from jax.sharding import PartitionSpec as P

D = 1024
HEADS = 16
HEAD = 64
ROT = 16


EPSILON = 1e-05


def layout(lengths, owners, device, row_count):
    owned = owners == device
    own_lengths = jnp.where(owned, lengths, 0)
    end_points = jnp.cumsum(own_lengths, dtype=jnp.int32)
    filled = jnp.sum(own_lengths, dtype=jnp.int32)
    places = jnp.arange(row_count, dtype=jnp.int32)
    passed = end_points[None, :] <= places[:, None]
    before_count = jnp.sum(passed.astype(jnp.int32), axis=1, dtype=jnp.int32)
    seq_start = jnp.max(jnp.where(passed, end_points[None, :], 0), axis=1)
    filled_row = places < filled
    seq_total = lengths.shape[0]
    segment = jnp.where(filled_row, before_count, seq_total + places)
    position = jnp.where(filled_row, places - seq_start, 0)
    return (segment, position)


def rotate(vectors, position, direction):
    half_rot = ROT // 2
    frequency = 10000.0 ** (-jnp.arange(half_rot, dtype=jnp.float32) / half_rot)
    angles = position.astype(jnp.float32)[:, None] * frequency[None, :]
    cosine = jnp.cos(angles)[:, None, :]
    sine_part = direction * jnp.sin(angles)[:, None, :]
    lead_part = vectors[..., :half_rot]
    trail_part = vectors[..., half_rot:ROT]
    turned_lead = lead_part * cosine - trail_part * sine_part
    turned_trail = trail_part * cosine + lead_part * sine_part
    return jnp.concatenate([turned_lead, turned_trail, vectors[..., ROT:]], axis=-1)


def normalize(values, gain, shift):
    centre = values - jnp.mean(values, axis=-1, keepdims=True)
    normed = centre * lax.rsqrt(jnp.mean(centre * centre, axis=-1, keepdims=True) + EPSILON)
    return (normed, normed * gain + shift)


def norm_back(grad_hidden, normed, gain, values):
    gain_grad = jnp.sum(grad_hidden * normed, axis=0)
    shift_grad = jnp.sum(grad_hidden, axis=0)
    grad_normed = grad_hidden * gain
    centre = values - jnp.mean(values, axis=-1, keepdims=True)
    factor = lax.rsqrt(jnp.mean(centre * centre, axis=-1, keepdims=True) + EPSILON)
    grad_values = factor * (
        grad_normed
        - jnp.mean(grad_normed, axis=-1, keepdims=True)
        - normed * jnp.mean(grad_normed * normed, axis=-1, keepdims=True)
    )
    return (gain_grad, shift_grad, grad_values)


def contract_rows(left, right):
    return lax.dot_general(
        left, right, (((0,), (0,)), ((), ())), preferred_element_type=jnp.float32
    )


def across(left, right):
    return lax.dot_general(
        left, right, (((1,), (1,)), ((), ())), preferred_element_type=jnp.float32
    )


def local(
    tokens,
    cotangent,
    lengths,
    owners,
    first_gain,
    first_bias,
    joint_weight,
    joint_bias,
    output_weight,
    output_bias,
    second_gain,
    second_bias,
    up_weight,
    up_bias,
    down_weight,
    down_bias,
):
    row_count = tokens.shape[0]
    score_scale = HEAD ** (-0.5)
    device = lax.axis_index(("rep", "shard"))
    segment, position = layout(lengths, owners, device, row_count)
    places = jnp.arange(row_count, dtype=jnp.int32)
    allowed = (segment[:, None] == segment[None, :]) & (places[None, :] <= places[:, None])
    gain_one, shift_one, joint_full, joint_offset, output_full, output_offset = (
        lax.all_gather(first_gain, "shard", axis=0, tiled=True),
        lax.all_gather(first_bias, "shard", axis=0, tiled=True),
        lax.all_gather(joint_weight, "shard", axis=0, tiled=True),
        lax.all_gather(joint_bias, "shard", axis=0, tiled=True),
        lax.all_gather(output_weight, "shard", axis=0, tiled=True),
        lax.all_gather(output_bias, "shard", axis=0, tiled=True),
    )
    gain_two, shift_two, up_full, up_offset, down_full, down_offset = (
        lax.all_gather(second_gain, "shard", axis=0, tiled=True),
        lax.all_gather(second_bias, "shard", axis=0, tiled=True),
        lax.all_gather(up_weight, "shard", axis=0, tiled=True),
        lax.all_gather(up_bias, "shard", axis=0, tiled=True),
        lax.all_gather(down_weight, "shard", axis=0, tiled=True),
        lax.all_gather(down_bias, "shard", axis=0, tiled=True),
    )
    values = tokens.astype(jnp.float32)
    normed_one, hidden_one = normalize(
        values, gain_one.astype(jnp.float32), shift_one.astype(jnp.float32)
    )
    input_one = hidden_one.astype(jnp.bfloat16)
    projected = jnp.dot(
        input_one, joint_full, preferred_element_type=jnp.float32
    ) + joint_offset.astype(jnp.float32)
    heads_view = projected.reshape(row_count, 3, HEADS, HEAD)
    query_low = rotate(heads_view[:, 0], position, 1.0).astype(jnp.bfloat16)
    keys_low = rotate(heads_view[:, 1], position, 1.0).astype(jnp.bfloat16)
    value_low = heads_view[:, 2].astype(jnp.bfloat16)
    masked = jnp.where(
        allowed[None],
        jnp.einsum("qhd,khd->hqk", query_low, keys_low, preferred_element_type=jnp.float32)
        * score_scale,
        -1e30,
    )
    row_peak = jnp.max(masked, axis=-1, keepdims=True)
    logsum = row_peak + jnp.log(jnp.sum(jnp.exp(masked - row_peak), axis=-1, keepdims=True))
    probs_low = jnp.exp(masked - logsum).astype(jnp.bfloat16)
    mixed_low = (
        jnp.einsum("hqk,khd->qhd", probs_low, value_low, preferred_element_type=jnp.float32)
        .reshape(row_count, D)
        .astype(jnp.bfloat16)
    )
    attention = jnp.dot(
        mixed_low, output_full, preferred_element_type=jnp.float32
    ) + output_offset.astype(jnp.float32)
    normed_two, hidden_two = normalize(
        values, gain_two.astype(jnp.float32), shift_two.astype(jnp.float32)
    )
    input_two = hidden_two.astype(jnp.bfloat16)
    before = jnp.dot(input_two, up_full, preferred_element_type=jnp.float32) + up_offset.astype(
        jnp.float32
    )
    active_low = jax.nn.gelu(before, approximate=False).astype(jnp.bfloat16)
    feed_out = jnp.dot(
        active_low, down_full, preferred_element_type=jnp.float32
    ) + down_offset.astype(jnp.float32)
    result = (values + attention + feed_out).astype(jnp.bfloat16)
    back_one = (
        lax.all_gather(first_gain, "shard", axis=0, tiled=True),
        lax.all_gather(joint_weight, "shard", axis=0, tiled=True),
        lax.all_gather(output_weight, "shard", axis=0, tiled=True),
    )
    back_two = (
        lax.all_gather(second_gain, "shard", axis=0, tiled=True),
        lax.all_gather(up_weight, "shard", axis=0, tiled=True),
        lax.all_gather(down_weight, "shard", axis=0, tiled=True),
    )
    gain_back_one, joint_back, output_back = back_one
    gain_back_two, up_back, down_back = back_two
    grad_out = cotangent.astype(jnp.float32)
    down_weight_grad = contract_rows(active_low, cotangent)
    down_bias_grad = jnp.sum(grad_out, axis=0)
    grad_active = across(cotangent, down_back)
    gelu_exact = partial(jax.nn.gelu, approximate=False)
    grad_before = jax.vjp(gelu_exact, before)[1](grad_active)[0].astype(jnp.bfloat16)
    up_weight_grad = contract_rows(input_two, grad_before)
    up_bias_grad = jnp.sum(grad_before.astype(jnp.float32), axis=0)
    gain_two_grad, shift_two_grad, grad_from_two = norm_back(
        across(grad_before, up_back), normed_two, gain_back_two.astype(jnp.float32), values
    )
    output_weight_grad = contract_rows(mixed_low, cotangent)
    grad_mixed = across(cotangent, output_back).astype(jnp.bfloat16).reshape(row_count, HEADS, HEAD)
    masked_again = jnp.where(
        allowed[None],
        jnp.einsum("qhd,khd->hqk", query_low, keys_low, preferred_element_type=jnp.float32)
        * score_scale,
        -1e30,
    )
    prob_back = jnp.exp(masked_again - logsum)
    prob_back_low = prob_back.astype(jnp.bfloat16)
    grad_probs = jnp.einsum(
        "qhd,khd->hqk", grad_mixed, value_low, preferred_element_type=jnp.float32
    )
    grad_value = jnp.einsum(
        "hqk,qhd->khd", prob_back_low, grad_mixed, preferred_element_type=jnp.float32
    )
    spread = jnp.sum(grad_probs * prob_back, axis=-1, keepdims=True)
    grad_scores = (prob_back * (grad_probs - spread)).astype(jnp.bfloat16)
    grad_query = rotate(
        jnp.einsum("hqk,khd->qhd", grad_scores, keys_low, preferred_element_type=jnp.float32)
        * score_scale,
        position,
        -1.0,
    )
    grad_keys = rotate(
        jnp.einsum("hqk,qhd->khd", grad_scores, query_low, preferred_element_type=jnp.float32)
        * score_scale,
        position,
        -1.0,
    )
    grad_joint = (
        jnp.stack([grad_query, grad_keys, grad_value], axis=1)
        .reshape(row_count, 3 * D)
        .astype(jnp.bfloat16)
    )
    joint_weight_grad = contract_rows(input_one, grad_joint)
    joint_bias_grad = jnp.sum(grad_joint.astype(jnp.float32), axis=0)
    gain_one_grad, shift_one_grad, grad_from_one = norm_back(
        across(grad_joint, joint_back), normed_one, gain_back_one.astype(jnp.float32), values
    )
    grad_tokens = grad_out + grad_from_one + grad_from_two
    group_shares = (
        lax.psum_scatter(gain_one_grad, "shard", scatter_dimension=0, tiled=True),
        lax.psum_scatter(shift_one_grad, "shard", scatter_dimension=0, tiled=True),
        lax.psum_scatter(joint_weight_grad, "shard", scatter_dimension=0, tiled=True),
        lax.psum_scatter(joint_bias_grad, "shard", scatter_dimension=0, tiled=True),
        lax.psum_scatter(output_weight_grad, "shard", scatter_dimension=0, tiled=True),
        lax.psum_scatter(down_bias_grad, "shard", scatter_dimension=0, tiled=True),
        lax.psum_scatter(gain_two_grad, "shard", scatter_dimension=0, tiled=True),
        lax.psum_scatter(shift_two_grad, "shard", scatter_dimension=0, tiled=True),
        lax.psum_scatter(up_weight_grad, "shard", scatter_dimension=0, tiled=True),
        lax.psum_scatter(up_bias_grad, "shard", scatter_dimension=0, tiled=True),
        lax.psum_scatter(down_weight_grad, "shard", scatter_dimension=0, tiled=True),
        lax.psum_scatter(down_bias_grad, "shard", scatter_dimension=0, tiled=True),
    )
    (
        share_gain_one,
        share_shift_one,
        share_joint_weight,
        share_joint_bias,
        share_output_weight,
        share_output_bias,
        share_gain_two,
        share_shift_two,
        share_up_weight,
        share_up_bias,
        share_down_weight,
        share_down_bias,
    ) = group_shares
    owned = lax.psum(
        (
            share_gain_one,
            share_shift_one,
            share_joint_weight,
            share_joint_bias,
            share_output_weight,
            share_output_bias,
            share_gain_two,
            share_shift_two,
            share_up_weight,
            share_up_bias,
            share_down_weight,
            share_down_bias,
        ),
        "rep",
    )
    return (
        result,
        grad_tokens,
        owned[0],
        owned[1],
        owned[2],
        owned[3],
        owned[4],
        owned[5],
        owned[6],
        owned[7],
        owned[8],
        owned[9],
        owned[10],
        owned[11],
    )


def solution(mesh):
    in_specs = (
        P(("rep", "shard"), None),
        P(("rep", "shard"), None),
        P(),
        P(),
        P("shard"),
        P("shard"),
        P("shard", None),
        P("shard"),
        P("shard", None),
        P("shard"),
        P("shard"),
        P("shard"),
        P("shard", None),
        P("shard"),
        P("shard", None),
        P("shard"),
    )
    out_specs = (
        P(("rep", "shard"), None),
        P(("rep", "shard"), None),
        P("shard"),
        P("shard"),
        P("shard", None),
        P("shard"),
        P("shard", None),
        P("shard"),
        P("shard"),
        P("shard"),
        P("shard", None),
        P("shard"),
        P("shard", None),
        P("shard"),
    )
    return jax.shard_map(local, mesh=mesh, in_specs=in_specs, out_specs=out_specs, check_vma=False)
```

profile of v0, /device:TPU:0, one launch (start us, length us, event | category | flops | bytes accessed | tf_op | source)
XLA Modules:
  0.0 948.7 jit_solution(13588980743445199123)
XLA Ops:
  7.2 0.7 all-gather.6.cloned.1.call-update
  8.0 0.7 all-gather.8.cloned.1.call-update
  8.7 0.7 all-gather.10.cloned.1.call-update
  9.4 0.5 all-gather.12.cloned.1.call-update
  10.0 1.3 fusion.61
  12.7 0.8 dynamic-update-slice.5
  13.5 0.8 dynamic-update-slice.4
  14.3 0.8 dynamic-update-slice.6
  15.2 0.8 dynamic-update-slice.1
  16.0 0.8 dynamic-update-slice
  16.9 0.8 dynamic-update-slice.3
  17.7 0.8 dynamic-update-slice.2
  18.5 64.1 %all-reduce.17 = (bf16[1024]{0:T(1024)(128)(2,1)S(1)}, bf16[1024]{0:T(1024)(128)(2,1)S(1)}, bf16[1024]{0:T(1024)(128)(2,1)S(1)}, bf16[3072]{0:T(1024)(128)(2,1)S...) all-reduce(bf16[1024]{0:T(1024)(128)(2,1)S(1)} %dynamic-update-slic, ...), channel_id=1, replica_groups=mesh['rep'=2,'shard'=16] {'shard'}, use_global_device_ids=true, to_apply=%add.5 | all-reduce | flops 9216 | bytes 36864
  82.6 1.3 fusion.53
  84.4 1.1 convert_reduce_fusion.2
  85.5 1.2 fusion.36
  86.7 0.7 add_select_fusion
  87.4 0.7 select_convert_fusion
  88.3 5.7 convolution_add_fusion.1
  94.0 2.2 copy.54
  96.5 1.4 copy-done
  98.0 0.7 fusion.6
  98.7 0.7 exponential_reduce_fusion
  99.4 2.0 convolution_convert_fusion
  101.5 0.8 copy-done.7
  102.2 2.8 fusion.63
  105.3 12.7 %all-gather.8.cloned.1.call-done = bf16[1024,1024]{1,0:T(8,128)(2,1)} async-done(((bf16[64,1024]{1,0:T(8,128)(2,1)}), bf16[1024,1024]{1,0:T(8,128)(2,1)}) %all-gather.8.cloned.1.call-update) | async-done | bytes 2097168 | tf_op jit(solution)/shard_map/all_gather | solution.py:107
  118.0 3.2 convolution_convert_fusion.1
  121.1 2.0 copy.57
  123.1 2.4 multiply_reduce_fusion
  125.5 0.8 multiply_convert_fusion
  126.5 0.4 fusion.9
  127.0 0.6 copy-done.11
  127.6 0.6 fusion.8
  128.7 0.8 convolution_bitcast_fusion
  129.5 0.5 convert_reduce_fusion
  130.0 6.5 fusion.57
  136.6 0.6 copy-done.18
  137.2 19.4 %all-gather = bf16[16,1,256]{2,1,0:T(2,128)(2,1)S(1)} all-gather(bf16[1,1,256]{2,1,0:T(2,128)(2,1)S(1)} %reshape.279), channel_id=1, replica_groups=mesh['rep'=2,'shard'=16] {'shard'}, dimensions={0}, use_global_device_ids=true | all-gather | bytes 8704 | tf_op jit(solution)/shard_map/all_gather | solution.py:114
  156.6 37.3 %all-gather.10.cloned.1.call-done = bf16[1024,4096]{1,0:T(8,128)(2,1)} async-done(((bf16[64,4096]{1,0:T(8,128)(2,1)}), bf16[1024,4096]{1,0:T(8,128)(2,1)}) %all-gather.10.cloned.1.call-update) | async-done | bytes 8388624 | tf_op jit(solution)/shard_map/all_gather | solution.py:113
  193.9 6.8 convolution_add_fusion
  200.6 68.4 %all-gather.12.cloned.1.call-done = bf16[4096,1024]{1,0:T(8,128)(2,1)} async-done(((bf16[256,1024]{1,0:T(8,128)(2,1)}), bf16[4096,1024]{1,0:T(8,128)(2,1)}) %all-gather.12.cloned.1.call-update) | async-done | bytes 8388624 | tf_op jit(solution)/shard_map/all_gather | solution.py:115
  269.1 12.7 %convert_reduce_fusion.1 = (f32[4096]{0:T(1024)S(1)}, bf16[176,4096]{1,0:T(8,128)(2,1)S(1)}, f32[176,4096]{1,0:T(8,128)}) fusion(f32[176,4096]{1,0:T(8,128)} %convolution_add_fusion, bf16[176,1024]{1,0:T(8,128)(2,1)S(1)} %copy-done.4, bf16[4096,1024]{1,0:T(8,128)(2,1)} %all-gather.12.cloned.1.call-done), kind=kOutput, calls=%fused_computation.6 | convolution fusion | flops 1529737216 | bytes 15974400 | tf_op jit(solution)/shard_map/dot_general | solution.py:73
  281.8 1.2 copy-done.14
  283.0 8.8 fusion.54
  291.9 3.1 multiply_convert_fusion.1
  295.0 8.5 fusion.64
  305.9 37.9 %reduce-scatter.7.cloned.1.call-done = f32[64,1024]{1,0:T(8,128)} async-done(((f32[1024,1024]{1,0:T(8,128)}), f32[64,1024]{1,0:T(8,128)}) %reduce-scatter.7.cloned.1.call-update) | async-done | bytes 262160 | tf_op jit(solution)/shard_map/reduce_scatter | solution.py:228
  343.8 138.1 %reduce-scatter.5.cloned.1.call-done = f32[64,3072]{1,0:T(8,128)} async-done(((f32[1024,3072]{1,0:T(8,128)}), f32[64,3072]{1,0:T(8,128)}) %reduce-scatter.5.cloned.1.call-update) | async-done | bytes 786448 | tf_op jit(solution)/shard_map/reduce_scatter | solution.py:226
  481.8 182.4 %reduce-scatter.9.cloned.1.call-done = f32[64,4096]{1,0:T(8,128)} async-done(((f32[1024,4096]{1,0:T(8,128)}), f32[64,4096]{1,0:T(8,128)}) %reduce-scatter.9.cloned.1.call-update) | async-done | bytes 1048592 | tf_op jit(solution)/shard_map/reduce_scatter | solution.py:232
  664.3 182.2 %reduce-scatter.11.cloned.1.call-done = f32[256,1024]{1,0:T(8,128)} async-done(((f32[4096,1024]{1,0:T(8,128)}), f32[256,1024]{1,0:T(8,128)}) %reduce-scatter.11.cloned.1.call-update) | async-done | bytes 1048592 | tf_op jit(solution)/shard_map/reduce_scatter | solution.py:234
  846.5 6.8 fusion.62
  853.3 5.9 fusion.34
  859.3 1.4 convert_reduce_fusion.3
  860.6 59.3 %all-reduce.14 = (f32[1024]{0:T(1024)S(1)}, f32[1024]{0:T(1024)S(1)}, f32[3072]{0:T(1024)S(1)}, f32[1024]{0:T(1024)S(1)}, f32[1024]{0:T(1024)S(1)}, /*index=5*/f32[1024]{0:T(1024)S(1)}, f32[4096]{0:T(1024)S(1)}) all-reduce(f32[1024]{0:T(1024)S(1)} %get-tuple-element.16, ...), channel_id=2, replica_groups=mesh['rep'=2,'shard'=16] {'shard'}, use_global_device_ids=true, to_apply=%region_14.15.clone | all-reduce | flops 12288 | bytes 98304
  920.4 5.7 all-reduce.15
  926.1 5.2 convolution_add_fusion.3
  931.4 1.3 fusion.12
  932.7 2.0 all-reduce.20.cloned.1.call-done
  934.7 0.5 copy.77
  935.2 2.1 copy.78
  937.2 1.7 copy.79
  938.9 2.3 copy.80
  941.2 1.0 copy.81
  (96 shorter events, 3.3 us)
Async XLA Ops:
  7.2 81.1 %all-gather.6.cloned.1.call-start = ((), (), s32[]{:S(2)}) async-start(), calls=%async_computation.4 | async-start | bytes 6684672 | tf_op jit(solution)/shard_map/all_gather | solution.py:105
  7.9 110.0 %all-gather.8.cloned.1.call-start = ((), (), s32[]{:S(2)}) async-start(), calls=%async_computation.5 | async-start | bytes 2228224 | tf_op jit(solution)/shard_map/all_gather | solution.py:107
  8.7 185.2 %all-gather.10.cloned.1.call-start = ((), (), s32[]{:S(2)}) async-start(), calls=%async_computation.6 | async-start | bytes 8912896 | tf_op jit(solution)/shard_map/all_gather | solution.py:113
  9.4 259.7 %all-gather.12.cloned.1.call-start = ((), (), s32[]{:S(2)}) async-start(), calls=%async_computation.7 | async-start | bytes 8912896 | tf_op jit(solution)/shard_map/all_gather | solution.py:115
  10.0 333.8 %reduce-scatter.7.cloned.1.call-start = ((), (), s32[]{:S(2)}) async-start(), calls=%async_computation.9 | async-start | bytes 4456448 | tf_op jit(solution)/shard_map/reduce_scatter | solution.py:228
  96.2 1.7 copy-start
  96.4 2.3 copy-start.12
  97.9 0.8 copy-start.10
  97.9 0.8 copy-start.16
  99.4 2.9 copy-start.3
  101.4 0.8 copy-start.7
  105.0 376.8 %reduce-scatter.5.cloned.1.call-start = ((), (), s32[]{:S(2)}) async-start(), calls=%async_computation.8 | async-start | bytes 13369344 | tf_op jit(solution)/shard_map/reduce_scatter | solution.py:226
  125.5 1.0 copy-start.13
  125.5 1.0 copy-start.17
  126.5 1.0 copy-start.11
  127.6 1.1 copy-start.9
  128.7 1.3 copy-start.1
  136.5 0.7 copy-start.18
  136.5 527.7 %reduce-scatter.9.cloned.1.call-start = ((), (), s32[]{:S(2)}) async-start(), calls=%async_computation.10 | async-start | bytes 17825792 | tf_op jit(solution)/shard_map/reduce_scatter | solution.py:232
  193.9 75.2 %copy-start.4 = (bf16[176,1024]{1,0:T(8,128)(2,1)S(1)}, bf16[176,1024]{1,0:T(8,128)(2,1)}, u32[]{:S(2)}) copy-start(bf16[176,1024]{1,0:T(8,128)(2,1)} %param.17) | copy-start | bytes 1081348
  281.8 1.2 copy-start.14
  291.9 554.6 %reduce-scatter.11.cloned.1.call-start = ((), (), s32[]{:S(2)}) async-start(), calls=%async_computation.11 | async-start | bytes 17825792 | tf_op jit(solution)/shard_map/reduce_scatter | solution.py:234
  291.9 3.1 copy-start.5
  303.5 631.1 %all-reduce.20.cloned.1.call-start = ((), (), s32[]{:S(2)}) async-start(), calls=%async_computation.12 | async-start | bytes 6291456 | tf_op jit(solution)/shard_map/psum | solution.py:251
  853.3 6.0 copy-start.6
  926.1 8.5 copy-start.19
  926.1 5.2 copy-start.2
  926.1 5.2 copy-start.8
  934.7 6.5 copy-start.15
Sparse Core Ops, SparseCore 0:
  10.3 65.4 all-gather.5
  77.9 40.0 all-gather.7
  120.1 73.6 all-gather.9
  195.9 73.1 all-gather.11
  272.8 70.9 reduce-scatter.6
  348.2 133.5 reduce-scatter.4
  486.5 177.7 reduce-scatter.8
  668.9 177.5 reduce-scatter.10
  849.1 85.4 all-reduce.19
where the time goes:
time: 949 us
  waiting for transfers between devices  664 us (70%)
  blocking collectives  148 us (16%)
  matrix products  81.1 us (9%)
  local copies, waits for them, and re-layouts  24.8 us (3%)
  between operations  17.5 us (2%)
  other arithmetic  12.3 us (1%)
    reduce_scatter x1, waiting for transfers between devices, local(): lax.psum_scatter(up_weight_grad, 'shard', scatter_dimension=0, tiled=True)  182 us
    reduce_scatter x1, waiting for transfers between devices, local(): lax.psum_scatter(down_weight_grad, 'shard', scatter_dimension=0, tiled=True)  182 us
    reduce_scatter x1, waiting for transfers between devices, local(): lax.psum_scatter(joint_weight_grad, 'shard', scatter_dimension=0, tiled=T...  138 us
    unnamed x2, blocking collectives  123 us
    all_gather x1, waiting for transfers between devices, local(): lax.all_gather(down_weight, 'shard', axis=0, tiled=True)  68.4 us
    reduce_scatter x1, waiting for transfers between devices, local(): lax.psum_scatter(output_weight_grad, 'shard', scatter_dimension=0, tiled=...  37.9 us
    all_gather x1, waiting for transfers between devices, local(): lax.all_gather(up_weight, 'shard', axis=0, tiled=True)  37.3 us
    dot_general x4, matrix products, across(): lax.dot_general(left, right, (((1,), (1,)), ((), ())), preferred_element_...  28.6 us
  transfers between devices with their start and end apart: 9, of which 8 were waited for; matrix products, arithmetic and copies ran while one was open for 11% of the time, Pallas kernels for 0%

commit v1 on v0

--- a/solution.py
+++ b/solution.py
@@ -3,7 +3,7 @@
 import jax
 import jax.numpy as jnp
 from jax import lax
-from jax.sharding import PartitionSpec as P
+from jax.sharding import Mesh, PartitionSpec as P
 
 D = 1024
 HEADS = 16
@@ -283,39 +283,298 @@
     )
 
 
+PAIR = [(0, 1), (1, 0)]
+BLOCKS = 8
+
+
+def swap(values, *axes):
+    if len(axes) == 1:
+        return lax.ppermute(values, axes[0], PAIR)
+    return lax.ppermute(values, axes, [(i, 3 - i) for i in range(4)])
+
+
+def join(own, other, at, axis=0):
+    first = at == 0
+    return jnp.concatenate(
+        [jnp.where(first, own, other), jnp.where(first, other, own)], axis=axis
+    )
+
+
+def stack(own, other, at, axis=0):
+    first = at == 0
+    return jnp.stack([jnp.where(first, own, other), jnp.where(first, other, own)], axis=axis)
+
+
+def take(values, at, axis=0):
+    return lax.dynamic_index_in_dim(values, at, axis, keepdims=False)
+
+
+def gather_rows(own):
+    lane = jnp.concatenate([own, swap(own, "x"), swap(own, "p"), swap(own, "x", "p")], axis=0)
+    return jnp.concatenate([lane, swap(lane, "c")], axis=0)
+
+
+def scatter_rows(partial_sums):
+    low = partial_sums.astype(jnp.bfloat16)
+    half = low.shape[0] // 2
+    rows = half // 4
+    lane = low[:half].astype(jnp.float32) + swap(low[half:], "c").astype(jnp.float32)
+    sent = lane[rows:].astype(jnp.bfloat16)
+    return (
+        lane[:rows]
+        + swap(sent[:rows], "x").astype(jnp.float32)
+        + swap(sent[rows : 2 * rows], "p").astype(jnp.float32)
+        + swap(sent[2 * rows :], "x", "p").astype(jnp.float32)
+    )
+
+
+def low(values):
+    return values.astype(jnp.bfloat16)
+
+
+def wide(values):
+    return values.astype(jnp.float32)
+
+
+def grouped(
+    tokens,
+    cotangent,
+    lengths,
+    owners,
+    first_gain,
+    first_bias,
+    joint_weight,
+    joint_bias,
+    output_weight,
+    output_bias,
+    second_gain,
+    second_bias,
+    up_weight,
+    up_bias,
+    down_weight,
+    down_bias,
+):
+    x, o, p, q, c = (lax.axis_index(name) for name in ("x", "o", "p", "q", "c"))
+    cap = tokens.shape[0]
+    rows = BLOCKS * cap
+    part = joint_weight.shape[0]
+    unit = up_weight.shape[1] // 32
+    score_scale = HEAD ** (-0.5)
+
+    small = jnp.concatenate(
+        [first_gain, first_bias, second_gain, second_bias, output_bias, down_bias, joint_bias, up_bias]
+    )[None]
+    for name, at in (("c", c), ("q", q), ("p", p), ("o", o)):
+        small = join(small, swap(small, name), at)
+
+    def vector(start, size):
+        return wide(small[:, start : start + size]).reshape(-1)
+
+    gain_one, shift_one, gain_two, shift_two, output_offset, down_offset = (
+        vector(i * part, part) for i in range(6)
+    )
+    joint_own = joint_bias.shape[0]
+    joint_offset = vector(6 * part, joint_own)
+    up_offset = vector(6 * part + joint_own, up_bias.shape[0])
+
+    all_tokens = gather_rows(tokens)
+
+    joint_cut = take(joint_weight.reshape(part, 3, 2, 2, 2, 2, HEAD), x, 2)
+    up_cut = take(up_weight.reshape(part, 2, 2, 2, 2, 2, unit), x, 5)
+    joint_cut = joint_cut.transpose(2, 4, 0, 1, 3, 5).reshape(2, 2, part, 6 * HEAD)
+    up_cut = up_cut.transpose(2, 4, 0, 1, 3, 5).reshape(2, 2, part, 4 * unit)
+
+    def turn(cut):
+        both = stack(take(cut, p), swap(take(cut, 1 - p), "p"), p)
+        return stack(take(both, c, 1), swap(take(both, 1 - c, 1), "c"), c, 1)
+
+    def spread(own):
+        other = swap(own, "o")
+        return stack(stack(own, swap(own, "q"), q), stack(other, swap(other, "q"), q), o)
+
+    joint_full = spread(turn(joint_cut)).transpose(0, 2, 1, 3, 4, 5).reshape(D, 6 * HEAD)
+    up_full = spread(turn(up_cut)).transpose(0, 2, 1, 3, 4, 5).reshape(D, 4 * unit)
+    down_full = spread(take(down_weight.reshape(2, unit, D), x)).reshape(4 * unit, D)
+    output_far = lax.ppermute(output_weight, ("x", "o"), [(0, 1), (3, 2)])
+    output_head = jnp.where(x == o, output_weight, output_far)
+    output_full = join(output_head, swap(output_head, "q"), q)
+    all_cotangent = gather_rows(cotangent)
+
+    joint_offset = take(take(take(joint_offset.reshape(3, 2, 2, 2, 2, HEAD), x, 1), p, 1), c, 2)
+    joint_offset = joint_offset.reshape(6 * HEAD)
+    up_offset = take(take(take(up_offset.reshape(2, 2, 2, 2, 2, unit), x, 4), c, 3), p, 1)
+    up_offset = up_offset.reshape(4 * unit)
+
+    blocks = [(cc, pp, xx) for cc in (0, 1) for pp in (0, 1) for xx in (0, 1)]
+    devices = jnp.stack(
+        [
+            ((((x ^ xx) * 2 + o) * 2 + (p ^ pp)) * 2 + q) * 2 + (c ^ cc)
+            for cc, pp, xx in blocks
+        ]
+    )
+    segment, position = jax.vmap(lambda device: layout(lengths, owners, device, cap))(devices)
+    places = jnp.arange(cap, dtype=jnp.int32)
+    allowed = (segment[:, :, None] == segment[:, None, :]) & (
+        places[None, None, :] <= places[None, :, None]
+    )
+    position = position.reshape(rows)
+
+    values = wide(all_tokens)
+    centre = values - jnp.mean(values, axis=-1, keepdims=True)
+    normed = centre * lax.rsqrt(jnp.mean(centre * centre, axis=-1, keepdims=True) + EPSILON)
+    input_one = low(normed * gain_one + shift_one)
+    input_two = low(normed * gain_two + shift_two)
+
+    projected = (
+        jnp.dot(input_one, joint_full, preferred_element_type=jnp.float32) + joint_offset
+    ).reshape(rows, 3, 2, HEAD)
+    query_low = low(rotate(projected[:, 0], position, 1.0)).reshape(BLOCKS, cap, 2, HEAD)
+    keys_low = low(rotate(projected[:, 1], position, 1.0)).reshape(BLOCKS, cap, 2, HEAD)
+    value_low = low(projected[:, 2]).reshape(BLOCKS, cap, 2, HEAD)
+    dot = partial(jnp.einsum, preferred_element_type=jnp.float32)
+    masked = jnp.where(
+        allowed[:, None], dot("bqhd,bkhd->bhqk", query_low, keys_low) * score_scale, -1e30
+    )
+    raised = jnp.exp(masked - jnp.max(masked, axis=-1, keepdims=True))
+    probs = raised / jnp.sum(raised, axis=-1, keepdims=True)
+    probs_low = low(probs)
+    mixed_low = low(dot("bhqk,bkhd->bqhd", probs_low, value_low)).reshape(rows, 2 * HEAD)
+    before = jnp.dot(input_two, up_full, preferred_element_type=jnp.float32) + up_offset
+    gelu_exact = partial(jax.nn.gelu, approximate=False)
+    active, gelu_back = jax.vjp(gelu_exact, before)
+    active_low = low(active)
+    lead = jnp.concatenate([mixed_low, active_low], axis=1)
+    tail_weight = jnp.concatenate([output_full, down_full], axis=0)
+    branches = scatter_rows(jnp.dot(lead, tail_weight, preferred_element_type=jnp.float32))
+    own_values = wide(tokens)
+    result = low(own_values + branches + output_offset + down_offset)
+
+    lead_grad = contract_rows(lead, all_cotangent)
+    output_grad = lead_grad[: 2 * HEAD].reshape(2, HEAD, D)
+    down_grad = lead_grad[2 * HEAD :].reshape(2, 2, unit, D)
+    grad_lead = across(all_cotangent, tail_weight)
+    grad_mixed = low(grad_lead[:, : 2 * HEAD]).reshape(BLOCKS, cap, 2, HEAD)
+    grad_before = low(gelu_back(grad_lead[:, 2 * HEAD :])[0])
+    up_grad = contract_rows(input_two, grad_before)
+    grad_probs = dot("bqhd,bkhd->bhqk", grad_mixed, value_low)
+    grad_value = dot("bhqk,bqhd->bkhd", probs_low, grad_mixed)
+    spread_sum = jnp.sum(grad_probs * probs, axis=-1, keepdims=True)
+    grad_scores = low(probs * (grad_probs - spread_sum))
+    grad_query = dot("bhqk,bkhd->bqhd", grad_scores, keys_low).reshape(rows, 2, HEAD)
+    grad_keys = dot("bhqk,bqhd->bkhd", grad_scores, query_low).reshape(rows, 2, HEAD)
+    grad_joint = low(
+        jnp.stack(
+            [
+                rotate(grad_query * score_scale, position, -1.0),
+                rotate(grad_keys * score_scale, position, -1.0),
+                grad_value.reshape(rows, 2, HEAD),
+            ],
+            axis=1,
+        ).reshape(rows, 6 * HEAD)
+    )
+    joint_grad = contract_rows(input_one, grad_joint)
+    grad_first = across(grad_joint, joint_full)
+    grad_second = across(grad_before, up_full)
+    pulled = scatter_rows(grad_first * gain_one + grad_second * gain_two)
+
+    def place(values, index, size, axis):
+        hot = (jnp.arange(size) == index).reshape([size if i == axis else 1 for i in range(values.ndim + 1)])
+        return jnp.where(hot, jnp.expand_dims(values, axis), 0.0)
+
+    joint_sum = jnp.sum(wide(grad_joint), axis=0).reshape(3, 2, HEAD)
+    joint_sum = place(place(place(joint_sum, c, 2, 2), p, 2, 1), x, 2, 1)
+    up_sum = jnp.sum(wide(grad_before), axis=0).reshape(2, 2, unit)
+    up_sum = place(place(place(up_sum, x, 2, 2), c, 2, 2), p, 2, 1)
+    sums = jnp.concatenate(
+        [
+            jnp.sum(grad_first * normed, axis=0).reshape(-1, part),
+            jnp.sum(grad_first, axis=0).reshape(-1, part),
+            jnp.sum(grad_second * normed, axis=0).reshape(-1, part),
+            jnp.sum(grad_second, axis=0).reshape(-1, part),
+            jnp.sum(wide(cotangent), axis=0).reshape(-1, part),
+            joint_sum.reshape(-1, joint_own),
+            up_sum.reshape(-1, up_bias.shape[0]),
+        ],
+        axis=1,
+    )
+    for name in ("c", "q", "p", "o", "x"):
+        sums = sums + swap(sums, name)
+    own_sums = take(sums, ((o * 2 + p) * 2 + q) * 2 + c)
+
+    def reduce(parts):
+        ours = take(parts, q, 1) + wide(swap(low(take(parts, 1 - q, 1)), "q"))
+        return take(ours, o) + wide(swap(low(take(ours, 1 - o)), "o"))
+
+    def settle(values):
+        low_values = low(values)
+        return low_values, swap(low_values, "x")
+
+    def hand(parts, columns):
+        final = low(reduce(parts.reshape(2, 2, 2, 2, part, columns).transpose(0, 2, 1, 3, 4, 5)))
+        both = stack(take(final, c, 1), swap(take(final, 1 - c, 1), "c"), c)
+        both = stack(take(both, p, 1), swap(take(both, 1 - p, 1), "p"), p)
+        return stack(both, swap(both, "x"), x)
+
+    down_own = low(reduce(down_grad))
+    down_own = wide(join(down_own, swap(down_own, "x"), x))
+    output_own = take(output_grad, q) + wide(swap(low(take(output_grad, 1 - q)), "q"))
+    output_own = low(output_own + wide(lax.ppermute(low(output_own), ("x", "o"), [(1, 0), (2, 3)])))
+    output_own = wide(
+        jnp.where(x == o, output_own, lax.ppermute(output_own, ("x", "o"), [(0, 2), (3, 1)]))
+    )
+    joint_own_grad = wide(
+        hand(joint_grad, 6 * HEAD)
+        .reshape(2, 2, 2, part, 3, 2, HEAD)
+        .transpose(3, 4, 0, 1, 5, 2, 6)
+        .reshape(part, 3 * D)
+    )
+    up_own_grad = wide(
+        hand(up_grad, 4 * unit)
+        .reshape(2, 2, 2, part, 2, 2, unit)
+        .transpose(3, 4, 1, 5, 2, 0, 6)
+        .reshape(part, 32 * unit)
+    )
+
+    own_centre = own_values - jnp.mean(own_values, axis=-1, keepdims=True)
+    factor = lax.rsqrt(jnp.mean(own_centre * own_centre, axis=-1, keepdims=True) + EPSILON)
+    own_normed = own_centre * factor
+    grad_tokens = wide(cotangent) + factor * (
+        pulled
+        - jnp.mean(pulled, axis=-1, keepdims=True)
+        - own_normed * jnp.mean(pulled * own_normed, axis=-1, keepdims=True)
+    )
+    pieces = [own_sums[i * part : (i + 1) * part] for i in range(5)]
+    return (
+        result,
+        grad_tokens,
+        pieces[0],
+        pieces[1],
+        joint_own_grad,
+        own_sums[5 * part : 5 * part + joint_own],
+        output_own,
+        pieces[4],
+        pieces[2],
+        pieces[3],
+        up_own_grad,
+        own_sums[5 * part + joint_own :],
+        down_own,
+        pieces[4],
+    )
+
+
 def solution(mesh):
-    in_specs = (
-        P(("rep", "shard"), None),
-        P(("rep", "shard"), None),
-        P(),
-        P(),
-        P("shard"),
-        P("shard"),
-        P("shard", None),
-        P("shard"),
-        P("shard", None),
-        P("shard"),
-        P("shard"),
-        P("shard"),
-        P("shard", None),
-        P("shard"),
-        P("shard", None),
-        P("shard"),
-    )
-    out_specs = (
-        P(("rep", "shard"), None),
-        P(("rep", "shard"), None),
-        P("shard"),
-        P("shard"),
-        P("shard", None),
-        P("shard"),
-        P("shard", None),
-        P("shard"),
-        P("shard"),
-        P("shard"),
-        P("shard", None),
-        P("shard"),
-        P("shard", None),
-        P("shard"),
-    )
-    return jax.shard_map(local, mesh=mesh, in_specs=in_specs, out_specs=out_specs, check_vma=False)
+    if mesh.shape["rep"] == 2 and mesh.shape["shard"] * HEAD == D:
+        work, body = Mesh(mesh.devices.reshape(2, 2, 2, 2, 2), ("x", "o", "p", "q", "c")), grouped
+        group = ("o", "p", "q", "c")
+        every = ("x", *group)
+    else:
+        work, body = mesh, local
+        group, every = "shard", ("rep", "shard")
+    row, vec, mat = P(every, None), P(group), P(group, None)
+    return jax.shard_map(
+        body,
+        mesh=work,
+        in_specs=(row, row, P(), P(), vec, vec, mat, vec, mat, vec, vec, vec, mat, vec, mat, vec),
+        out_specs=(row, row, vec, vec, mat, vec, mat, vec, vec, vec, mat, vec, mat, vec),
+        check_vma=False,
+    )

time: 949 us -> 414 us (0.44)
  waiting for transfers between devices: 664 us -> 122 us
  blocking collectives: 148 us -> 0 us
  local copies, waits for them, and re-layouts: 24.8 us -> 128 us
  starting transfers between devices: 0.8 us -> 57.6 us
  other arithmetic: 12.3 us -> 41.3 us
  matrix products: 81.1 us -> 55.7 us
  between operations: 17.5 us -> 2.02 us
    reduce_scatter x4 -> x0, waiting for transfers between devices: 541 us -> none  [the longest x1 182 us: local(): lax.psum_scatter(up_weight_grad, 'shard', scatter_dimension=0, tiled=True)]
    unnamed x2 -> x0, blocking collectives: 123 us -> none
    ppermute x0 -> x56, waiting for transfers between devices: none -> 122 us  [the longest x49 109 us: swap(): return lax.ppermute(values, axes[0], PAIR)]
    all_gather x4 -> x0, waiting for transfers between devices: 118 us -> none  [the longest x1 68.4 us: local(): lax.all_gather(down_weight, 'shard', axis=0, tiled=True)]
    ppermute x0 -> x56, starting transfers between devices: none -> 57.6 us  [the longest x49 48.1 us: swap(): return lax.ppermute(values, axes[0], PAIR)]
    reshape x0 -> x13, local copies, waits for them, and re-layouts: none -> 24.3 us  [the longest x2 6.11 us: grouped(): grad_mixed = low(grad_lead[:, :2 * HEAD]).reshape(BLOCKS, cap, 2, HEAD)]
    concatenate x0 -> x11, local copies, waits for them, and re-layouts: none -> 20.9 us  [the longest x7 12 us: rotate(): jnp.concatenate([turned_lead, turned_trail, vectors[..., ROT:]], axis=-1)]
    all_gather x1 -> x0, blocking collectives: 19.4 us -> none  [local(): lax.all_gather(up_bias, 'shard', axis=0, tiled=True)]
  transfers between devices with their start and end apart: 9 -> 56, of which waited for: 8 -> 28; matrix products, arithmetic and copies ran while one was open for 11% -> 33% of each run, Pallas kernels for 0% -> 0%
where the time goes in v1:
time: 414 us; the launch traced here: 407 us
  local copies, waits for them, and re-layouts  128 us (31%)
  waiting for transfers between devices  122 us (29%)
  starting transfers between devices  57.6 us (14%)
  matrix products  55.7 us (13%)
  other arithmetic  41.3 us (10%)
    ppermute x49, waiting for transfers between devices, swap(): return lax.ppermute(values, axes[0], PAIR)  109 us
    ppermute x49, starting transfers between devices, swap(): return lax.ppermute(values, axes[0], PAIR)  48.1 us
    dot_general x3, matrix products, across(): lax.dot_general(left, right, (((1,), (1,)), ((), ())), preferred_element_...  17 us
    unnamed x119, local copies, waits for them, and re-layouts  15.6 us
    concatenate x7, local copies, waits for them, and re-layouts, rotate(): jnp.concatenate([turned_lead, turned_trail, vectors[..., ROT:]], axis=-1)  12 us
    dot_general x1, matrix products, grouped(): jnp.dot(input_two, up_full, preferred_element_type=jnp.float32) + up_offset  10.7 us
    dot_general x3, matrix products, contract_rows(): lax.dot_general(left, right, (((0,), (0,)), ((), ())), preferred_element_...  9.49 us
    convert_element_type x4, local copies, waits for them, and re-layouts, wide(): return values.astype(jnp.float32)  8.71 us
  transfers between devices with their start and end apart: 56, of which 28 were waited for; matrix products, arithmetic and copies ran while one was open for 33% of the time, Pallas kernels for 0%

profile of v1, /device:TPU:0, one launch (start us, length us, event | category | flops | bytes accessed | tf_op | source)
XLA Modules:
  0.0 406.8 jit_solution(12954428437972508878)
XLA Ops:
  2.3 4.0 collective-permute-start.21
  7.9 2.5 collective-permute-start.29
  10.8 5.4 %concatenate.159 = bf16[832]{0:T(1024)(128)(2,1)S(1)} concatenate(bf16[64]{0:T(256)(128)(2,1)} %param.20, bf16[64]{0:T(256)(128)(2,1)} %param.21, bf16[64]{0:T(256)(128)(2,1)} %param.26, bf16[64]{0:T(256)(128)(2,1)} %param.27, bf16[64]{0:T(256)(128)(2,1)} %param.25, bf16[64]{0:T(256)(128)(2,1)} %param.31, bf16[192]{0:T(256)(128)(2,1)} %param.23, bf16[256]{0:T(256)(128)(2,1)} %param.29), dimensions={0} | concatenate | bytes 3328 | tf_op jit(solution)/shard_map/concatenate | solution.py:364
  23.7 2.2 reshape.832
  28.8 2.5 reshape.827
  40.7 2.6 collective-permute-done.5
  63.5 3.6 collective-permute-done.13
  67.1 3.5 collective-permute-start.18
  70.7 2.6 collective-permute-done.18
  74.6 3.7 collective-permute-start.27
  80.0 3.8 collective-permute-done.19
  85.2 2.1 collective-permute-done.27
  94.9 9.3 %collective-permute-done = bf16[176,1024]{1,0:T(8,128)(2,1)S(1)} collective-permute-done((bf16[176,1024]{1,0:T(8,128)(2,1)S(1)}, bf16[176,1024]{1,0:T(8,128)(2,1)S(1)}, u32[]{:S(2)}, u32[]{:S(2)}) %collective-permute-start) | collective-permute-done | bytes 360480 | tf_op jit(solution)/shard_map/ppermute | solution.py:292
  104.7 2.3 pad_maximum_fusion.2
  109.4 2.5 collective-permute-done.10
  112.6 9.7 %collective-permute-done.22 = bf16[128,1024]{1,0:T(8,128)(2,1)S(1)} collective-permute-done((bf16[128,1024]{1,0:T(8,128)(2,1)}, bf16[128,1024]{1,0:T(8,128)(2,1)S(1)}, u32[]{:S(2)}, u32[]{:S(2)}) %collective-permute-start.22) | collective-permute-done | bytes 262176 | tf_op jit(solution)/shard_map/ppermute | solution.py:292
  126.6 3.5 collective-permute-done.12
  130.4 3.5 collective-permute-done.17
  147.0 2.3 concatenate.170
  150.6 2.6 convert_element_type.239
  156.3 2.6 constant_dynamic-update-slice_fusion.5
  158.8 4.3 %fusion.46 = f32[1408,640]{1,0:T(8,128)S(1)} fusion(bf16[1408,1024]{1,0:T(8,128)(2,1)} %constant_dynamic-update-slice_fusion.5, bf16[512,1024]{1,0:T(8,128)(2,1)S(1)} %bitcast.331, bf16[64,1024]{1,0:T(8,128)(2,1)S(1)} %copy-done.31, bf16[64,1024]{1,0:T(8,128)(2,1)S(1)} %copy-done.30), kind=kOutput, calls=%fused_computation.108 | convolution fusion | flops 1849425920 | bytes 7798784 | tf_op jit(solution)/shard_map/dot_general | solution.py:73
  165.7 3.2 reshape.858
  168.9 2.9 copy.130
  173.1 2.2 copy_dynamic-update-slice_fusion
  175.4 4.2 %fusion.125 = (f32[8,2,176]{2,1,0:T(2,128)S(1)}, f32[8,2,176,176]{2,3,1,0:T(8,128)}) fusion(pred[8,176,176]{1,2,0:T(8,128)(4,1)} %compare_and_fusion, bf16[8,176,2,64]{1,3,2,0:T(8,128)(2,1)} %get-tuple-element.133, bf16[8,176,2,64]{1,3,2,0:T(8,128)(2,1)} %get-tuple-element.132), kind=kOutput, calls=%fused_computation.358 | convolution fusion | flops 65421488 | bytes 2962432 | tf_op jit(solution)/shard_map/sub | solution.py:438
  179.5 3.3 fusion.26
  189.0 3.0 copy.149
  192.0 2.7 reshape.857
  194.6 10.7 %convert_reduce_fusion.1 = (f32[512]{0:T(512)S(1)}, bf16[1408,512]{1,0:T(8,128)(2,1)S(1)}, f32[1408,512]{1,0:T(8,128)S(1)}, f32[1408,512]{1,0:T(8,128)S(1)}) fusion(f32[1408,640]{1,0:T(8,128)} %copy-done.34, f32[512]{0:T(512)S(1)} %bitcast.341, bf16[1024,512]{1,0:T(8,128)(2,1)} %bitcast.333, bf16[1408,1024]{1,0:T(8,128)(2,1)S(1)} %constant_dynamic-update-slice_fusion, ...), kind=kOutput, calls=%fused_computation.22 | convolution fusion | flops 1539112448 | bytes 14048256 | tf_op jit(solution)/shard_map/dot_general | solution.py:442
  207.3 2.3 fusion.28
  209.6 4.0 convolution_convert_fusion
  216.1 3.4 fusion.115
  219.4 4.2 %fusion.126 = f32[1408,1024]{1,0:T(8,128)} fusion(bf16[1408,512]{1,0:T(8,128)(2,1)S(1)} %get-tuple-element.23, bf16[1024,512]{1,0:T(8,128)(2,1)S(1)} %bitcast.334), kind=kOutput, calls=%fused_computation.359 | convolution fusion | flops 1476395008 | bytes 8257536 | tf_op jit(solution)/shard_map/dot_general | solution.py:73
  224.7 2.3 stack_reshape.4
  227.0 2.8 copy.133
  229.8 2.5 mul.410
  232.3 2.8 copy.135
  235.1 2.5 mul.419
  244.4 2.1 fusion.48
  247.9 2.6 slice.250
  253.2 8.5 %fusion.118 = (f32[1024]{0:T(1024)}, f32[1024]{0:T(1024)}, bf16[1408,1024]{1,0:T(8,128)(2,1)}, f32[1024]{0:T(1024)}, f32[1024]{0:T(1024)}, /*index=5*/bf16[1024,1408]{0,1:T(8,128)(2,1)}) fusion(f32[1408,1024]{1,0:T(8,128)} %fusion.126, f32[1408]{0:T(1024)S(1)} %add_rsqrt_fusion, f32[1408]{0:T(1024)S(1)} %broadcast_multiply_fusion.1, ...), kind=kOutput, calls=%fused_computation.353 | convolution fusion | flops 1130360832 | bytes 16325632 | tf_op jit(solution)/shard_map/dot_general | solution.py:73
  266.1 2.6 slice.266
  268.7 2.8 copy.139
  271.6 3.9 fusion.127
  278.5 8.4 %collective-permute-done.46 = bf16[64,1024]{1,0:T(8,128)(2,1)S(1)} collective-permute-done((bf16[64,1024]{1,0:T(8,128)(2,1)S(1)}, bf16[64,1024]{1,0:T(8,128)(2,1)S(1)}, u32[]{:S(2)}, u32[]{:S(2)}) %collective-permute-start.46) | collective-permute-done | bytes 131104 | tf_op jit(solution)/shard_map/ppermute | solution.py:521
  287.0 2.2 collective-permute-start.47
  289.4 2.7 collective-permute-done.47
  292.1 2.9 collective-permute-start.41
  298.3 12.4 %collective-permute-done.41 = bf16[2,2,64,384]{3,2,1,0:T(8,128)(2,1)S(1)} collective-permute-done((bf16[2,2,64,384]{3,2,1,0:T(8,128)(2,1)S(1)}, bf16[2,2,64,384]{3,2,1,0:T(8,128)(2,1)S(1)}, u32[]{:S(2)}, u32[]{:S(2)}) %collective-permute-start.41) | collective-permute-done | bytes 196640 | tf_op jit(solution)/shard_map/ppermute | solution.py:292
  313.2 7.6 %collective-permute-done.54 = bf16[128,1024]{1,0:T(8,128)(2,1)S(1)} collective-permute-done((bf16[128,1024]{1,0:T(8,128)(2,1)S(1)}, bf16[128,1024]{1,0:T(8,128)(2,1)S(1)}, u32[]{:S(2)}, u32[]{:S(2)}) %collective-permute-start.54) | collective-permute-done | bytes 262176 | tf_op jit(solution)/shard_map/ppermute | solution.py:292
  323.3 2.6 collective-permute-done.49
  326.1 2.3 collective-permute-start.44
  328.5 5.6 %collective-permute-done.44 = bf16[2,2,64,384]{3,2,1,0:T(8,128)(2,1)S(1)} collective-permute-done((bf16[2,2,64,384]{3,2,1,0:T(8,128)(2,1)S(1)}, bf16[2,2,64,384]{3,2,1,0:T(8,128)(2,1)S(1)}, u32[]{:S(2)}, u32[]{:S(2)}) %collective-permute-start.44) | collective-permute-done | bytes 196640 | tf_op jit(solution)/shard_map/ppermute | solution.py:292
  335.8 2.4 copy.141
  338.1 3.7 reshape.854
  342.8 2.7 convert_add_fusion
  353.1 11.5 %collective-permute-done.32 = bf16[176,1024]{1,0:T(8,128)(2,1)S(1)} collective-permute-done((bf16[176,1024]{1,0:T(8,128)(2,1)S(1)}, bf16[176,1024]{1,0:T(8,128)(2,1)S(1)}, u32[]{:S(2)}, u32[]{:S(2)}) %collective-permute-start.32) | collective-permute-done | bytes 360480 | tf_op jit(solution)/shard_map/ppermute | solution.py:292
  364.6 3.2 collective-permute-start.25
  368.3 10.9 %collective-permute-done.24 = bf16[176,1024]{1,0:T(8,128)(2,1)S(1)} collective-permute-done((bf16[176,1024]{1,0:T(8,128)(2,1)S(1)}, bf16[176,1024]{1,0:T(8,128)(2,1)S(1)}, u32[]{:S(2)}, u32[]{:S(2)}) %collective-permute-start.24) | collective-permute-done | bytes 360480 | tf_op jit(solution)/shard_map/ppermute | solution.py:292
  379.3 2.4 collective-permute-done.25
  388.6 2.1 collective-permute-done.36
  391.9 3.0 collective-permute-done.37
  395.1 4.8 %collective-permute-done.38 = f32[16,768]{1,0:T(8,128)S(1)} collective-permute-done((f32[16,768]{1,0:T(8,128)S(1)}, f32[16,768]{1,0:T(8,128)S(1)}, u32[]{:S(2)}, u32[]{:S(2)}) %collective-permute-start.38) | collective-permute-done | bytes 49184 | tf_op jit(solution)/shard_map/ppermute | solution.py:292
  (374 shorter events, 148.9 us)
Async XLA Ops:
  2.3 104.7 %collective-permute-start.21 = (bf16[128,1024]{1,0:T(8,128)(2,1)}, bf16[128,1024]{1,0:T(8,128)(2,1)}, u32[]{:S(2)}, u32[]{:S(2)}) collective-permute-start(bf16[128,1024]{1,0:T(8,128)(2,1)} %dynamic-slice_bitcast_fusion), channel_id=1, source_target_pairs={{0,8},{8,0},{1,9},{9,1},{2,10},{10,2},{3,11},{11,3},{4,12},{12,4},... | collective-permute-start | bytes 786440 | tf_op jit(solution)/shard_map/ppermute | solution.py:292
  6.4 72.0 %collective-permute-start.20 = (bf16[128,1024]{1,0:T(8,128)(2,1)}, bf16[128,1024]{1,0:T(8,128)(2,1)}, u32[]{:S(2)}, u32[]{:S(2)}) collective-permute-start(bf16[128,1024]{1,0:T(8,128)(2,1)} %dynamic-slice_bitcast_fusion), channel_id=1, source_target_pairs={{0,2},{2,0},{1,3},{3,1},{4,6},{6,4},{5,7},{7,5},{8,10},{10,8},{9,1... | collective-permute-start | bytes 786440 | tf_op jit(solution)/shard_map/ppermute | solution.py:292
  7.9 83.7 %collective-permute-start.29 = (bf16[176,1024]{1,0:T(8,128)(2,1)}, bf16[176,1024]{1,0:T(8,128)(2,1)}, u32[]{:S(2)}, u32[]{:S(2)}) collective-permute-start(bf16[176,1024]{1,0:T(8,128)(2,1)} %param.17), channel_id=1, source_target_pairs={{0,20},{4,16},{16,4},{20,0},{1,21},{5,17},{17,5},{21,1},{2,22},{6,... | collective-permute-start | bytes 1081352 | tf_op jit(solution)/shard_map/ppermute | solution.py:293
  10.4 79.4 %collective-permute-start.28 = (bf16[176,1024]{1,0:T(8,128)(2,1)}, bf16[176,1024]{1,0:T(8,128)(2,1)}, u32[]{:S(2)}, u32[]{:S(2)}) collective-permute-start(bf16[176,1024]{1,0:T(8,128)(2,1)} %param.17), channel_id=1, source_target_pairs={{0,4},{4,0},{1,5},{5,1},{2,6},{6,2},{3,7},{7,3},{8,12},{12,8},{9,1... | collective-permute-start | bytes 1081352 | tf_op jit(solution)/shard_map/ppermute | solution.py:292
  16.3 23.3 %collective-permute-start.4 = (bf16[1,832]{1,0:T(2,128)(2,1)S(1)}, bf16[1,832]{1,0:T(2,128)(2,1)S(1)}, u32[]{:S(2)}, u32[]{:S(2)}) collective-permute-start(bf16[1,832]{1,0:T(2,128)(2,1)S(1)} %broadcast_in_dim.211), channel_id=1, source_target_pairs={{0,1},{1,0},{2,3},{3,2},{4,5},{5,4},{6,7},{7,6},{8,9},{9,8},{10,11... | collective-permute-start | bytes 5000 | tf_op jit(solution)/shard_map/ppermute | solution.py:292
  37.4 47.7 %copy-start = (bf16[176,1024]{1,0:T(8,128)(2,1)S(1)}, bf16[176,1024]{1,0:T(8,128)(2,1)}, u32[]{:S(2)}) copy-start(bf16[176,1024]{1,0:T(8,128)(2,1)} %param.16) | copy-start | bytes 1081348
  39.6 3.7 collective-permute-start.5
  43.3 3.7 collective-permute-start.6
  47.1 4.8 %collective-permute-start.7 = (bf16[8,832]{1,0:T(8,128)(2,1)S(1)}, bf16[8,832]{1,0:T(8,128)(2,1)S(1)}, u32[]{:S(2)}, u32[]{:S(2)}) collective-permute-start(bf16[8,832]{1,0:T(8,128)(2,1)S(1)} %pad_maximum_fusion.22), channel_id=1, source_target_pairs={{0,8},{8,0},{1,9},{9,1},{2,10},{10,2},{3,11},{11,3},{4,12},{12,4},... | collective-permute-start | bytes 39944 | tf_op jit(solution)/shard_map/ppermute | solution.py:292
  51.9 10.1 %collective-permute-start.8 = (bf16[2,64,384]{2,1,0:T(8,128)(2,1)}, bf16[2,64,384]{2,1,0:T(8,128)(2,1)}, u32[]{:S(2)}, u32[]{:S(2)}) collective-permute-start(bf16[2,64,384]{2,1,0:T(8,128)(2,1)} %dynamic-slice_bitcast_fusion.4), channel_id=1, source_target_pairs={{0,4},{4,0},{1,5},{5,1},{2,6},{6,2},{3,7},{7,3},{8,12},{12,8},{9,1... | collective-permute-start | bytes 294920 | tf_op jit(solution)/shard_map/ppermute | solution.py:292
  58.3 157.7 %copy-start.40 = (f32[1024]{0:T(1024)}, f32[1024]{0:T(1024)S(1)}, u32[]{:S(2)}) copy-start(f32[1024]{0:T(1024)S(1)} %reshape.849) | copy-start | bytes 12292
  59.1 77.5 %copy-start.42 = (f32[1024]{0:T(1024)}, f32[1024]{0:T(1024)S(1)}, u32[]{:S(2)}) copy-start(f32[1024]{0:T(1024)S(1)} %reshape.846) | copy-start | bytes 12292
  59.9 76.7 %copy-start.44 = (f32[1024]{0:T(1024)}, f32[1024]{0:T(1024)S(1)}, u32[]{:S(2)}) copy-start(f32[1024]{0:T(1024)S(1)} %reshape.847) | copy-start | bytes 12292
  61.9 5.2 %collective-permute-start.13 = (bf16[2,64,512]{2,1,0:T(8,128)(2,1)}, bf16[2,64,512]{2,1,0:T(8,128)(2,1)S(1)}, u32[]{:S(2)}, u32[]{:S(2)}) collective-permute-start(bf16[2,64,512]{2,1,0:T(8,128)(2,1)} %dynamic-slice_bitcast_fusion.2), channel_id=1, source_target_pairs={{0,4},{4,0},{1,5},{5,1},{2,6},{6,2},{3,7},{7,3},{8,12},{12,8},{9,1... | collective-permute-start | bytes 393224 | tf_op jit(solution)/shard_map/ppermute | solution.py:292
  67.1 6.1 %collective-permute-start.18 = (bf16[64,1024]{1,0:T(8,128)(2,1)}, bf16[64,1024]{1,0:T(8,128)(2,1)S(1)}, u32[]{:S(2)}, u32[]{:S(2)}) collective-permute-start(bf16[64,1024]{1,0:T(8,128)(2,1)} %param.24), channel_id=1, source_target_pairs={{0,8},{24,16},{1,9},{25,17},{2,10},{26,18},{3,11},{27,19},{4,12},{... | collective-permute-start | bytes 393224 | tf_op jit(solution)/shard_map/ppermute | solution.py:398
  73.3 1.3 collective-permute-start.9
  74.6 12.7 %collective-permute-start.27 = (bf16[176,1024]{1,0:T(8,128)(2,1)}, bf16[176,1024]{1,0:T(8,128)(2,1)S(1)}, u32[]{:S(2)}, u32[]{:S(2)}) collective-permute-start(bf16[176,1024]{1,0:T(8,128)(2,1)} %param.17), channel_id=1, source_target_pairs={{0,16},{16,0},{1,17},{17,1},{2,18},{18,2},{3,19},{19,3},{4,20},{20... | collective-permute-start | bytes 1081352 | tf_op jit(solution)/shard_map/ppermute | solution.py:292
  78.4 26.3 %copy-start.2 = (bf16[176,1024]{1,0:T(8,128)(2,1)S(1)}, bf16[176,1024]{1,0:T(8,128)(2,1)}, u32[]{:S(2)}) copy-start(bf16[176,1024]{1,0:T(8,128)(2,1)} %param.17) | copy-start | bytes 1081348
  78.4 5.3 %collective-permute-start.19 = (bf16[64,1024]{1,0:T(8,128)(2,1)S(1)}, bf16[64,1024]{1,0:T(8,128)(2,1)S(1)}, u32[]{:S(2)}, u32[]{:S(2)}) collective-permute-start(bf16[64,1024]{1,0:T(8,128)(2,1)S(1)} %broadcast_select_fusion.12), channel_id=1, source_target_pairs={{0,2},{2,0},{1,3},{3,1},{4,6},{6,4},{5,7},{7,5},{8,10},{10,8},{9,1... | collective-permute-start | bytes 393224 | tf_op jit(solution)/shard_map/ppermute | solution.py:292
  83.7 1.3 collective-permute-start.14
  85.1 22.1 %collective-permute-start.2 = (bf16[176,1024]{1,0:T(8,128)(2,1)S(1)}, bf16[176,1024]{1,0:T(8,128)(2,1)S(1)}, u32[]{:S(2)}, u32[]{:S(2)}) collective-permute-start(bf16[176,1024]{1,0:T(8,128)(2,1)S(1)} %copy-done), channel_id=1, source_target_pairs={{0,20},{4,16},{16,4},{20,0},{1,21},{5,17},{17,5},{21,1},{2,22},{6,... | collective-permute-start | bytes 1081352 | tf_op jit(solution)/shard_map/ppermute | solution.py:293
  87.3 16.9 %collective-permute-start = (bf16[176,1024]{1,0:T(8,128)(2,1)S(1)}, bf16[176,1024]{1,0:T(8,128)(2,1)S(1)}, u32[]{:S(2)}, u32[]{:S(2)}) collective-permute-start(bf16[176,1024]{1,0:T(8,128)(2,1)S(1)} %copy-done), channel_id=1, source_target_pairs={{0,16},{16,0},{1,17},{17,1},{2,18},{18,2},{3,19},{19,3},{4,20},{20... | collective-permute-start | bytes 1081352 | tf_op jit(solution)/shard_map/ppermute | solution.py:292
  89.8 18.9 %collective-permute-start.1 = (bf16[176,1024]{1,0:T(8,128)(2,1)S(1)}, bf16[176,1024]{1,0:T(8,128)(2,1)S(1)}, u32[]{:S(2)}, u32[]{:S(2)}) collective-permute-start(bf16[176,1024]{1,0:T(8,128)(2,1)S(1)} %copy-done), channel_id=1, source_target_pairs={{0,4},{4,0},{1,5},{5,1},{2,6},{6,2},{3,7},{7,3},{8,12},{12,8},{9,1... | collective-permute-start | bytes 1081352 | tf_op jit(solution)/shard_map/ppermute | solution.py:292
  91.5 20.5 %collective-permute-start.11 = (bf16[2,2,64,384]{3,2,1,0:T(8,128)(2,1)S(1)}, bf16[2,2,64,384]{3,2,1,0:T(8,128)(2,1)S(1)}, u32[]{:S(2)}, u32[]{:S(2)}) collective-permute-start(bf16[2,2,64,384]{3,2,1,0:T(8,128)(2,1)S(1)} %pad_maximum_fusion.20), channel_id=1, source_target_pairs={{0,8},{8,0},{1,9},{9,1},{2,10},{10,2},{3,11},{11,3},{4,12},{12,4},... | collective-permute-start | bytes 589832 | tf_op jit(solution)/shard_map/ppermute | solution.py:292
  104.2 7.8 %collective-permute-start.10 = (bf16[2,2,64,384]{3,2,1,0:T(8,128)(2,1)S(1)}, bf16[2,2,64,384]{3,2,1,0:T(8,128)(2,1)S(1)}, u32[]{:S(2)}, u32[]{:S(2)}) collective-permute-start(bf16[2,2,64,384]{3,2,1,0:T(8,128)(2,1)S(1)} %pad_maximum_fusion.20), channel_id=1, source_target_pairs={{0,2},{2,0},{1,3},{3,1},{4,6},{6,4},{5,7},{7,5},{8,10},{10,8},{9,1... | collective-permute-start | bytes 589832 | tf_op jit(solution)/shard_map/ppermute | solution.py:292
  107.0 16.8 %collective-permute-start.16 = (bf16[2,2,64,512]{3,2,1,0:T(8,128)(2,1)S(1)}, bf16[2,2,64,512]{3,2,1,0:T(8,128)(2,1)S(1)}, u32[]{:S(2)}, u32[]{:S(2)}) collective-permute-start(bf16[2,2,64,512]{3,2,1,0:T(8,128)(2,1)S(1)} %pad_maximum_fusion.18), channel_id=1, source_target_pairs={{0,8},{8,0},{1,9},{9,1},{2,10},{10,2},{3,11},{11,3},{4,12},{12,4},... | collective-permute-start | bytes 786440 | tf_op jit(solution)/shard_map/ppermute | solution.py:292
  107.2 19.3 %collective-permute-start.15 = (bf16[2,2,64,512]{3,2,1,0:T(8,128)(2,1)S(1)}, bf16[2,2,64,512]{3,2,1,0:T(8,128)(2,1)S(1)}, u32[]{:S(2)}, u32[]{:S(2)}) collective-permute-start(bf16[2,2,64,512]{3,2,1,0:T(8,128)(2,1)S(1)} %pad_maximum_fusion.18), channel_id=1, source_target_pairs={{0,2},{2,0},{1,3},{3,1},{4,6},{6,4},{5,7},{7,5},{8,10},{10,8},{9,1... | collective-permute-start | bytes 786440 | tf_op jit(solution)/shard_map/ppermute | solution.py:292
  108.7 13.5 %collective-permute-start.22 = (bf16[128,1024]{1,0:T(8,128)(2,1)}, bf16[128,1024]{1,0:T(8,128)(2,1)S(1)}, u32[]{:S(2)}, u32[]{:S(2)}) collective-permute-start(bf16[128,1024]{1,0:T(8,128)(2,1)} %collective-permute-done.21), channel_id=1, source_target_pairs={{0,2},{2,0},{1,3},{3,1},{4,6},{6,4},{5,7},{7,5},{8,10},{10,8},{9,1... | collective-permute-start | bytes 786440 | tf_op jit(solution)/shard_map/ppermute | solution.py:292
  112.0 44.3 %collective-permute-start.30 = (bf16[704,1024]{1,0:T(8,128)(2,1)}, bf16[704,1024]{1,0:T(8,128)(2,1)}, u32[]{:S(2)}, u32[]{:S(2)}) collective-permute-start(bf16[704,1024]{1,0:T(8,128)(2,1)} %pad_maximum_fusion.2), channel_id=1, source_target_pairs={{0,1},{1,0},{2,3},{3,2},{4,5},{5,4},{6,7},{7,6},{8,9},{9,8},{10,11... | collective-permute-start | bytes 4325384 | tf_op jit(solution)/shard_map/ppermute | solution.py:292
  112.0 23.0 %collective-permute-start.3 = (bf16[704,1024]{1,0:T(8,128)(2,1)S(1)}, bf16[704,1024]{1,0:T(8,128)(2,1)S(1)}, u32[]{:S(2)}, u32[]{:S(2)}) collective-permute-start(bf16[704,1024]{1,0:T(8,128)(2,1)S(1)} %pad_maximum_fusion.1), channel_id=1, source_target_pairs={{0,1},{1,0},{2,3},{3,2},{4,5},{5,4},{6,7},{7,6},{8,9},{9,8},{10,11... | collective-permute-start | bytes 4325384 | tf_op jit(solution)/shard_map/ppermute | solution.py:292
  122.2 7.8 %collective-permute-start.12 = (bf16[2,2,64,384]{3,2,1,0:T(8,128)(2,1)S(1)}, bf16[2,2,64,384]{3,2,1,0:T(8,128)(2,1)S(1)}, u32[]{:S(2)}, u32[]{:S(2)}) collective-permute-start(bf16[2,2,64,384]{3,2,1,0:T(8,128)(2,1)S(1)} %collective-permute-done.11), channel_id=1, source_target_pairs={{0,2},{2,0},{1,3},{3,1},{4,6},{6,4},{5,7},{7,5},{8,10},{10,8},{9,1... | collective-permute-start | bytes 589832 | tf_op jit(solution)/shard_map/ppermute | solution.py:292
  123.9 10.0 %collective-permute-start.17 = (bf16[2,2,64,512]{3,2,1,0:T(8,128)(2,1)S(1)}, bf16[2,2,64,512]{3,2,1,0:T(8,128)(2,1)S(1)}, u32[]{:S(2)}, u32[]{:S(2)}) collective-permute-start(bf16[2,2,64,512]{3,2,1,0:T(8,128)(2,1)S(1)} %collective-permute-done.16), channel_id=1, source_target_pairs={{0,2},{2,0},{1,3},{3,1},{4,6},{6,4},{5,7},{7,5},{8,10},{10,8},{9,1... | collective-permute-start | bytes 786440 | tf_op jit(solution)/shard_map/ppermute | solution.py:292
  243.7 33.4 %collective-permute-start.45 = (bf16[64,1024]{1,0:T(8,128)(2,1)S(1)}, bf16[64,1024]{1,0:T(8,128)(2,1)S(1)}, u32[]{:S(2)}, u32[]{:S(2)}) collective-permute-start(bf16[64,1024]{1,0:T(8,128)(2,1)S(1)} %fusion.62), channel_id=1, source_target_pairs={{0,2},{2,0},{1,3},{3,1},{4,6},{6,4},{5,7},{7,5},{8,10},{10,8},{9,1... | collective-permute-start | bytes 393224 | tf_op jit(solution)/shard_map/ppermute | solution.py:292
  246.5 49.2 %collective-permute-start.53 = (bf16[2,128,1024]{2,1,0:T(8,128)(2,1)}, bf16[2,128,1024]{2,1,0:T(8,128)(2,1)}, u32[]{:S(2)}, u32[]{:S(2)}) collective-permute-start(bf16[2,128,1024]{2,1,0:T(8,128)(2,1)} %fusion.48), channel_id=1, source_target_pairs={{0,2},{2,0},{1,3},{3,1},{4,6},{6,4},{5,7},{7,5},{8,10},{10,8},{9,1... | collective-permute-start | bytes 1572872 | tf_op jit(solution)/shard_map/ppermute | solution.py:292
  250.5 98.7 %collective-permute-start.23 = (bf16[704,1024]{1,0:T(8,128)(2,1)}, bf16[704,1024]{1,0:T(8,128)(2,1)}, u32[]{:S(2)}, u32[]{:S(2)}) collective-permute-start(bf16[704,1024]{1,0:T(8,128)(2,1)} %slice.250), channel_id=1, source_target_pairs={{0,1},{1,0},{2,3},{3,2},{4,5},{5,4},{6,7},{7,6},{8,9},{9,8},{10,11... | collective-permute-start | bytes 4325384 | tf_op jit(solution)/shard_map/ppermute | solution.py:292
  252.6 44.5 %collective-permute-start.48 = (bf16[2,2,2,64,512]{4,3,2,1,0:T(8,128)(2,1)}, bf16[2,2,2,64,512]{4,3,2,1,0:T(8,128)(2,1)}, u32[]{:S(2)}, u32[]{:S(2)}) collective-permute-start(bf16[2,2,2,64,512]{4,3,2,1,0:T(8,128)(2,1)} %fusion.47), channel_id=1, source_target_pairs={{0,2},{2,0},{1,3},{3,1},{4,6},{6,4},{5,7},{7,5},{8,10},{10,8},{9,1... | collective-permute-start | bytes 1572872 | tf_op jit(solution)/shard_map/ppermute | solution.py:292
  275.6 11.4 %collective-permute-start.40 = (bf16[2,2,2,64,384]{4,3,2,1,0:T(8,128)(2,1)S(1)}, bf16[2,2,2,64,384]{4,3,2,1,0:T(8,128)(2,1)S(1)}, u32[]{:S(2)}, u32[]{:S(2)}) collective-permute-start(bf16[2,2,2,64,384]{4,3,2,1,0:T(8,128)(2,1)S(1)} %fusion.54), channel_id=1, source_target_pairs={{0,2},{2,0},{1,3},{3,1},{4,6},{6,4},{5,7},{7,5},{8,10},{10,8},{9,1... | collective-permute-start | bytes 1179656 | tf_op jit(solution)/shard_map/ppermute | solution.py:292
  277.1 9.8 %collective-permute-start.46 = (bf16[64,1024]{1,0:T(8,128)(2,1)S(1)}, bf16[64,1024]{1,0:T(8,128)(2,1)S(1)}, u32[]{:S(2)}, u32[]{:S(2)}) collective-permute-start(bf16[64,1024]{1,0:T(8,128)(2,1)S(1)} %fusion.61), channel_id=1, source_target_pairs={{8,0},{16,24},{9,1},{17,25},{10,2},{18,26},{11,3},{19,27},{12,4},{... | collective-permute-start | bytes 393224 | tf_op jit(solution)/shard_map/ppermute | solution.py:521
  286.9 55.9 %collective-permute-start.31 = (bf16[704,1024]{1,0:T(8,128)(2,1)}, bf16[704,1024]{1,0:T(8,128)(2,1)}, u32[]{:S(2)}, u32[]{:S(2)}) collective-permute-start(bf16[704,1024]{1,0:T(8,128)(2,1)} %slice.266), channel_id=1, source_target_pairs={{0,1},{1,0},{2,3},{3,2},{4,5},{5,4},{6,7},{7,6},{8,9},{9,8},{10,11... | collective-permute-start | bytes 4325384 | tf_op jit(solution)/shard_map/ppermute | solution.py:292
  287.0 5.1 %collective-permute-start.47 = (bf16[64,1024]{1,0:T(8,128)(2,1)S(1)}, bf16[64,1024]{1,0:T(8,128)(2,1)S(1)}, u32[]{:S(2)}, u32[]{:S(2)}) collective-permute-start(bf16[64,1024]{1,0:T(8,128)(2,1)S(1)} %add_convert_fusion.2), channel_id=1, source_target_pairs={{0,16},{24,8},{1,17},{25,9},{2,18},{26,10},{3,19},{27,11},{4,20},{... | collective-permute-start | bytes 393224 | tf_op jit(solution)/shard_map/ppermute | solution.py:523
  292.1 18.6 %collective-permute-start.41 = (bf16[2,2,64,384]{3,2,1,0:T(8,128)(2,1)S(1)}, bf16[2,2,64,384]{3,2,1,0:T(8,128)(2,1)S(1)}, u32[]{:S(2)}, u32[]{:S(2)}) collective-permute-start(bf16[2,2,64,384]{3,2,1,0:T(8,128)(2,1)S(1)} %fusion.60), channel_id=1, source_target_pairs={{0,8},{8,0},{1,9},{9,1},{2,10},{10,2},{3,11},{11,3},{4,12},{12,4},... | collective-permute-start | bytes 589832 | tf_op jit(solution)/shard_map/ppermute | solution.py:292
  296.9 23.9 %collective-permute-start.54 = (bf16[128,1024]{1,0:T(8,128)(2,1)S(1)}, bf16[128,1024]{1,0:T(8,128)(2,1)S(1)}, u32[]{:S(2)}, u32[]{:S(2)}) collective-permute-start(bf16[128,1024]{1,0:T(8,128)(2,1)S(1)} %fusion.57), channel_id=1, source_target_pairs={{0,8},{8,0},{1,9},{9,1},{2,10},{10,2},{3,11},{11,3},{4,12},{12,4},... | collective-permute-start | bytes 786440 | tf_op jit(solution)/shard_map/ppermute | solution.py:292
  310.7 1.4 collective-permute-start.42
  310.9 15.0 %collective-permute-start.49 = (bf16[2,2,64,512]{3,2,1,0:T(8,128)(2,1)S(1)}, bf16[2,2,64,512]{3,2,1,0:T(8,128)(2,1)S(1)}, u32[]{:S(2)}, u32[]{:S(2)}) collective-permute-start(bf16[2,2,64,512]{3,2,1,0:T(8,128)(2,1)S(1)} %fusion.56), channel_id=1, source_target_pairs={{0,8},{8,0},{1,9},{9,1},{2,10},{10,2},{3,11},{11,3},{4,12},{12,4},... | collective-permute-start | bytes 786440 | tf_op jit(solution)/shard_map/ppermute | solution.py:292
  312.2 13.9 %collective-permute-start.43 = (bf16[2,64,384]{2,1,0:T(8,128)(2,1)S(1)}, bf16[2,64,384]{2,1,0:T(8,128)(2,1)S(1)}, u32[]{:S(2)}, u32[]{:S(2)}) collective-permute-start(bf16[2,64,384]{2,1,0:T(8,128)(2,1)S(1)} %fusion.76), channel_id=1, source_target_pairs={{0,4},{4,0},{1,5},{5,1},{2,6},{6,2},{3,7},{7,3},{8,12},{12,8},{9,1... | collective-permute-start | bytes 294920 | tf_op jit(solution)/shard_map/ppermute | solution.py:292
  321.5 66.0 %collective-permute-start.55 = (bf16[128,1024]{1,0:T(8,128)(2,1)}, bf16[128,1024]{1,0:T(8,128)(2,1)}, u32[]{:S(2)}, u32[]{:S(2)}) collective-permute-start(bf16[128,1024]{1,0:T(8,128)(2,1)} %fusion.49), channel_id=1, source_target_pairs={{0,16},{16,0},{1,17},{17,1},{2,18},{18,2},{3,19},{19,3},{4,20},{20... | collective-permute-start | bytes 786440 | tf_op jit(solution)/shard_map/ppermute | solution.py:292
  325.9 2.4 collective-permute-start.50
  326.1 8.0 %collective-permute-start.44 = (bf16[2,2,64,384]{3,2,1,0:T(8,128)(2,1)S(1)}, bf16[2,2,64,384]{3,2,1,0:T(8,128)(2,1)S(1)}, u32[]{:S(2)}, u32[]{:S(2)}) collective-permute-start(bf16[2,2,64,384]{3,2,1,0:T(8,128)(2,1)S(1)} %pad_maximum_fusion.21), channel_id=1, source_target_pairs={{0,16},{16,0},{1,17},{17,1},{2,18},{18,2},{3,19},{19,3},{4,20},{20... | collective-permute-start | bytes 589832 | tf_op jit(solution)/shard_map/ppermute | solution.py:292
  328.4 13.4 %collective-permute-start.51 = (bf16[2,64,512]{2,1,0:T(8,128)(2,1)S(1)}, bf16[2,64,512]{2,1,0:T(8,128)(2,1)}, u32[]{:S(2)}, u32[]{:S(2)}) collective-permute-start(bf16[2,64,512]{2,1,0:T(8,128)(2,1)S(1)} %fusion.64), channel_id=1, source_target_pairs={{0,4},{4,0},{1,5},{5,1},{2,6},{6,2},{3,7},{7,3},{8,12},{12,8},{9,1... | collective-permute-start | bytes 393224 | tf_op jit(solution)/shard_map/ppermute | solution.py:292
  345.6 19.1 %collective-permute-start.32 = (bf16[176,1024]{1,0:T(8,128)(2,1)S(1)}, bf16[176,1024]{1,0:T(8,128)(2,1)S(1)}, u32[]{:S(2)}, u32[]{:S(2)}) collective-permute-start(bf16[176,1024]{1,0:T(8,128)(2,1)S(1)} %get-tuple-element.38), channel_id=1, source_target_pairs={{0,16},{16,0},{1,17},{17,1},{2,18},{18,2},{3,19},{19,3},{4,20},{20... | collective-permute-start | bytes 1081352 | tf_op jit(solution)/shard_map/ppermute | solution.py:292
  347.4 17.2 %collective-permute-start.34 = (bf16[176,1024]{1,0:T(8,128)(2,1)S(1)}, bf16[176,1024]{1,0:T(8,128)(2,1)S(1)}, u32[]{:S(2)}, u32[]{:S(2)}) collective-permute-start(bf16[176,1024]{1,0:T(8,128)(2,1)S(1)} %get-tuple-element.39), channel_id=1, source_target_pairs={{0,20},{4,16},{16,4},{20,0},{1,21},{5,17},{17,5},{21,1},{2,22},{6,... | collective-permute-start | bytes 1081352 | tf_op jit(solution)/shard_map/ppermute | solution.py:293
  347.4 20.5 %collective-permute-start.33 = (bf16[176,1024]{1,0:T(8,128)(2,1)S(1)}, bf16[176,1024]{1,0:T(8,128)(2,1)S(1)}, u32[]{:S(2)}, u32[]{:S(2)}) collective-permute-start(bf16[176,1024]{1,0:T(8,128)(2,1)S(1)} %get-tuple-element.40), channel_id=1, source_target_pairs={{0,4},{4,0},{1,5},{5,1},{2,6},{6,2},{3,7},{7,3},{8,12},{12,8},{9,1... | collective-permute-start | bytes 1081352 | tf_op jit(solution)/shard_map/ppermute | solution.py:292
  351.2 30.5 %copy-start.3 = (bf16[176,1024]{1,0:T(8,128)(2,1)S(1)}, bf16[176,1024]{1,0:T(8,128)(2,1)}, u32[]{:S(2)}) copy-start(bf16[176,1024]{1,0:T(8,128)(2,1)} %param.17) | copy-start | bytes 1081348
  351.2 30.5 %copy-start.35 = (f32[1024]{0:T(1024)S(1)}, f32[1024]{0:T(1024)}, u32[]{:S(2)}) copy-start(f32[1024]{0:T(1024)} %reshape.852) | copy-start | bytes 12292
  351.2 30.5 %copy-start.36 = (f32[1024]{0:T(1024)S(1)}, f32[1024]{0:T(1024)}, u32[]{:S(2)}) copy-start(f32[1024]{0:T(1024)} %reshape.853) | copy-start | bytes 12292
  351.3 27.9 %collective-permute-start.24 = (bf16[176,1024]{1,0:T(8,128)(2,1)S(1)}, bf16[176,1024]{1,0:T(8,128)(2,1)S(1)}, u32[]{:S(2)}, u32[]{:S(2)}) collective-permute-start(bf16[176,1024]{1,0:T(8,128)(2,1)S(1)} %get-tuple-element.41), channel_id=1, source_target_pairs={{0,16},{16,0},{1,17},{17,1},{2,18},{18,2},{3,19},{19,3},{4,20},{20... | collective-permute-start | bytes 1081352 | tf_op jit(solution)/shard_map/ppermute | solution.py:292
  364.6 14.6 %collective-permute-start.26 = (bf16[176,1024]{1,0:T(8,128)(2,1)S(1)}, bf16[176,1024]{1,0:T(8,128)(2,1)S(1)}, u32[]{:S(2)}, u32[]{:S(2)}) collective-permute-start(bf16[176,1024]{1,0:T(8,128)(2,1)S(1)} %get-tuple-element.42), channel_id=1, source_target_pairs={{0,20},{4,16},{16,4},{20,0},{1,21},{5,17},{17,5},{21,1},{2,22},{6,... | collective-permute-start | bytes 1081352 | tf_op jit(solution)/shard_map/ppermute | solution.py:293
  364.6 17.0 %collective-permute-start.25 = (bf16[176,1024]{1,0:T(8,128)(2,1)S(1)}, bf16[176,1024]{1,0:T(8,128)(2,1)S(1)}, u32[]{:S(2)}, u32[]{:S(2)}) collective-permute-start(bf16[176,1024]{1,0:T(8,128)(2,1)S(1)} %get-tuple-element.43), channel_id=1, source_target_pairs={{0,4},{4,0},{1,5},{5,1},{2,6},{6,2},{3,7},{7,3},{8,12},{12,8},{9,1... | collective-permute-start | bytes 1081352 | tf_op jit(solution)/shard_map/ppermute | solution.py:292
  385.3 1.3 collective-permute-start.35
  385.4 9.6 %collective-permute-start.52 = (bf16[2,2,64,512]{3,2,1,0:T(8,128)(2,1)S(1)}, bf16[2,2,64,512]{3,2,1,0:T(8,128)(2,1)S(1)}, u32[]{:S(2)}, u32[]{:S(2)}) collective-permute-start(bf16[2,2,64,512]{3,2,1,0:T(8,128)(2,1)S(1)} %pad_maximum_fusion.19), channel_id=1, source_target_pairs={{0,16},{16,0},{1,17},{17,1},{2,18},{18,2},{3,19},{19,3},{4,20},{20... | collective-permute-start | bytes 786440 | tf_op jit(solution)/shard_map/ppermute | solution.py:292
  386.6 4.2 %collective-permute-start.36 = (f32[16,768]{1,0:T(8,128)S(1)}, f32[16,768]{1,0:T(8,128)S(1)}, u32[]{:S(2)}, u32[]{:S(2)}) collective-permute-start(f32[16,768]{1,0:T(8,128)S(1)} %add.436), channel_id=1, source_target_pairs={{0,2},{2,0},{1,3},{3,1},{4,6},{6,4},{5,7},{7,5},{8,10},{10,8},{9,1... | collective-permute-start | bytes 147464 | tf_op jit(solution)/shard_map/ppermute | solution.py:292
  390.7 4.2 %collective-permute-start.37 = (f32[16,768]{1,0:T(8,128)S(1)}, f32[16,768]{1,0:T(8,128)S(1)}, u32[]{:S(2)}, u32[]{:S(2)}) collective-permute-start(f32[16,768]{1,0:T(8,128)S(1)} %add.437), channel_id=1, source_target_pairs={{0,4},{4,0},{1,5},{5,1},{2,6},{6,2},{3,7},{7,3},{8,12},{12,8},{9,1... | collective-permute-start | bytes 147464 | tf_op jit(solution)/shard_map/ppermute | solution.py:292
  394.9 5.0 %collective-permute-start.38 = (f32[16,768]{1,0:T(8,128)S(1)}, f32[16,768]{1,0:T(8,128)S(1)}, u32[]{:S(2)}, u32[]{:S(2)}) collective-permute-start(f32[16,768]{1,0:T(8,128)S(1)} %add.438), channel_id=1, source_target_pairs={{0,8},{8,0},{1,9},{9,1},{2,10},{10,2},{3,11},{11,3},{4,12},{12,4},... | collective-permute-start | bytes 147464 | tf_op jit(solution)/shard_map/ppermute | solution.py:292
  399.9 4.3 %collective-permute-start.39 = (f32[16,768]{1,0:T(8,128)S(1)}, f32[16,768]{1,0:T(8,128)S(1)}, u32[]{:S(2)}, u32[]{:S(2)}) collective-permute-start(f32[16,768]{1,0:T(8,128)S(1)} %add.439), channel_id=1, source_target_pairs={{0,16},{16,0},{1,17},{17,1},{2,18},{18,2},{3,19},{19,3},{4,20},{20... | collective-permute-start | bytes 147464 | tf_op jit(solution)/shard_map/ppermute | solution.py:292
  (45 other events, 299.5 us)

commit v2 on v0

--- a/solution.py
+++ b/solution.py
@@ -3,7 +3,9 @@
 import jax
 import jax.numpy as jnp
 from jax import lax
-from jax.sharding import PartitionSpec as P
+from jax.experimental import pallas as pl
+from jax.experimental.pallas import tpu as pltpu
+from jax.sharding import Mesh, PartitionSpec as P
 
 D = 1024
 HEADS = 16
@@ -283,39 +285,760 @@
     )
 
 
+PAIR = [(0, 1), (1, 0)]
+BLOCKS = 8
+LANE = 128
+GROUP = ("o", "p", "q", "c")
+VMEM_BYTES = 56 * 1024 * 1024
+
+
+def swap(values, *axes):
+    if len(axes) == 1:
+        return lax.ppermute(values, axes[0], PAIR)
+    return lax.ppermute(values, axes, [(i, 3 - i) for i in range(4)])
+
+
+def join(own, other, at, axis=0):
+    first = at == 0
+    return jnp.concatenate(
+        [jnp.where(first, own, other), jnp.where(first, other, own)], axis=axis
+    )
+
+
+def take(values, at, axis=0):
+    return lax.dynamic_index_in_dim(values, at, axis, keepdims=False)
+
+
+def low(values):
+    return values.astype(jnp.bfloat16)
+
+
+def wide(values):
+    return values.astype(jnp.float32)
+
+
+def times(left, right):
+    return jnp.dot(left, right, preferred_element_type=jnp.float32)
+
+
+def places_of(ids_ref):
+    return tuple(ids_ref[i] for i in range(5))
+
+
+def call(kernel, outs, scratch, flops, *operands, memory):
+    whole = pl.BlockSpec(memory_space=pltpu.VMEM)
+    specs = {
+        "s": pl.BlockSpec(memory_space=pltpu.SMEM),
+        "v": whole,
+        "h": pl.BlockSpec(memory_space=pl.ANY),
+    }
+    size = sum(leaf.size * leaf.dtype.itemsize for leaf in (*operands, *outs))
+    return pl.pallas_call(
+        kernel,
+        out_shape=tuple(outs),
+        in_specs=[specs[kind] for kind in memory],
+        out_specs=tuple(whole for _ in outs),
+        scratch_shapes=scratch,
+        compiler_params=pltpu.CompilerParams(vmem_limit_bytes=VMEM_BYTES),
+        cost_estimate=pl.CostEstimate(flops=flops, bytes_accessed=size, transcendentals=0),
+    )(*operands)
+
+
+def fetch(pairs, sems):
+    copies = [
+        pltpu.make_async_copy(source, target, sems.at[i])
+        for i, (source, target) in enumerate(pairs)
+    ]
+    for copy in copies:
+        copy.start()
+    return copies
+
+
+def finish(copies):
+    for copy in copies:
+        copy.wait()
+
+
+def row_pairs(near, far, target, start, cap):
+    return [
+        (source.at[k, pl.ds(start, cap)], target.at[pl.ds((half * 4 + k) * cap, cap)])
+        for half, source in enumerate((near, far))
+        for k in range(4)
+    ]
+
+
+def sheet_pairs(pieces, target, places):
+    x, o, p, q, c = places
+    pairs = []
+    for index, piece in enumerate(pieces):
+        jo, jq = index // 2, index % 2
+        rows = piece.shape[1]
+        for k in range(4):
+            jc, jp = k // 2, k % 2
+            at = ((((o ^ jo) * 2 + (p ^ jp)) * 2 + (q ^ jq)) * 2 + (c ^ jc)) * rows
+            pairs.append((piece.at[k], target.at[pl.ds(pl.multiple_of(at, rows), rows)]))
+    return pairs
+
+
+def tall_pairs(pieces, target, places):
+    x, o, p, q, c = places
+    pairs = []
+    for index, piece in enumerate(pieces):
+        jo, jq = index // 2, index % 2
+        rows = piece.shape[0]
+        at = ((o ^ jo) * 2 + (q ^ jq)) * rows
+        pairs.append((piece, target.at[pl.ds(pl.multiple_of(at, rows), rows)]))
+    return pairs
+
+
+def norm_of(tokens):
+    values = wide(tokens)
+    centre = values - jnp.mean(values, axis=-1, keepdims=True)
+    return centre * lax.rsqrt(jnp.mean(centre * centre, axis=-1, keepdims=True) + EPSILON)
+
+
+def fold(values):
+    rows, columns = values.shape
+    return jnp.sum(values.reshape(rows // 8, 8, columns), axis=0)
+
+
+def block_rows(block, cap):
+    return pl.ds(pl.multiple_of(block * cap, 16), cap)
+
+
+def cut_kernel(ids, joint, up, down, keep, send, half):
+    x, o, p, q, c = places_of(ids)
+    parts = joint.shape[1] // D
+
+    def block(ref, index):
+        return ref[:, pl.ds(pl.multiple_of(index * LANE, LANE), LANE)]
+
+    for jp, target in ((0, keep), (1, send)):
+        for jc in (0, 1):
+            pp, cc = p ^ jp, c ^ jc
+            for part in range(parts):
+                target[jc, :, part * LANE : (part + 1) * LANE] = block(
+                    joint, part * 8 + x * 4 + pp * 2 + cc
+                )
+            for k in range(4):
+                oo, qq = k // 2, k % 2
+                at = (parts + k) * LANE
+                target[jc, :, at : at + LANE] = block(
+                    up, (((oo * 2 + pp) * 2 + qq) * 2 + cc) * 2 + x
+                )
+    rows = half.shape[0]
+    half[...] = down[pl.ds(pl.multiple_of(x * rows, rows), rows), :]
+
+
+def attention_kernel(
+    ids,
+    near,
+    far,
+    sheet_0,
+    sheet_1,
+    sheet_2,
+    sheet_3,
+    output_weight,
+    cosine,
+    sine,
+    position,
+    gain,
+    shift,
+    offset,
+    mixed_ref,
+    grad_ref,
+    home,
+    away,
+    output_grad,
+    grad_sum,
+    tokens,
+    cotangent,
+    joint,
+    inputs,
+    total,
+    sems,
+):
+    places = places_of(ids)
+    cap = near.shape[1] // 2
+    copies = fetch(
+        sheet_pairs((sheet_0, sheet_1, sheet_2, sheet_3), joint, places)
+        + row_pairs(near, far, tokens, 0, cap)
+        + row_pairs(near, far, cotangent, cap, cap),
+        sems,
+    )
+    finish(copies)
+    total[...] = jnp.zeros_like(total)
+    lane = lax.broadcasted_iota(jnp.int32, (cap, LANE), 1)
+    lead = lane % HEAD < ROT // 2
+    mine = (lane < HEAD, lane >= HEAD)
+    down = lax.broadcasted_iota(jnp.int32, (cap, cap), 0)
+    along = lax.broadcasted_iota(jnp.int32, (cap, cap), 1)
+    scale = HEAD ** (-0.5)
+    half_rot = ROT // 2
+
+    def turn(values, cos_part, sin_part):
+        other = jnp.where(
+            lead, pltpu.roll(values, LANE - half_rot, 1), pltpu.roll(values, half_rot, 1)
+        )
+        return values * cos_part + other * sin_part
+
+    def step(block, carry):
+        rows = block_rows(block, cap)
+        input_low = low(norm_of(tokens[rows, :]) * gain[...] + shift[...])
+        inputs[rows, :] = input_low
+        projected = times(input_low, joint[...]) + offset[...]
+        cos_part, sin_part = cosine[rows, :], sine[rows, :]
+        query = low(turn(projected[:, :LANE], cos_part, sin_part))
+        keys = low(turn(projected[:, LANE : 2 * LANE], cos_part, sin_part))
+        value = low(projected[:, 2 * LANE :])
+        grad_mixed = low(across(cotangent[rows, :], output_weight[...]))
+        allowed = (along <= down) & (along >= down - position[rows, :])
+        found = []
+        for head in (0, 1):
+            own = mine[head]
+            query_own = jnp.where(own, query, jnp.zeros_like(query))
+            grad_own = jnp.where(own, grad_mixed, jnp.zeros_like(grad_mixed))
+            scores = jnp.where(allowed, across(query_own, keys) * scale, -1e30)
+            raised = jnp.exp(scores - jnp.max(scores, axis=-1, keepdims=True))
+            probs = raised / jnp.sum(raised, axis=-1, keepdims=True)
+            probs_low = low(probs)
+            grad_probs = across(grad_own, value)
+            spread = jnp.sum(grad_probs * probs, axis=-1, keepdims=True)
+            grad_scores = low(probs * (grad_probs - spread))
+            found.append(
+                (
+                    times(probs_low, value),
+                    times(grad_scores, keys) * scale,
+                    contract_rows(grad_scores, query) * scale,
+                    contract_rows(probs_low, grad_mixed),
+                )
+            )
+        mixed, grad_query, grad_keys, grad_value = (
+            jnp.where(mine[0], first, second) for first, second in zip(*found)
+        )
+        mixed_ref[rows, :] = low(mixed)
+        grad_joint = low(
+            jnp.concatenate(
+                [
+                    turn(grad_query, cos_part, -sin_part),
+                    turn(grad_keys, cos_part, -sin_part),
+                    grad_value,
+                ],
+                axis=1,
+            )
+        )
+        grad_ref[rows, :] = grad_joint
+        total[...] += fold(wide(grad_joint))
+        return carry
+
+    lax.fori_loop(0, BLOCKS, step, 0)
+    grad_sum[...] = jnp.sum(total[...], axis=0, keepdims=True)
+    output_grad[...] = low(contract_rows(mixed_ref[...], cotangent[...]))
+    sheet_grads(inputs, grad_ref, home, away, places)
+
+
+def sheet_grads(inputs, grads, home, away, places):
+    x, o, p, q, c = places
+    rows = home.shape[2]
+    for oo in (0, 1):
+        found = contract_rows(inputs[:, oo * D // 2 : (oo + 1) * D // 2], grads[...])
+        found = low(found).reshape(2, 2, 2, rows, -1)
+        for pp in (0, 1):
+            for cc in (0, 1):
+                at = (c ^ cc) * 2 + (p ^ pp)
+                home[o ^ oo, at] = jnp.where(q == 0, found[pp, 0, cc], found[pp, 1, cc])
+                away[o ^ oo, at] = jnp.where(q == 0, found[pp, 1, cc], found[pp, 0, cc])
+
+
+def forward_kernel(
+    ids,
+    near,
+    far,
+    sheet_0,
+    sheet_1,
+    sheet_2,
+    sheet_3,
+    tall_0,
+    tall_1,
+    tall_2,
+    tall_3,
+    output_weight,
+    mixed,
+    gain,
+    shift,
+    offset,
+    inputs,
+    before_ref,
+    near_out,
+    far_out,
+    home,
+    away,
+    tokens,
+    cotangent,
+    up,
+    down,
+    active_all,
+    sems,
+):
+    places = places_of(ids)
+    x, o, p, q, c = places
+    cap = near.shape[1] // 2
+    copies = fetch(
+        sheet_pairs((sheet_0, sheet_1, sheet_2, sheet_3), up, places)
+        + tall_pairs((tall_0, tall_1, tall_2, tall_3), down, places)
+        + row_pairs(near, far, tokens, 0, cap)
+        + row_pairs(near, far, cotangent, cap, cap),
+        sems,
+    )
+    finish(copies)
+
+    def step(block, target):
+        rows = block_rows(block, cap)
+        input_low = low(norm_of(tokens[rows, :]) * gain[...] + shift[...])
+        inputs[rows, :] = input_low
+        before = times(input_low, up[...]) + offset[...]
+        before_ref[rows, :] = before
+        active = low(before * (0.5 + 0.5 * lax.erf(before * 0.5**0.5)))
+        active_all[rows, :] = active
+        return times(mixed[rows, :], output_weight[...]) + times(active, down[...])
+
+    def first(block, carry):
+        near_out[block_rows(block, cap), :] = step(block, None)
+        return carry
+
+    def second(block, carry):
+        far_out[block_rows(block, cap), :] = low(step(block + BLOCKS // 2, None))
+        return carry
+
+    lax.fori_loop(0, BLOCKS // 2, first, 0)
+    lax.fori_loop(0, BLOCKS // 2, second, 0)
+    unit = home.shape[1]
+    for oo in (0, 1):
+        found = low(contract_rows(active_all[:, oo * 2 * unit : (oo + 1) * 2 * unit], cotangent[...]))
+        home[o ^ oo] = jnp.where(q == 0, found[:unit], found[unit:])
+        away[o ^ oo] = jnp.where(q == 0, found[unit:], found[:unit])
+
+
+def backward_kernel(
+    ids,
+    near,
+    far,
+    sheet_0,
+    sheet_1,
+    sheet_2,
+    sheet_3,
+    tall_0,
+    tall_1,
+    tall_2,
+    tall_3,
+    join_0,
+    join_1,
+    join_2,
+    join_3,
+    inputs,
+    before_all,
+    grad_joint,
+    gain_one,
+    gain_two,
+    near_out,
+    far_out,
+    home,
+    away,
+    sums,
+    grad_sum,
+    tokens,
+    cotangent,
+    up,
+    down,
+    joint,
+    grad_all,
+    totals,
+    total,
+    sems,
+):
+    places = places_of(ids)
+    cap = near.shape[1] // 2
+    copies = fetch(
+        sheet_pairs((sheet_0, sheet_1, sheet_2, sheet_3), up, places)
+        + sheet_pairs((join_0, join_1, join_2, join_3), joint, places)
+        + tall_pairs((tall_0, tall_1, tall_2, tall_3), down, places)
+        + row_pairs(near, far, tokens, 0, cap)
+        + row_pairs(near, far, cotangent, cap, cap),
+        sems,
+    )
+    finish(copies)
+    totals[...] = jnp.zeros_like(totals)
+    total[...] = jnp.zeros_like(total)
+
+    def step(block, unused):
+        rows = block_rows(block, cap)
+        before = before_all[rows, :]
+        grad_active = across(cotangent[rows, :], down[...])
+        slope = 0.5 + 0.5 * lax.erf(before * 0.5**0.5)
+        slope = slope + before * jnp.exp(-0.5 * before * before) * (0.5 / jnp.pi) ** 0.5
+        grad_before = low(grad_active * slope)
+        grad_all[rows, :] = grad_before
+        total[...] += fold(wide(grad_before))
+        normed = norm_of(tokens[rows, :])
+        grad_first = across(grad_joint[rows, :], joint[...])
+        grad_second = across(grad_before, up[...])
+        totals[0] += fold(grad_first * normed)
+        totals[1] += fold(grad_first)
+        totals[2] += fold(grad_second * normed)
+        totals[3] += fold(grad_second)
+        return grad_first * gain_one[...] + grad_second * gain_two[...]
+
+    def first(block, carry):
+        near_out[block_rows(block, cap), :] = step(block, None)
+        return carry
+
+    def second(block, carry):
+        far_out[block_rows(block, cap), :] = low(step(block + BLOCKS // 2, None))
+        return carry
+
+    lax.fori_loop(0, BLOCKS // 2, first, 0)
+    lax.fori_loop(0, BLOCKS // 2, second, 0)
+    sums[...] = jnp.sum(totals[...], axis=1)
+    grad_sum[...] = jnp.sum(total[...], axis=0, keepdims=True)
+    sheet_grads(inputs, grad_all, home, away, places)
+
+
+def lay_kernel(blocks, ids, own, other, out):
+    x, o, p, q, c = places_of(ids)
+    for xx, source in ((0, own), (1, other)):
+        for pp in (0, 1):
+            for cc in (0, 1):
+                values = wide(source[pp, cc])
+                for k, at in enumerate(blocks(x ^ xx, p ^ pp, c ^ cc)):
+                    out[:, pl.ds(pl.multiple_of(at * LANE, LANE), LANE)] = values[
+                        :, k * LANE : (k + 1) * LANE
+                    ]
+
+
+def joint_blocks(x, p, c):
+    return [part * 8 + x * 4 + p * 2 + c for part in range(3)]
+
+
+def up_blocks(x, p, c):
+    return [(((oo * 2 + p) * 2 + qq) * 2 + c) * 2 + x for oo in (0, 1) for qq in (0, 1)]
+
+
+def scatter_rows(near, far):
+    lane = near + wide(swap(far, "c"))
+    rows = lane.shape[0] // 4
+    sent = low(lane[rows:])
+    return (
+        lane[:rows]
+        + wide(swap(sent[:rows], "x"))
+        + wide(swap(sent[rows : 2 * rows], "p"))
+        + wide(swap(sent[2 * rows :], "x", "p"))
+    )
+
+
+def grouped(
+    tokens,
+    cotangent,
+    lengths,
+    owners,
+    first_gain,
+    first_bias,
+    joint_weight,
+    joint_bias,
+    output_weight,
+    output_bias,
+    second_gain,
+    second_bias,
+    up_weight,
+    up_bias,
+    down_weight,
+    down_bias,
+):
+    x, o, p, q, c = (lax.axis_index(name) for name in ("x", *GROUP))
+    ids = jnp.stack([x, o, p, q, c]).astype(jnp.int32)
+    cap = tokens.shape[0]
+    rows = BLOCKS * cap
+    part = joint_weight.shape[0]
+    hidden = up_weight.shape[1] // 8
+    unit = hidden // 4
+    bf, f32 = jnp.bfloat16, jnp.float32
+
+    def like(shape, kind):
+        return jax.ShapeDtypeStruct(shape, kind)
+
+    small = jnp.concatenate(
+        [first_gain, first_bias, second_gain, second_bias, output_bias, down_bias, joint_bias, up_bias]
+    )[None]
+    for name, at in (("c", c), ("q", q), ("p", p), ("o", o)):
+        small = join(small, swap(small, name), at)
+
+    def vector(start, size):
+        return wide(small[:, start : start + size]).reshape(1, -1)
+
+    gain_one, shift_one, gain_two, shift_two, output_offset, down_offset = (
+        vector(i * part, part) for i in range(6)
+    )
+    joint_own = joint_bias.shape[0]
+    joint_offset = vector(6 * part, joint_own)
+    up_offset = vector(6 * part + joint_own, up_bias.shape[0])
+    joint_offset = take(joint_offset.reshape(3, 8, LANE), x * 4 + p * 2 + c, 1).reshape(1, 3 * LANE)
+    up_offset = take(take(take(up_offset.reshape(2, 2, 2, 2, 2, unit), x, 4), c, 3), p, 1)
+    up_offset = up_offset.reshape(1, hidden)
+
+    pair = jnp.concatenate([tokens, cotangent], axis=0)
+    near = jnp.stack([pair, swap(pair, "x"), swap(pair, "p"), swap(pair, "x", "p")], axis=0)
+    far = swap(near, "c")
+
+    keep, send, down_half = call(
+        cut_kernel,
+        [
+            like((2, part, 3 * LANE + hidden), bf),
+            like((2, part, 3 * LANE + hidden), bf),
+            like((unit, D), bf),
+        ],
+        [],
+        0,
+        ids,
+        joint_weight,
+        up_weight,
+        down_weight,
+        memory="svvv",
+    )
+    came = swap(send, "p")
+    turned = jnp.concatenate(
+        [keep[:1], came[:1], swap(jnp.concatenate([keep[1:], came[1:]], axis=0), "c")], axis=0
+    )
+
+    def spread(own):
+        other = swap(own, "o")
+        return own, swap(own, "q"), other, swap(other, "q")
+
+    joint_sheets = spread(turned[:, :, : 3 * LANE])
+    up_sheets = spread(turned[:, :, 3 * LANE :])
+    down_talls = spread(down_half)
+    turn_over = [
+        (((a * 2 + b) * 2 + e) * 2 + f, ((b * 2 + a) * 2 + f) * 2 + e)
+        for a in (0, 1)
+        for b in (0, 1)
+        for e in (0, 1)
+        for f in (0, 1)
+    ]
+    cross = ("x", "o", "q", "c")
+    output_pair = lax.ppermute(join(output_weight, swap(output_weight, "c"), c), cross, turn_over)
+
+    devices = jnp.stack(
+        [
+            ((((x ^ xx) * 2 + o) * 2 + (p ^ pp)) * 2 + q) * 2 + (c ^ cc)
+            for cc in (0, 1)
+            for pp in (0, 1)
+            for xx in (0, 1)
+        ]
+    )
+    position = jax.vmap(lambda device: layout(lengths, owners, device, cap)[1])(devices)
+    position = position.reshape(rows, 1)
+    place = jnp.arange(LANE) % HEAD
+    half_rot = ROT // 2
+    frequency = 10000.0 ** (-jnp.arange(half_rot, dtype=f32) / half_rot)
+    angles = position.astype(f32) * jnp.tile(frequency, LANE // half_rot)[None, :]
+    cosine = jnp.where(place < ROT, jnp.cos(angles), 1.0)
+    sine = jnp.sin(angles)
+    sine = jnp.where(place < half_rot, -sine, jnp.where(place < ROT, sine, 0.0))
+
+    sheet = (4, part, 3 * LANE)
+    copies = pltpu.SemaphoreType.DMA
+    mixed, grad_joint, joint_home, joint_away, output_grad, joint_sum = call(
+        attention_kernel,
+        [
+            like((rows, LANE), bf),
+            like((rows, 3 * LANE), bf),
+            like((2, *sheet), bf),
+            like((2, *sheet), bf),
+            like((LANE, D), bf),
+            like((1, 3 * LANE), f32),
+        ],
+        [
+            pltpu.VMEM((rows, D), bf),
+            pltpu.VMEM((rows, D), bf),
+            pltpu.VMEM((D, 3 * LANE), bf),
+            pltpu.VMEM((rows, D), bf),
+            pltpu.VMEM((8, 3 * LANE), f32),
+            copies((32,)),
+        ],
+        rows * D * LANE * 16,
+        ids,
+        near,
+        far,
+        *joint_sheets,
+        output_pair,
+        cosine,
+        sine,
+        position,
+        gain_one,
+        shift_one,
+        joint_offset,
+        memory="shhhhhhvvvvvvv",
+    )
+
+    tall = (unit, D)
+    sheet = (4, part, hidden)
+    inputs, before, near_part, far_part, down_home, down_away = call(
+        forward_kernel,
+        [
+            like((rows, D), bf),
+            like((rows, hidden), f32),
+            like((rows // 2, D), f32),
+            like((rows // 2, D), bf),
+            like((2, *tall), bf),
+            like((2, *tall), bf),
+        ],
+        [
+            pltpu.VMEM((rows, D), bf),
+            pltpu.VMEM((rows, D), bf),
+            pltpu.VMEM((D, hidden), bf),
+            pltpu.VMEM((hidden, D), bf),
+            pltpu.VMEM((rows, hidden), bf),
+            copies((36,)),
+        ],
+        rows * D * hidden * 6,
+        ids,
+        near,
+        far,
+        *up_sheets,
+        *down_talls,
+        output_pair,
+        mixed,
+        gain_two,
+        shift_two,
+        up_offset,
+        memory="shhhhhhhhhhvvvvv",
+    )
+    own_values = wide(tokens)
+    result = low(own_values + scatter_rows(near_part, far_part) + output_offset + down_offset)
+
+    near_part, far_part, up_home, up_away, norm_sums, up_sum = call(
+        backward_kernel,
+        [
+            like((rows // 2, D), f32),
+            like((rows // 2, D), bf),
+            like((2, *sheet), bf),
+            like((2, *sheet), bf),
+            like((4, D), f32),
+            like((1, hidden), f32),
+        ],
+        [
+            pltpu.VMEM((rows, D), bf),
+            pltpu.VMEM((rows, D), bf),
+            pltpu.VMEM((D, hidden), bf),
+            pltpu.VMEM((hidden, D), bf),
+            pltpu.VMEM((D, 3 * LANE), bf),
+            pltpu.VMEM((rows, hidden), bf),
+            pltpu.VMEM((4, 8, D), f32),
+            pltpu.VMEM((8, hidden), f32),
+            copies((52,)),
+        ],
+        rows * D * (hidden * 6 + LANE * 6),
+        ids,
+        near,
+        far,
+        *up_sheets,
+        *down_talls,
+        *joint_sheets,
+        inputs,
+        before,
+        grad_joint,
+        gain_one,
+        gain_two,
+        memory="shhhhhhhhhhhhhhvvvvv",
+    )
+    pulled = scatter_rows(near_part, far_part)
+
+    def put(values, index, size, axis):
+        hot = (jnp.arange(size) == index).reshape([size if i == axis else 1 for i in range(values.ndim + 1)])
+        return jnp.where(hot, jnp.expand_dims(values, axis), 0.0)
+
+    joint_sum = put(joint_sum.reshape(3, LANE), x * 4 + p * 2 + c, 8, 1)
+    up_sum = put(put(put(up_sum.reshape(2, 2, unit), x, 2, 2), c, 2, 2), p, 2, 1)
+    sums = jnp.concatenate(
+        [
+            *(norm_sums[i].reshape(-1, part) for i in range(4)),
+            jnp.sum(wide(cotangent), axis=0).reshape(-1, part),
+            joint_sum.reshape(-1, joint_own),
+            up_sum.reshape(-1, up_bias.shape[0]),
+        ],
+        axis=1,
+    )
+    for name in ("c", "q", "p", "o", "x"):
+        sums = sums + swap(sums, name)
+    own_sums = take(sums, ((o * 2 + p) * 2 + q) * 2 + c)
+
+    def reduce(home, away):
+        both = wide(home) + wide(swap(away, "q"))
+        return both[0] + wide(swap(low(both[1]), "o"))
+
+    def hand(home, away, blocks):
+        final = low(reduce(home, away))
+        both = jnp.stack([final[:2], swap(final[2:], "c")])
+        both = jnp.stack([both[:, 0], swap(both[:, 1], "p")])
+        columns = both.shape[-1] * 8
+        (out,) = call(
+            partial(lay_kernel, blocks),
+            [like((part, columns), f32)],
+            [],
+            0,
+            ids,
+            both,
+            swap(both, "x"),
+            memory="svv",
+        )
+        return out
+
+    joint_own_grad = hand(joint_home, joint_away, joint_blocks)
+    up_own_grad = hand(up_home, up_away, up_blocks)
+    down_own = low(reduce(down_home, down_away))
+    down_own = wide(join(down_own, swap(down_own, "x"), x))
+    output_part = lax.ppermute(output_grad, cross, turn_over).reshape(2, part, D)
+    output_own = wide(take(output_part, c)) + wide(swap(take(output_part, 1 - c), "c"))
+    output_own = low(output_own)
+    output_own = wide(output_own) + wide(swap(output_own, "x"))
+
+    own_normed = norm_of(tokens)
+    centre = own_values - jnp.mean(own_values, axis=-1, keepdims=True)
+    factor = lax.rsqrt(jnp.mean(centre * centre, axis=-1, keepdims=True) + EPSILON)
+    grad_tokens = wide(cotangent) + factor * (
+        pulled
+        - jnp.mean(pulled, axis=-1, keepdims=True)
+        - own_normed * jnp.mean(pulled * own_normed, axis=-1, keepdims=True)
+    )
+    pieces = [own_sums[i * part : (i + 1) * part] for i in range(5)]
+    return (
+        result,
+        grad_tokens,
+        pieces[0],
+        pieces[1],
+        joint_own_grad,
+        own_sums[5 * part : 5 * part + joint_own],
+        output_own,
+        pieces[4],
+        pieces[2],
+        pieces[3],
+        up_own_grad,
+        own_sums[5 * part + joint_own :],
+        down_own,
+        pieces[4],
+    )
+
+
 def solution(mesh):
-    in_specs = (
-        P(("rep", "shard"), None),
-        P(("rep", "shard"), None),
-        P(),
-        P(),
-        P("shard"),
-        P("shard"),
-        P("shard", None),
-        P("shard"),
-        P("shard", None),
-        P("shard"),
-        P("shard"),
-        P("shard"),
-        P("shard", None),
-        P("shard"),
-        P("shard", None),
-        P("shard"),
-    )
-    out_specs = (
-        P(("rep", "shard"), None),
-        P(("rep", "shard"), None),
-        P("shard"),
-        P("shard"),
-        P("shard", None),
-        P("shard"),
-        P("shard", None),
-        P("shard"),
-        P("shard"),
-        P("shard"),
-        P("shard", None),
-        P("shard"),
-        P("shard", None),
-        P("shard"),
-    )
-    return jax.shard_map(local, mesh=mesh, in_specs=in_specs, out_specs=out_specs, check_vma=False)
+    if mesh.shape["rep"] == 2 and mesh.shape["shard"] * HEAD == D:
+        work, body = Mesh(mesh.devices.reshape(2, 2, 2, 2, 2), ("x", *GROUP)), grouped
+        group, every = GROUP, ("x", *GROUP)
+    else:
+        work, body = mesh, local
+        group, every = "shard", ("rep", "shard")
+    row, vec, mat = P(every, None), P(group), P(group, None)
+    return jax.shard_map(
+        body,
+        mesh=work,
+        in_specs=(row, row, P(), P(), vec, vec, mat, vec, mat, vec, vec, vec, mat, vec, mat, vec),
+        out_specs=(row, row, vec, vec, mat, vec, mat, vec, vec, vec, mat, vec, mat, vec),
+        check_vma=False,
+    )

time: 949 us -> 296 us (0.31)
  waiting for transfers between devices: 664 us -> 110 us
  blocking collectives: 148 us -> 0 us
  matrix products: 81.1 us -> 0 us
  Pallas kernels: 0 us -> 66 us
  starting transfers between devices: 0.8 us -> 64.4 us
  between operations: 17.5 us -> 1.4 us
  other arithmetic: 12.3 us -> 24.1 us
    reduce_scatter x4 -> x0, waiting for transfers between devices: 541 us -> none  [the longest x1 182 us: local(): lax.psum_scatter(up_weight_grad, 'shard', scatter_dimension=0, tiled=True)]
    unnamed x2 -> x0, blocking collectives: 123 us -> none
    all_gather x4 -> x0, waiting for transfers between devices: 118 us -> none  [the longest x1 68.4 us: local(): lax.all_gather(down_weight, 'shard', axis=0, tiled=True)]
    ppermute x0 -> x50, waiting for transfers between devices: none -> 110 us  [the longest x45 87.3 us: swap(): return lax.ppermute(values, axes[0], PAIR)]
    dot_general x18 -> x0, matrix products: 81.1 us -> none  [the longest x4 28.6 us: across(): lax.dot_general(left, right, (((1,), (1,)), ((), ())), preferred_element_...]
    pallas_call x0 -> x6, Pallas kernels: none -> 66 us  [call(): pl.pallas_call(kernel, out_shape=tuple(outs), in_specs=[specs[kind] for k...]
    ppermute x0 -> x50, starting transfers between devices: none -> 64.4 us  [the longest x45 51.2 us: swap(): return lax.ppermute(values, axes[0], PAIR)]
    all_gather x1 -> x0, blocking collectives: 19.4 us -> none  [local(): lax.all_gather(up_bias, 'shard', axis=0, tiled=True)]
  transfers between devices with their start and end apart: 9 -> 50, of which waited for: 8 -> 19; matrix products, arithmetic and copies ran while one was open for 11% -> 15% of each run, Pallas kernels for 0% -> 17%
where the time goes in v2:
time: 296 us; the launch traced here: 294 us
  waiting for transfers between devices  110 us (37%)
  Pallas kernels  66 us (22%)
  starting transfers between devices  64.4 us (22%)
  local copies, waits for them, and re-layouts  28.5 us (10%)
  other arithmetic  24.1 us (8%)
    ppermute x45, waiting for transfers between devices, swap(): return lax.ppermute(values, axes[0], PAIR)  87.3 us
    pallas_call x6, Pallas kernels, call(): pl.pallas_call(kernel, out_shape=tuple(outs), in_specs=[specs[kind] for k...  66 us
    ppermute x45, starting transfers between devices, swap(): return lax.ppermute(values, axes[0], PAIR)  51.2 us
    ppermute x3, waiting for transfers between devices, swap(): return lax.ppermute(values, axes, [(i, 3 - i) for i in range(4)])  22.7 us
    ppermute x3, starting transfers between devices, swap(): return lax.ppermute(values, axes, [(i, 3 - i) for i in range(4)])  6.04 us
  transfers between devices with their start and end apart: 50, of which 19 were waited for; matrix products, arithmetic and copies ran while one was open for 15% of the time, Pallas kernels for 17%

profile of v2, /device:TPU:0, one launch (start us, length us, event | category | flops | bytes accessed | tf_op | source)
XLA Modules:
  0.0 294.5 jit_solution(13588917971371368295)
XLA Ops:
  0.7 1.1 constant_dynamic-update-slice_fusion.1
  1.7 1.0 constant_dynamic-update-slice_fusion
  2.8 3.0 %collective-permute-start = (bf16[352,1024]{1,0:T(8,128)(2,1)S(1)}, bf16[352,1024]{1,0:T(8,128)(2,1)S(1)}, u32[]{:S(2)}, u32[]{:S(2)}) collective-permute-start(bf16[352,1024]{1,0:T(8,128)(2,1)S(1)} %constant_dynamic-update-slice_fusion), channel_id=1, source_target_pairs={{0,16},{16,0},{1,17},{17,1},{2,18},{18,2},{3,19},{19,3},{4,20},{20... | collective-permute-start | bytes 2162696 | tf_op jit(solution)/shard_map/ppermute | solution.py:297
  5.8 1.6 collective-permute-start.1
  7.3 5.4 %concatenate.37 = bf16[832]{0:T(1024)(128)(2,1)S(1)} concatenate(bf16[64]{0:T(256)(128)(2,1)} %param.20, bf16[64]{0:T(256)(128)(2,1)} %param.21, bf16[64]{0:T(256)(128)(2,1)} %param.26, bf16[64]{0:T(256)(128)(2,1)} %param.27, bf16[64]{0:T(256)(128)(2,1)} %param.25, bf16[64]{0:T(256)(128)(2,1)} %param.31, bf16[192]{0:T(256)(128)(2,1)} %param.23, bf16[256]{0:T(256)(128)(2,1)} %param.29), dimensions={0} | concatenate | bytes 3328 | tf_op jit(solution)/shard_map/concatenate | solution.py:768
  13.4 2.3 shard_map.263
  15.8 2.0 collective-permute-start.4
  19.3 1.0 fusion.58
  21.2 3.7 %fusion.10 = (f32[1408,128]{1,0:T(8,128)}, f32[1408,128]{1,0:T(8,128)}) fusion(f32[128]{0:T(128)S(1)} %mul.130, f32[1408]{0:T(1024)S(1)} %convert_element_type.127, pred[128]{0:T(512)(128)(4,1)S(1)} %get-tuple-element.117, pred[128]{0:T(512)(128)(4,1)S(1)} %get-tuple-element.118), kind=kLoop, calls=%fused_computation.23 | loop fusion | flops 901120 | bytes 1448192 | tf_op jit(solution)/shard_map/jit(_where)/select_n | solution.py:844
  25.2 2.6 collective-permute-start.10
  27.7 17.6 %collective-permute-done.2 = bf16[352,1024]{1,0:T(8,128)(2,1)S(1)} collective-permute-done((bf16[352,1024]{1,0:T(8,128)(2,1)S(1)}, bf16[352,1024]{1,0:T(8,128)(2,1)S(1)}, u32[]{:S(2)}, u32[]{:S(2)}) %collective-permute-start.2) | collective-permute-done | bytes 720928 | tf_op jit(solution)/shard_map/ppermute | solution.py:298
  46.2 1.9 pad_maximum_fusion.near
  48.3 2.1 collective-permute-start.18
  50.9 1.1 collective-permute-done.18
  52.2 3.6 %collective-permute-done.19 = bf16[4,832]{1,0:T(4,128)(2,1)S(1)} collective-permute-done((bf16[4,832]{1,0:T(4,128)(2,1)S(1)}, bf16[4,832]{1,0:T(4,128)(2,1)S(1)}, u32[]{:S(2)}, u32[]{:S(2)}) %collective-permute-start.19) | collective-permute-done | bytes 6688 | tf_op jit(solution)/shard_map/ppermute | solution.py:297
  55.8 2.7 collective-permute-start.20
  59.1 1.1 select_n.225.position
  61.6 1.0 fusion.59
  62.7 1.0 broadcast_select_fusion.3
  64.4 3.6 %collective-permute-start.13 = (bf16[128,1024]{1,0:T(8,128)(2,1)}, bf16[128,1024]{1,0:T(8,128)(2,1)}, u32[]{:S(2)}, u32[]{:S(2)}) collective-permute-start(bf16[128,1024]{1,0:T(8,128)(2,1)} %pad_maximum_fusion.2), channel_id=1, source_target_pairs={{0,0},{1,2},{2,1},{3,3},{8,16},{9,18},{10,17},{11,19},{16,8},{17,1... | collective-permute-start | bytes 786440 | tf_op jit(solution)/shard_map/ppermute | solution.py:826
  68.7 2.4 collective-permute-start.15
  72.6 1.4 reshape.260.gain.gain_one
  73.9 1.4 reshape.262.shift
  75.3 1.4 reshape.265.gain.gain_two
  76.7 1.4 reshape.267.shift
  78.2 1.1 collective-permute-start.14
  79.3 17.8 %collective-permute-done.15.sheet_2.join_2 = bf16[4,64,384]{2,1,0:T(8,128)(2,1)} collective-permute-done((bf16[4,64,384]{2,1,0:T(8,128)(2,1)}, bf16[4,64,384]{2,1,0:T(8,128)(2,1)}, u32[]{:S(2)}, u32[]{:S(2)}) %collective-permute-start.15) | collective-permute-done | bytes 196640 | tf_op jit(solution)/shard_map/ppermute | solution.py:297
  97.1 1.8 collective-permute-start.16
  98.9 1.3 dynamic-slice_bitcast_fusion.1.offset
  101.0 1.8 collective-permute-start.11
  102.8 1.2 collective-permute-start.6
  104.0 1.0 collective-permute-done.16.sheet_3.join_3
  105.9 22.9 %shard_map.264 = (bf16[1408,128]{1,0:T(8,128)(2,1)}, bf16[1408,384]{1,0:T(8,128)(2,1)}, bf16[2,4,64,384]{3,2,1,0:T(8,128)(2,1)}, bf16[2,4,64,384]{3,2,1,0:T(8,12...) custom-call(s32[5]{0:T(128)} %stack.95.ids, bf16[4,352,1024]{2,1,0:T(8,128)(2,1)} %copy-done.1, ...), custom_call_target="tpu_custom_call" | custom-call | flops 2952790016 | bytes 10764820 | tf_op jit(solution)/shard_map/pallas_call | solution.py:336
  129.9 16.3 %shard_map.265 = (bf16[1408,1024]{1,0:T(8,128)(2,1)}, f32[1408,512]{1,0:T(8,128)}, f32[704,1024]{1,0:T(8,128)}, bf16[704,1024]{1,0:T(8,128)(2,1)}, bf16[2,128,10...) custom-call(s32[5]{0:T(128)} %stack.95.ids, bf16[4,352,1024]{2,1,0:T(8,128)(2,1)} %copy-done.1, ...), custom_call_target="tpu_custom_call" | custom-call | flops 4429185024 | bytes 19638292 | tf_op jit(solution)/shard_map/pallas_call | solution.py:336
  146.2 1.3 collective-permute-start.47
  147.5 20.3 %shard_map.266 = (f32[704,1024]{1,0:T(8,128)}, bf16[704,1024]{1,0:T(8,128)(2,1)}, bf16[2,4,64,512]{3,2,1,0:T(8,128)(2,1)}, bf16[2,4,64,512]{3,2,1,0:T(8,128)(2,1)}, f32[4,1024]{1,0:T(4,128)}, /*index=5*/f32[1,512]{1,0:T(1,128)}) custom-call(s32[5]{0:T(128)} %stack.95.ids, bf16[4,352,1024]{2,1,0:T(8,128)(2,1)} %copy-done.1, ...), custom_call_target="tpu_custom_call" | custom-call | flops 5536481280 | bytes 20899860 | tf_op jit(solution)/shard_map/pallas_call | solution.py:336
  168.8 3.6 %collective-permute-start.39 = (bf16[128,1024]{1,0:T(8,128)(2,1)}, bf16[128,1024]{1,0:T(8,128)(2,1)}, u32[]{:S(2)}, u32[]{:S(2)}) collective-permute-start(bf16[128,1024]{1,0:T(8,128)(2,1)} %get-tuple-element.51), channel_id=1, source_target_pairs={{0,0},{1,2},{2,1},{3,3},{8,16},{9,18},{10,17},{11,19},{16,8},{17,1... | collective-permute-start | bytes 786440 | tf_op jit(solution)/shard_map/ppermute | solution.py:998
  175.5 13.4 %collective-permute-start.40 = (bf16[64,1024]{1,0:T(8,128)(2,1)S(1)}, bf16[64,1024]{1,0:T(8,128)(2,1)S(1)}, u32[]{:S(2)}, u32[]{:S(2)}) collective-permute-start(bf16[64,1024]{1,0:T(8,128)(2,1)S(1)} %dynamic-slice_bitcast_fusion), channel_id=1, source_target_pairs={{0,1},{1,0},{2,3},{3,2},{4,5},{5,4},{6,7},{7,6},{8,9},{9,8},{10,11... | collective-permute-start | bytes 393224 | tf_op jit(solution)/shard_map/ppermute | solution.py:297
  191.2 1.1 collective-permute-done.34
  192.4 1.1 convert_add_fusion.6
  193.6 1.2 convert_add_fusion.3
  194.8 3.0 %collective-permute-start.48 = (bf16[128,1024]{1,0:T(8,128)(2,1)S(1)}, bf16[128,1024]{1,0:T(8,128)(2,1)S(1)}, u32[]{:S(2)}, u32[]{:S(2)}) collective-permute-start(bf16[128,1024]{1,0:T(8,128)(2,1)S(1)} %fusion.26), channel_id=1, source_target_pairs={{0,8},{8,0},{1,9},{9,1},{2,10},{10,2},{3,11},{11,3},{4,12},{12,4},... | collective-permute-start | bytes 786440 | tf_op jit(solution)/shard_map/ppermute | solution.py:297
  197.8 1.2 convert_add_fusion.4
  199.0 11.2 %collective-permute-done.35 = bf16[4,64,384]{2,1,0:T(8,128)(2,1)S(1)} collective-permute-done((bf16[4,64,384]{2,1,0:T(8,128)(2,1)S(1)}, bf16[4,64,384]{2,1,0:T(8,128)(2,1)S(1)}, u32[]{:S(2)}, u32[]{:S(2)}) %collective-permute-start.35) | collective-permute-done | bytes 196640 | tf_op jit(solution)/shard_map/ppermute | solution.py:297
  210.4 1.2 collective-permute-done.36
  211.7 9.8 %collective-permute-done.48 = bf16[128,1024]{1,0:T(8,128)(2,1)S(1)} collective-permute-done((bf16[128,1024]{1,0:T(8,128)(2,1)S(1)}, bf16[128,1024]{1,0:T(8,128)(2,1)S(1)}, u32[]{:S(2)}, u32[]{:S(2)}) %collective-permute-start.48) | collective-permute-done | bytes 262176 | tf_op jit(solution)/shard_map/ppermute | solution.py:297
  221.5 5.6 %collective-permute-done.43 = bf16[4,64,512]{2,1,0:T(8,128)(2,1)S(1)} collective-permute-done((bf16[4,64,512]{2,1,0:T(8,128)(2,1)S(1)}, bf16[4,64,512]{2,1,0:T(8,128)(2,1)S(1)}, u32[]{:S(2)}, u32[]{:S(2)}) %collective-permute-start.43) | collective-permute-done | bytes 262176 | tf_op jit(solution)/shard_map/ppermute | solution.py:297
  227.5 1.6 collective-permute-done.37
  230.4 3.2 %collective-permute-start.28 = (bf16[176,1024]{1,0:T(8,128)(2,1)S(1)}, bf16[176,1024]{1,0:T(8,128)(2,1)S(1)}, u32[]{:S(2)}, u32[]{:S(2)}) collective-permute-start(bf16[176,1024]{1,0:T(8,128)(2,1)S(1)} %get-tuple-element.70), channel_id=1, source_target_pairs={{0,20},{4,16},{16,4},{20,0},{1,21},{5,17},{17,5},{21,1},{2,22},{6,... | collective-permute-start | bytes 1081352 | tf_op jit(solution)/shard_map/ppermute | solution.py:298
  234.4 16.2 %collective-permute-done.26 = bf16[176,1024]{1,0:T(8,128)(2,1)S(1)} collective-permute-done((bf16[176,1024]{1,0:T(8,128)(2,1)S(1)}, bf16[176,1024]{1,0:T(8,128)(2,1)S(1)}, u32[]{:S(2)}, u32[]{:S(2)}) %collective-permute-start.26) | collective-permute-done | bytes 360480 | tf_op jit(solution)/shard_map/ppermute | solution.py:297
  251.3 2.9 collective-permute-start.24
  254.6 6.5 %collective-permute-done.22 = bf16[176,1024]{1,0:T(8,128)(2,1)S(1)} collective-permute-done((bf16[176,1024]{1,0:T(8,128)(2,1)S(1)}, bf16[176,1024]{1,0:T(8,128)(2,1)S(1)}, u32[]{:S(2)}, u32[]{:S(2)}) %collective-permute-start.22) | collective-permute-done | bytes 360480 | tf_op jit(solution)/shard_map/ppermute | solution.py:297
  261.1 1.2 collective-permute-done.23
  262.3 1.7 collective-permute-start.38
  264.1 5.0 %collective-permute-done.24 = bf16[176,1024]{1,0:T(8,128)(2,1)S(1)} collective-permute-done((bf16[176,1024]{1,0:T(8,128)(2,1)S(1)}, bf16[176,1024]{1,0:T(8,128)(2,1)S(1)}, u32[]{:S(2)}, u32[]{:S(2)}) %collective-permute-start.24) | collective-permute-done | bytes 360480 | tf_op jit(solution)/shard_map/ppermute | solution.py:298
  269.1 1.4 convert_reduce_fusion.1
  271.9 1.8 collective-permute-start.30
  273.7 1.6 convert_add_fusion.8
  276.1 2.0 shard_map.267
  278.1 1.0 collective-permute-start.31
  279.5 2.8 collective-permute-done.31
  283.0 4.8 %collective-permute-done.32 = f32[16,768]{1,0:T(8,128)S(1)} collective-permute-done((f32[16,768]{1,0:T(8,128)S(1)}, f32[16,768]{1,0:T(8,128)S(1)}, u32[]{:S(2)}, u32[]{:S(2)}) %collective-permute-start.32) | collective-permute-done | bytes 49184 | tf_op jit(solution)/shard_map/ppermute | solution.py:297
  288.2 1.1 maximum_convert_fusion
  290.0 2.2 shard_map.268
  (217 shorter events, 29.6 us)
Async XLA Ops:
  2.7 42.6 %copy-start.4 = (bf16[352,1024]{1,0:T(8,128)(2,1)}, bf16[352,1024]{1,0:T(8,128)(2,1)S(1)}, u32[]{:S(2)}) copy-start(bf16[352,1024]{1,0:T(8,128)(2,1)S(1)} %constant_dynamic-update-slice_fusion) | copy-start | bytes 2162692
  2.8 22.1 %collective-permute-start = (bf16[352,1024]{1,0:T(8,128)(2,1)S(1)}, bf16[352,1024]{1,0:T(8,128)(2,1)S(1)}, u32[]{:S(2)}, u32[]{:S(2)}) collective-permute-start(bf16[352,1024]{1,0:T(8,128)(2,1)S(1)} %constant_dynamic-update-slice_fusion), channel_id=1, source_target_pairs={{0,16},{16,0},{1,17},{17,1},{2,18},{18,2},{3,19},{19,3},{4,20},{20... | collective-permute-start | bytes 2162696 | tf_op jit(solution)/shard_map/ppermute | solution.py:297
  5.8 19.4 %collective-permute-start.1 = (bf16[352,1024]{1,0:T(8,128)(2,1)S(1)}, bf16[352,1024]{1,0:T(8,128)(2,1)S(1)}, u32[]{:S(2)}, u32[]{:S(2)}) collective-permute-start(bf16[352,1024]{1,0:T(8,128)(2,1)S(1)} %constant_dynamic-update-slice_fusion), channel_id=1, source_target_pairs={{0,4},{4,0},{1,5},{5,1},{2,6},{6,2},{3,7},{7,3},{8,12},{12,8},{9,1... | collective-permute-start | bytes 2162696 | tf_op jit(solution)/shard_map/ppermute | solution.py:297
  7.3 38.0 %collective-permute-start.2 = (bf16[352,1024]{1,0:T(8,128)(2,1)S(1)}, bf16[352,1024]{1,0:T(8,128)(2,1)S(1)}, u32[]{:S(2)}, u32[]{:S(2)}) collective-permute-start(bf16[352,1024]{1,0:T(8,128)(2,1)S(1)} %constant_dynamic-update-slice_fusion), channel_id=1, source_target_pairs={{0,20},{4,16},{16,4},{20,0},{1,21},{5,17},{17,5},{21,1},{2,22},{6,... | collective-permute-start | bytes 2162696 | tf_op jit(solution)/shard_map/ppermute | solution.py:298
  12.8 35.5 %collective-permute-start.17 = (bf16[1,832]{1,0:T(2,128)(2,1)S(1)}, bf16[1,832]{1,0:T(2,128)(2,1)S(1)}, u32[]{:S(2)}, u32[]{:S(2)}) collective-permute-start(bf16[1,832]{1,0:T(2,128)(2,1)S(1)} %broadcast_in_dim.157), channel_id=1, source_target_pairs={{0,1},{1,0},{2,3},{3,2},{4,5},{5,4},{6,7},{7,6},{8,9},{9,8},{10,11... | collective-permute-start | bytes 5000 | tf_op jit(solution)/shard_map/ppermute | solution.py:297
  15.8 45.8 %collective-permute-start.4 = (bf16[2,64,896]{2,1,0:T(8,128)(2,1)}, bf16[2,64,896]{2,1,0:T(8,128)(2,1)}, u32[]{:S(2)}, u32[]{:S(2)}) collective-permute-start(bf16[2,64,896]{2,1,0:T(8,128)(2,1)} %get-tuple-element.36), channel_id=1, source_target_pairs={{0,4},{4,0},{1,5},{5,1},{2,6},{6,2},{3,7},{7,3},{8,12},{12,8},{9,1... | collective-permute-start | bytes 688136 | tf_op jit(solution)/shard_map/ppermute | solution.py:297
  20.3 27.9 %copy-start.17 = (f32[176]{0:T(256)}, f32[176]{0:T(256)S(1)}, u32[]{:S(2)}) copy-start(f32[176]{0:T(256)S(1)} %broadcast_multiply_fusion.2) | copy-start | bytes 2116
  24.9 37.8 %collective-permute-start.12 = (bf16[64,1024]{1,0:T(8,128)(2,1)}, bf16[64,1024]{1,0:T(8,128)(2,1)}, u32[]{:S(2)}, u32[]{:S(2)}) collective-permute-start(bf16[64,1024]{1,0:T(8,128)(2,1)} %param.24), channel_id=1, source_target_pairs={{0,1},{1,0},{2,3},{3,2},{4,5},{5,4},{6,7},{7,6},{8,9},{9,8},{10,11... | collective-permute-start | bytes 393224 | tf_op jit(solution)/shard_map/ppermute | solution.py:297
  25.2 53.0 %collective-permute-start.10 = (bf16[128,1024]{1,0:T(8,128)(2,1)}, bf16[128,1024]{1,0:T(8,128)(2,1)}, u32[]{:S(2)}, u32[]{:S(2)}) collective-permute-start(bf16[128,1024]{1,0:T(8,128)(2,1)} %get-tuple-element.37.tall_0), channel_id=1, source_target_pairs={{0,8},{8,0},{1,9},{9,1},{2,10},{10,2},{3,11},{11,3},{4,12},{12,4},... | collective-permute-start | bytes 786440 | tf_op jit(solution)/shard_map/ppermute | solution.py:297
  48.2 57.7 %copy-start.1 = (bf16[4,352,1024]{2,1,0:T(8,128)(2,1)}, bf16[4,352,1024]{2,1,0:T(8,128)(2,1)S(1)}, u32[]{:S(2)}) copy-start(bf16[4,352,1024]{2,1,0:T(8,128)(2,1)S(1)} %pad_maximum_fusion.near) | copy-start | bytes 8650756
  48.2 57.7 %collective-permute-start.3 = (bf16[4,352,1024]{2,1,0:T(8,128)(2,1)S(1)}, bf16[4,352,1024]{2,1,0:T(8,128)(2,1)}, u32[]{:S(2)}, u32[]{:S(2)}) collective-permute-start(bf16[4,352,1024]{2,1,0:T(8,128)(2,1)S(1)} %pad_maximum_fusion.near), channel_id=1, source_target_pairs={{0,1},{1,0},{2,3},{3,2},{4,5},{5,4},{6,7},{7,6},{8,9},{9,8},{10,11... | collective-permute-start | bytes 8650760 | tf_op jit(solution)/shard_map/ppermute | solution.py:297
  48.3 3.7 %collective-permute-start.18 = (bf16[2,832]{1,0:T(2,128)(2,1)S(1)}, bf16[2,832]{1,0:T(2,128)(2,1)S(1)}, u32[]{:S(2)}, u32[]{:S(2)}) collective-permute-start(bf16[2,832]{1,0:T(2,128)(2,1)S(1)} %pad_maximum_fusion.12), channel_id=1, source_target_pairs={{0,2},{2,0},{1,3},{3,1},{4,6},{6,4},{5,7},{7,5},{8,10},{10,8},{9,1... | collective-permute-start | bytes 9992 | tf_op jit(solution)/shard_map/ppermute | solution.py:297
  52.0 3.7 %collective-permute-start.19 = (bf16[4,832]{1,0:T(4,128)(2,1)S(1)}, bf16[4,832]{1,0:T(4,128)(2,1)S(1)}, u32[]{:S(2)}, u32[]{:S(2)}) collective-permute-start(bf16[4,832]{1,0:T(4,128)(2,1)S(1)} %pad_maximum_fusion.10), channel_id=1, source_target_pairs={{0,4},{4,0},{1,5},{5,1},{2,6},{6,2},{3,7},{7,3},{8,12},{12,8},{9,1... | collective-permute-start | bytes 19976 | tf_op jit(solution)/shard_map/ppermute | solution.py:297
  55.8 5.1 %collective-permute-start.20 = (bf16[8,832]{1,0:T(8,128)(2,1)S(1)}, bf16[8,832]{1,0:T(8,128)(2,1)S(1)}, u32[]{:S(2)}, u32[]{:S(2)}) collective-permute-start(bf16[8,832]{1,0:T(8,128)(2,1)S(1)} %pad_maximum_fusion.9), channel_id=1, source_target_pairs={{0,8},{8,0},{1,9},{9,1},{2,10},{10,2},{3,11},{11,3},{4,12},{12,4},... | collective-permute-start | bytes 39944 | tf_op jit(solution)/shard_map/ppermute | solution.py:297
  62.6 5.4 %collective-permute-start.5 = (bf16[2,64,896]{2,1,0:T(8,128)(2,1)S(1)}, bf16[2,64,896]{2,1,0:T(8,128)(2,1)S(1)}, u32[]{:S(2)}, u32[]{:S(2)}) collective-permute-start(bf16[2,64,896]{2,1,0:T(8,128)(2,1)S(1)} %pad_maximum_fusion.4), channel_id=1, source_target_pairs={{0,1},{1,0},{2,3},{3,2},{4,5},{5,4},{6,7},{7,6},{8,9},{9,8},{10,11... | collective-permute-start | bytes 688136 | tf_op jit(solution)/shard_map/ppermute | solution.py:297
  64.4 36.3 %collective-permute-start.13 = (bf16[128,1024]{1,0:T(8,128)(2,1)}, bf16[128,1024]{1,0:T(8,128)(2,1)}, u32[]{:S(2)}, u32[]{:S(2)}) collective-permute-start(bf16[128,1024]{1,0:T(8,128)(2,1)} %pad_maximum_fusion.2), channel_id=1, source_target_pairs={{0,0},{1,2},{2,1},{3,3},{8,16},{9,18},{10,17},{11,19},{16,8},{17,1... | collective-permute-start | bytes 786440 | tf_op jit(solution)/shard_map/ppermute | solution.py:826
  68.7 28.3 %collective-permute-start.15 = (bf16[4,64,384]{2,1,0:T(8,128)(2,1)}, bf16[4,64,384]{2,1,0:T(8,128)(2,1)}, u32[]{:S(2)}, u32[]{:S(2)}) collective-permute-start(bf16[4,64,384]{2,1,0:T(8,128)(2,1)} %pad_maximum_fusion.5.sheet_0.join_0), channel_id=1, source_target_pairs={{0,8},{8,0},{1,9},{9,1},{2,10},{10,2},{3,11},{11,3},{4,12},{12,4},... | collective-permute-start | bytes 589832 | tf_op jit(solution)/shard_map/ppermute | solution.py:297
  71.3 57.6 %copy-start.14 = (bf16[4,64,512]{2,1,0:T(8,128)(2,1)}, bf16[4,64,512]{2,1,0:T(8,128)(2,1)S(1)}, u32[]{:S(2)}) copy-start(bf16[4,64,512]{2,1,0:T(8,128)(2,1)S(1)} %slice.231.sheet_0) | copy-start | bytes 786436
  71.3 31.5 %collective-permute-start.7 = (bf16[4,64,512]{2,1,0:T(8,128)(2,1)S(1)}, bf16[4,64,512]{2,1,0:T(8,128)(2,1)}, u32[]{:S(2)}, u32[]{:S(2)}) collective-permute-start(bf16[4,64,512]{2,1,0:T(8,128)(2,1)S(1)} %slice.231.sheet_0), channel_id=1, source_target_pairs={{0,8},{8,0},{1,9},{9,1},{2,10},{10,2},{3,11},{11,3},{4,12},{12,4},... | collective-permute-start | bytes 786440 | tf_op jit(solution)/shard_map/ppermute | solution.py:297
  78.2 22.8 %collective-permute-start.14 = (bf16[4,64,384]{2,1,0:T(8,128)(2,1)}, bf16[4,64,384]{2,1,0:T(8,128)(2,1)S(1)}, u32[]{:S(2)}, u32[]{:S(2)}) collective-permute-start(bf16[4,64,384]{2,1,0:T(8,128)(2,1)} %pad_maximum_fusion.5.sheet_0.join_0), channel_id=1, source_target_pairs={{0,2},{2,0},{1,3},{3,1},{4,6},{6,4},{5,7},{7,5},{8,10},{10,8},{9,1... | collective-permute-start | bytes 589832 | tf_op jit(solution)/shard_map/ppermute | solution.py:297
  97.1 8.0 %collective-permute-start.16 = (bf16[4,64,384]{2,1,0:T(8,128)(2,1)}, bf16[4,64,384]{2,1,0:T(8,128)(2,1)S(1)}, u32[]{:S(2)}, u32[]{:S(2)}) collective-permute-start(bf16[4,64,384]{2,1,0:T(8,128)(2,1)} %collective-permute-done.15.sheet_2.join_2), channel_id=1, source_target_pairs={{0,2},{2,0},{1,3},{3,1},{4,6},{6,4},{5,7},{7,5},{8,10},{10,8},{9,1... | collective-permute-start | bytes 589832 | tf_op jit(solution)/shard_map/ppermute | solution.py:297
  100.7 28.1 %collective-permute-start.9 = (bf16[128,1024]{1,0:T(8,128)(2,1)}, bf16[128,1024]{1,0:T(8,128)(2,1)S(1)}, u32[]{:S(2)}, u32[]{:S(2)}) collective-permute-start(bf16[128,1024]{1,0:T(8,128)(2,1)} %get-tuple-element.37.tall_0), channel_id=1, source_target_pairs={{0,2},{2,0},{1,3},{3,1},{4,6},{6,4},{5,7},{7,5},{8,10},{10,8},{9,1... | collective-permute-start | bytes 786440 | tf_op jit(solution)/shard_map/ppermute | solution.py:297
  101.0 27.9 %collective-permute-start.11 = (bf16[128,1024]{1,0:T(8,128)(2,1)}, bf16[128,1024]{1,0:T(8,128)(2,1)S(1)}, u32[]{:S(2)}, u32[]{:S(2)}) collective-permute-start(bf16[128,1024]{1,0:T(8,128)(2,1)} %collective-permute-done.10.tall_2), channel_id=1, source_target_pairs={{0,2},{2,0},{1,3},{3,1},{4,6},{6,4},{5,7},{7,5},{8,10},{10,8},{9,1... | collective-permute-start | bytes 786440 | tf_op jit(solution)/shard_map/ppermute | solution.py:297
  102.8 26.1 %collective-permute-start.6 = (bf16[4,64,512]{2,1,0:T(8,128)(2,1)S(1)}, bf16[4,64,512]{2,1,0:T(8,128)(2,1)S(1)}, u32[]{:S(2)}, u32[]{:S(2)}) collective-permute-start(bf16[4,64,512]{2,1,0:T(8,128)(2,1)S(1)} %slice.231.sheet_0), channel_id=1, source_target_pairs={{0,2},{2,0},{1,3},{3,1},{4,6},{6,4},{5,7},{7,5},{8,10},{10,8},{9,1... | collective-permute-start | bytes 786440 | tf_op jit(solution)/shard_map/ppermute | solution.py:297
  105.1 23.8 %collective-permute-start.8 = (bf16[4,64,512]{2,1,0:T(8,128)(2,1)}, bf16[4,64,512]{2,1,0:T(8,128)(2,1)S(1)}, u32[]{:S(2)}, u32[]{:S(2)}) collective-permute-start(bf16[4,64,512]{2,1,0:T(8,128)(2,1)} %collective-permute-done.7.sheet_2), channel_id=1, source_target_pairs={{0,2},{2,0},{1,3},{3,1},{4,6},{6,4},{5,7},{7,5},{8,10},{10,8},{9,1... | collective-permute-start | bytes 786440 | tf_op jit(solution)/shard_map/ppermute | solution.py:297
  146.2 47.2 %collective-permute-start.47 = (bf16[2,128,1024]{2,1,0:T(8,128)(2,1)}, bf16[2,128,1024]{2,1,0:T(8,128)(2,1)}, u32[]{:S(2)}, u32[]{:S(2)}) collective-permute-start(bf16[2,128,1024]{2,1,0:T(8,128)(2,1)} %get-tuple-element.55), channel_id=1, source_target_pairs={{0,2},{2,0},{1,3},{3,1},{4,6},{6,4},{5,7},{7,5},{8,10},{10,8},{9,1... | collective-permute-start | bytes 1572872 | tf_op jit(solution)/shard_map/ppermute | solution.py:297
  147.5 25.6 %copy-start.21 = (f32[1,384]{1,0:T(1,128)S(1)}, f32[1,384]{1,0:T(1,128)}, u32[]{:S(2)}) copy-start(f32[1,384]{1,0:T(1,128)} %get-tuple-element.47) | copy-start | bytes 4612
  147.5 25.6 %copy-start.27 = (pred[8]{0:T(512)(128)(4,1)S(1)}, pred[8]{0:T(512)(128)(4,1)}, u32[]{:S(2)}) copy-start(pred[8]{0:T(512)(128)(4,1)} %iota_compare_fusion.5) | copy-start | bytes 28
  147.5 27.0 %copy-start.24 = (pred[2]{0:T(512)(128)(4,1)S(1)}, pred[2]{0:T(512)(128)(4,1)}, u32[]{:S(2)}) copy-start(pred[2]{0:T(512)(128)(4,1)} %iota_compare_fusion.3) | copy-start | bytes 10
  147.5 41.4 %copy-start.20 = (pred[16]{0:T(512)(128)(4,1)S(1)}, pred[16]{0:T(512)(128)(4,1)}, u32[]{:S(2)}) copy-start(pred[16]{0:T(512)(128)(4,1)} %broadcast_in_dim.163) | copy-start | bytes 52
  147.5 44.8 %copy-start.13 = (bf16[2,4,64,384]{3,2,1,0:T(8,128)(2,1)S(1)}, bf16[2,4,64,384]{3,2,1,0:T(8,128)(2,1)}, u32[]{:S(2)}) copy-start(bf16[2,4,64,384]{3,2,1,0:T(8,128)(2,1)} %get-tuple-element.49) | copy-start | bytes 1179652
  167.8 25.7 %copy-start.11 = (bf16[2,128,1024]{2,1,0:T(8,128)(2,1)S(1)}, bf16[2,128,1024]{2,1,0:T(8,128)(2,1)}, u32[]{:S(2)}) copy-start(bf16[2,128,1024]{2,1,0:T(8,128)(2,1)} %get-tuple-element.54) | copy-start | bytes 1572868
  167.9 30.0 %copy-start.12 = (bf16[2,4,64,512]{3,2,1,0:T(8,128)(2,1)S(1)}, bf16[2,4,64,512]{3,2,1,0:T(8,128)(2,1)}, u32[]{:S(2)}) copy-start(bf16[2,4,64,512]{3,2,1,0:T(8,128)(2,1)} %get-tuple-element.52) | copy-start | bytes 1572868
  167.9 27.0 %collective-permute-start.42 = (bf16[2,4,64,512]{3,2,1,0:T(8,128)(2,1)}, bf16[2,4,64,512]{3,2,1,0:T(8,128)(2,1)}, u32[]{:S(2)}, u32[]{:S(2)}) collective-permute-start(bf16[2,4,64,512]{3,2,1,0:T(8,128)(2,1)} %get-tuple-element.53), channel_id=1, source_target_pairs={{0,2},{2,0},{1,3},{3,1},{4,6},{6,4},{5,7},{7,5},{8,10},{10,8},{9,1... | collective-permute-start | bytes 1572872 | tf_op jit(solution)/shard_map/ppermute | solution.py:297
  168.8 5.8 %collective-permute-start.39 = (bf16[128,1024]{1,0:T(8,128)(2,1)}, bf16[128,1024]{1,0:T(8,128)(2,1)}, u32[]{:S(2)}, u32[]{:S(2)}) collective-permute-start(bf16[128,1024]{1,0:T(8,128)(2,1)} %get-tuple-element.51), channel_id=1, source_target_pairs={{0,0},{1,2},{2,1},{3,3},{8,16},{9,18},{10,17},{11,19},{16,8},{17,1... | collective-permute-start | bytes 786440 | tf_op jit(solution)/shard_map/ppermute | solution.py:998
  172.4 20.0 %collective-permute-start.34 = (bf16[2,4,64,384]{3,2,1,0:T(8,128)(2,1)}, bf16[2,4,64,384]{3,2,1,0:T(8,128)(2,1)}, u32[]{:S(2)}, u32[]{:S(2)}) collective-permute-start(bf16[2,4,64,384]{3,2,1,0:T(8,128)(2,1)} %get-tuple-element.50), channel_id=1, source_target_pairs={{0,2},{2,0},{1,3},{3,1},{4,6},{6,4},{5,7},{7,5},{8,10},{10,8},{9,1... | collective-permute-start | bytes 1179656 | tf_op jit(solution)/shard_map/ppermute | solution.py:297
  172.4 58.0 %collective-permute-start.21 = (bf16[704,1024]{1,0:T(8,128)(2,1)}, bf16[704,1024]{1,0:T(8,128)(2,1)S(1)}, u32[]{:S(2)}, u32[]{:S(2)}) collective-permute-start(bf16[704,1024]{1,0:T(8,128)(2,1)} %get-tuple-element.40), channel_id=1, source_target_pairs={{0,1},{1,0},{2,3},{3,2},{4,5},{5,4},{6,7},{7,6},{8,9},{9,8},{10,11... | collective-permute-start | bytes 4325384 | tf_op jit(solution)/shard_map/ppermute | solution.py:297
  175.5 14.4 %collective-permute-start.40 = (bf16[64,1024]{1,0:T(8,128)(2,1)S(1)}, bf16[64,1024]{1,0:T(8,128)(2,1)S(1)}, u32[]{:S(2)}, u32[]{:S(2)}) collective-permute-start(bf16[64,1024]{1,0:T(8,128)(2,1)S(1)} %dynamic-slice_bitcast_fusion), channel_id=1, source_target_pairs={{0,1},{1,0},{2,3},{3,2},{4,5},{5,4},{6,7},{7,6},{8,9},{9,8},{10,11... | collective-permute-start | bytes 393224 | tf_op jit(solution)/shard_map/ppermute | solution.py:297
  189.9 39.2 %collective-permute-start.25 = (bf16[704,1024]{1,0:T(8,128)(2,1)}, bf16[704,1024]{1,0:T(8,128)(2,1)S(1)}, u32[]{:S(2)}, u32[]{:S(2)}) collective-permute-start(bf16[704,1024]{1,0:T(8,128)(2,1)} %get-tuple-element.45), channel_id=1, source_target_pairs={{0,1},{1,0},{2,3},{3,2},{4,5},{5,4},{6,7},{7,6},{8,9},{9,8},{10,11... | collective-permute-start | bytes 4325384 | tf_op jit(solution)/shard_map/ppermute | solution.py:297
  192.4 81.4 %collective-permute-start.41 = (bf16[64,1024]{1,0:T(8,128)(2,1)S(1)}, bf16[64,1024]{1,0:T(8,128)(2,1)}, u32[]{:S(2)}, u32[]{:S(2)}) collective-permute-start(bf16[64,1024]{1,0:T(8,128)(2,1)S(1)} %fusion.27), channel_id=1, source_target_pairs={{0,16},{16,0},{1,17},{17,1},{2,18},{18,2},{3,19},{19,3},{4,20},{20... | collective-permute-start | bytes 393224 | tf_op jit(solution)/shard_map/ppermute | solution.py:297
  193.5 16.7 %collective-permute-start.35 = (bf16[4,64,384]{2,1,0:T(8,128)(2,1)S(1)}, bf16[4,64,384]{2,1,0:T(8,128)(2,1)S(1)}, u32[]{:S(2)}, u32[]{:S(2)}) collective-permute-start(bf16[4,64,384]{2,1,0:T(8,128)(2,1)S(1)} %fusion.28), channel_id=1, source_target_pairs={{0,8},{8,0},{1,9},{9,1},{2,10},{10,2},{3,11},{11,3},{4,12},{12,4},... | collective-permute-start | bytes 589832 | tf_op jit(solution)/shard_map/ppermute | solution.py:297
  194.8 26.6 %collective-permute-start.48 = (bf16[128,1024]{1,0:T(8,128)(2,1)S(1)}, bf16[128,1024]{1,0:T(8,128)(2,1)S(1)}, u32[]{:S(2)}, u32[]{:S(2)}) collective-permute-start(bf16[128,1024]{1,0:T(8,128)(2,1)S(1)} %fusion.26), channel_id=1, source_target_pairs={{0,8},{8,0},{1,9},{9,1},{2,10},{10,2},{3,11},{11,3},{4,12},{12,4},... | collective-permute-start | bytes 786440 | tf_op jit(solution)/shard_map/ppermute | solution.py:297
  199.0 30.1 %copy-start.3 = (f32[704,1024]{1,0:T(8,128)S(1)}, f32[704,1024]{1,0:T(8,128)}, u32[]{:S(2)}) copy-start(f32[704,1024]{1,0:T(8,128)} %get-tuple-element.44) | copy-start | bytes 8650756
  210.3 1.4 collective-permute-start.36
  211.6 15.4 %collective-permute-start.43 = (bf16[4,64,512]{2,1,0:T(8,128)(2,1)S(1)}, bf16[4,64,512]{2,1,0:T(8,128)(2,1)S(1)}, u32[]{:S(2)}, u32[]{:S(2)}) collective-permute-start(bf16[4,64,512]{2,1,0:T(8,128)(2,1)S(1)} %fusion.25), channel_id=1, source_target_pairs={{0,8},{8,0},{1,9},{9,1},{2,10},{10,2},{3,11},{11,3},{4,12},{12,4},... | collective-permute-start | bytes 786440 | tf_op jit(solution)/shard_map/ppermute | solution.py:297
  221.4 7.6 %collective-permute-start.37 = (bf16[2,64,384]{2,1,0:T(8,128)(2,1)S(1)}, bf16[2,64,384]{2,1,0:T(8,128)(2,1)S(1)}, u32[]{:S(2)}, u32[]{:S(2)}) collective-permute-start(bf16[2,64,384]{2,1,0:T(8,128)(2,1)S(1)} %get-tuple-element.91), channel_id=1, source_target_pairs={{0,4},{4,0},{1,5},{5,1},{2,6},{6,2},{3,7},{7,3},{8,12},{12,8},{9,1... | collective-permute-start | bytes 294920 | tf_op jit(solution)/shard_map/ppermute | solution.py:297
  227.1 55.9 %collective-permute-start.49 = (bf16[128,1024]{1,0:T(8,128)(2,1)S(1)}, bf16[128,1024]{1,0:T(8,128)(2,1)S(1)}, u32[]{:S(2)}, u32[]{:S(2)}) collective-permute-start(bf16[128,1024]{1,0:T(8,128)(2,1)S(1)} %fusion.20), channel_id=1, source_target_pairs={{0,16},{16,0},{1,17},{17,1},{2,18},{18,2},{3,19},{19,3},{4,20},{20... | collective-permute-start | bytes 786440 | tf_op jit(solution)/shard_map/ppermute | solution.py:297
  229.1 33.2 %copy-start.7 = (bf16[2,2,64,384]{3,2,1,0:T(8,128)(2,1)}, bf16[2,2,64,384]{3,2,1,0:T(8,128)(2,1)S(1)}, u32[]{:S(2)}) copy-start(bf16[2,2,64,384]{3,2,1,0:T(8,128)(2,1)S(1)} %pad_maximum_fusion.6.own) | copy-start | bytes 589828
  230.0 20.7 %collective-permute-start.26 = (bf16[176,1024]{1,0:T(8,128)(2,1)S(1)}, bf16[176,1024]{1,0:T(8,128)(2,1)S(1)}, u32[]{:S(2)}, u32[]{:S(2)}) collective-permute-start(bf16[176,1024]{1,0:T(8,128)(2,1)S(1)} %get-tuple-element.69), channel_id=1, source_target_pairs={{0,16},{16,0},{1,17},{17,1},{2,18},{18,2},{3,19},{19,3},{4,20},{20... | collective-permute-start | bytes 1081352 | tf_op jit(solution)/shard_map/ppermute | solution.py:297
  230.4 20.6 %collective-permute-start.27 = (bf16[176,1024]{1,0:T(8,128)(2,1)S(1)}, bf16[176,1024]{1,0:T(8,128)(2,1)S(1)}, u32[]{:S(2)}, u32[]{:S(2)}) collective-permute-start(bf16[176,1024]{1,0:T(8,128)(2,1)S(1)} %get-tuple-element.71), channel_id=1, source_target_pairs={{0,4},{4,0},{1,5},{5,1},{2,6},{6,2},{3,7},{7,3},{8,12},{12,8},{9,1... | collective-permute-start | bytes 1081352 | tf_op jit(solution)/shard_map/ppermute | solution.py:297
  230.4 20.9 %collective-permute-start.28 = (bf16[176,1024]{1,0:T(8,128)(2,1)S(1)}, bf16[176,1024]{1,0:T(8,128)(2,1)S(1)}, u32[]{:S(2)}, u32[]{:S(2)}) collective-permute-start(bf16[176,1024]{1,0:T(8,128)(2,1)S(1)} %get-tuple-element.70), channel_id=1, source_target_pairs={{0,20},{4,16},{16,4},{20,0},{1,21},{5,17},{17,5},{21,1},{2,22},{6,... | collective-permute-start | bytes 1081352 | tf_op jit(solution)/shard_map/ppermute | solution.py:298
  234.4 34.8 %copy-start.5 = (bf16[176,1024]{1,0:T(8,128)(2,1)S(1)}, bf16[176,1024]{1,0:T(8,128)(2,1)}, u32[]{:S(2)}) copy-start(bf16[176,1024]{1,0:T(8,128)(2,1)} %param.17) | copy-start | bytes 1081348
  250.7 10.4 %collective-permute-start.22 = (bf16[176,1024]{1,0:T(8,128)(2,1)S(1)}, bf16[176,1024]{1,0:T(8,128)(2,1)S(1)}, u32[]{:S(2)}, u32[]{:S(2)}) collective-permute-start(bf16[176,1024]{1,0:T(8,128)(2,1)S(1)} %get-tuple-element.72), channel_id=1, source_target_pairs={{0,16},{16,0},{1,17},{17,1},{2,18},{18,2},{3,19},{19,3},{4,20},{20... | collective-permute-start | bytes 1081352 | tf_op jit(solution)/shard_map/ppermute | solution.py:297
  251.0 11.3 %collective-permute-start.23 = (bf16[176,1024]{1,0:T(8,128)(2,1)S(1)}, bf16[176,1024]{1,0:T(8,128)(2,1)S(1)}, u32[]{:S(2)}, u32[]{:S(2)}) collective-permute-start(bf16[176,1024]{1,0:T(8,128)(2,1)S(1)} %get-tuple-element.74), channel_id=1, source_target_pairs={{0,4},{4,0},{1,5},{5,1},{2,6},{6,2},{3,7},{7,3},{8,12},{12,8},{9,1... | collective-permute-start | bytes 1081352 | tf_op jit(solution)/shard_map/ppermute | solution.py:297
  251.3 17.8 %collective-permute-start.24 = (bf16[176,1024]{1,0:T(8,128)(2,1)S(1)}, bf16[176,1024]{1,0:T(8,128)(2,1)S(1)}, u32[]{:S(2)}, u32[]{:S(2)}) collective-permute-start(bf16[176,1024]{1,0:T(8,128)(2,1)S(1)} %get-tuple-element.73), channel_id=1, source_target_pairs={{0,20},{4,16},{16,4},{20,0},{1,21},{5,17},{17,5},{21,1},{2,22},{6,... | collective-permute-start | bytes 1081352 | tf_op jit(solution)/shard_map/ppermute | solution.py:298
  261.1 9.6 %collective-permute-start.44 = (bf16[2,64,512]{2,1,0:T(8,128)(2,1)S(1)}, bf16[2,64,512]{2,1,0:T(8,128)(2,1)S(1)}, u32[]{:S(2)}, u32[]{:S(2)}) collective-permute-start(bf16[2,64,512]{2,1,0:T(8,128)(2,1)S(1)} %get-tuple-element.83), channel_id=1, source_target_pairs={{0,1},{1,0},{2,3},{3,2},{4,5},{5,4},{6,7},{7,6},{8,9},{9,8},{10,11... | collective-permute-start | bytes 393224 | tf_op jit(solution)/shard_map/ppermute | solution.py:297
  262.3 13.0 %collective-permute-start.38 = (bf16[2,2,64,384]{3,2,1,0:T(8,128)(2,1)S(1)}, bf16[2,2,64,384]{3,2,1,0:T(8,128)(2,1)S(1)}, u32[]{:S(2)}, u32[]{:S(2)}) collective-permute-start(bf16[2,2,64,384]{3,2,1,0:T(8,128)(2,1)S(1)} %pad_maximum_fusion.6.own), channel_id=1, source_target_pairs={{0,16},{16,0},{1,17},{17,1},{2,18},{18,2},{3,19},{19,3},{4,20},{20... | collective-permute-start | bytes 589832 | tf_op jit(solution)/shard_map/ppermute | solution.py:297
  270.7 1.3 collective-permute-start.29
  270.8 8.3 %collective-permute-start.45 = (bf16[2,64,512]{2,1,0:T(8,128)(2,1)S(1)}, bf16[2,64,512]{2,1,0:T(8,128)(2,1)S(1)}, u32[]{:S(2)}, u32[]{:S(2)}) collective-permute-start(bf16[2,64,512]{2,1,0:T(8,128)(2,1)S(1)} %get-tuple-element.81), channel_id=1, source_target_pairs={{0,4},{4,0},{1,5},{5,1},{2,6},{6,2},{3,7},{7,3},{8,12},{12,8},{9,1... | collective-permute-start | bytes 393224 | tf_op jit(solution)/shard_map/ppermute | solution.py:297
  271.9 6.1 %collective-permute-start.30 = (f32[16,768]{1,0:T(8,128)S(1)}, f32[16,768]{1,0:T(8,128)S(1)}, u32[]{:S(2)}, u32[]{:S(2)}) collective-permute-start(f32[16,768]{1,0:T(8,128)S(1)} %add.281), channel_id=1, source_target_pairs={{0,2},{2,0},{1,3},{3,1},{4,6},{6,4},{5,7},{7,5},{8,10},{10,8},{9,1... | collective-permute-start | bytes 147464 | tf_op jit(solution)/shard_map/ppermute | solution.py:297
  278.1 4.2 %collective-permute-start.31 = (f32[16,768]{1,0:T(8,128)S(1)}, f32[16,768]{1,0:T(8,128)S(1)}, u32[]{:S(2)}, u32[]{:S(2)}) collective-permute-start(f32[16,768]{1,0:T(8,128)S(1)} %add.282), channel_id=1, source_target_pairs={{0,4},{4,0},{1,5},{5,1},{2,6},{6,2},{3,7},{7,3},{8,12},{12,8},{9,1... | collective-permute-start | bytes 147464 | tf_op jit(solution)/shard_map/ppermute | solution.py:297
  279.1 10.1 %collective-permute-start.46 = (bf16[2,2,64,512]{3,2,1,0:T(8,128)(2,1)S(1)}, bf16[2,2,64,512]{3,2,1,0:T(8,128)(2,1)S(1)}, u32[]{:S(2)}, u32[]{:S(2)}) collective-permute-start(bf16[2,2,64,512]{3,2,1,0:T(8,128)(2,1)S(1)} %pad_maximum_fusion.3.own), channel_id=1, source_target_pairs={{0,16},{16,0},{1,17},{17,1},{2,18},{18,2},{3,19},{19,3},{4,20},{20... | collective-permute-start | bytes 786440 | tf_op jit(solution)/shard_map/ppermute | solution.py:297
  282.2 5.6 %collective-permute-start.32 = (f32[16,768]{1,0:T(8,128)S(1)}, f32[16,768]{1,0:T(8,128)S(1)}, u32[]{:S(2)}, u32[]{:S(2)}) collective-permute-start(f32[16,768]{1,0:T(8,128)S(1)} %add.283), channel_id=1, source_target_pairs={{0,8},{8,0},{1,9},{9,1},{2,10},{10,2},{3,11},{11,3},{4,12},{12,4},... | collective-permute-start | bytes 147464 | tf_op jit(solution)/shard_map/ppermute | solution.py:297
  287.8 4.3 %collective-permute-start.33 = (f32[16,768]{1,0:T(8,128)S(1)}, f32[16,768]{1,0:T(8,128)S(1)}, u32[]{:S(2)}, u32[]{:S(2)}) collective-permute-start(f32[16,768]{1,0:T(8,128)S(1)} %add.284), channel_id=1, source_target_pairs={{0,16},{16,0},{1,17},{17,1},{2,18},{18,2},{3,19},{19,3},{4,20},{20... | collective-permute-start | bytes 147464 | tf_op jit(solution)/shard_map/ppermute | solution.py:297
  (20 other events, 187.3 us)

commit v3 on v2

--- a/solution.py
+++ b/solution.py
@@ -287,9 +287,10 @@
 
 PAIR = [(0, 1), (1, 0)]
 BLOCKS = 8
+NEAR, FAR = (0, 4, 1, 5), (2, 6, 3, 7)
 LANE = 128
 GROUP = ("o", "p", "q", "c")
-VMEM_BYTES = 56 * 1024 * 1024
+VMEM_BYTES = 28 * 1024 * 1024
 
 
 def swap(values, *axes):
@@ -305,6 +306,10 @@
     )
 
 
+def pin(*values):
+    return lax.optimization_barrier(values)
+
+
 def take(values, at, axis=0):
     return lax.dynamic_index_in_dim(values, at, axis, keepdims=False)
 
@@ -325,7 +330,7 @@
     return tuple(ids_ref[i] for i in range(5))
 
 
-def call(kernel, outs, scratch, flops, *operands, memory):
+def call(kernel, outs, scratch, micros, *operands, memory):
     whole = pl.BlockSpec(memory_space=pltpu.VMEM)
     specs = {
         "s": pl.BlockSpec(memory_space=pltpu.SMEM),
@@ -340,7 +345,9 @@
         out_specs=tuple(whole for _ in outs),
         scratch_shapes=scratch,
         compiler_params=pltpu.CompilerParams(vmem_limit_bytes=VMEM_BYTES),
-        cost_estimate=pl.CostEstimate(flops=flops, bytes_accessed=size, transcendentals=0),
+        cost_estimate=pl.CostEstimate(
+            flops=int(micros * 1.15e9), bytes_accessed=size, transcendentals=0
+        ),
     )(*operands)
 
 
@@ -359,11 +366,11 @@
         copy.wait()
 
 
-def row_pairs(near, far, target, start, cap):
+def row_pairs(sources, target):
     return [
-        (source.at[k, pl.ds(start, cap)], target.at[pl.ds((half * 4 + k) * cap, cap)])
-        for half, source in enumerate((near, far))
-        for k in range(4)
+        (source.at[k], target.at[pl.ds(block * source.shape[1], source.shape[1])])
+        for source, blocks in sources
+        for k, block in enumerate(blocks)
     ]
 
 
@@ -430,8 +437,42 @@
     half[...] = down[pl.ds(pl.multiple_of(x * rows, rows), rows), :]
 
 
+def turner(cap):
+    lane = lax.broadcasted_iota(jnp.int32, (cap, LANE), 1)
+    lead = lane % HEAD < ROT // 2
+
+    def turn(values, cos_part, sin_part):
+        other = jnp.where(
+            lead, pltpu.roll(values, LANE - ROT // 2, 1), pltpu.roll(values, ROT // 2, 1)
+        )
+        return values * cos_part + other * sin_part
+
+    return turn, (lane < HEAD, lane >= HEAD)
+
+
+def token_pairs(sources, target):
+    return row_pairs(zip(sources, ((0, 1), (2, 3), (4, 5), (6, 7))), target)
+
+
+def both_ways(step, near_out, far_out, cap):
+    def first(block, carry):
+        near_out[block_rows(block, cap), :] = step(block // 2 * 4 + block % 2)
+        return carry
+
+    def second(block, carry):
+        far_out[block_rows(block, cap), :] = low(step(block // 2 * 4 + block % 2 + 2))
+        return carry
+
+    lax.fori_loop(0, BLOCKS // 2, first, 0)
+    lax.fori_loop(0, BLOCKS // 2, second, 0)
+
+
 def attention_kernel(
     ids,
+    block_0,
+    block_1,
+    block_2,
+    block_3,
     near,
     far,
     sheet_0,
@@ -439,15 +480,18 @@
     sheet_2,
     sheet_3,
     output_weight,
+    fed,
     cosine,
     sine,
     position,
     gain,
     shift,
     offset,
-    mixed_ref,
+    near_out,
+    far_out,
     grad_ref,
-    home,
+    home_0,
+    home_1,
     away,
     output_grad,
     grad_sum,
@@ -455,34 +499,26 @@
     cotangent,
     joint,
     inputs,
+    mixed_all,
     total,
     sems,
 ):
-    places = places_of(ids)
-    cap = near.shape[1] // 2
-    copies = fetch(
-        sheet_pairs((sheet_0, sheet_1, sheet_2, sheet_3), joint, places)
-        + row_pairs(near, far, tokens, 0, cap)
-        + row_pairs(near, far, cotangent, cap, cap),
-        sems,
-    )
-    finish(copies)
+    cap = block_0.shape[1]
+    finish(
+        fetch(
+            sheet_pairs((sheet_0, sheet_1, sheet_2, sheet_3), joint, places_of(ids))
+            + token_pairs((block_0, block_1, block_2, block_3), tokens)
+            + row_pairs(((near, NEAR), (far, FAR)), cotangent),
+            sems,
+        )
+    )
     total[...] = jnp.zeros_like(total)
-    lane = lax.broadcasted_iota(jnp.int32, (cap, LANE), 1)
-    lead = lane % HEAD < ROT // 2
-    mine = (lane < HEAD, lane >= HEAD)
+    turn, mine = turner(cap)
     down = lax.broadcasted_iota(jnp.int32, (cap, cap), 0)
     along = lax.broadcasted_iota(jnp.int32, (cap, cap), 1)
     scale = HEAD ** (-0.5)
-    half_rot = ROT // 2
-
-    def turn(values, cos_part, sin_part):
-        other = jnp.where(
-            lead, pltpu.roll(values, LANE - half_rot, 1), pltpu.roll(values, half_rot, 1)
-        )
-        return values * cos_part + other * sin_part
-
-    def step(block, carry):
+
+    def step(block):
         rows = block_rows(block, cap)
         input_low = low(norm_of(tokens[rows, :]) * gain[...] + shift[...])
         inputs[rows, :] = input_low
@@ -494,8 +530,7 @@
         grad_mixed = low(across(cotangent[rows, :], output_weight[...]))
         allowed = (along <= down) & (along >= down - position[rows, :])
         found = []
-        for head in (0, 1):
-            own = mine[head]
+        for own in mine:
             query_own = jnp.where(own, query, jnp.zeros_like(query))
             grad_own = jnp.where(own, grad_mixed, jnp.zeros_like(grad_mixed))
             scores = jnp.where(allowed, across(query_own, keys) * scale, -1e30)
@@ -516,7 +551,8 @@
         mixed, grad_query, grad_keys, grad_value = (
             jnp.where(mine[0], first, second) for first, second in zip(*found)
         )
-        mixed_ref[rows, :] = low(mixed)
+        mixed = low(mixed)
+        mixed_all[rows, :] = mixed
         grad_joint = low(
             jnp.concatenate(
                 [
@@ -529,29 +565,47 @@
         )
         grad_ref[rows, :] = grad_joint
         total[...] += fold(wide(grad_joint))
-        return carry
-
-    lax.fori_loop(0, BLOCKS, step, 0)
+        return times(mixed, output_weight[...]) + wide(fed[rows, :])
+
+    both_ways(step, near_out, far_out, cap)
     grad_sum[...] = jnp.sum(total[...], axis=0, keepdims=True)
-    output_grad[...] = low(contract_rows(mixed_ref[...], cotangent[...]))
-    sheet_grads(inputs, grad_ref, home, away, places)
-
-
-def sheet_grads(inputs, grads, home, away, places):
+    output_grad[...] = low(contract_rows(mixed_all[...], cotangent[...]))
+    half = away.shape[0] // 2
+    here = home_0, away.at[pl.ds(0, half)]
+    there = home_1, away.at[pl.ds(half, half)]
+    sheet_grads(inputs, grad_ref, here, there, 0, places_of(ids))
+
+
+def for_place(at, here, there, store):
+    pl.when(at)(lambda: store(*here))
+    pl.when(jnp.logical_not(at))(lambda: store(*there))
+
+
+def sheet_grads(inputs, grads, here, there, base, places):
     x, o, p, q, c = places
-    rows = home.shape[2]
+    columns = grads.shape[1]
+    rows = D // 16
     for oo in (0, 1):
         found = contract_rows(inputs[:, oo * D // 2 : (oo + 1) * D // 2], grads[...])
-        found = low(found).reshape(2, 2, 2, rows, -1)
-        for pp in (0, 1):
-            for cc in (0, 1):
-                at = (c ^ cc) * 2 + (p ^ pp)
-                home[o ^ oo, at] = jnp.where(q == 0, found[pp, 0, cc], found[pp, 1, cc])
-                away[o ^ oo, at] = jnp.where(q == 0, found[pp, 1, cc], found[pp, 0, cc])
-
-
-def forward_kernel(
+        found = low(found).reshape(2, 2, 2, rows, columns)
+
+        def store(home, away, found=found):
+            for pp in (0, 1):
+                for cc in (0, 1):
+                    down = pl.ds(pl.multiple_of(base + (p ^ pp) * rows, rows), rows)
+                    along = pl.ds(pl.multiple_of((c ^ cc) * columns, LANE), columns)
+                    home[down, along] = jnp.where(q == 0, found[pp, 0, cc], found[pp, 1, cc])
+                    away[down, along] = jnp.where(q == 0, found[pp, 1, cc], found[pp, 0, cc])
+
+        for_place(o == oo, here, there, store)
+
+
+def feed_kernel(
     ids,
+    block_0,
+    block_1,
+    block_2,
+    block_3,
     near,
     far,
     sheet_0,
@@ -562,177 +616,152 @@
     tall_1,
     tall_2,
     tall_3,
-    output_weight,
-    mixed,
     gain,
     shift,
     offset,
-    inputs,
-    before_ref,
-    near_out,
-    far_out,
-    home,
-    away,
-    tokens,
-    cotangent,
-    up,
-    down,
-    active_all,
-    sems,
-):
-    places = places_of(ids)
-    x, o, p, q, c = places
-    cap = near.shape[1] // 2
-    copies = fetch(
-        sheet_pairs((sheet_0, sheet_1, sheet_2, sheet_3), up, places)
-        + tall_pairs((tall_0, tall_1, tall_2, tall_3), down, places)
-        + row_pairs(near, far, tokens, 0, cap)
-        + row_pairs(near, far, cotangent, cap, cap),
-        sems,
-    )
-    finish(copies)
-
-    def step(block, target):
-        rows = block_rows(block, cap)
-        input_low = low(norm_of(tokens[rows, :]) * gain[...] + shift[...])
-        inputs[rows, :] = input_low
-        before = times(input_low, up[...]) + offset[...]
-        before_ref[rows, :] = before
-        active = low(before * (0.5 + 0.5 * lax.erf(before * 0.5**0.5)))
-        active_all[rows, :] = active
-        return times(mixed[rows, :], output_weight[...]) + times(active, down[...])
-
-    def first(block, carry):
-        near_out[block_rows(block, cap), :] = step(block, None)
-        return carry
-
-    def second(block, carry):
-        far_out[block_rows(block, cap), :] = low(step(block + BLOCKS // 2, None))
-        return carry
-
-    lax.fori_loop(0, BLOCKS // 2, first, 0)
-    lax.fori_loop(0, BLOCKS // 2, second, 0)
-    unit = home.shape[1]
-    for oo in (0, 1):
-        found = low(contract_rows(active_all[:, oo * 2 * unit : (oo + 1) * 2 * unit], cotangent[...]))
-        home[o ^ oo] = jnp.where(q == 0, found[:unit], found[unit:])
-        away[o ^ oo] = jnp.where(q == 0, found[unit:], found[:unit])
-
-
-def backward_kernel(
-    ids,
-    near,
-    far,
-    sheet_0,
-    sheet_1,
-    sheet_2,
-    sheet_3,
-    tall_0,
-    tall_1,
-    tall_2,
-    tall_3,
-    join_0,
-    join_1,
-    join_2,
-    join_3,
-    inputs,
-    before_all,
-    grad_joint,
-    gain_one,
-    gain_two,
-    near_out,
-    far_out,
-    home,
-    away,
-    sums,
+    fed,
+    grad_all,
+    home_0,
+    home_1,
+    away_0,
+    away_1,
     grad_sum,
     tokens,
     cotangent,
     up,
     down,
-    joint,
-    grad_all,
-    totals,
+    inputs,
+    active_all,
     total,
     sems,
 ):
     places = places_of(ids)
-    cap = near.shape[1] // 2
-    copies = fetch(
-        sheet_pairs((sheet_0, sheet_1, sheet_2, sheet_3), up, places)
-        + sheet_pairs((join_0, join_1, join_2, join_3), joint, places)
-        + tall_pairs((tall_0, tall_1, tall_2, tall_3), down, places)
-        + row_pairs(near, far, tokens, 0, cap)
-        + row_pairs(near, far, cotangent, cap, cap),
-        sems,
-    )
-    finish(copies)
-    totals[...] = jnp.zeros_like(totals)
+    x, o, p, q, c = places
+    cap = block_0.shape[1]
+    finish(
+        fetch(
+            sheet_pairs((sheet_0, sheet_1, sheet_2, sheet_3), up, places)
+            + token_pairs((block_0, block_1, block_2, block_3), tokens)
+            + row_pairs(((near, NEAR), (far, FAR)), cotangent)
+            + tall_pairs((tall_0, tall_1, tall_2, tall_3), down, places),
+            sems,
+        )
+    )
     total[...] = jnp.zeros_like(total)
 
-    def step(block, unused):
+    def step(block, carry):
         rows = block_rows(block, cap)
-        before = before_all[rows, :]
-        grad_active = across(cotangent[rows, :], down[...])
+        input_low = low(norm_of(tokens[rows, :]) * gain[...] + shift[...])
+        inputs[rows, :] = input_low
+        before = times(input_low, up[...]) + offset[...]
         slope = 0.5 + 0.5 * lax.erf(before * 0.5**0.5)
+        active = low(before * slope)
+        active_all[rows, :] = active
         slope = slope + before * jnp.exp(-0.5 * before * before) * (0.5 / jnp.pi) ** 0.5
-        grad_before = low(grad_active * slope)
+        grad_before = low(across(cotangent[rows, :], down[...]) * slope)
         grad_all[rows, :] = grad_before
         total[...] += fold(wide(grad_before))
+        fed[rows, :] = low(times(active, down[...]))
+        return carry
+
+    lax.fori_loop(0, BLOCKS, step, 0)
+    grad_sum[...] = jnp.sum(total[...], axis=0, keepdims=True)
+    unit = home_0.shape[0] // 2
+    here, there = (home_0, away_0), (home_1, away_1)
+    for oo in (0, 1):
+        found = low(contract_rows(active_all[:, oo * 2 * unit : (oo + 1) * 2 * unit], cotangent[...]))
+
+        def store(home, away, found=found):
+            home[:unit, :] = jnp.where(q == 0, found[:unit], found[unit:])
+            away[:unit, :] = jnp.where(q == 0, found[unit:], found[:unit])
+
+        for_place(o == oo, here, there, store)
+    sheet_grads(inputs, grad_all, here, there, unit, places)
+
+
+def pull_kernel(
+    ids,
+    block_0,
+    block_1,
+    block_2,
+    block_3,
+    join_0,
+    join_1,
+    join_2,
+    join_3,
+    sheet_0,
+    sheet_1,
+    sheet_2,
+    sheet_3,
+    grad_joint,
+    grad_before,
+    gain_one,
+    gain_two,
+    near_out,
+    far_out,
+    sums,
+    tokens,
+    joint,
+    up,
+    totals,
+    sems,
+):
+    places = places_of(ids)
+    cap = block_0.shape[1]
+    finish(
+        fetch(
+            token_pairs((block_0, block_1, block_2, block_3), tokens)
+            + sheet_pairs((join_0, join_1, join_2, join_3), joint, places)
+            + sheet_pairs((sheet_0, sheet_1, sheet_2, sheet_3), up, places),
+            sems,
+        )
+    )
+    totals[...] = jnp.zeros_like(totals)
+
+    def step(block):
+        rows = block_rows(block, cap)
         normed = norm_of(tokens[rows, :])
         grad_first = across(grad_joint[rows, :], joint[...])
-        grad_second = across(grad_before, up[...])
+        grad_second = across(grad_before[rows, :], up[...])
         totals[0] += fold(grad_first * normed)
         totals[1] += fold(grad_first)
         totals[2] += fold(grad_second * normed)
         totals[3] += fold(grad_second)
         return grad_first * gain_one[...] + grad_second * gain_two[...]
 
-    def first(block, carry):
-        near_out[block_rows(block, cap), :] = step(block, None)
-        return carry
-
-    def second(block, carry):
-        far_out[block_rows(block, cap), :] = low(step(block + BLOCKS // 2, None))
-        return carry
-
-    lax.fori_loop(0, BLOCKS // 2, first, 0)
-    lax.fori_loop(0, BLOCKS // 2, second, 0)
+    both_ways(step, near_out, far_out, cap)
     sums[...] = jnp.sum(totals[...], axis=1)
-    grad_sum[...] = jnp.sum(total[...], axis=0, keepdims=True)
-    sheet_grads(inputs, grad_all, home, away, places)
-
-
-def lay_kernel(blocks, ids, own, other, out):
+
+
+def lay_kernel(ids, own, other, joint, up):
     x, o, p, q, c = places_of(ids)
+    parts = joint.shape[1] // D
     for xx, source in ((0, own), (1, other)):
         for pp in (0, 1):
             for cc in (0, 1):
                 values = wide(source[pp, cc])
-                for k, at in enumerate(blocks(x ^ xx, p ^ pp, c ^ cc)):
+                at_x, at_p, at_c = x ^ xx, p ^ pp, c ^ cc
+                blocks = [(joint, part * 8 + at_x * 4 + at_p * 2 + at_c) for part in range(parts)]
+                blocks += [
+                    (up, (((k // 2 * 2 + at_p) * 2 + k % 2) * 2 + at_c) * 2 + at_x) for k in range(4)
+                ]
+                for k, (out, at) in enumerate(blocks):
                     out[:, pl.ds(pl.multiple_of(at * LANE, LANE), LANE)] = values[
                         :, k * LANE : (k + 1) * LANE
                     ]
 
 
-def joint_blocks(x, p, c):
-    return [part * 8 + x * 4 + p * 2 + c for part in range(3)]
-
-
-def up_blocks(x, p, c):
-    return [(((oo * 2 + p) * 2 + qq) * 2 + c) * 2 + x for oo in (0, 1) for qq in (0, 1)]
-
-
-def scatter_rows(near, far):
-    lane = near + wide(swap(far, "c"))
+def lane_sum(near, came):
+    lane = near + wide(came)
     rows = lane.shape[0] // 4
-    sent = low(lane[rows:])
-    return (
-        lane[:rows]
-        + wide(swap(sent[:rows], "x"))
-        + wide(swap(sent[rows : 2 * rows], "p"))
-        + wide(swap(sent[2 * rows :], "x", "p"))
-    )
+    return lane[:rows], *(low(lane[i * rows : (i + 1) * rows]) for i in (1, 2, 3))
+
+
+def total(*parts):
+    found = wide(parts[0])
+    for part in parts[1:]:
+        found += wide(part)
+    return found
 
 
 def grouped(
@@ -753,7 +782,7 @@
     down_weight,
     down_bias,
 ):
-    x, o, p, q, c = (lax.axis_index(name) for name in ("x", *GROUP))
+    x, o, p, q, c = (lax.axis_index(name) for name in ("x", "o", "p", "q", "c"))
     ids = jnp.stack([x, o, p, q, c]).astype(jnp.int32)
     cap = tokens.shape[0]
     rows = BLOCKS * cap
@@ -764,29 +793,6 @@
 
     def like(shape, kind):
         return jax.ShapeDtypeStruct(shape, kind)
-
-    small = jnp.concatenate(
-        [first_gain, first_bias, second_gain, second_bias, output_bias, down_bias, joint_bias, up_bias]
-    )[None]
-    for name, at in (("c", c), ("q", q), ("p", p), ("o", o)):
-        small = join(small, swap(small, name), at)
-
-    def vector(start, size):
-        return wide(small[:, start : start + size]).reshape(1, -1)
-
-    gain_one, shift_one, gain_two, shift_two, output_offset, down_offset = (
-        vector(i * part, part) for i in range(6)
-    )
-    joint_own = joint_bias.shape[0]
-    joint_offset = vector(6 * part, joint_own)
-    up_offset = vector(6 * part + joint_own, up_bias.shape[0])
-    joint_offset = take(joint_offset.reshape(3, 8, LANE), x * 4 + p * 2 + c, 1).reshape(1, 3 * LANE)
-    up_offset = take(take(take(up_offset.reshape(2, 2, 2, 2, 2, unit), x, 4), c, 3), p, 1)
-    up_offset = up_offset.reshape(1, hidden)
-
-    pair = jnp.concatenate([tokens, cotangent], axis=0)
-    near = jnp.stack([pair, swap(pair, "x"), swap(pair, "p"), swap(pair, "x", "p")], axis=0)
-    far = swap(near, "c")
 
     keep, send, down_half = call(
         cut_kernel,
@@ -804,17 +810,43 @@
         memory="svvv",
     )
     came = swap(send, "p")
+    along_p = swap(pin(tokens, send)[0], "p")
+    along_x = swap(tokens, "x")
+    down_other = swap(down_half, "o")
+
     turned = jnp.concatenate(
         [keep[:1], came[:1], swap(jnp.concatenate([keep[1:], came[1:]], axis=0), "c")], axis=0
     )
 
-    def spread(own):
-        other = swap(own, "o")
-        return own, swap(own, "q"), other, swap(other, "q")
-
-    joint_sheets = spread(turned[:, :, : 3 * LANE])
-    up_sheets = spread(turned[:, :, 3 * LANE :])
-    down_talls = spread(down_half)
+    tokens_0 = jnp.stack([tokens, along_x])
+    tokens_2 = jnp.stack([along_p, swap(along_p, "x")])
+
+    joint_own, up_own = turned[:, :, : 3 * LANE], turned[:, :, 3 * LANE :]
+    up_other, up_side = swap(up_own, "o"), swap(up_own, "q")
+    joint_other = swap(pin(joint_own, up_other)[0], "o")
+
+    vectors = (first_gain, first_bias, second_gain, second_bias, output_bias, down_bias, joint_bias, up_bias)
+    small = jnp.concatenate(pin(*vectors, send)[:-1])[None]
+    for name, at in (("c", c), ("p", p)):
+        small = join(small, swap(small, name), at)
+    small = pin(small, up_other)[0]
+    for name, at in (("q", q), ("o", o)):
+        small = join(small, swap(small, name), at)
+    small = small.reshape(2, 2, 2, 2, -1).transpose(0, 2, 1, 3, 4).reshape(16, -1)
+
+    def vector(start, size):
+        return wide(small[:, start : start + size]).reshape(1, -1)
+
+    gain_one, shift_one, gain_two, shift_two, output_offset, down_offset = (
+        vector(i * part, part) for i in range(6)
+    )
+    joint_size = joint_bias.shape[0]
+    joint_offset = vector(6 * part, joint_size)
+    up_offset = vector(6 * part + joint_size, up_bias.shape[0])
+    joint_offset = take(joint_offset.reshape(3, 8, LANE), x * 4 + p * 2 + c, 1).reshape(1, 3 * LANE)
+    up_offset = take(take(take(up_offset.reshape(2, 2, 2, 2, 2, unit), x, 4), c, 3), p, 1)
+    up_offset = up_offset.reshape(1, hidden)
+
     turn_over = [
         (((a * 2 + b) * 2 + e) * 2 + f, ((b * 2 + a) * 2 + f) * 2 + e)
         for a in (0, 1)
@@ -823,13 +855,13 @@
         for f in (0, 1)
     ]
     cross = ("x", "o", "q", "c")
-    output_pair = lax.ppermute(join(output_weight, swap(output_weight, "c"), c), cross, turn_over)
+    output_pair = join(output_weight, swap(output_weight, "c"), c)
 
     devices = jnp.stack(
         [
             ((((x ^ xx) * 2 + o) * 2 + (p ^ pp)) * 2 + q) * 2 + (c ^ cc)
+            for pp in (0, 1)
             for cc in (0, 1)
-            for pp in (0, 1)
             for xx in (0, 1)
         ]
     )
@@ -843,113 +875,159 @@
     sine = jnp.sin(angles)
     sine = jnp.where(place < half_rot, -sine, jnp.where(place < ROT, sine, 0.0))
 
-    sheet = (4, part, 3 * LANE)
     copies = pltpu.SemaphoreType.DMA
-    mixed, grad_joint, joint_home, joint_away, output_grad, joint_sum = call(
+
+    tokens_1, tokens_3 = swap(tokens_0, "c"), swap(tokens_2, "c")
+    grad_along_p = swap(pin(cotangent, along_p)[0], "p")
+    grad_pair = jnp.stack([cotangent, grad_along_p])
+    near_grad = jnp.concatenate([grad_pair, swap(grad_pair, "x")])
+    far_grad = swap(near_grad, "c")
+    up_sheets = up_own, up_side, up_other, swap(up_other, "q")
+    down_far = swap(jnp.stack([down_half, down_other]), "q")
+    down_talls = down_half, down_far[0], down_other, down_far[1]
+    joint_own, joint_other, output_pair, tokens_0 = pin(joint_own, joint_other, output_pair, tokens_0)
+    joint_side, joint_corner = swap(joint_own, "q"), swap(joint_other, "q")
+    output_pair = lax.ppermute(output_pair, cross, turn_over)
+    tall = (rows, D)
+    found = call(
+        feed_kernel,
+        [
+            like(tall, bf),
+            like((rows, hidden), bf),
+            *(like((2 * unit, D), bf) for _ in range(4)),
+            like((1, hidden), f32),
+        ],
+        [
+            pltpu.VMEM(tall, bf),
+            pltpu.VMEM(tall, bf),
+            pltpu.VMEM((D, hidden), bf),
+            pltpu.VMEM((hidden, D), bf),
+            pltpu.VMEM(tall, bf),
+            pltpu.VMEM((rows, hidden), bf),
+            pltpu.VMEM((8, hidden), f32),
+            copies((36,)),
+        ],
+        20,
+        ids,
+        tokens_0,
+        tokens_1,
+        tokens_2,
+        tokens_3,
+        near_grad,
+        far_grad,
+        *up_sheets,
+        *down_talls,
+        gain_two,
+        shift_two,
+        up_offset,
+        memory="shhhhhhhhhhhhhhvvv",
+    )
+    joint_side, joint_corner, output_pair, *found = pin(joint_side, joint_corner, output_pair, *found)
+    joint_sheets = joint_own, joint_side, joint_other, joint_corner
+    fed, grad_before, up_home_0, up_home_1, up_away_0, up_away_1, up_sum = found
+    up_away_1 = swap(up_away_1, "q")
+
+    found = call(
         attention_kernel,
         [
-            like((rows, LANE), bf),
+            like((rows // 2, D), f32),
+            like((rows // 2, D), bf),
             like((rows, 3 * LANE), bf),
-            like((2, *sheet), bf),
-            like((2, *sheet), bf),
+            like((2 * part, 6 * LANE), bf),
+            like((2 * part, 6 * LANE), bf),
+            like((4 * part, 6 * LANE), bf),
             like((LANE, D), bf),
             like((1, 3 * LANE), f32),
         ],
         [
-            pltpu.VMEM((rows, D), bf),
-            pltpu.VMEM((rows, D), bf),
+            pltpu.VMEM(tall, bf),
+            pltpu.VMEM(tall, bf),
             pltpu.VMEM((D, 3 * LANE), bf),
-            pltpu.VMEM((rows, D), bf),
+            pltpu.VMEM(tall, bf),
+            pltpu.VMEM((rows, LANE), bf),
             pltpu.VMEM((8, 3 * LANE), f32),
             copies((32,)),
         ],
-        rows * D * LANE * 16,
+        22,
         ids,
-        near,
-        far,
+        tokens_0,
+        tokens_1,
+        tokens_2,
+        tokens_3,
+        near_grad,
+        far_grad,
         *joint_sheets,
         output_pair,
+        fed,
         cosine,
         sine,
         position,
         gain_one,
         shift_one,
         joint_offset,
-        memory="shhhhhhvvvvvvv",
-    )
-
-    tall = (unit, D)
-    sheet = (4, part, hidden)
-    inputs, before, near_part, far_part, down_home, down_away = call(
-        forward_kernel,
+        memory="shhhhhhhhhhvvvvvvvv",
+    )
+    up_away_1, up_away_0, *found = pin(up_away_1, up_away_0, *found)
+    near_part, far_part, grad_joint, joint_home_0, joint_home_1, joint_away, output_grad, joint_sum = found
+
+    def lane_sum(near, came, block):
+        at = slice(block * cap, (block + 1) * cap)
+        return near[at] + wide(came[at])
+
+    up_sent = swap(low(total(up_home_1, up_away_1)), "o")
+    joint_away, up_away_0 = swap(joint_away, "q"), swap(up_away_0, "q")
+    result_lane = near_part, swap(far_part, "c")
+    result_sent, grad_joint = pin(
+        low(jnp.concatenate([lane_sum(*result_lane, 1), lane_sum(*result_lane, 3)])), grad_joint
+    )
+    result_came = swap(result_sent, "x")
+    output_part = lax.ppermute(output_grad, cross, turn_over)
+    found = call(
+        pull_kernel,
+        [like((rows // 2, D), f32), like((rows // 2, D), bf), like((4, D), f32)],
         [
-            like((rows, D), bf),
-            like((rows, hidden), f32),
-            like((rows // 2, D), f32),
-            like((rows // 2, D), bf),
-            like((2, *tall), bf),
-            like((2, *tall), bf),
+            pltpu.VMEM(tall, bf),
+            pltpu.VMEM((D, 3 * LANE), bf),
+            pltpu.VMEM((D, hidden), bf),
+            pltpu.VMEM((4, 8, D), f32),
+            copies((40,)),
         ],
-        [
-            pltpu.VMEM((rows, D), bf),
-            pltpu.VMEM((rows, D), bf),
-            pltpu.VMEM((D, hidden), bf),
-            pltpu.VMEM((hidden, D), bf),
-            pltpu.VMEM((rows, hidden), bf),
-            copies((36,)),
-        ],
-        rows * D * hidden * 6,
+        11,
         ids,
-        near,
-        far,
+        tokens_0,
+        tokens_1,
+        tokens_2,
+        tokens_3,
+        *joint_sheets,
         *up_sheets,
-        *down_talls,
-        output_pair,
-        mixed,
-        gain_two,
-        shift_two,
-        up_offset,
-        memory="shhhhhhhhhhvvvvv",
-    )
-    own_values = wide(tokens)
-    result = low(own_values + scatter_rows(near_part, far_part) + output_offset + down_offset)
-
-    near_part, far_part, up_home, up_away, norm_sums, up_sum = call(
-        backward_kernel,
-        [
-            like((rows // 2, D), f32),
-            like((rows // 2, D), bf),
-            like((2, *sheet), bf),
-            like((2, *sheet), bf),
-            like((4, D), f32),
-            like((1, hidden), f32),
-        ],
-        [
-            pltpu.VMEM((rows, D), bf),
-            pltpu.VMEM((rows, D), bf),
-            pltpu.VMEM((D, hidden), bf),
-            pltpu.VMEM((hidden, D), bf),
-            pltpu.VMEM((D, 3 * LANE), bf),
-            pltpu.VMEM((rows, hidden), bf),
-            pltpu.VMEM((4, 8, D), f32),
-            pltpu.VMEM((8, hidden), f32),
-            copies((52,)),
-        ],
-        rows * D * (hidden * 6 + LANE * 6),
-        ids,
-        near,
-        far,
-        *up_sheets,
-        *down_talls,
-        *joint_sheets,
-        inputs,
-        before,
         grad_joint,
+        grad_before,
         gain_one,
         gain_two,
-        memory="shhhhhhhhhhhhhhvvvvv",
-    )
-    pulled = scatter_rows(near_part, far_part)
+        memory="shhhhhhhhhhhhvvvv",
+    )
+    up_sent, up_away_0, joint_away, result_came, output_part, *found = pin(
+        up_sent, up_away_0, joint_away, result_came, output_part, *found
+    )
+    near_part, far_part, norm_sums = found
+    lane = near_part, swap(far_part, "c")
+    joint_sent = swap(low(total(joint_home_1, joint_away[2 * part :])), "o")
+    corner, side, up_sent, result_came = pin(
+        low(lane_sum(*lane, 3)), low(lane_sum(*lane, 1)), up_sent, result_came
+    )
+    corner, side = swap(corner, "x"), swap(side, "x")
+    result_kept = lane_sum(*result_lane, 0) + wide(result_came[:cap])
+    result_came = swap(low(lane_sum(*result_lane, 2) + wide(result_came[cap:])), "p")
+    far_side = swap(low(lane_sum(*lane, 2) + wide(corner)), "p")
+    output_part = output_part.reshape(2, part, D)
+    output_sent = swap(take(output_part, 1 - c), "c")
+    output_own = low(total(take(output_part, c), output_sent))
+    own_values = wide(tokens)
+    result = low(own_values + total(result_kept, result_came) + output_offset + down_offset)
+    output_own = total(output_own, swap(output_own, "x"))
+    up_final = low(total(up_home_0, up_away_0, up_sent))
+    joint_final = low(total(joint_home_0, joint_away[: 2 * part], joint_sent))
+    down_own = wide(join(up_final[:unit], swap(up_final[:unit], "x"), x))
 
     def put(values, index, size, axis):
         hot = (jnp.arange(size) == index).reshape([size if i == axis else 1 for i in range(values.ndim + 1)])
@@ -961,44 +1039,37 @@
         [
             *(norm_sums[i].reshape(-1, part) for i in range(4)),
             jnp.sum(wide(cotangent), axis=0).reshape(-1, part),
-            joint_sum.reshape(-1, joint_own),
+            joint_sum.reshape(-1, joint_size),
             up_sum.reshape(-1, up_bias.shape[0]),
         ],
         axis=1,
     )
-    for name in ("c", "q", "p", "o", "x"):
-        sums = sums + swap(sums, name)
+    sums = sums + swap(sums, "c")
+    sums = (sums + swap(sums, "x")) + (swap(sums, "p") + swap(sums, "x", "p"))
+    sums, side, far_side = pin(sums, side, far_side)
+    pulled = lane_sum(*lane, 0) + wide(side) + wide(far_side)
+    sums = (sums + swap(sums, "o")) + (swap(sums, "q") + swap(sums, "o", "q"))
     own_sums = take(sums, ((o * 2 + p) * 2 + q) * 2 + c)
 
-    def reduce(home, away):
-        both = wide(home) + wide(swap(away, "q"))
-        return both[0] + wide(swap(low(both[1]), "o"))
-
-    def hand(home, away, blocks):
-        final = low(reduce(home, away))
-        both = jnp.stack([final[:2], swap(final[2:], "c")])
-        both = jnp.stack([both[:, 0], swap(both[:, 1], "p")])
-        columns = both.shape[-1] * 8
-        (out,) = call(
-            partial(lay_kernel, blocks),
-            [like((part, columns), f32)],
-            [],
-            0,
-            ids,
-            both,
-            swap(both, "x"),
-            memory="svv",
-        )
-        return out
-
-    joint_own_grad = hand(joint_home, joint_away, joint_blocks)
-    up_own_grad = hand(up_home, up_away, up_blocks)
-    down_own = low(reduce(down_home, down_away))
-    down_own = wide(join(down_own, swap(down_own, "x"), x))
-    output_part = lax.ppermute(output_grad, cross, turn_over).reshape(2, part, D)
-    output_own = wide(take(output_part, c)) + wide(swap(take(output_part, 1 - c), "c"))
-    output_own = low(output_own)
-    output_own = wide(output_own) + wide(swap(output_own, "x"))
+    final = jnp.concatenate(
+        [
+            joint_final.reshape(2, part, 2, 3 * LANE).transpose(2, 0, 1, 3),
+            up_final[unit:].reshape(2, part, 2, hidden).transpose(2, 0, 1, 3),
+        ],
+        axis=3,
+    )
+    both = jnp.stack([final[0], swap(final[1], "c")])
+    both = jnp.stack([both[:, 0], swap(both[:, 1], "p")])
+    joint_own_grad, up_own_grad = call(
+        lay_kernel,
+        [like((part, 3 * D), f32), like((part, up_weight.shape[1]), f32)],
+        [],
+        1,
+        ids,
+        both,
+        swap(both, "x"),
+        memory="svv",
+    )
 
     own_normed = norm_of(tokens)
     centre = own_values - jnp.mean(own_values, axis=-1, keepdims=True)
@@ -1015,13 +1086,13 @@
         pieces[0],
         pieces[1],
         joint_own_grad,
-        own_sums[5 * part : 5 * part + joint_own],
+        own_sums[5 * part : 5 * part + joint_size],
         output_own,
         pieces[4],
         pieces[2],
         pieces[3],
         up_own_grad,
-        own_sums[5 * part + joint_own :],
+        own_sums[5 * part + joint_size :],
         down_own,
         pieces[4],
     )

time: 296 us -> 255 us (0.86)
  waiting for transfers between devices: 110 us -> 72.6 us
  Pallas kernels: 66 us -> 55.4 us
  other arithmetic: 24.1 us -> 31.9 us
  starting transfers between devices: 64.4 us -> 57.2 us
  local copies, waits for them, and re-layouts: 28.5 us -> 35.1 us
    ppermute x3 -> x2, waiting for transfers between devices: 22.7 us -> 0.9 us  [swap(): return lax.ppermute(values, axes, [(i, 3 - i) for i in range(4)])]
    unnamed x70 -> x153, local copies, waits for them, and re-layouts: 4.91 us -> 23.2 us
    ppermute x45 -> x46, waiting for transfers between devices: 87.3 us -> 71.7 us  [swap(): return lax.ppermute(values, axes[0], PAIR)]
    pallas_call x6 -> x5, Pallas kernels: 66 us -> 55.4 us  [call(): pl.pallas_call(kernel, out_shape=tuple(outs), in_specs=[specs[kind] for k...]
    convert_element_type x4 -> x8, other arithmetic: 1.11 us -> 9.32 us  [low(): return values.astype(jnp.bfloat16)]
    concatenate x2 -> x1, local copies, waits for them, and re-layouts: 6.43 us -> 0.09 us  [grouped(): small = jnp.concatenate(pin(*vectors, send)[:-1])[None]]
    reshape x4, local copies, waits for them, and re-layouts: 5.45 us -> 0.31 us  [vector(): return wide(small[:, start:start + size]).reshape(1, -1)]
    ppermute x2, starting transfers between devices: 7.18 us -> 2.48 us  [the longest x1 1.6 us: grouped(): output_pair = lax.ppermute(output_pair, cross, turn_over)]
  transfers between devices with their start and end apart: 50 -> 50, of which waited for: 19 -> 17; matrix products, arithmetic and copies ran while one was open for 15% -> 17% of each run, Pallas kernels for 17% -> 21%
where the time goes in v3:
time: 255 us; the launch traced here: 254 us
  waiting for transfers between devices  72.6 us (28%)
  starting transfers between devices  57.2 us (22%)
  Pallas kernels  55.4 us (22%)
  local copies, waits for them, and re-layouts  35.1 us (14%)
  other arithmetic  31.9 us (13%)
    ppermute x46, waiting for transfers between devices, swap(): return lax.ppermute(values, axes[0], PAIR)  71.7 us
    pallas_call x5, Pallas kernels, call(): pl.pallas_call(kernel, out_shape=tuple(outs), in_specs=[specs[kind] for k...  55.4 us
    ppermute x46, starting transfers between devices, swap(): return lax.ppermute(values, axes[0], PAIR)  50.3 us
    unnamed x153, local copies, waits for them, and re-layouts  23.2 us
    convert_element_type x8, other arithmetic, low(): return values.astype(jnp.bfloat16)  9.32 us
  transfers between devices with their start and end apart: 50, of which 17 were waited for; matrix products, arithmetic and copies ran while one was open for 17% of the time, Pallas kernels for 21%

profile of v3, /device:TPU:0, one launch (start us, length us, event | category | flops | bytes accessed | tf_op | source)
XLA Modules:
  0.0 253.8 jit_solution(3395007254129318003)
XLA Ops:
  4.6 3.1 %collective-permute-start = (bf16[2,64,896]{2,1,0:T(8,128)(2,1)S(1)}, bf16[2,64,896]{2,1,0:T(8,128)(2,1)S(1)}, u32[]{:S(2)}, u32[]{:S(2)}) collective-permute-start(bf16[2,64,896]{2,1,0:T(8,128)(2,1)S(1)} %get-tuple-element.91), channel_id=1, source_target_pairs={{0,4},{4,0},{1,5},{5,1},{2,6},{6,2},{3,7},{7,3},{8,12},{12,8},{9,1... | collective-permute-start | bytes 688136 | tf_op jit(solution)/shard_map/ppermute | solution.py:298
  8.4 1.5 collective-permute-start.5
  11.4 3.7 %fusion.10 = (f32[1408,128]{1,0:T(8,128)}, f32[1408,128]{1,0:T(8,128)}) fusion(f32[128]{0:T(128)S(1)} %mul.130, f32[1408]{0:T(1024)S(1)} %convert_element_type.150, pred[128]{0:T(512)(128)(4,1)S(1)} %get-tuple-element.219, pred[128]{0:T(512)(128)(4,1)S(1)} %get-tuple-element.220), kind=kLoop, calls=%fused_computation.20 | loop fusion | flops 901120 | bytes 1448192 | tf_op jit(solution)/shard_map/jit(_where)/select_n | solution.py:876
  15.2 1.6 collective-permute-start.21
  16.9 1.1 select_n.225.position
  18.0 3.1 %collective-permute-done.21 = bf16[2,832]{1,0:T(2,128)(2,1)S(1)} collective-permute-done((bf16[2,832]{1,0:T(2,128)(2,1)S(1)}, bf16[2,832]{1,0:T(2,128)(2,1)S(1)}, u32[]{:S(2)}, u32[]{:S(2)}) %collective-permute-start.21) | collective-permute-done | bytes 3360 | tf_op jit(solution)/shard_map/ppermute | solution.py:298
  21.1 2.8 %collective-permute-start.18 = (bf16[128,1024]{1,0:T(8,128)(2,1)S(1)}, bf16[128,1024]{1,0:T(8,128)(2,1)S(1)}, u32[]{:S(2)}, u32[]{:S(2)}) collective-permute-start(bf16[128,1024]{1,0:T(8,128)(2,1)S(1)} %get-tuple-element.99.tall_0), channel_id=1, source_target_pairs={{0,8},{8,0},{1,9},{9,1},{2,10},{10,2},{3,11},{11,3},{4,12},{12,4},... | collective-permute-start | bytes 786440 | tf_op jit(solution)/shard_map/ppermute | solution.py:298
  24.1 1.6 collective-permute-start.13
  26.5 1.5 collective-permute-start.11
  28.4 14.2 %collective-permute-done.13 = bf16[176,1024]{1,0:T(8,128)(2,1)S(1)} collective-permute-done((bf16[176,1024]{1,0:T(8,128)(2,1)S(1)}, bf16[176,1024]{1,0:T(8,128)(2,1)S(1)}, u32[]{:S(2)}, u32[]{:S(2)}) %collective-permute-start.13) | collective-permute-done | bytes 360480 | tf_op jit(solution)/shard_map/ppermute | solution.py:298
  42.7 1.6 collective-permute-start.14
  45.1 1.5 collective-permute-start.19
  50.2 8.5 %collective-permute-done.22 = bf16[4,832]{1,0:T(4,128)(2,1)S(1)} collective-permute-done((bf16[4,832]{1,0:T(4,128)(2,1)S(1)}, bf16[4,832]{1,0:T(4,128)(2,1)S(1)}, u32[]{:S(2)}, u32[]{:S(2)}) %collective-permute-start.22) | collective-permute-done | bytes 6688 | tf_op jit(solution)/shard_map/ppermute | solution.py:298
  58.8 1.7 collective-permute-done.14
  60.5 1.3 collective-permute-start.23
  61.9 7.0 %collective-permute-done.23 = bf16[8,832]{1,0:T(8,128)(2,1)S(1)} collective-permute-done((bf16[8,832]{1,0:T(8,128)(2,1)S(1)}, bf16[8,832]{1,0:T(8,128)(2,1)S(1)}, u32[]{:S(2)}, u32[]{:S(2)}) %collective-permute-start.23) | collective-permute-done | bytes 13344 | tf_op jit(solution)/shard_map/ppermute | solution.py:298
  69.4 1.6 collective-permute-start.16
  71.8 1.1 slice_bitcast_fusion
  72.8 5.8 %collective-permute-done.16.sheet_1 = bf16[4,64,512]{2,1,0:T(8,128)(2,1)} collective-permute-done((bf16[4,64,512]{2,1,0:T(8,128)(2,1)S(1)}, bf16[4,64,512]{2,1,0:T(8,128)(2,1)}, u32[]{:S(2)}, u32[]{:S(2)}) %collective-permute-start.16) | collective-permute-done | bytes 262176 | tf_op jit(solution)/shard_map/ppermute | solution.py:298
  78.6 1.6 collective-permute-start.8
  80.2 3.6 %collective-permute-done.17.sheet_3 = bf16[4,64,512]{2,1,0:T(8,128)(2,1)} collective-permute-done((bf16[4,64,512]{2,1,0:T(8,128)(2,1)S(1)}, bf16[4,64,512]{2,1,0:T(8,128)(2,1)}, u32[]{:S(2)}, u32[]{:S(2)}) %collective-permute-start.17) | collective-permute-done | bytes 262176 | tf_op jit(solution)/shard_map/ppermute | solution.py:298
  83.8 1.5 collective-permute-start.6
  89.7 17.9 %shard_map.264 = (bf16[1408,1024]{1,0:T(8,128)(2,1)S(1)}, bf16[1408,512]{1,0:T(8,128)(2,1)S(1)}, bf16[256,1024]{1,0:T(8,128)(2,1)S(1)}, bf16[256,1024]{1,0:T(8,1...) custom-call(s32[5]{0:T(128)S(1)} %stack.98.ids, ...), custom_call_target="tpu_custom_call" | custom-call | flops 23000000512 | bytes 14299156 | tf_op jit(solution)/shard_map/pallas_call | solution.py:341
  109.2 1.2 copy-done.41
  110.4 1.6 collective-permute-start.24
  112.0 1.4 copy-done.2
  113.4 1.1 copy-done.6
  114.5 1.1 copy-done.9
  115.6 23.1 %shard_map.265 = (f32[704,1024]{1,0:T(8,128)S(1)}, bf16[704,1024]{1,0:T(8,128)(2,1)}, bf16[1408,384]{1,0:T(8,128)(2,1)S(1)}, bf16[128,768]{1,0:T(8,128)(2,1)S(1)...) custom-call(s32[5]{0:T(128)S(1)} %stack.98.ids, ...), custom_call_target="tpu_custom_call" | custom-call | flops 25300000768 | bytes 17613332 | tf_op jit(solution)/shard_map/pallas_call | solution.py:341
  141.6 1.1 copy-done.43
  143.7 1.1 convert_reduce_fusion
  144.8 1.2 fusion.9
  146.3 1.3 add_convert_fusion.1
  148.2 1.5 collective-permute-start.28
  150.7 1.5 add_convert_fusion.7
  152.3 5.6 %collective-permute-start.29 = (bf16[352,1024]{1,0:T(8,128)(2,1)S(1)}, bf16[352,1024]{1,0:T(8,128)(2,1)}, u32[]{:S(2)}, u32[]{:S(2)}) collective-permute-start(bf16[352,1024]{1,0:T(8,128)(2,1)S(1)} %pad_maximum_fusion.4), channel_id=1, source_target_pairs={{0,16},{16,0},{1,17},{17,1},{2,18},{18,2},{3,19},{19,3},{4,20},{20... | collective-permute-start | bytes 2162696 | tf_op jit(solution)/shard_map/ppermute | solution.py:298
  157.9 1.2 copy-done.44
  159.2 11.8 %shard_map.266 = (f32[704,1024]{1,0:T(8,128)S(1)}, bf16[704,1024]{1,0:T(8,128)(2,1)}, f32[4,1024]{1,0:T(4,128)S(1)}) custom-call(s32[5]{0:T(128)S(1)} %stack.98.ids, bf16[2,176,1024]{2,1,0:T(8,128)(2,1)S(1)} %copy-done.7, bf16[2,176,1024]{2,1,0:T(8,128)(2,1)} %collective-permute-done.9.block_1, bf16[2,176,1024]{2,1,0:T(8,128)(2,1)S(1)} %copy-done.10, ...), custom_call_target="tpu_custom_call" | custom-call | flops 12650000384 | bytes 11591700 | tf_op jit(solution)/shard_map/pallas_call | solution.py:341
  170.9 1.6 copy-done
  172.6 6.8 %collective-permute-done.26 = bf16[256,1024]{1,0:T(8,128)(2,1)S(1)} collective-permute-done((bf16[256,1024]{1,0:T(8,128)(2,1)S(1)}, bf16[256,1024]{1,0:T(8,128)(2,1)S(1)}, u32[]{:S(2)}, u32[]{:S(2)}) %collective-permute-start.26) | collective-permute-done | bytes 524320 | tf_op jit(solution)/shard_map/ppermute | solution.py:298
  183.6 7.3 %collective-permute-start.34 = (f32[16,768]{1,0:T(8,128)S(1)}, f32[16,768]{1,0:T(8,128)S(1)}, u32[]{:S(2)}, u32[]{:S(2)}) collective-permute-start(f32[16,768]{1,0:T(8,128)S(1)} %add.307), channel_id=1, source_target_pairs={{0,16},{16,0},{1,17},{17,1},{2,18},{18,2},{3,19},{19,3},{4,20},{20... | collective-permute-start | bytes 147464 | tf_op jit(solution)/shard_map/ppermute | solution.py:298
  190.9 1.5 collective-permute-start.36
  196.7 1.1 collective-permute-start.48
  197.7 2.6 %add_convert_fusion.4 = (bf16[176,1024]{1,0:T(8,128)(2,1)}, bf16[176,1024]{1,0:T(8,128)(2,1)}) fusion(f32[704,1024]{1,0:T(8,128)} %copy-done, bf16[704,1024]{1,0:T(8,128)(2,1)} %collective-permute-done.31), kind=kLoop, calls=%fused_computation.32 | loop fusion | flops 1081344 | bytes 2883584 | tf_op jit(solution)/shard_map/convert_element_type | solution.py:318
  202.3 2.6 %collective-permute-done.43 = bf16[128,768]{1,0:T(8,128)(2,1)S(1)} collective-permute-done((bf16[128,768]{1,0:T(8,128)(2,1)S(1)}, bf16[128,768]{1,0:T(8,128)(2,1)S(1)}, u32[]{:S(2)}, u32[]{:S(2)}) %collective-permute-start.43) | collective-permute-done | bytes 196640 | tf_op jit(solution)/shard_map/ppermute | solution.py:298
  205.7 1.7 reshape.269
  207.3 1.6 copy.56
  208.9 1.7 convert_add_fusion.4
  210.6 1.5 collective-permute-start.38
  212.7 1.9 broadcast_select_fusion.1
  214.5 1.1 reshape.270
  216.8 5.4 %collective-permute-done.38 = bf16[176,1024]{1,0:T(8,128)(2,1)} collective-permute-done((bf16[176,1024]{1,0:T(8,128)(2,1)}, bf16[176,1024]{1,0:T(8,128)(2,1)}, u32[]{:S(2)}, u32[]{:S(2)}) %collective-permute-start.38) | collective-permute-done | bytes 360480 | tf_op jit(solution)/shard_map/ppermute | solution.py:298
  222.2 1.5 add_convert_fusion.2
  223.9 2.1 collective-permute-start.45
  225.9 1.2 add_convert_fusion.3
  227.3 1.1 maximum_convert_fusion
  229.0 7.2 %collective-permute-done.39 = bf16[176,1024]{1,0:T(8,128)(2,1)S(1)} collective-permute-done((bf16[176,1024]{1,0:T(8,128)(2,1)S(1)}, bf16[176,1024]{1,0:T(8,128)(2,1)S(1)}, u32[]{:S(2)}, u32[]{:S(2)}) %collective-permute-start.39) | collective-permute-done | bytes 360480 | tf_op jit(solution)/shard_map/ppermute | solution.py:298
  236.2 1.4 collective-permute-start.41
  237.6 3.0 %collective-permute-start.42 = (f32[16,768]{1,0:T(8,128)S(1)}, f32[16,768]{1,0:T(8,128)S(1)}, u32[]{:S(2)}, u32[]{:S(2)}) collective-permute-start(f32[16,768]{1,0:T(8,128)S(1)} %add_add_fusion), channel_id=1, source_target_pairs={{0,10},{2,8},{8,2},{10,0},{1,11},{3,9},{9,3},{11,1},{4,14},{6,12},... | collective-permute-start | bytes 147464 | tf_op jit(solution)/shard_map/ppermute | solution.py:299
  241.7 1.5 collective-permute-start.46
  243.2 1.7 fusion.25
  245.0 2.1 collective-permute-done.32
  247.0 2.5 convert_add_fusion.1
  251.4 2.0 shard_map.267
  (303 shorter events, 41.9 us)
Async XLA Ops:
  4.6 39.7 %copy-start.17 = (bf16[128,1024]{1,0:T(8,128)(2,1)}, bf16[128,1024]{1,0:T(8,128)(2,1)S(1)}, u32[]{:S(2)}) copy-start(bf16[128,1024]{1,0:T(8,128)(2,1)S(1)} %get-tuple-element.99.tall_0) | copy-start | bytes 786436
  4.6 19.3 %collective-permute-start = (bf16[2,64,896]{2,1,0:T(8,128)(2,1)S(1)}, bf16[2,64,896]{2,1,0:T(8,128)(2,1)S(1)}, u32[]{:S(2)}, u32[]{:S(2)}) collective-permute-start(bf16[2,64,896]{2,1,0:T(8,128)(2,1)S(1)} %get-tuple-element.91), channel_id=1, source_target_pairs={{0,4},{4,0},{1,5},{5,1},{2,6},{6,2},{3,7},{7,3},{8,12},{12,8},{9,1... | collective-permute-start | bytes 688136 | tf_op jit(solution)/shard_map/ppermute | solution.py:298
  7.9 7.3 %collective-permute-start.20 = (bf16[1,832]{1,0:T(2,128)(2,1)S(1)}, bf16[1,832]{1,0:T(2,128)(2,1)S(1)}, u32[]{:S(2)}, u32[]{:S(2)}) collective-permute-start(bf16[1,832]{1,0:T(2,128)(2,1)S(1)} %broadcast_in_dim.149), channel_id=1, source_target_pairs={{0,1},{1,0},{2,3},{3,2},{4,5},{5,4},{6,7},{7,6},{8,9},{9,8},{10,11... | collective-permute-start | bytes 5000 | tf_op jit(solution)/shard_map/ppermute | solution.py:298
  8.0 17.8 %collective-permute-start.4 = (bf16[64,1024]{1,0:T(8,128)(2,1)S(1)}, bf16[64,1024]{1,0:T(8,128)(2,1)S(1)}, u32[]{:S(2)}, u32[]{:S(2)}) collective-permute-start(bf16[64,1024]{1,0:T(8,128)(2,1)S(1)} %copy-done.64), channel_id=1, source_target_pairs={{0,1},{1,0},{2,3},{3,2},{4,5},{5,4},{6,7},{7,6},{8,9},{9,8},{10,11... | collective-permute-start | bytes 393224 | tf_op jit(solution)/shard_map/ppermute | solution.py:298
  8.4 38.2 %collective-permute-start.5 = (bf16[176,1024]{1,0:T(8,128)(2,1)S(1)}, bf16[176,1024]{1,0:T(8,128)(2,1)S(1)}, u32[]{:S(2)}, u32[]{:S(2)}) collective-permute-start(bf16[176,1024]{1,0:T(8,128)(2,1)S(1)} %copy-done.45), channel_id=1, source_target_pairs={{0,16},{16,0},{1,17},{17,1},{2,18},{18,2},{3,19},{19,3},{4,20},{20... | collective-permute-start | bytes 1081352 | tf_op jit(solution)/shard_map/ppermute | solution.py:298
  9.9 14.1 %collective-permute-start.10 = (bf16[176,1024]{1,0:T(8,128)(2,1)S(1)}, bf16[176,1024]{1,0:T(8,128)(2,1)S(1)}, u32[]{:S(2)}, u32[]{:S(2)}) collective-permute-start(bf16[176,1024]{1,0:T(8,128)(2,1)S(1)} %copy-done.45), channel_id=1, source_target_pairs={{0,4},{4,0},{1,5},{5,1},{2,6},{6,2},{3,7},{7,3},{8,12},{12,8},{9,1... | collective-permute-start | bytes 1081352 | tf_op jit(solution)/shard_map/ppermute | solution.py:298
  15.2 5.9 %collective-permute-start.21 = (bf16[2,832]{1,0:T(2,128)(2,1)S(1)}, bf16[2,832]{1,0:T(2,128)(2,1)S(1)}, u32[]{:S(2)}, u32[]{:S(2)}) collective-permute-start(bf16[2,832]{1,0:T(2,128)(2,1)S(1)} %pad_maximum_fusion.17), channel_id=1, source_target_pairs={{0,4},{4,0},{1,5},{5,1},{2,6},{6,2},{3,7},{7,3},{8,12},{12,8},{9,1... | collective-permute-start | bytes 9992 | tf_op jit(solution)/shard_map/ppermute | solution.py:298
  21.1 23.1 %collective-permute-start.18 = (bf16[128,1024]{1,0:T(8,128)(2,1)S(1)}, bf16[128,1024]{1,0:T(8,128)(2,1)S(1)}, u32[]{:S(2)}, u32[]{:S(2)}) collective-permute-start(bf16[128,1024]{1,0:T(8,128)(2,1)S(1)} %get-tuple-element.99.tall_0), channel_id=1, source_target_pairs={{0,8},{8,0},{1,9},{9,1},{2,10},{10,2},{3,11},{11,3},{4,12},{12,4},... | collective-permute-start | bytes 786440 | tf_op jit(solution)/shard_map/ppermute | solution.py:298
  24.0 4.0 %collective-permute-start.1 = (bf16[2,64,896]{2,1,0:T(8,128)(2,1)S(1)}, bf16[2,64,896]{2,1,0:T(8,128)(2,1)S(1)}, u32[]{:S(2)}, u32[]{:S(2)}) collective-permute-start(bf16[2,64,896]{2,1,0:T(8,128)(2,1)S(1)} %pad_maximum_fusion.12), channel_id=1, source_target_pairs={{0,1},{1,0},{2,3},{3,2},{4,5},{5,4},{6,7},{7,6},{8,9},{9,8},{10,11... | collective-permute-start | bytes 688136 | tf_op jit(solution)/shard_map/ppermute | solution.py:298
  24.1 18.6 %copy-start.59 = (bf16[176,1024]{1,0:T(8,128)(2,1)}, bf16[176,1024]{1,0:T(8,128)(2,1)S(1)}, u32[]{:S(2)}) copy-start(bf16[176,1024]{1,0:T(8,128)(2,1)S(1)} %collective-permute-done.10) | copy-start | bytes 1081348
  24.1 18.5 %collective-permute-start.13 = (bf16[176,1024]{1,0:T(8,128)(2,1)S(1)}, bf16[176,1024]{1,0:T(8,128)(2,1)S(1)}, u32[]{:S(2)}, u32[]{:S(2)}) collective-permute-start(bf16[176,1024]{1,0:T(8,128)(2,1)S(1)} %copy-done.47), channel_id=1, source_target_pairs={{0,4},{4,0},{1,5},{5,1},{2,6},{6,2},{3,7},{7,3},{8,12},{12,8},{9,1... | collective-permute-start | bytes 1081352 | tf_op jit(solution)/shard_map/ppermute | solution.py:298
  26.5 23.3 %collective-permute-start.11 = (bf16[176,1024]{1,0:T(8,128)(2,1)S(1)}, bf16[176,1024]{1,0:T(8,128)(2,1)S(1)}, u32[]{:S(2)}, u32[]{:S(2)}) collective-permute-start(bf16[176,1024]{1,0:T(8,128)(2,1)S(1)} %collective-permute-done.10), channel_id=1, source_target_pairs={{0,16},{16,0},{1,17},{17,1},{2,18},{18,2},{3,19},{19,3},{4,20},{20... | collective-permute-start | bytes 1081352 | tf_op jit(solution)/shard_map/ppermute | solution.py:298
  28.0 41.4 %copy-start.19 = (bf16[4,64,512]{2,1,0:T(8,128)(2,1)}, bf16[4,64,512]{2,1,0:T(8,128)(2,1)S(1)}, u32[]{:S(2)}) copy-start(bf16[4,64,512]{2,1,0:T(8,128)(2,1)S(1)} %pad_maximum_fusion.7.sheet_0) | copy-start | bytes 786436
  28.0 21.2 %collective-permute-start.2 = (bf16[4,64,512]{2,1,0:T(8,128)(2,1)S(1)}, bf16[4,64,512]{2,1,0:T(8,128)(2,1)S(1)}, u32[]{:S(2)}, u32[]{:S(2)}) collective-permute-start(bf16[4,64,512]{2,1,0:T(8,128)(2,1)S(1)} %pad_maximum_fusion.7.sheet_0), channel_id=1, source_target_pairs={{0,8},{8,0},{1,9},{9,1},{2,10},{10,2},{3,11},{11,3},{4,12},{12,4},... | collective-permute-start | bytes 786440 | tf_op jit(solution)/shard_map/ppermute | solution.py:298
  42.7 17.7 %collective-permute-start.14 = (bf16[2,176,1024]{2,1,0:T(8,128)(2,1)S(1)}, bf16[2,176,1024]{2,1,0:T(8,128)(2,1)S(1)}, u32[]{:S(2)}, u32[]{:S(2)}) collective-permute-start(bf16[2,176,1024]{2,1,0:T(8,128)(2,1)S(1)} %pad_maximum_fusion.3), channel_id=1, source_target_pairs={{0,16},{16,0},{1,17},{17,1},{2,18},{18,2},{3,19},{19,3},{4,20},{20... | collective-permute-start | bytes 2162696 | tf_op jit(solution)/shard_map/ppermute | solution.py:298
  45.1 24.2 %collective-permute-start.19 = (bf16[2,128,1024]{2,1,0:T(8,128)(2,1)}, bf16[2,128,1024]{2,1,0:T(8,128)(2,1)}, u32[]{:S(2)}, u32[]{:S(2)}) collective-permute-start(bf16[2,128,1024]{2,1,0:T(8,128)(2,1)} %pad_maximum_fusion.5), channel_id=1, source_target_pairs={{0,2},{2,0},{1,3},{3,1},{4,6},{6,4},{5,7},{7,5},{8,10},{10,8},{9,1... | collective-permute-start | bytes 1572872 | tf_op jit(solution)/shard_map/ppermute | solution.py:298
  48.4 37.4 %copy-start.5 = (bf16[2,176,1024]{2,1,0:T(8,128)(2,1)}, bf16[2,176,1024]{2,1,0:T(8,128)(2,1)S(1)}, u32[]{:S(2)}) copy-start(bf16[2,176,1024]{2,1,0:T(8,128)(2,1)S(1)} %pad_maximum_fusion.1.block_0) | copy-start | bytes 2162692
  48.5 36.9 %collective-permute-start.9 = (bf16[2,176,1024]{2,1,0:T(8,128)(2,1)S(1)}, bf16[2,176,1024]{2,1,0:T(8,128)(2,1)}, u32[]{:S(2)}, u32[]{:S(2)}) collective-permute-start(bf16[2,176,1024]{2,1,0:T(8,128)(2,1)S(1)} %pad_maximum_fusion.1.block_0), channel_id=1, source_target_pairs={{0,1},{1,0},{2,3},{3,2},{4,5},{5,4},{6,7},{7,6},{8,9},{9,8},{10,11... | collective-permute-start | bytes 2162696 | tf_op jit(solution)/shard_map/ppermute | solution.py:298
  49.3 21.7 %copy-start.32 = (bf16[4,64,512]{2,1,0:T(8,128)(2,1)}, bf16[4,64,512]{2,1,0:T(8,128)(2,1)S(1)}, u32[]{:S(2)}) copy-start(bf16[4,64,512]{2,1,0:T(8,128)(2,1)S(1)} %collective-permute-done.2.sheet_2) | copy-start | bytes 786436
  49.3 9.5 %collective-permute-start.22 = (bf16[4,832]{1,0:T(4,128)(2,1)S(1)}, bf16[4,832]{1,0:T(4,128)(2,1)S(1)}, u32[]{:S(2)}, u32[]{:S(2)}) collective-permute-start(bf16[4,832]{1,0:T(4,128)(2,1)S(1)} %pad_maximum_fusion.16), channel_id=1, source_target_pairs={{0,2},{2,0},{1,3},{3,1},{4,6},{6,4},{5,7},{7,5},{8,10},{10,8},{9,1... | collective-permute-start | bytes 19976 | tf_op jit(solution)/shard_map/ppermute | solution.py:298
  49.9 36.0 %copy-start.8 = (bf16[2,176,1024]{2,1,0:T(8,128)(2,1)}, bf16[2,176,1024]{2,1,0:T(8,128)(2,1)S(1)}, u32[]{:S(2)}) copy-start(bf16[2,176,1024]{2,1,0:T(8,128)(2,1)S(1)} %pad_maximum_fusion.2.block_2) | copy-start | bytes 2162692
  49.9 36.0 %collective-permute-start.12 = (bf16[2,176,1024]{2,1,0:T(8,128)(2,1)S(1)}, bf16[2,176,1024]{2,1,0:T(8,128)(2,1)}, u32[]{:S(2)}, u32[]{:S(2)}) collective-permute-start(bf16[2,176,1024]{2,1,0:T(8,128)(2,1)S(1)} %pad_maximum_fusion.2.block_2), channel_id=1, source_target_pairs={{0,1},{1,0},{2,3},{3,2},{4,5},{5,4},{6,7},{7,6},{8,9},{9,8},{10,11... | collective-permute-start | bytes 2162696 | tf_op jit(solution)/shard_map/ppermute | solution.py:298
  58.7 12.2 %collective-permute-start.3 = (bf16[4,64,384]{2,1,0:T(8,128)(2,1)}, bf16[4,64,384]{2,1,0:T(8,128)(2,1)}, u32[]{:S(2)}, u32[]{:S(2)}) collective-permute-start(bf16[4,64,384]{2,1,0:T(8,128)(2,1)} %pad_maximum_fusion.13.sheet_0.join_0), channel_id=1, source_target_pairs={{0,8},{8,0},{1,9},{9,1},{2,10},{10,2},{3,11},{11,3},{4,12},{12,4},... | collective-permute-start | bytes 589832 | tf_op jit(solution)/shard_map/ppermute | solution.py:298
  60.5 8.5 %collective-permute-start.23 = (bf16[8,832]{1,0:T(8,128)(2,1)S(1)}, bf16[8,832]{1,0:T(8,128)(2,1)S(1)}, u32[]{:S(2)}, u32[]{:S(2)}) collective-permute-start(bf16[8,832]{1,0:T(8,128)(2,1)S(1)} %pad_maximum_fusion.15), channel_id=1, source_target_pairs={{0,8},{8,0},{1,9},{9,1},{2,10},{10,2},{3,11},{11,3},{4,12},{12,4},... | collective-permute-start | bytes 39944 | tf_op jit(solution)/shard_map/ppermute | solution.py:298
  61.9 45.7 %copy-start.1 = (bf16[4,176,1024]{2,1,0:T(8,128)(2,1)}, bf16[4,176,1024]{2,1,0:T(8,128)(2,1)S(1)}, u32[]{:S(2)}) copy-start(bf16[4,176,1024]{2,1,0:T(8,128)(2,1)S(1)} %pad_maximum_fusion.near) | copy-start | bytes 4325380
  69.0 16.9 %collective-permute-start.15 = (bf16[4,176,1024]{2,1,0:T(8,128)(2,1)S(1)}, bf16[4,176,1024]{2,1,0:T(8,128)(2,1)}, u32[]{:S(2)}, u32[]{:S(2)}) collective-permute-start(bf16[4,176,1024]{2,1,0:T(8,128)(2,1)S(1)} %pad_maximum_fusion.near), channel_id=1, source_target_pairs={{0,1},{1,0},{2,3},{3,2},{4,5},{5,4},{6,7},{7,6},{8,9},{9,8},{10,11... | collective-permute-start | bytes 4325384 | tf_op jit(solution)/shard_map/ppermute | solution.py:298
  69.4 9.3 %collective-permute-start.16 = (bf16[4,64,512]{2,1,0:T(8,128)(2,1)S(1)}, bf16[4,64,512]{2,1,0:T(8,128)(2,1)}, u32[]{:S(2)}, u32[]{:S(2)}) collective-permute-start(bf16[4,64,512]{2,1,0:T(8,128)(2,1)S(1)} %pad_maximum_fusion.7.sheet_0), channel_id=1, source_target_pairs={{0,2},{2,0},{1,3},{3,1},{4,6},{6,4},{5,7},{7,5},{8,10},{10,8},{9,1... | collective-permute-start | bytes 786440 | tf_op jit(solution)/shard_map/ppermute | solution.py:298
  70.9 12.9 %collective-permute-start.17 = (bf16[4,64,512]{2,1,0:T(8,128)(2,1)S(1)}, bf16[4,64,512]{2,1,0:T(8,128)(2,1)}, u32[]{:S(2)}, u32[]{:S(2)}) collective-permute-start(bf16[4,64,512]{2,1,0:T(8,128)(2,1)S(1)} %collective-permute-done.2.sheet_2), channel_id=1, source_target_pairs={{0,2},{2,0},{1,3},{3,1},{4,6},{6,4},{5,7},{7,5},{8,10},{10,8},{9,1... | collective-permute-start | bytes 786440 | tf_op jit(solution)/shard_map/ppermute | solution.py:298
  78.6 31.8 %collective-permute-start.8 = (bf16[128,1024]{1,0:T(8,128)(2,1)}, bf16[128,1024]{1,0:T(8,128)(2,1)S(1)}, u32[]{:S(2)}, u32[]{:S(2)}) collective-permute-start(bf16[128,1024]{1,0:T(8,128)(2,1)} %pad_maximum_fusion.9), channel_id=1, source_target_pairs={{0,0},{1,2},{2,1},{3,3},{8,16},{9,18},{10,17},{11,19},{16,8},{17,1... | collective-permute-start | bytes 786440 | tf_op jit(solution)/shard_map/ppermute | solution.py:890
  83.8 26.5 %collective-permute-start.6 = (bf16[4,64,384]{2,1,0:T(8,128)(2,1)}, bf16[4,64,384]{2,1,0:T(8,128)(2,1)S(1)}, u32[]{:S(2)}, u32[]{:S(2)}) collective-permute-start(bf16[4,64,384]{2,1,0:T(8,128)(2,1)} %pad_maximum_fusion.13.sheet_0.join_0), channel_id=1, source_target_pairs={{0,2},{2,0},{1,3},{3,1},{4,6},{6,4},{5,7},{7,5},{8,10},{10,8},{9,1... | collective-permute-start | bytes 589832 | tf_op jit(solution)/shard_map/ppermute | solution.py:298
  85.4 25.0 %collective-permute-start.7 = (bf16[4,64,384]{2,1,0:T(8,128)(2,1)}, bf16[4,64,384]{2,1,0:T(8,128)(2,1)S(1)}, u32[]{:S(2)}, u32[]{:S(2)}) collective-permute-start(bf16[4,64,384]{2,1,0:T(8,128)(2,1)} %collective-permute-done.3.sheet_2.join_2), channel_id=1, source_target_pairs={{0,2},{2,0},{1,3},{3,1},{4,6},{6,4},{5,7},{7,5},{8,10},{10,8},{9,1... | collective-permute-start | bytes 589832 | tf_op jit(solution)/shard_map/ppermute | solution.py:298
  89.7 22.3 %copy-start.3 = (f32[1408,128]{1,0:T(8,128)S(1)}, f32[1408,128]{1,0:T(8,128)}, u32[]{:S(2)}) copy-start(f32[1408,128]{1,0:T(8,128)} %get-tuple-element.206.sine) | copy-start | bytes 2162692
  89.7 22.3 %copy-start.4 = (f32[1408,128]{1,0:T(8,128)S(1)}, f32[1408,128]{1,0:T(8,128)}, u32[]{:S(2)}) copy-start(f32[1408,128]{1,0:T(8,128)} %get-tuple-element.207.cosine) | copy-start | bytes 2162692
  89.7 22.3 %copy-start.11 = (s32[1408,1]{1,0:T(8,128)S(1)}, s32[1408,1]{1,0:T(8,128)}, u32[]{:S(2)}) copy-start(s32[1408,1]{1,0:T(8,128)} %select_n.225.position) | copy-start | bytes 16900
  110.4 28.3 %copy-start.37 = (bf16[4,64,384]{2,1,0:T(8,128)(2,1)}, bf16[4,64,384]{2,1,0:T(8,128)(2,1)S(1)}, u32[]{:S(2)}) copy-start(bf16[4,64,384]{2,1,0:T(8,128)(2,1)S(1)} %collective-permute-done.6.sheet_1.join_1) | copy-start | bytes 589828
  110.4 28.3 %copy-start.39 = (bf16[4,64,384]{2,1,0:T(8,128)(2,1)}, bf16[4,64,384]{2,1,0:T(8,128)(2,1)S(1)}, u32[]{:S(2)}) copy-start(bf16[4,64,384]{2,1,0:T(8,128)(2,1)S(1)} %collective-permute-done.7.sheet_3.join_3) | copy-start | bytes 589828
  110.4 32.2 %collective-permute-start.24 = (bf16[256,1024]{1,0:T(8,128)(2,1)S(1)}, bf16[256,1024]{1,0:T(8,128)(2,1)S(1)}, u32[]{:S(2)}, u32[]{:S(2)}) collective-permute-start(bf16[256,1024]{1,0:T(8,128)(2,1)S(1)} %get-tuple-element.116), channel_id=1, source_target_pairs={{0,2},{2,0},{1,3},{3,1},{4,6},{6,4},{5,7},{7,5},{8,10},{10,8},{9,1... | collective-permute-start | bytes 1572872 | tf_op jit(solution)/shard_map/ppermute | solution.py:298
  143.4 7.3 %collective-permute-start.25 = (bf16[704,1024]{1,0:T(8,128)(2,1)}, bf16[704,1024]{1,0:T(8,128)(2,1)}, u32[]{:S(2)}, u32[]{:S(2)}) collective-permute-start(bf16[704,1024]{1,0:T(8,128)(2,1)} %get-tuple-element.131), channel_id=1, source_target_pairs={{0,1},{1,0},{2,3},{3,2},{4,5},{5,4},{6,7},{7,6},{8,9},{9,8},{10,11... | collective-permute-start | bytes 4325384 | tf_op jit(solution)/shard_map/ppermute | solution.py:298
  147.6 31.8 %collective-permute-start.26 = (bf16[256,1024]{1,0:T(8,128)(2,1)S(1)}, bf16[256,1024]{1,0:T(8,128)(2,1)S(1)}, u32[]{:S(2)}, u32[]{:S(2)}) collective-permute-start(bf16[256,1024]{1,0:T(8,128)(2,1)S(1)} %add_convert_fusion.1), channel_id=1, source_target_pairs={{0,8},{8,0},{1,9},{9,1},{2,10},{10,2},{3,11},{11,3},{4,12},{12,4},... | collective-permute-start | bytes 1572872 | tf_op jit(solution)/shard_map/ppermute | solution.py:298
  147.7 31.7 %collective-permute-start.27 = (bf16[256,1024]{1,0:T(8,128)(2,1)S(1)}, bf16[256,1024]{1,0:T(8,128)(2,1)S(1)}, u32[]{:S(2)}, u32[]{:S(2)}) collective-permute-start(bf16[256,1024]{1,0:T(8,128)(2,1)S(1)} %copy-done.29), channel_id=1, source_target_pairs={{0,2},{2,0},{1,3},{3,1},{4,6},{6,4},{5,7},{7,5},{8,10},{10,8},{9,1... | collective-permute-start | bytes 1572872 | tf_op jit(solution)/shard_map/ppermute | solution.py:298
  148.2 24.3 %collective-permute-start.28 = (bf16[256,768]{1,0:T(8,128)(2,1)S(1)}, bf16[256,768]{1,0:T(8,128)(2,1)S(1)}, u32[]{:S(2)}, u32[]{:S(2)}) collective-permute-start(bf16[256,768]{1,0:T(8,128)(2,1)S(1)} %copy-done.31), channel_id=1, source_target_pairs={{0,2},{2,0},{1,3},{3,1},{4,6},{6,4},{5,7},{7,5},{8,10},{10,8},{9,1... | collective-permute-start | bytes 1179656 | tf_op jit(solution)/shard_map/ppermute | solution.py:298
  149.8 22.8 %collective-permute-start.30 = (bf16[128,1024]{1,0:T(8,128)(2,1)S(1)}, bf16[128,1024]{1,0:T(8,128)(2,1)S(1)}, u32[]{:S(2)}, u32[]{:S(2)}) collective-permute-start(bf16[128,1024]{1,0:T(8,128)(2,1)S(1)} %copy-done.36), channel_id=1, source_target_pairs={{0,0},{1,2},{2,1},{3,3},{8,16},{9,18},{10,17},{11,19},{16,8},{17,1... | collective-permute-start | bytes 786440 | tf_op jit(solution)/shard_map/ppermute | solution.py:984
  152.3 40.2 %copy-start.27 = (bf16[128,768]{1,0:T(8,128)(2,1)S(1)}, bf16[128,768]{1,0:T(8,128)(2,1)}, u32[]{:S(2)}) copy-start(bf16[128,768]{1,0:T(8,128)(2,1)} %copy-done.26) | copy-start | bytes 589828
  152.3 27.1 %collective-permute-start.29 = (bf16[352,1024]{1,0:T(8,128)(2,1)S(1)}, bf16[352,1024]{1,0:T(8,128)(2,1)}, u32[]{:S(2)}, u32[]{:S(2)}) collective-permute-start(bf16[352,1024]{1,0:T(8,128)(2,1)S(1)} %pad_maximum_fusion.4), channel_id=1, source_target_pairs={{0,16},{16,0},{1,17},{17,1},{2,18},{18,2},{3,19},{19,3},{4,20},{20... | collective-permute-start | bytes 2162696 | tf_op jit(solution)/shard_map/ppermute | solution.py:298
  180.3 17.4 %collective-permute-start.31 = (bf16[704,1024]{1,0:T(8,128)(2,1)}, bf16[704,1024]{1,0:T(8,128)(2,1)}, u32[]{:S(2)}, u32[]{:S(2)}) collective-permute-start(bf16[704,1024]{1,0:T(8,128)(2,1)} %get-tuple-element.145), channel_id=1, source_target_pairs={{0,1},{1,0},{2,3},{3,2},{4,5},{5,4},{6,7},{7,6},{8,9},{9,8},{10,11... | collective-permute-start | bytes 4325384 | tf_op jit(solution)/shard_map/ppermute | solution.py:298
  181.1 2.5 collective-permute-start.33
  182.5 13.4 %collective-permute-start.47 = (bf16[64,1024]{1,0:T(8,128)(2,1)S(1)}, bf16[64,1024]{1,0:T(8,128)(2,1)S(1)}, u32[]{:S(2)}, u32[]{:S(2)}) collective-permute-start(bf16[64,1024]{1,0:T(8,128)(2,1)S(1)} %dynamic-slice_bitcast_fusion), channel_id=1, source_target_pairs={{0,1},{1,0},{2,3},{3,2},{4,5},{5,4},{6,7},{7,6},{8,9},{9,8},{10,11... | collective-permute-start | bytes 393224 | tf_op jit(solution)/shard_map/ppermute | solution.py:298
  183.6 9.8 %collective-permute-start.34 = (f32[16,768]{1,0:T(8,128)S(1)}, f32[16,768]{1,0:T(8,128)S(1)}, u32[]{:S(2)}, u32[]{:S(2)}) collective-permute-start(f32[16,768]{1,0:T(8,128)S(1)} %add.307), channel_id=1, source_target_pairs={{0,16},{16,0},{1,17},{17,1},{2,18},{18,2},{3,19},{19,3},{4,20},{20... | collective-permute-start | bytes 147464 | tf_op jit(solution)/shard_map/ppermute | solution.py:298
  190.9 4.1 %collective-permute-start.35 = (f32[16,768]{1,0:T(8,128)S(1)}, f32[16,768]{1,0:T(8,128)S(1)}, u32[]{:S(2)}, u32[]{:S(2)}) collective-permute-start(f32[16,768]{1,0:T(8,128)S(1)} %add.307), channel_id=1, source_target_pairs={{0,4},{4,0},{1,5},{5,1},{2,6},{6,2},{3,7},{7,3},{8,12},{12,8},{9,1... | collective-permute-start | bytes 147464 | tf_op jit(solution)/shard_map/ppermute | solution.py:298
  190.9 5.0 %collective-permute-start.36 = (f32[16,768]{1,0:T(8,128)S(1)}, f32[16,768]{1,0:T(8,128)S(1)}, u32[]{:S(2)}, u32[]{:S(2)}) collective-permute-start(f32[16,768]{1,0:T(8,128)S(1)} %add.307), channel_id=1, source_target_pairs={{0,20},{4,16},{16,4},{20,0},{1,21},{5,17},{17,5},{21,1},{2,22},{6,... | collective-permute-start | bytes 147464 | tf_op jit(solution)/shard_map/ppermute | solution.py:299
  193.5 11.4 %collective-permute-start.43 = (bf16[128,768]{1,0:T(8,128)(2,1)S(1)}, bf16[128,768]{1,0:T(8,128)(2,1)S(1)}, u32[]{:S(2)}, u32[]{:S(2)}) collective-permute-start(bf16[128,768]{1,0:T(8,128)(2,1)S(1)} %add_convert_fusion.9), channel_id=1, source_target_pairs={{0,8},{8,0},{1,9},{9,1},{2,10},{10,2},{3,11},{11,3},{4,12},{12,4},... | collective-permute-start | bytes 589832 | tf_op jit(solution)/shard_map/ppermute | solution.py:298
  196.7 12.3 %collective-permute-start.48 = (bf16[64,1024]{1,0:T(8,128)(2,1)}, bf16[64,1024]{1,0:T(8,128)(2,1)}, u32[]{:S(2)}, u32[]{:S(2)}) collective-permute-start(bf16[64,1024]{1,0:T(8,128)(2,1)} %fusion.15), channel_id=1, source_target_pairs={{0,16},{16,0},{1,17},{17,1},{2,18},{18,2},{3,19},{19,3},{4,20},{20... | collective-permute-start | bytes 393224 | tf_op jit(solution)/shard_map/ppermute | solution.py:298
  201.4 11.3 %collective-permute-start.49 = (bf16[128,1024]{1,0:T(8,128)(2,1)}, bf16[128,1024]{1,0:T(8,128)(2,1)}, u32[]{:S(2)}, u32[]{:S(2)}) collective-permute-start(bf16[128,1024]{1,0:T(8,128)(2,1)} %slice.273), channel_id=1, source_target_pairs={{0,16},{16,0},{1,17},{17,1},{2,18},{18,2},{3,19},{19,3},{4,20},{20... | collective-permute-start | bytes 786440 | tf_op jit(solution)/shard_map/ppermute | solution.py:298
  210.6 11.6 %collective-permute-start.38 = (bf16[176,1024]{1,0:T(8,128)(2,1)}, bf16[176,1024]{1,0:T(8,128)(2,1)}, u32[]{:S(2)}, u32[]{:S(2)}) collective-permute-start(bf16[176,1024]{1,0:T(8,128)(2,1)} %get-tuple-element.153), channel_id=1, source_target_pairs={{0,16},{16,0},{1,17},{17,1},{2,18},{18,2},{3,19},{19,3},{4,20},{20... | collective-permute-start | bytes 1081352 | tf_op jit(solution)/shard_map/ppermute | solution.py:298
  212.1 16.9 %collective-permute-start.37 = (bf16[176,1024]{1,0:T(8,128)(2,1)}, bf16[176,1024]{1,0:T(8,128)(2,1)}, u32[]{:S(2)}, u32[]{:S(2)}) collective-permute-start(bf16[176,1024]{1,0:T(8,128)(2,1)} %get-tuple-element.152), channel_id=1, source_target_pairs={{0,16},{16,0},{1,17},{17,1},{2,18},{18,2},{3,19},{19,3},{4,20},{20... | collective-permute-start | bytes 1081352 | tf_op jit(solution)/shard_map/ppermute | solution.py:298
  216.7 7.1 %collective-permute-start.44 = (bf16[2,64,896]{2,1,0:T(8,128)(2,1)S(1)}, bf16[2,64,896]{2,1,0:T(8,128)(2,1)S(1)}, u32[]{:S(2)}, u32[]{:S(2)}) collective-permute-start(bf16[2,64,896]{2,1,0:T(8,128)(2,1)S(1)} %get-tuple-element.187), channel_id=1, source_target_pairs={{0,1},{1,0},{2,3},{3,2},{4,5},{5,4},{6,7},{7,6},{8,9},{9,8},{10,11... | collective-permute-start | bytes 688136 | tf_op jit(solution)/shard_map/ppermute | solution.py:298
  223.7 12.5 %collective-permute-start.39 = (bf16[176,1024]{1,0:T(8,128)(2,1)S(1)}, bf16[176,1024]{1,0:T(8,128)(2,1)S(1)}, u32[]{:S(2)}, u32[]{:S(2)}) collective-permute-start(bf16[176,1024]{1,0:T(8,128)(2,1)S(1)} %add_convert_fusion.2), channel_id=1, source_target_pairs={{0,4},{4,0},{1,5},{5,1},{2,6},{6,2},{3,7},{7,3},{8,12},{12,8},{9,1... | collective-permute-start | bytes 1081352 | tf_op jit(solution)/shard_map/ppermute | solution.py:298
  223.9 17.8 %collective-permute-start.45 = (bf16[2,64,896]{2,1,0:T(8,128)(2,1)S(1)}, bf16[2,64,896]{2,1,0:T(8,128)(2,1)S(1)}, u32[]{:S(2)}, u32[]{:S(2)}) collective-permute-start(bf16[2,64,896]{2,1,0:T(8,128)(2,1)S(1)} %get-tuple-element.185), channel_id=1, source_target_pairs={{0,4},{4,0},{1,5},{5,1},{2,6},{6,2},{3,7},{7,3},{8,12},{12,8},{9,1... | collective-permute-start | bytes 688136 | tf_op jit(solution)/shard_map/ppermute | solution.py:298
  227.2 16.0 %copy-start.46 = (bf16[176,1024]{1,0:T(8,128)(2,1)S(1)}, bf16[176,1024]{1,0:T(8,128)(2,1)}, u32[]{:S(2)}) copy-start(bf16[176,1024]{1,0:T(8,128)(2,1)} %param.16) | copy-start | bytes 1081348
  227.2 19.8 %collective-permute-start.32 = (bf16[176,1024]{1,0:T(8,128)(2,1)S(1)}, bf16[176,1024]{1,0:T(8,128)(2,1)S(1)}, u32[]{:S(2)}, u32[]{:S(2)}) collective-permute-start(bf16[176,1024]{1,0:T(8,128)(2,1)S(1)} %add_convert_fusion.3), channel_id=1, source_target_pairs={{0,4},{4,0},{1,5},{5,1},{2,6},{6,2},{3,7},{7,3},{8,12},{12,8},{9,1... | collective-permute-start | bytes 1081352 | tf_op jit(solution)/shard_map/ppermute | solution.py:298
  236.2 13.3 %collective-permute-start.40 = (f32[16,768]{1,0:T(8,128)S(1)}, f32[16,768]{1,0:T(8,128)S(1)}, u32[]{:S(2)}, u32[]{:S(2)}) collective-permute-start(f32[16,768]{1,0:T(8,128)S(1)} %add_add_fusion), channel_id=1, source_target_pairs={{0,8},{8,0},{1,9},{9,1},{2,10},{10,2},{3,11},{11,3},{4,12},{12,4},... | collective-permute-start | bytes 147464 | tf_op jit(solution)/shard_map/ppermute | solution.py:298
  236.2 13.3 %collective-permute-start.41 = (f32[16,768]{1,0:T(8,128)S(1)}, f32[16,768]{1,0:T(8,128)S(1)}, u32[]{:S(2)}, u32[]{:S(2)}) collective-permute-start(f32[16,768]{1,0:T(8,128)S(1)} %add_add_fusion), channel_id=1, source_target_pairs={{0,2},{2,0},{1,3},{3,1},{4,6},{6,4},{5,7},{7,5},{8,10},{10,8},{9,1... | collective-permute-start | bytes 147464 | tf_op jit(solution)/shard_map/ppermute | solution.py:298
  237.6 11.9 %collective-permute-start.42 = (f32[16,768]{1,0:T(8,128)S(1)}, f32[16,768]{1,0:T(8,128)S(1)}, u32[]{:S(2)}, u32[]{:S(2)}) collective-permute-start(f32[16,768]{1,0:T(8,128)S(1)} %add_add_fusion), channel_id=1, source_target_pairs={{0,10},{2,8},{8,2},{10,0},{1,11},{3,9},{9,3},{11,1},{4,14},{6,12},... | collective-permute-start | bytes 147464 | tf_op jit(solution)/shard_map/ppermute | solution.py:299
  241.7 9.7 %collective-permute-start.46 = (bf16[2,2,64,896]{3,2,1,0:T(8,128)(2,1)S(1)}, bf16[2,2,64,896]{3,2,1,0:T(8,128)(2,1)S(1)}, u32[]{:S(2)}, u32[]{:S(2)}) collective-permute-start(bf16[2,2,64,896]{3,2,1,0:T(8,128)(2,1)S(1)} %pad_maximum_fusion.6.own), channel_id=1, source_target_pairs={{0,16},{16,0},{1,17},{17,1},{2,18},{18,2},{3,19},{19,3},{4,20},{20... | collective-permute-start | bytes 1376264 | tf_op jit(solution)/shard_map/ppermute | solution.py:298
  (62 other events, 263.1 us)

commit v4 on v3

--- a/solution.py
+++ b/solution.py
@@ -287,10 +287,10 @@
 
 PAIR = [(0, 1), (1, 0)]
 BLOCKS = 8
-NEAR, FAR = (0, 4, 1, 5), (2, 6, 3, 7)
 LANE = 128
+EXTRA = 16
 GROUP = ("o", "p", "q", "c")
-VMEM_BYTES = 28 * 1024 * 1024
+VMEM_BYTES = 58 * 1024 * 1024
 
 
 def swap(values, *axes):
@@ -366,25 +366,30 @@
         copy.wait()
 
 
-def row_pairs(sources, target):
-    return [
-        (source.at[k], target.at[pl.ds(block * source.shape[1], source.shape[1])])
-        for source, blocks in sources
-        for k, block in enumerate(blocks)
-    ]
-
-
-def sheet_pairs(pieces, target, places):
+def sheet_pairs(pieces, target, small, places):
     x, o, p, q, c = places
     pairs = []
     for index, piece in enumerate(pieces):
         jo, jq = index // 2, index % 2
-        rows = piece.shape[1]
+        rows = piece.shape[1] - EXTRA
         for k in range(4):
             jc, jp = k // 2, k % 2
-            at = ((((o ^ jo) * 2 + (p ^ jp)) * 2 + (q ^ jq)) * 2 + (c ^ jc)) * rows
-            pairs.append((piece.at[k], target.at[pl.ds(pl.multiple_of(at, rows), rows)]))
+            shard = (((o ^ jo) * 2 + (p ^ jp)) * 2 + (q ^ jq)) * 2 + (c ^ jc)
+            at = pl.multiple_of(shard * rows, rows)
+            pairs.append((piece.at[k, pl.ds(0, rows)], target.at[pl.ds(at, rows)]))
+            at = pl.multiple_of(shard * EXTRA, EXTRA)
+            pairs.append((piece.at[k, pl.ds(rows, EXTRA)], small.at[pl.ds(at, EXTRA)]))
     return pairs
+
+
+def vector_of(small, start, size=HEAD):
+    parts = [
+        wide(small[shard * EXTRA : (shard + 1) * EXTRA, start + at : start + at + HEAD])[:1]
+        for shard in range(16)
+        for at in range(0, size, HEAD)
+    ]
+    pairs = [jnp.concatenate(parts[i : i + 2], axis=1) for i in range(0, len(parts), 2)]
+    return jnp.concatenate(pairs, axis=1)
 
 
 def tall_pairs(pieces, target, places):
@@ -409,13 +414,10 @@
     return jnp.sum(values.reshape(rows // 8, 8, columns), axis=0)
 
 
-def block_rows(block, cap):
-    return pl.ds(pl.multiple_of(block * cap, 16), cap)
-
-
-def cut_kernel(ids, joint, up, down, keep, send, half):
+def cut_kernel(ids, joint, up, small, keep, send):
     x, o, p, q, c = places_of(ids)
     parts = joint.shape[1] // D
+    height = joint.shape[0]
 
     def block(ref, index):
         return ref[:, pl.ds(pl.multiple_of(index * LANE, LANE), LANE)]
@@ -423,18 +425,17 @@
     for jp, target in ((0, keep), (1, send)):
         for jc in (0, 1):
             pp, cc = p ^ jp, c ^ jc
+            target[jc, height:, :] = jnp.broadcast_to(small[...], (EXTRA, small.shape[1]))
             for part in range(parts):
-                target[jc, :, part * LANE : (part + 1) * LANE] = block(
+                target[jc, :height, part * LANE : (part + 1) * LANE] = block(
                     joint, part * 8 + x * 4 + pp * 2 + cc
                 )
             for k in range(4):
                 oo, qq = k // 2, k % 2
                 at = (parts + k) * LANE
-                target[jc, :, at : at + LANE] = block(
+                target[jc, :height, at : at + LANE] = block(
                     up, (((oo * 2 + pp) * 2 + qq) * 2 + cc) * 2 + x
                 )
-    rows = half.shape[0]
-    half[...] = down[pl.ds(pl.multiple_of(x * rows, rows), rows), :]
 
 
 def turner(cap):
@@ -450,21 +451,22 @@
     return turn, (lane < HEAD, lane >= HEAD)
 
 
-def token_pairs(sources, target):
-    return row_pairs(zip(sources, ((0, 1), (2, 3), (4, 5), (6, 7))), target)
-
-
-def both_ways(step, near_out, far_out, cap):
-    def first(block, carry):
-        near_out[block_rows(block, cap), :] = step(block // 2 * 4 + block % 2)
-        return carry
-
-    def second(block, carry):
-        far_out[block_rows(block, cap), :] = low(step(block // 2 * 4 + block % 2 + 2))
-        return carry
-
-    lax.fori_loop(0, BLOCKS // 2, first, 0)
-    lax.fori_loop(0, BLOCKS // 2, second, 0)
+def block_pairs(sources, tokens, cotangent):
+    cap = sources[0].shape[1]
+    return [
+        (source.at[2 * k + which], target.at[pl.ds((2 * i + k) * cap, cap)])
+        for i, source in enumerate(sources)
+        for k in (0, 1)
+        for which, target in enumerate((tokens, cotangent))
+        if target is not None
+    ]
+
+
+def both_ways(step, near_out, far_out, size):
+    for i in (0, 1):
+        near_out[i * size : (i + 1) * size, :] = step(2 * i)
+    for i in (0, 1):
+        far_out[i * size : (i + 1) * size, :] = low(step(2 * i + 1))
 
 
 def attention_kernel(
@@ -473,8 +475,6 @@
     block_1,
     block_2,
     block_3,
-    near,
-    far,
     sheet_0,
     sheet_1,
     sheet_2,
@@ -484,9 +484,6 @@
     cosine,
     sine,
     position,
-    gain,
-    shift,
-    offset,
     near_out,
     far_out,
     grad_ref,
@@ -501,56 +498,73 @@
     inputs,
     mixed_all,
     total,
+    small,
+    gain,
+    shift,
+    offset,
     sems,
 ):
+    x, o, p, q, c = places_of(ids)
     cap = block_0.shape[1]
     finish(
         fetch(
-            sheet_pairs((sheet_0, sheet_1, sheet_2, sheet_3), joint, places_of(ids))
-            + token_pairs((block_0, block_1, block_2, block_3), tokens)
-            + row_pairs(((near, NEAR), (far, FAR)), cotangent),
+            sheet_pairs((sheet_0, sheet_1, sheet_2, sheet_3), joint, small, places_of(ids))
+            + block_pairs((block_0, block_1, block_2, block_3), tokens, cotangent),
             sems,
         )
     )
+    gain[...] = vector_of(small, 0)
+    shift[...] = vector_of(small, HEAD)
+    offset[...] = vector_of(small, 2 * HEAD, 3 * HEAD)
+    starts = [pl.multiple_of((part * 8 + x * 4 + p * 2 + c) * LANE, LANE) for part in range(3)]
+    bias = jnp.concatenate([offset[:, pl.ds(at, LANE)] for at in starts], axis=1)
     total[...] = jnp.zeros_like(total)
-    turn, mine = turner(cap)
+    turn, mine = turner(2 * cap)
+    own = mine[0][:cap]
     down = lax.broadcasted_iota(jnp.int32, (cap, cap), 0)
     along = lax.broadcasted_iota(jnp.int32, (cap, cap), 1)
     scale = HEAD ** (-0.5)
 
-    def step(block):
-        rows = block_rows(block, cap)
+    def by_head(values):
+        none = jnp.zeros_like(values)
+        return jnp.concatenate([jnp.where(own, values, none), jnp.where(own, none, values)])
+
+    def attend(query, keys, value, grad_mixed, place):
+        allowed = ((along <= down) & (along >= down - place))[None]
+        query_two, grad_two = by_head(query), by_head(grad_mixed)
+        scores = across(query_two, keys).reshape(2, cap, cap) * scale
+        scores = jnp.where(allowed, scores, -1e30)
+        raised = jnp.exp(scores - jnp.max(scores, axis=-1, keepdims=True))
+        probs = raised / jnp.sum(raised, axis=-1, keepdims=True)
+        probs_low = low(probs).reshape(2 * cap, cap)
+        grad_probs = across(grad_two, value).reshape(2, cap, cap)
+        spread = jnp.sum(grad_probs * probs, axis=-1, keepdims=True)
+        grad_scores = low(probs * (grad_probs - spread)).reshape(2 * cap, cap)
+        mixed = times(probs_low, value)
+        grad_query = times(grad_scores, keys)
+        return (
+            jnp.where(own, mixed[:cap], mixed[cap:]),
+            jnp.where(own, grad_query[:cap], grad_query[cap:]) * scale,
+            contract_rows(grad_scores, query_two) * scale,
+            contract_rows(probs_low, grad_two),
+        )
+
+    def step(pair):
+        rows = slice(pair * 2 * cap, (pair + 1) * 2 * cap)
         input_low = low(norm_of(tokens[rows, :]) * gain[...] + shift[...])
         inputs[rows, :] = input_low
-        projected = times(input_low, joint[...]) + offset[...]
+        projected = times(input_low, joint[...]) + bias
         cos_part, sin_part = cosine[rows, :], sine[rows, :]
         query = low(turn(projected[:, :LANE], cos_part, sin_part))
         keys = low(turn(projected[:, LANE : 2 * LANE], cos_part, sin_part))
         value = low(projected[:, 2 * LANE :])
         grad_mixed = low(across(cotangent[rows, :], output_weight[...]))
-        allowed = (along <= down) & (along >= down - position[rows, :])
-        found = []
-        for own in mine:
-            query_own = jnp.where(own, query, jnp.zeros_like(query))
-            grad_own = jnp.where(own, grad_mixed, jnp.zeros_like(grad_mixed))
-            scores = jnp.where(allowed, across(query_own, keys) * scale, -1e30)
-            raised = jnp.exp(scores - jnp.max(scores, axis=-1, keepdims=True))
-            probs = raised / jnp.sum(raised, axis=-1, keepdims=True)
-            probs_low = low(probs)
-            grad_probs = across(grad_own, value)
-            spread = jnp.sum(grad_probs * probs, axis=-1, keepdims=True)
-            grad_scores = low(probs * (grad_probs - spread))
-            found.append(
-                (
-                    times(probs_low, value),
-                    times(grad_scores, keys) * scale,
-                    contract_rows(grad_scores, query) * scale,
-                    contract_rows(probs_low, grad_mixed),
-                )
-            )
-        mixed, grad_query, grad_keys, grad_value = (
-            jnp.where(mine[0], first, second) for first, second in zip(*found)
-        )
+        place = position[rows, :]
+        found = [
+            attend(query[at], keys[at], value[at], grad_mixed[at], place[at, :1])
+            for at in (slice(0, cap), slice(cap, 2 * cap))
+        ]
+        mixed, grad_query, grad_keys, grad_value = (jnp.concatenate(both) for both in zip(*found))
         mixed = low(mixed)
         mixed_all[rows, :] = mixed
         grad_joint = low(
@@ -567,7 +581,7 @@
         total[...] += fold(wide(grad_joint))
         return times(mixed, output_weight[...]) + wide(fed[rows, :])
 
-    both_ways(step, near_out, far_out, cap)
+    both_ways(step, near_out, far_out, 2 * cap)
     grad_sum[...] = jnp.sum(total[...], axis=0, keepdims=True)
     output_grad[...] = low(contract_rows(mixed_all[...], cotangent[...]))
     half = away.shape[0] // 2
@@ -606,8 +620,6 @@
     block_1,
     block_2,
     block_3,
-    near,
-    far,
     sheet_0,
     sheet_1,
     sheet_2,
@@ -616,10 +628,8 @@
     tall_1,
     tall_2,
     tall_3,
-    gain,
-    shift,
-    offset,
     fed,
+    late_offset,
     grad_all,
     home_0,
     home_1,
@@ -633,6 +643,9 @@
     inputs,
     active_all,
     total,
+    small,
+    gain,
+    shift,
     sems,
 ):
     places = places_of(ids)
@@ -640,20 +653,30 @@
     cap = block_0.shape[1]
     finish(
         fetch(
-            sheet_pairs((sheet_0, sheet_1, sheet_2, sheet_3), up, places)
-            + token_pairs((block_0, block_1, block_2, block_3), tokens)
-            + row_pairs(((near, NEAR), (far, FAR)), cotangent)
+            sheet_pairs((sheet_0, sheet_1, sheet_2, sheet_3), up, small, places)
+            + block_pairs((block_0, block_1, block_2, block_3), tokens, cotangent)
             + tall_pairs((tall_0, tall_1, tall_2, tall_3), down, places),
             sems,
         )
     )
+    gain[...] = vector_of(small, 0)
+    shift[...] = vector_of(small, HEAD)
+    width = 4 * LANE
+    late_offset[...] = vector_of(small, width - 2 * HEAD) + vector_of(small, width - HEAD)
+    along = pl.ds(pl.multiple_of((x + 1) * LANE, LANE), LANE)
+    bias = [
+        small[pl.ds(pl.multiple_of((((oo * 2 + p) * 2 + qq) * 2 + c) * EXTRA, EXTRA), EXTRA), along]
+        for oo in (0, 1)
+        for qq in (0, 1)
+    ]
+    bias = wide(jnp.concatenate(bias, axis=1))[:1]
     total[...] = jnp.zeros_like(total)
 
-    def step(block, carry):
-        rows = block_rows(block, cap)
+    for pair in range(BLOCKS // 2):
+        rows = slice(pair * 2 * cap, (pair + 1) * 2 * cap)
         input_low = low(norm_of(tokens[rows, :]) * gain[...] + shift[...])
         inputs[rows, :] = input_low
-        before = times(input_low, up[...]) + offset[...]
+        before = times(input_low, up[...]) + bias
         slope = 0.5 + 0.5 * lax.erf(before * 0.5**0.5)
         active = low(before * slope)
         active_all[rows, :] = active
@@ -662,9 +685,7 @@
         grad_all[rows, :] = grad_before
         total[...] += fold(wide(grad_before))
         fed[rows, :] = low(times(active, down[...]))
-        return carry
-
-    lax.fori_loop(0, BLOCKS, step, 0)
+
     grad_sum[...] = jnp.sum(total[...], axis=0, keepdims=True)
     unit = home_0.shape[0] // 2
     here, there = (home_0, away_0), (home_1, away_1)
@@ -695,8 +716,8 @@
     sheet_3,
     grad_joint,
     grad_before,
-    gain_one,
-    gain_two,
+    joint_sum,
+    up_sum,
     near_out,
     far_out,
     sums,
@@ -704,22 +725,31 @@
     joint,
     up,
     totals,
+    small_one,
+    small_two,
+    gain_one,
+    gain_two,
+    own,
     sems,
 ):
     places = places_of(ids)
+    x, o, p, q, c = places
     cap = block_0.shape[1]
     finish(
         fetch(
-            token_pairs((block_0, block_1, block_2, block_3), tokens)
-            + sheet_pairs((join_0, join_1, join_2, join_3), joint, places)
-            + sheet_pairs((sheet_0, sheet_1, sheet_2, sheet_3), up, places),
+            block_pairs((block_0, block_1, block_2, block_3), tokens, None)
+            + sheet_pairs((join_0, join_1, join_2, join_3), joint, small_one, places)
+            + sheet_pairs((sheet_0, sheet_1, sheet_2, sheet_3), up, small_two, places)
+            + [(block_0.at[1], own)],
             sems,
         )
     )
+    gain_one[...] = vector_of(small_one, 0)
+    gain_two[...] = vector_of(small_two, 0)
     totals[...] = jnp.zeros_like(totals)
 
-    def step(block):
-        rows = block_rows(block, cap)
+    def step(pair):
+        rows = slice(pair * 2 * cap, (pair + 1) * 2 * cap)
         normed = norm_of(tokens[rows, :])
         grad_first = across(grad_joint[rows, :], joint[...])
         grad_second = across(grad_before[rows, :], up[...])
@@ -729,8 +759,45 @@
         totals[3] += fold(grad_second)
         return grad_first * gain_one[...] + grad_second * gain_two[...]
 
-    both_ways(step, near_out, far_out, cap)
-    sums[...] = jnp.sum(totals[...], axis=1)
+    both_ways(step, near_out, far_out, 2 * cap)
+    sums[...] = jnp.zeros_like(sums)
+    sums[0:4, :] = jnp.sum(totals[...], axis=1)
+    sums[4:5, :] = jnp.sum(wide(own[...]), axis=0, keepdims=True)
+    at = pl.ds(pl.multiple_of((x * 4 + p * 2 + c) * LANE, LANE), LANE)
+    for part in range(3):
+        sums[5 + part : 6 + part, at] = joint_sum[:, part * LANE : (part + 1) * LANE]
+    for k in range(4):
+        at = pl.ds(pl.multiple_of((k % 2 * 4 + c * 2 + x) * LANE, LANE), LANE)
+        for pp in (0, 1):
+            row = 8 + k // 2 * 2 + pp
+            found = up_sum[:, k * LANE : (k + 1) * LANE]
+            sums[row : row + 1, at] = jnp.where(p == pp, found, jnp.zeros_like(found))
+
+
+def final_kernel(
+    up_home,
+    up_away,
+    down_sent,
+    up_sent,
+    joint_home,
+    joint_away,
+    joint_sent,
+    out_0,
+    out_1,
+    out_2,
+    out_3,
+    down,
+):
+    rows = down.shape[0]
+    down[...] = low(total(up_home[:rows, :], up_away[:rows, :], down_sent[...]))
+    found = low(total(up_home[rows:, :], up_away[rows:, :], up_sent[...]))
+    joint = low(total(joint_home[...], joint_away[:rows, :], joint_sent[...]))
+    half, width = rows // 2, joint.shape[1] // 2
+    hidden = found.shape[1] // 2
+    for k, out in enumerate((out_0, out_1, out_2, out_3)):
+        jp, jc = k // 2, k % 2
+        out[:, :width] = joint[jp * half : (jp + 1) * half, jc * width : (jc + 1) * width]
+        out[:, width:] = found[jp * half : (jp + 1) * half, jc * hidden : (jc + 1) * hidden]
 
 
 def lay_kernel(ids, own, other, joint, up):
@@ -794,59 +861,74 @@
     def like(shape, kind):
         return jax.ShapeDtypeStruct(shape, kind)
 
-    keep, send, down_half = call(
+    pair = jnp.stack([tokens, cotangent])
+    along_x = swap(pair, "x")
+
+    rest = jnp.zeros((HEAD,), bf)
+    small = jnp.concatenate(
+        [first_gain, first_bias, joint_bias, rest, second_gain, second_bias, up_bias, output_bias, down_bias]
+    )[None]
+    down_half = take(down_weight.reshape(2, unit, D), x)
+    keep, send = call(
         cut_kernel,
         [
-            like((2, part, 3 * LANE + hidden), bf),
-            like((2, part, 3 * LANE + hidden), bf),
-            like((unit, D), bf),
+            like((2, part + EXTRA, 3 * LANE + hidden), bf),
+            like((2, part + EXTRA, 3 * LANE + hidden), bf),
         ],
         [],
         0,
         ids,
         joint_weight,
         up_weight,
-        down_weight,
+        small,
         memory="svvv",
     )
-    came = swap(send, "p")
+    came, down_other, down_side = swap(send, "p"), swap(down_half, "o"), swap(down_half, "q")
     along_p = swap(pin(tokens, send)[0], "p")
-    along_x = swap(tokens, "x")
-    down_other = swap(down_half, "o")
-
-    turned = jnp.concatenate(
-        [keep[:1], came[:1], swap(jnp.concatenate([keep[1:], came[1:]], axis=0), "c")], axis=0
-    )
-
-    tokens_0 = jnp.stack([tokens, along_x])
-    tokens_2 = jnp.stack([along_p, swap(along_p, "x")])
-
-    joint_own, up_own = turned[:, :, : 3 * LANE], turned[:, :, 3 * LANE :]
+
+    came, down_other, down_side, along_x, along_p, lengths = pin(
+        came, down_other, down_side, along_x, along_p, lengths
+    )
+
+    turn_came, output_came = swap(jnp.concatenate([keep[1:], came[1:]]), "c"), swap(output_weight, "c")
+    turn_came, output_came, along_p = pin(turn_came, output_came, along_p)
+
+    turned = jnp.concatenate([keep[:1], came[:1], turn_came])
+    first, up_own, joint_own, along_p = pin(
+        jnp.concatenate([pair, along_x]),
+        turned[:, :, 3 * LANE :],
+        turned[:, :, : 3 * LANE],
+        along_p,
+    )
     up_other, up_side = swap(up_own, "o"), swap(up_own, "q")
-    joint_other = swap(pin(joint_own, up_other)[0], "o")
-
-    vectors = (first_gain, first_bias, second_gain, second_bias, output_bias, down_bias, joint_bias, up_bias)
-    small = jnp.concatenate(pin(*vectors, send)[:-1])[None]
-    for name, at in (("c", c), ("p", p)):
-        small = join(small, swap(small, name), at)
-    small = pin(small, up_other)[0]
-    for name, at in (("q", q), ("o", o)):
-        small = join(small, swap(small, name), at)
-    small = small.reshape(2, 2, 2, 2, -1).transpose(0, 2, 1, 3, 4).reshape(16, -1)
-
-    def vector(start, size):
-        return wide(small[:, start : start + size]).reshape(1, -1)
-
-    gain_one, shift_one, gain_two, shift_two, output_offset, down_offset = (
-        vector(i * part, part) for i in range(6)
-    )
-    joint_size = joint_bias.shape[0]
-    joint_offset = vector(6 * part, joint_size)
-    up_offset = vector(6 * part + joint_size, up_bias.shape[0])
-    joint_offset = take(joint_offset.reshape(3, 8, LANE), x * 4 + p * 2 + c, 1).reshape(1, 3 * LANE)
-    up_offset = take(take(take(up_offset.reshape(2, 2, 2, 2, 2, unit), x, 4), c, 3), p, 1)
-    up_offset = up_offset.reshape(1, hidden)
-
+    grad_along_p, along_both = swap(pin(cotangent, along_p)[0], "p"), swap(along_p, "x")
+    first_came = swap(first, "c")
+
+    devices = jnp.stack(
+        [
+            ((((x ^ xx) * 2 + o) * 2 + (p ^ pp)) * 2 + q) * 2 + (c ^ cc)
+            for pp in (0, 1)
+            for cc in (0, 1)
+            for xx in (0, 1)
+        ]
+    )
+    position = jax.vmap(lambda device: layout(lengths, owners, device, cap)[1])(devices)
+    position = position.reshape(rows, 1)
+    place = jnp.arange(LANE) % HEAD
+    half_rot = ROT // 2
+    frequency = 10000.0 ** (-jnp.arange(half_rot, dtype=f32) / half_rot)
+    angles = position.astype(f32) * jnp.tile(frequency, LANE // half_rot)[None, :]
+    position = jnp.broadcast_to(position, (rows, LANE))
+    cosine = jnp.where(place < ROT, jnp.cos(angles), 1.0)
+    sine = jnp.sin(angles)
+    sine = jnp.where(place < half_rot, -sine, jnp.where(place < ROT, sine, 0.0))
+
+    cosine, sine, position, up_other, up_side, grad_along_p, along_both, first_came, joint_own, down_other = pin(
+        cosine, sine, position, up_other, up_side, grad_along_p, along_both, first_came, joint_own, down_other
+    )
+
+    up_corner, joint_other = swap(up_other, "q"), swap(joint_own, "o")
+    grad_along_both, down_corner = swap(grad_along_p, "x"), swap(down_other, "q")
     turn_over = [
         (((a * 2 + b) * 2 + e) * 2 + f, ((b * 2 + a) * 2 + f) * 2 + e)
         for a in (0, 1)
@@ -855,44 +937,26 @@
         for f in (0, 1)
     ]
     cross = ("x", "o", "q", "c")
-    output_pair = join(output_weight, swap(output_weight, "c"), c)
-
-    devices = jnp.stack(
-        [
-            ((((x ^ xx) * 2 + o) * 2 + (p ^ pp)) * 2 + q) * 2 + (c ^ cc)
-            for pp in (0, 1)
-            for cc in (0, 1)
-            for xx in (0, 1)
-        ]
-    )
-    position = jax.vmap(lambda device: layout(lengths, owners, device, cap)[1])(devices)
-    position = position.reshape(rows, 1)
-    place = jnp.arange(LANE) % HEAD
-    half_rot = ROT // 2
-    frequency = 10000.0 ** (-jnp.arange(half_rot, dtype=f32) / half_rot)
-    angles = position.astype(f32) * jnp.tile(frequency, LANE // half_rot)[None, :]
-    cosine = jnp.where(place < ROT, jnp.cos(angles), 1.0)
-    sine = jnp.sin(angles)
-    sine = jnp.where(place < half_rot, -sine, jnp.where(place < ROT, sine, 0.0))
-
+    up_corner, down_corner, joint_other, grad_along_both, output_pair = pin(
+        up_corner, down_corner, joint_other, grad_along_both, join(output_weight, output_came, c)
+    )
+    second = jnp.stack([along_p, grad_along_p, along_both, grad_along_both])
+    second_came = swap(second, "c")
+    joint_pair, output_pair, second_came = pin(
+        jnp.stack([joint_own, joint_other]), output_pair, second_came
+    )
+    blocks = first, first_came, second, second_came
+    up_sheets = up_own, up_side, up_other, up_corner
+    down_talls = down_half, down_side, down_other, down_corner
+    joint_far = swap(joint_pair, "q")
+    output_pair = lax.ppermute(output_pair, cross, turn_over)
     copies = pltpu.SemaphoreType.DMA
-
-    tokens_1, tokens_3 = swap(tokens_0, "c"), swap(tokens_2, "c")
-    grad_along_p = swap(pin(cotangent, along_p)[0], "p")
-    grad_pair = jnp.stack([cotangent, grad_along_p])
-    near_grad = jnp.concatenate([grad_pair, swap(grad_pair, "x")])
-    far_grad = swap(near_grad, "c")
-    up_sheets = up_own, up_side, up_other, swap(up_other, "q")
-    down_far = swap(jnp.stack([down_half, down_other]), "q")
-    down_talls = down_half, down_far[0], down_other, down_far[1]
-    joint_own, joint_other, output_pair, tokens_0 = pin(joint_own, joint_other, output_pair, tokens_0)
-    joint_side, joint_corner = swap(joint_own, "q"), swap(joint_other, "q")
-    output_pair = lax.ppermute(output_pair, cross, turn_over)
     tall = (rows, D)
     found = call(
         feed_kernel,
         [
             like(tall, bf),
+            like((1, D), f32),
             like((rows, hidden), bf),
             *(like((2 * unit, D), bf) for _ in range(4)),
             like((1, hidden), f32),
@@ -905,26 +969,21 @@
             pltpu.VMEM(tall, bf),
             pltpu.VMEM((rows, hidden), bf),
             pltpu.VMEM((8, hidden), f32),
-            copies((36,)),
+            pltpu.VMEM((16 * EXTRA, hidden), bf),
+            pltpu.VMEM((1, D), f32),
+            pltpu.VMEM((1, D), f32),
+            copies((52,)),
         ],
         20,
         ids,
-        tokens_0,
-        tokens_1,
-        tokens_2,
-        tokens_3,
-        near_grad,
-        far_grad,
+        *blocks,
         *up_sheets,
         *down_talls,
-        gain_two,
-        shift_two,
-        up_offset,
-        memory="shhhhhhhhhhhhhhvvv",
-    )
-    joint_side, joint_corner, output_pair, *found = pin(joint_side, joint_corner, output_pair, *found)
-    joint_sheets = joint_own, joint_side, joint_other, joint_corner
-    fed, grad_before, up_home_0, up_home_1, up_away_0, up_away_1, up_sum = found
+        memory="shhhhhhhhhhhh",
+    )
+    joint_far, output_pair, *found = pin(joint_far, output_pair, *found)
+    joint_sheets = joint_own, joint_far[0], joint_other, joint_far[1]
+    fed, late_offset, grad_before, up_home_0, up_home_1, up_away_0, up_away_1, up_sum = found
     up_away_1 = swap(up_away_1, "q")
 
     found = call(
@@ -946,26 +1005,22 @@
             pltpu.VMEM(tall, bf),
             pltpu.VMEM((rows, LANE), bf),
             pltpu.VMEM((8, 3 * LANE), f32),
-            copies((32,)),
+            pltpu.VMEM((16 * EXTRA, 3 * LANE), bf),
+            pltpu.VMEM((1, D), f32),
+            pltpu.VMEM((1, D), f32),
+            pltpu.VMEM((1, 3 * D), f32),
+            copies((48,)),
         ],
         22,
         ids,
-        tokens_0,
-        tokens_1,
-        tokens_2,
-        tokens_3,
-        near_grad,
-        far_grad,
+        *blocks,
         *joint_sheets,
         output_pair,
         fed,
         cosine,
         sine,
         position,
-        gain_one,
-        shift_one,
-        joint_offset,
-        memory="shhhhhhhhhhvvvvvvvv",
+        memory="shhhhhhhhvvvvv",
     )
     up_away_1, up_away_0, *found = pin(up_away_1, up_away_0, *found)
     near_part, far_part, grad_joint, joint_home_0, joint_home_1, joint_away, output_grad, joint_sum = found
@@ -974,7 +1029,8 @@
         at = slice(block * cap, (block + 1) * cap)
         return near[at] + wide(came[at])
 
-    up_sent = swap(low(total(up_home_1, up_away_1)), "o")
+    up_sent = low(total(up_home_1, up_away_1))
+    down_sent = swap(up_sent[:unit], "o")
     joint_away, up_away_0 = swap(joint_away, "q"), swap(up_away_0, "q")
     result_lane = near_part, swap(far_part, "c")
     result_sent, grad_joint = pin(
@@ -984,82 +1040,104 @@
     output_part = lax.ppermute(output_grad, cross, turn_over)
     found = call(
         pull_kernel,
-        [like((rows // 2, D), f32), like((rows // 2, D), bf), like((4, D), f32)],
+        [like((rows // 2, D), f32), like((rows // 2, D), bf), like((16, D), f32)],
         [
             pltpu.VMEM(tall, bf),
             pltpu.VMEM((D, 3 * LANE), bf),
             pltpu.VMEM((D, hidden), bf),
             pltpu.VMEM((4, 8, D), f32),
-            copies((40,)),
+            pltpu.VMEM((16 * EXTRA, 3 * LANE), bf),
+            pltpu.VMEM((16 * EXTRA, hidden), bf),
+            pltpu.VMEM((1, D), f32),
+            pltpu.VMEM((1, D), f32),
+            pltpu.VMEM((cap, D), bf),
+            copies((73,)),
         ],
         11,
         ids,
-        tokens_0,
-        tokens_1,
-        tokens_2,
-        tokens_3,
+        *blocks,
         *joint_sheets,
         *up_sheets,
         grad_joint,
         grad_before,
-        gain_one,
-        gain_two,
+        joint_sum,
+        up_sum,
         memory="shhhhhhhhhhhhvvvv",
     )
-    up_sent, up_away_0, joint_away, result_came, output_part, *found = pin(
-        up_sent, up_away_0, joint_away, result_came, output_part, *found
-    )
-    near_part, far_part, norm_sums = found
-    lane = near_part, swap(far_part, "c")
-    joint_sent = swap(low(total(joint_home_1, joint_away[2 * part :])), "o")
-    corner, side, up_sent, result_came = pin(
-        low(lane_sum(*lane, 3)), low(lane_sum(*lane, 1)), up_sent, result_came
-    )
-    corner, side = swap(corner, "x"), swap(side, "x")
+    down_sent, up_away_0, joint_away, result_came, output_part, *found = pin(
+        down_sent, up_away_0, joint_away, result_came, output_part, *found
+    )
+    near_part, far_part, sums = found
+    came, sums_came = swap(far_part, "c"), swap(sums, "c")
+    output_part = output_part.reshape(2, part, D)
     result_kept = lane_sum(*result_lane, 0) + wide(result_came[:cap])
-    result_came = swap(low(lane_sum(*result_lane, 2) + wide(result_came[cap:])), "p")
-    far_side = swap(low(lane_sum(*lane, 2) + wide(corner)), "p")
-    output_part = output_part.reshape(2, part, D)
-    output_sent = swap(take(output_part, 1 - c), "c")
-    output_own = low(total(take(output_part, c), output_sent))
+
+    joint_sent, result_sent, output_sent, up_sent, came, sums_came = pin(
+        low(total(joint_home_1, joint_away[2 * part :])),
+        low(lane_sum(*result_lane, 2) + wide(result_came[cap:])),
+        take(output_part, 1 - c),
+        up_sent[unit:],
+        came,
+        sums_came,
+    )
+
+    lane = near_part, came
+    sums = sums + sums_came
+    top = low(sums)
+    rest = low(sums - wide(top))
+    sums, *sent = pin(
+        wide(top) + wide(rest),
+        *(jnp.concatenate([low(lane_sum(*lane, i)), top, rest]) for i in (1, 2, 3)),
+    )
+    side, far_side, corner = swap(sent[0], "x"), swap(sent[1], "p"), swap(sent[2], "x", "p")
+    joint_sent, up_sent = swap(joint_sent, "o"), swap(up_sent, "o")
+    side, far_side, corner, joint_sent, up_sent, output_sent = pin(
+        side, far_side, corner, joint_sent, up_sent, output_sent
+    )
+
+    def rest_of(values):
+        return wide(values[cap : cap + 16]) + wide(values[cap + 16 :])
+
+    *final, down_final = call(
+        final_kernel,
+        [*(like((part, 3 * LANE + hidden), bf) for _ in range(4)), like((unit, D), bf)],
+        [],
+        1,
+        up_home_0,
+        up_away_0,
+        down_sent,
+        up_sent,
+        joint_home_0,
+        joint_away,
+        joint_sent,
+        memory="vvvvvvv",
+    )
+    sums = (sums + rest_of(side)) + (rest_of(far_side) + rest_of(corner))
+    *final, down_final, sums = pin(*final, down_final, sums)
+    sent = swap(final[1], "c"), swap(final[2], "p"), swap(final[3], "p", "c")
+    down_came, sums_came, output_sent = swap(down_final, "x"), swap(sums, "o"), swap(output_sent, "c")
+    pulled = lane_sum(*lane, 0) + wide(side[:cap]) + wide(far_side[:cap]) + wide(corner[:cap])
+    *sent, down_came, sums_came, output_sent = pin(*sent, down_came, sums_came, output_sent)
+
+    both, sums, output_own, result_sent = pin(
+        jnp.stack([final[0], *sent]).reshape(2, 2, part, -1),
+        sums + sums_came,
+        low(total(take(output_part, c), output_sent)),
+        result_sent,
+    )
+    both_came, sums_came, output_came = swap(both, "x"), swap(sums, "q"), swap(output_own, "x")
+    result_came = swap(result_sent, "p")
     own_values = wide(tokens)
-    result = low(own_values + total(result_kept, result_came) + output_offset + down_offset)
-    output_own = total(output_own, swap(output_own, "x"))
-    up_final = low(total(up_home_0, up_away_0, up_sent))
-    joint_final = low(total(joint_home_0, joint_away[: 2 * part], joint_sent))
-    down_own = wide(join(up_final[:unit], swap(up_final[:unit], "x"), x))
-
-    def put(values, index, size, axis):
-        hot = (jnp.arange(size) == index).reshape([size if i == axis else 1 for i in range(values.ndim + 1)])
-        return jnp.where(hot, jnp.expand_dims(values, axis), 0.0)
-
-    joint_sum = put(joint_sum.reshape(3, LANE), x * 4 + p * 2 + c, 8, 1)
-    up_sum = put(put(put(up_sum.reshape(2, 2, unit), x, 2, 2), c, 2, 2), p, 2, 1)
-    sums = jnp.concatenate(
-        [
-            *(norm_sums[i].reshape(-1, part) for i in range(4)),
-            jnp.sum(wide(cotangent), axis=0).reshape(-1, part),
-            joint_sum.reshape(-1, joint_size),
-            up_sum.reshape(-1, up_bias.shape[0]),
-        ],
-        axis=1,
-    )
-    sums = sums + swap(sums, "c")
-    sums = (sums + swap(sums, "x")) + (swap(sums, "p") + swap(sums, "x", "p"))
-    sums, side, far_side = pin(sums, side, far_side)
-    pulled = lane_sum(*lane, 0) + wide(side) + wide(far_side)
-    sums = (sums + swap(sums, "o")) + (swap(sums, "q") + swap(sums, "o", "q"))
-    own_sums = take(sums, ((o * 2 + p) * 2 + q) * 2 + c)
-
-    final = jnp.concatenate(
-        [
-            joint_final.reshape(2, part, 2, 3 * LANE).transpose(2, 0, 1, 3),
-            up_final[unit:].reshape(2, part, 2, hidden).transpose(2, 0, 1, 3),
-        ],
-        axis=3,
-    )
-    both = jnp.stack([final[0], swap(final[1], "c")])
-    both = jnp.stack([both[:, 0], swap(both[:, 1], "p")])
+    result = low(own_values + total(result_kept, result_came) + late_offset)
+    sums = sums + sums_came
+    shard = ((o * 2 + p) * 2 + q) * 2 + c
+
+    def own_part(values):
+        size = values.size // 16
+        return lax.dynamic_slice_in_dim(values.reshape(-1), shard * size, size)
+
+    output_own = total(output_own, output_came)
+    down_own = wide(join(down_final, down_came, x))
     joint_own_grad, up_own_grad = call(
         lay_kernel,
         [like((part, 3 * D), f32), like((part, up_weight.shape[1]), f32)],
@@ -1067,7 +1145,7 @@
         1,
         ids,
         both,
-        swap(both, "x"),
+        both_came,
         memory="svv",
     )
 
@@ -1079,22 +1157,22 @@
         - jnp.mean(pulled, axis=-1, keepdims=True)
         - own_normed * jnp.mean(pulled * own_normed, axis=-1, keepdims=True)
     )
-    pieces = [own_sums[i * part : (i + 1) * part] for i in range(5)]
+    norm_grads = [own_part(sums[i]) for i in range(5)]
     return (
         result,
         grad_tokens,
-        pieces[0],
-        pieces[1],
+        norm_grads[0],
+        norm_grads[1],
         joint_own_grad,
-        own_sums[5 * part : 5 * part + joint_size],
+        own_part(sums[5:8]),
         output_own,
-        pieces[4],
-        pieces[2],
-        pieces[3],
+        norm_grads[4],
+        norm_grads[2],
+        norm_grads[3],
         up_own_grad,
-        own_sums[5 * part + joint_size :],
+        own_part(sums[8:12]),
         down_own,
-        pieces[4],
+        norm_grads[4],
     )
 
 

time: 255 us -> 232 us (0.910)
  local copies, waits for them, and re-layouts: 35.1 us -> 14.8 us
  waiting for transfers between devices: 72.6 us -> 81.2 us
  other arithmetic: 31.9 us -> 25 us
  starting transfers between devices: 57.2 us -> 53.3 us
    unnamed x153 -> x115, local copies, waits for them, and re-layouts: 23.2 us -> 2.92 us
    ppermute x46 -> x39, waiting for transfers between devices: 71.7 us -> 79.6 us  [swap(): return lax.ppermute(values, axes[0], PAIR)]
    reshape x12 -> x1, local copies, waits for them, and re-layouts: 4.89 us -> 0.01 us  [own_part(): return lax.dynamic_slice_in_dim(values.reshape(-1), shard * size, size)]
    convert_element_type x8 -> x5, other arithmetic: 9.32 us -> 4.67 us  [low(): return values.astype(jnp.bfloat16)]
    dynamic_slice x1 -> x7, local copies, waits for them, and re-layouts: 0.01 us -> 4.19 us  [own_part(): return lax.dynamic_slice_in_dim(values.reshape(-1), shard * size, size)]
    ppermute x2, starting transfers between devices: 4.5 us -> 1.02 us  [swap(): return lax.ppermute(values, axes, [(i, 3 - i) for i in range(4)])]
    ppermute x46 -> x39, starting transfers between devices: 50.3 us -> 50.9 us  [swap(): return lax.ppermute(values, axes[0], PAIR)]
    pallas_call x5 -> x6, Pallas kernels: 55.4 us -> 56 us  [call(): pl.pallas_call(kernel, out_shape=tuple(outs), in_specs=[specs[kind] for k...]
  transfers between devices with their start and end apart: 50 -> 43, of which waited for: 17 -> 17; matrix products, arithmetic and copies ran while one was open for 17% -> 12% of each run, Pallas kernels for 21% -> 22%
where the time goes in v4:
time: 232 us
  waiting for transfers between devices  81.2 us (35%)
  Pallas kernels  56 us (24%)
  starting transfers between devices  53.3 us (23%)
  other arithmetic  25 us (11%)
  local copies, waits for them, and re-layouts  14.8 us (6%)
    ppermute x39, waiting for transfers between devices, swap(): return lax.ppermute(values, axes[0], PAIR)  79.6 us
    pallas_call x6, Pallas kernels, call(): pl.pallas_call(kernel, out_shape=tuple(outs), in_specs=[specs[kind] for k...  56 us
    ppermute x39, starting transfers between devices, swap(): return lax.ppermute(values, axes[0], PAIR)  50.9 us
    convert_element_type x5, other arithmetic, low(): return values.astype(jnp.bfloat16)  4.67 us
  transfers between devices with their start and end apart: 43, of which 17 were waited for; matrix products, arithmetic and copies ran while one was open for 12% of the time, Pallas kernels for 22%

profile of v4, /device:TPU:0, one launch (start us, length us, event | category | flops | bytes accessed | tf_op | source)
XLA Modules:
  0.0 231.8 jit_solution(9916148886016367404)
XLA Ops:
  0.8 1.3 pad_maximum_fusion.2
  2.0 3.0 %collective-permute-start.3 = (bf16[2,176,1024]{2,1,0:T(8,128)(2,1)S(1)}, bf16[2,176,1024]{2,1,0:T(8,128)(2,1)S(1)}, u32[]{:S(2)}, u32[]{:S(2)}) collective-permute-start(bf16[2,176,1024]{2,1,0:T(8,128)(2,1)S(1)} %pad_maximum_fusion.2), channel_id=1, source_target_pairs={{0,16},{16,0},{1,17},{17,1},{2,18},{18,2},{3,19},{19,3},{4,20},{20... | collective-permute-start | bytes 2162696 | tf_op jit(solution)/shard_map/ppermute | solution.py:298
  6.4 2.2 shard_map.263
  8.5 1.6 collective-permute-start
  10.6 2.7 %collective-permute-start.1 = (bf16[128,1024]{1,0:T(8,128)(2,1)S(1)}, bf16[128,1024]{1,0:T(8,128)(2,1)S(1)}, u32[]{:S(2)}, u32[]{:S(2)}) collective-permute-start(bf16[128,1024]{1,0:T(8,128)(2,1)S(1)} %dynamic-slice_bitcast_fusion.tall_0), channel_id=1, source_target_pairs={{0,8},{8,0},{1,9},{9,1},{2,10},{10,2},{3,11},{11,3},{4,12},{12,4},... | collective-permute-start | bytes 786440 | tf_op jit(solution)/shard_map/ppermute | solution.py:298
  13.3 1.5 collective-permute-start.2
  14.8 1.0 fusion.26
  15.8 13.7 %collective-permute-done.1.tall_2 = bf16[128,1024]{1,0:T(8,128)(2,1)S(1)} collective-permute-done((bf16[128,1024]{1,0:T(8,128)(2,1)S(1)}, bf16[128,1024]{1,0:T(8,128)(2,1)S(1)}, u32[]{:S(2)}, u32[]{:S(2)}) %collective-permute-start.1) | collective-permute-done | bytes 262176 | tf_op jit(solution)/shard_map/ppermute | solution.py:298
  29.5 0.9 collective-permute-done.4
  30.4 0.7 copy-done.14
  31.1 1.0 fusion.27
  33.0 1.1 collective-permute-done.6
  34.2 0.8 slice.180.sheet_0
  36.5 2.7 %collective-permute-start.7 = (bf16[4,80,512]{2,1,0:T(8,128)(2,1)}, bf16[4,80,512]{2,1,0:T(8,128)(2,1)S(1)}, u32[]{:S(2)}, u32[]{:S(2)}) collective-permute-start(bf16[4,80,512]{2,1,0:T(8,128)(2,1)} %slice.180.sheet_0), channel_id=1, source_target_pairs={{0,8},{8,0},{1,9},{9,1},{2,10},{10,2},{3,11},{11,3},{4,12},{12,4},... | collective-permute-start | bytes 983048 | tf_op jit(solution)/shard_map/ppermute | solution.py:298
  39.2 1.5 collective-permute-start.8
  40.7 1.6 collective-permute-start.9
  42.3 3.7 %fusion.11 = (f32[1408,128]{1,0:T(8,128)}, f32[1408,128]{1,0:T(8,128)}) fusion(f32[128]{0:T(128)S(1)} %mul.135, f32[1408]{0:T(1024)S(1)} %convert_element_type.144, pred[128]{0:T(512)(128)(4,1)S(1)} %get-tuple-element.297, pred[128]{0:T(512)(128)(4,1)S(1)} %get-tuple-element.298), kind=kLoop, calls=%fused_computation.19 | loop fusion | flops 901120 | bytes 1448192 | tf_op jit(solution)/shard_map/jit(_where)/select_n | solution.py:924
  46.0 8.4 %collective-permute-done.7.sheet_2 = bf16[4,80,512]{2,1,0:T(8,128)(2,1)S(1)} collective-permute-done((bf16[4,80,512]{2,1,0:T(8,128)(2,1)}, bf16[4,80,512]{2,1,0:T(8,128)(2,1)S(1)}, u32[]{:S(2)}, u32[]{:S(2)}) %collective-permute-start.7) | collective-permute-done | bytes 327712 | tf_op jit(solution)/shard_map/ppermute | solution.py:298
  54.5 0.9 collective-permute-done.9
  56.1 1.1 broadcast_in_dim.75.position
  57.2 1.6 collective-permute-start.15
  58.8 1.3 collective-permute-start.12
  60.9 2.5 %collective-permute-start.14 = (bf16[4,80,384]{2,1,0:T(8,128)(2,1)S(1)}, bf16[4,80,384]{2,1,0:T(8,128)(2,1)S(1)}, u32[]{:S(2)}, u32[]{:S(2)}) collective-permute-start(bf16[4,80,384]{2,1,0:T(8,128)(2,1)S(1)} %pad_maximum_fusion.15.sheet_0.join_0), channel_id=1, source_target_pairs={{0,8},{8,0},{1,9},{9,1},{2,10},{10,2},{3,11},{11,3},{4,12},{12,4},... | collective-permute-start | bytes 737288 | tf_op jit(solution)/shard_map/ppermute | solution.py:298
  63.4 0.9 broadcast_select_fusion.3
  64.4 8.8 %collective-permute-done.14.sheet_2.join_2 = bf16[4,80,384]{2,1,0:T(8,128)(2,1)S(1)} collective-permute-done((bf16[4,80,384]{2,1,0:T(8,128)(2,1)S(1)}, bf16[4,80,384]{2,1,0:T(8,128)(2,1)S(1)}, u32[]{:S(2)}, u32[]{:S(2)}) %collective-permute-start.14) | collective-permute-done | bytes 245792 | tf_op jit(solution)/shard_map/ppermute | solution.py:298
  73.9 1.2 pad_maximum_fusion.1.block_2
  75.2 3.1 %collective-permute-done.16.block_3 = bf16[4,176,1024]{2,1,0:T(8,128)(2,1)S(1)} collective-permute-done((bf16[4,176,1024]{2,1,0:T(8,128)(2,1)S(1)}, bf16[4,176,1024]{2,1,0:T(8,128)(2,1)S(1)}, u32[]{:S(2)}, u32[]{:S(2)}) %collective-permute-start.16) | collective-permute-done | bytes 1441824 | tf_op jit(solution)/shard_map/ppermute | solution.py:298
  78.4 1.5 collective-permute-start.17
  80.6 18.0 %shard_map.264 = (bf16[1408,1024]{1,0:T(8,128)(2,1)}, f32[1,1024]{1,0:T(1,128)}, bf16[1408,512]{1,0:T(8,128)(2,1)}, bf16[256,1024]{1,0:T(8,128)(2,1)}, bf16[256,...) custom-call(s32[5]{0:T(128)} %stack.107.ids, ...), custom_call_target="tpu_custom_call" | custom-call | flops 23000000512 | bytes 14555156 | tf_op jit(solution)/shard_map/pallas_call | solution.py:341
  98.6 0.8 slice_bitcast_fusion
  99.4 2.7 %collective-permute-start.19 = (bf16[256,1024]{1,0:T(8,128)(2,1)}, bf16[256,1024]{1,0:T(8,128)(2,1)S(1)}, u32[]{:S(2)}, u32[]{:S(2)}) collective-permute-start(bf16[256,1024]{1,0:T(8,128)(2,1)} %get-tuple-element.177), channel_id=1, source_target_pairs={{0,2},{2,0},{1,3},{3,1},{4,6},{6,4},{5,7},{7,5},{8,10},{10,8},{9,1... | collective-permute-start | bytes 1572872 | tf_op jit(solution)/shard_map/ppermute | solution.py:298
  102.2 20.6 %shard_map.265 = (f32[704,1024]{1,0:T(8,128)}, bf16[704,1024]{1,0:T(8,128)(2,1)}, bf16[1408,384]{1,0:T(8,128)(2,1)}, bf16[128,768]{1,0:T(8,128)(2,1)}, bf16[128,...) custom-call(s32[5]{0:T(128)} %stack.107.ids, ...), custom_call_target="tpu_custom_call" | custom-call | flops 25300000768 | bytes 18515476 | tf_op jit(solution)/shard_map/pallas_call | solution.py:341
  123.1 0.7 fusion.25
  123.9 2.3 %collective-permute-start.21 = (bf16[128,1024]{1,0:T(8,128)(2,1)S(1)}, bf16[128,1024]{1,0:T(8,128)(2,1)S(1)}, u32[]{:S(2)}, u32[]{:S(2)}) collective-permute-start(bf16[128,1024]{1,0:T(8,128)(2,1)S(1)} %get-tuple-element.274), channel_id=1, source_target_pairs={{0,8},{8,0},{1,9},{9,1},{2,10},{10,2},{3,11},{11,3},{4,12},{12,4},... | collective-permute-start | bytes 786440 | tf_op jit(solution)/shard_map/ppermute | solution.py:298
  126.2 1.5 collective-permute-start.22
  128.9 2.1 add_convert_fusion.6
  131.1 3.3 %collective-permute-start.24 = (bf16[352,1024]{1,0:T(8,128)(2,1)S(1)}, bf16[352,1024]{1,0:T(8,128)(2,1)S(1)}, u32[]{:S(2)}, u32[]{:S(2)}) collective-permute-start(bf16[352,1024]{1,0:T(8,128)(2,1)S(1)} %pad_maximum_fusion.3), channel_id=1, source_target_pairs={{0,16},{16,0},{1,17},{17,1},{2,18},{18,2},{3,19},{19,3},{4,20},{20... | collective-permute-start | bytes 2162696 | tf_op jit(solution)/shard_map/ppermute | solution.py:298
  134.4 10.1 %shard_map.266 = (f32[704,1024]{1,0:T(8,128)}, bf16[704,1024]{1,0:T(8,128)(2,1)}, f32[16,1024]{1,0:T(8,128)}) custom-call(s32[5]{0:T(128)} %stack.107.ids, bf16[4,176,1024]{2,1,0:T(8,128)(2,1)} %copy-done.4, bf16[4,176,1024]{2,1,0:T(8,128)(2,1)} %collective-permute-done.11.block_1, bf16[4,176,1024]{2,1,0:T(8,128)(2,1)} %copy-done.5, ...), custom_call_target="tpu_custom_call" | custom-call | flops 12650000384 | bytes 14978580 | tf_op jit(solution)/shard_map/pallas_call | solution.py:341
  145.1 3.6 %collective-permute-done.23.joint_away = bf16[256,768]{1,0:T(8,128)(2,1)S(1)} collective-permute-done((bf16[256,768]{1,0:T(8,128)(2,1)S(1)}, bf16[256,768]{1,0:T(8,128)(2,1)S(1)}, u32[]{:S(2)}, u32[]{:S(2)}) %collective-permute-start.23) | collective-permute-done | bytes 393248 | tf_op jit(solution)/shard_map/ppermute | solution.py:298
  148.7 7.9 %collective-permute-done.24 = bf16[352,1024]{1,0:T(8,128)(2,1)S(1)} collective-permute-done((bf16[352,1024]{1,0:T(8,128)(2,1)S(1)}, bf16[352,1024]{1,0:T(8,128)(2,1)S(1)}, u32[]{:S(2)}, u32[]{:S(2)}) %collective-permute-start.24) | collective-permute-done | bytes 720928 | tf_op jit(solution)/shard_map/ppermute | solution.py:298
  157.4 1.9 add_convert_fusion.7
  159.3 2.1 add_convert_fusion.4
  163.1 1.1 pad_maximum_fusion.4
  164.3 2.5 %collective-permute-start.28 = (bf16[208,1024]{1,0:T(8,128)(2,1)}, bf16[208,1024]{1,0:T(8,128)(2,1)S(1)}, u32[]{:S(2)}, u32[]{:S(2)}) collective-permute-start(bf16[208,1024]{1,0:T(8,128)(2,1)} %get-tuple-element.221), channel_id=1, source_target_pairs={{0,16},{16,0},{1,17},{17,1},{2,18},{18,2},{3,19},{19,3},{4,20},{20... | collective-permute-start | bytes 1277960 | tf_op jit(solution)/shard_map/ppermute | solution.py:298
  167.4 0.9 collective-permute-start.30
  168.3 3.3 %collective-permute-start.32 = (bf16[128,1024]{1,0:T(8,128)(2,1)}, bf16[128,1024]{1,0:T(8,128)(2,1)}, u32[]{:S(2)}, u32[]{:S(2)}) collective-permute-start(bf16[128,1024]{1,0:T(8,128)(2,1)} %get-tuple-element.225), channel_id=1, source_target_pairs={{0,8},{8,0},{1,9},{9,1},{2,10},{10,2},{3,11},{11,3},{4,12},{12,4},... | collective-permute-start | bytes 786440 | tf_op jit(solution)/shard_map/ppermute | solution.py:298
  171.9 23.8 %collective-permute-done.31.joint_sent = bf16[128,768]{1,0:T(8,128)(2,1)S(1)} collective-permute-done((bf16[128,768]{1,0:T(8,128)(2,1)}, bf16[128,768]{1,0:T(8,128)(2,1)S(1)}, u32[]{:S(2)}, u32[]{:S(2)}) %collective-permute-start.31) | collective-permute-done | bytes 196640 | tf_op jit(solution)/shard_map/ppermute | solution.py:298
  195.7 1.6 collective-permute-done.30
  197.2 0.9 add_add_fusion
  198.1 2.5 %shard_map.267 = (bf16[64,896]{1,0:T(8,128)(2,1)}, bf16[64,896]{1,0:T(8,128)(2,1)}, bf16[64,896]{1,0:T(8,128)(2,1)}, bf16[64,896]{1,0:T(8,128)(2,1)}, bf16[128,1024]{1,0:T(8,128)(2,1)}) custom-call(bf16[256,1024]{1,0:T(8,128)(2,1)} %get-tuple-element.210.up_home, bf16[256,1024]{1,0:T(8,128)(2,1)} %copy-done.42, bf16[128,1024]{1,0:T(8,128)(2,1)} %copy-done.50, ...), custom_call_target="tpu_custom_call" | custom-call | flops 1150000000 | bytes 3080192 | tf_op jit(solution)/shard_map/pallas_call | solution.py:341
  200.7 1.8 collective-permute-start.36
  202.5 1.9 collective-permute-start.34
  204.6 1.4 collective-permute-start.37
  206.0 1.9 fusion.23
  207.9 3.7 %collective-permute-done.37 = f32[16,1024]{1,0:T(8,128)S(1)} collective-permute-done((f32[16,1024]{1,0:T(8,128)S(1)}, f32[16,1024]{1,0:T(8,128)S(1)}, u32[]{:S(2)}, u32[]{:S(2)}) %collective-permute-start.37) | collective-permute-done | bytes 65568 | tf_op jit(solution)/shard_map/ppermute | solution.py:298
  212.2 0.8 collective-permute-done.38
  213.4 1.7 collective-permute-start.41
  215.2 2.1 collective-permute-start.39
  217.4 1.1 maximum_convert_fusion
  218.5 1.0 collective-permute-done.40
  223.7 0.7 convert_add_fusion.3
  224.5 1.4 collective-permute-done.39
  225.9 2.7 %fusion.9 = (f32[176,1024]{1,0:T(8,128)}, bf16[176,1024]{1,0:T(8,128)(2,1)}) fusion(bf16[176,1024]{1,0:T(8,128)(2,1)S(1)} %copy-done.1, f32[176,1024]{1,0:T(8,128)S(1)} %get-tuple-element.262, bf16[176,1024]{1,0:T(8,128)(2,1)S(1)} %copy-done.2, f32[176]{0:T(256)S(1)} %broadcast_multiply_fusion, f32[176]{0:T(256)} %broadcast_multiply_fusion.1, ...), kind=kLoop, calls=%fused_computation.17 | loop fusion | flops 3244032 | bytes 4332288 | tf_op jit(solution)/shard_map/add | solution.py:1155
  228.7 2.6 %shard_map.268 = (f32[64,3072]{1,0:T(8,128)}, f32[64,4096]{1,0:T(8,128)}) custom-call(s32[5]{0:T(128)} %stack.107.ids, bf16[2,2,64,896]{3,2,1,0:T(8,128)(2,1)} %bitcast.62, bf16[2,2,64,896]{3,2,1,0:T(8,128)(2,1)} %collective-permute-done.41.other), custom_call_target="tpu_custom_call" | custom-call | flops 1150000000 | bytes 2752532 | tf_op jit(solution)/shard_map/pallas_call | solution.py:341
  (210 shorter events, 18.9 us)
Async XLA Ops:
  0.7 9.9 %copy-start = (bf16[256,1024]{1,0:T(8,128)(2,1)S(1)}, bf16[256,1024]{1,0:T(8,128)(2,1)}, u32[]{:S(2)}) copy-start(bf16[256,1024]{1,0:T(8,128)(2,1)} %param.30) | copy-start | bytes 1572868
  0.7 9.5 %copy-start.1 = (bf16[176,1024]{1,0:T(8,128)(2,1)S(1)}, bf16[176,1024]{1,0:T(8,128)(2,1)}, u32[]{:S(2)}) copy-start(bf16[176,1024]{1,0:T(8,128)(2,1)} %param.16) | copy-start | bytes 1081348
  2.0 29.1 %collective-permute-start.3 = (bf16[2,176,1024]{2,1,0:T(8,128)(2,1)S(1)}, bf16[2,176,1024]{2,1,0:T(8,128)(2,1)S(1)}, u32[]{:S(2)}, u32[]{:S(2)}) collective-permute-start(bf16[2,176,1024]{2,1,0:T(8,128)(2,1)S(1)} %pad_maximum_fusion.2), channel_id=1, source_target_pairs={{0,16},{16,0},{1,17},{17,1},{2,18},{18,2},{3,19},{19,3},{4,20},{20... | collective-permute-start | bytes 2162696 | tf_op jit(solution)/shard_map/ppermute | solution.py:298
  6.4 25.9 %copy-start.24 = (bf16[64,1024]{1,0:T(8,128)(2,1)S(1)}, bf16[64,1024]{1,0:T(8,128)(2,1)}, u32[]{:S(2)}) copy-start(bf16[64,1024]{1,0:T(8,128)(2,1)} %param.24) | copy-start | bytes 393220
  6.4 26.4 %copy-start.2 = (bf16[176,1024]{1,0:T(8,128)(2,1)S(1)}, bf16[176,1024]{1,0:T(8,128)(2,1)}, u32[]{:S(2)}) copy-start(bf16[176,1024]{1,0:T(8,128)(2,1)} %param.17) | copy-start | bytes 1081348
  8.5 21.0 %collective-permute-start = (bf16[2,80,896]{2,1,0:T(8,128)(2,1)}, bf16[2,80,896]{2,1,0:T(8,128)(2,1)}, u32[]{:S(2)}, u32[]{:S(2)}) collective-permute-start(bf16[2,80,896]{2,1,0:T(8,128)(2,1)} %get-tuple-element.137), channel_id=1, source_target_pairs={{0,4},{4,0},{1,5},{5,1},{2,6},{6,2},{3,7},{7,3},{8,12},{12,8},{9,1... | collective-permute-start | bytes 860168 | tf_op jit(solution)/shard_map/ppermute | solution.py:298
  10.1 20.3 %collective-permute-start.4 = (bf16[176,1024]{1,0:T(8,128)(2,1)S(1)}, bf16[176,1024]{1,0:T(8,128)(2,1)S(1)}, u32[]{:S(2)}, u32[]{:S(2)}) collective-permute-start(bf16[176,1024]{1,0:T(8,128)(2,1)S(1)} %copy-done.1), channel_id=1, source_target_pairs={{0,4},{4,0},{1,5},{5,1},{2,6},{6,2},{3,7},{7,3},{8,12},{12,8},{9,1... | collective-permute-start | bytes 1081352 | tf_op jit(solution)/shard_map/ppermute | solution.py:298
  10.6 21.5 %copy-start.18 = (bf16[128,1024]{1,0:T(8,128)(2,1)}, bf16[128,1024]{1,0:T(8,128)(2,1)S(1)}, u32[]{:S(2)}) copy-start(bf16[128,1024]{1,0:T(8,128)(2,1)S(1)} %dynamic-slice_bitcast_fusion.tall_0) | copy-start | bytes 786436
  10.6 18.9 %collective-permute-start.1 = (bf16[128,1024]{1,0:T(8,128)(2,1)S(1)}, bf16[128,1024]{1,0:T(8,128)(2,1)S(1)}, u32[]{:S(2)}, u32[]{:S(2)}) collective-permute-start(bf16[128,1024]{1,0:T(8,128)(2,1)S(1)} %dynamic-slice_bitcast_fusion.tall_0), channel_id=1, source_target_pairs={{0,8},{8,0},{1,9},{9,1},{2,10},{10,2},{3,11},{11,3},{4,12},{12,4},... | collective-permute-start | bytes 786440 | tf_op jit(solution)/shard_map/ppermute | solution.py:298
  13.3 16.2 %collective-permute-start.2 = (bf16[128,1024]{1,0:T(8,128)(2,1)S(1)}, bf16[128,1024]{1,0:T(8,128)(2,1)S(1)}, u32[]{:S(2)}, u32[]{:S(2)}) collective-permute-start(bf16[128,1024]{1,0:T(8,128)(2,1)S(1)} %dynamic-slice_bitcast_fusion.tall_0), channel_id=1, source_target_pairs={{0,2},{2,0},{1,3},{3,1},{4,6},{6,4},{5,7},{7,5},{8,10},{10,8},{9,1... | collective-permute-start | bytes 786440 | tf_op jit(solution)/shard_map/ppermute | solution.py:298
  32.2 1.8 collective-permute-start.5
  32.3 1.7 collective-permute-start.6
  32.9 13.1 %copy-start.4 = (bf16[4,176,1024]{2,1,0:T(8,128)(2,1)}, bf16[4,176,1024]{2,1,0:T(8,128)(2,1)S(1)}, u32[]{:S(2)}) copy-start(bf16[4,176,1024]{2,1,0:T(8,128)(2,1)S(1)} %pad_maximum_fusion.block_0) | copy-start | bytes 4325380
  34.1 41.1 %copy-start.7 = (bf16[4,80,384]{2,1,0:T(8,128)(2,1)}, bf16[4,80,384]{2,1,0:T(8,128)(2,1)S(1)}, u32[]{:S(2)}) copy-start(bf16[4,80,384]{2,1,0:T(8,128)(2,1)S(1)} %pad_maximum_fusion.15.sheet_0.join_0) | copy-start | bytes 737284
  34.9 20.5 %collective-permute-start.11 = (bf16[4,176,1024]{2,1,0:T(8,128)(2,1)S(1)}, bf16[4,176,1024]{2,1,0:T(8,128)(2,1)}, u32[]{:S(2)}, u32[]{:S(2)}) collective-permute-start(bf16[4,176,1024]{2,1,0:T(8,128)(2,1)S(1)} %pad_maximum_fusion.block_0), channel_id=1, source_target_pairs={{0,1},{1,0},{2,3},{3,2},{4,5},{5,4},{6,7},{7,6},{8,9},{9,8},{10,11... | collective-permute-start | bytes 4325384 | tf_op jit(solution)/shard_map/ppermute | solution.py:298
  36.0 19.3 %collective-permute-start.10 = (bf16[176,1024]{1,0:T(8,128)(2,1)S(1)}, bf16[176,1024]{1,0:T(8,128)(2,1)S(1)}, u32[]{:S(2)}, u32[]{:S(2)}) collective-permute-start(bf16[176,1024]{1,0:T(8,128)(2,1)S(1)} %copy-done.15), channel_id=1, source_target_pairs={{0,16},{16,0},{1,17},{17,1},{2,18},{18,2},{3,19},{19,3},{4,20},{20... | collective-permute-start | bytes 1081352 | tf_op jit(solution)/shard_map/ppermute | solution.py:298
  36.5 18.0 %collective-permute-start.7 = (bf16[4,80,512]{2,1,0:T(8,128)(2,1)}, bf16[4,80,512]{2,1,0:T(8,128)(2,1)S(1)}, u32[]{:S(2)}, u32[]{:S(2)}) collective-permute-start(bf16[4,80,512]{2,1,0:T(8,128)(2,1)} %slice.180.sheet_0), channel_id=1, source_target_pairs={{0,8},{8,0},{1,9},{9,1},{2,10},{10,2},{3,11},{11,3},{4,12},{12,4},... | collective-permute-start | bytes 983048 | tf_op jit(solution)/shard_map/ppermute | solution.py:298
  39.2 15.3 %collective-permute-start.8 = (bf16[4,80,512]{2,1,0:T(8,128)(2,1)}, bf16[4,80,512]{2,1,0:T(8,128)(2,1)S(1)}, u32[]{:S(2)}, u32[]{:S(2)}) collective-permute-start(bf16[4,80,512]{2,1,0:T(8,128)(2,1)} %slice.180.sheet_0), channel_id=1, source_target_pairs={{0,2},{2,0},{1,3},{3,1},{4,6},{6,4},{5,7},{7,5},{8,10},{10,8},{9,1... | collective-permute-start | bytes 983048 | tf_op jit(solution)/shard_map/ppermute | solution.py:298
  40.7 14.7 %collective-permute-start.9 = (bf16[176,1024]{1,0:T(8,128)(2,1)S(1)}, bf16[176,1024]{1,0:T(8,128)(2,1)}, u32[]{:S(2)}, u32[]{:S(2)}) collective-permute-start(bf16[176,1024]{1,0:T(8,128)(2,1)S(1)} %copy-done.2), channel_id=1, source_target_pairs={{0,4},{4,0},{1,5},{5,1},{2,6},{6,2},{3,7},{7,3},{8,12},{12,8},{9,1... | collective-permute-start | bytes 1081352 | tf_op jit(solution)/shard_map/ppermute | solution.py:298
  56.1 17.7 %copy-start.17 = (bf16[176,1024]{1,0:T(8,128)(2,1)S(1)}, bf16[176,1024]{1,0:T(8,128)(2,1)}, u32[]{:S(2)}) copy-start(bf16[176,1024]{1,0:T(8,128)(2,1)} %copy-done.16) | copy-start | bytes 1081348
  57.2 15.9 %collective-permute-start.15 = (bf16[176,1024]{1,0:T(8,128)(2,1)}, bf16[176,1024]{1,0:T(8,128)(2,1)S(1)}, u32[]{:S(2)}, u32[]{:S(2)}) collective-permute-start(bf16[176,1024]{1,0:T(8,128)(2,1)} %collective-permute-done.9), channel_id=1, source_target_pairs={{0,16},{16,0},{1,17},{17,1},{2,18},{18,2},{3,19},{19,3},{4,20},{20... | collective-permute-start | bytes 1081352 | tf_op jit(solution)/shard_map/ppermute | solution.py:298
  58.8 14.3 %collective-permute-start.12 = (bf16[4,80,512]{2,1,0:T(8,128)(2,1)}, bf16[4,80,512]{2,1,0:T(8,128)(2,1)S(1)}, u32[]{:S(2)}, u32[]{:S(2)}) collective-permute-start(bf16[4,80,512]{2,1,0:T(8,128)(2,1)} %copy-done.45), channel_id=1, source_target_pairs={{0,2},{2,0},{1,3},{3,1},{4,6},{6,4},{5,7},{7,5},{8,10},{10,8},{9,1... | collective-permute-start | bytes 983048 | tf_op jit(solution)/shard_map/ppermute | solution.py:298
  60.2 13.0 %collective-permute-start.13 = (bf16[128,1024]{1,0:T(8,128)(2,1)}, bf16[128,1024]{1,0:T(8,128)(2,1)S(1)}, u32[]{:S(2)}, u32[]{:S(2)}) collective-permute-start(bf16[128,1024]{1,0:T(8,128)(2,1)} %copy-done.48), channel_id=1, source_target_pairs={{0,2},{2,0},{1,3},{3,1},{4,6},{6,4},{5,7},{7,5},{8,10},{10,8},{9,1... | collective-permute-start | bytes 786440 | tf_op jit(solution)/shard_map/ppermute | solution.py:298
  60.9 12.3 %collective-permute-start.14 = (bf16[4,80,384]{2,1,0:T(8,128)(2,1)S(1)}, bf16[4,80,384]{2,1,0:T(8,128)(2,1)S(1)}, u32[]{:S(2)}, u32[]{:S(2)}) collective-permute-start(bf16[4,80,384]{2,1,0:T(8,128)(2,1)S(1)} %pad_maximum_fusion.15.sheet_0.join_0), channel_id=1, source_target_pairs={{0,8},{8,0},{1,9},{9,1},{2,10},{10,2},{3,11},{11,3},{4,12},{12,4},... | collective-permute-start | bytes 737288 | tf_op jit(solution)/shard_map/ppermute | solution.py:298
  75.1 3.3 %collective-permute-start.16 = (bf16[4,176,1024]{2,1,0:T(8,128)(2,1)S(1)}, bf16[4,176,1024]{2,1,0:T(8,128)(2,1)S(1)}, u32[]{:S(2)}, u32[]{:S(2)}) collective-permute-start(bf16[4,176,1024]{2,1,0:T(8,128)(2,1)S(1)} %pad_maximum_fusion.1.block_2), channel_id=1, source_target_pairs={{0,1},{1,0},{2,3},{3,2},{4,5},{5,4},{6,7},{7,6},{8,9},{9,8},{10,11... | collective-permute-start | bytes 4325384 | tf_op jit(solution)/shard_map/ppermute | solution.py:298
  78.4 20.2 %collective-permute-start.17 = (bf16[2,4,80,384]{3,2,1,0:T(8,128)(2,1)S(1)}, bf16[2,4,80,384]{3,2,1,0:T(8,128)(2,1)S(1)}, u32[]{:S(2)}, u32[]{:S(2)}) collective-permute-start(bf16[2,4,80,384]{3,2,1,0:T(8,128)(2,1)S(1)} %pad_maximum_fusion.11), channel_id=1, source_target_pairs={{0,2},{2,0},{1,3},{3,1},{4,6},{6,4},{5,7},{7,5},{8,10},{10,8},{9,1... | collective-permute-start | bytes 1474568 | tf_op jit(solution)/shard_map/ppermute | solution.py:298
  79.9 18.7 %collective-permute-start.18 = (bf16[128,1024]{1,0:T(8,128)(2,1)S(1)}, bf16[128,1024]{1,0:T(8,128)(2,1)S(1)}, u32[]{:S(2)}, u32[]{:S(2)}) collective-permute-start(bf16[128,1024]{1,0:T(8,128)(2,1)S(1)} %pad_maximum_fusion.14), channel_id=1, source_target_pairs={{0,0},{1,2},{2,1},{3,3},{8,16},{9,18},{10,17},{11,19},{16,8},{17,1... | collective-permute-start | bytes 786440 | tf_op jit(solution)/shard_map/ppermute | solution.py:952
  99.4 23.4 %collective-permute-start.19 = (bf16[256,1024]{1,0:T(8,128)(2,1)}, bf16[256,1024]{1,0:T(8,128)(2,1)S(1)}, u32[]{:S(2)}, u32[]{:S(2)}) collective-permute-start(bf16[256,1024]{1,0:T(8,128)(2,1)} %get-tuple-element.177), channel_id=1, source_target_pairs={{0,2},{2,0},{1,3},{3,1},{4,6},{6,4},{5,7},{7,5},{8,10},{10,8},{9,1... | collective-permute-start | bytes 1572872 | tf_op jit(solution)/shard_map/ppermute | solution.py:298
  102.2 20.8 %copy-start.10 = (bf16[256,1024]{1,0:T(8,128)(2,1)S(1)}, bf16[256,1024]{1,0:T(8,128)(2,1)}, u32[]{:S(2)}) copy-start(bf16[256,1024]{1,0:T(8,128)(2,1)} %get-tuple-element.195) | copy-start | bytes 1572868
  122.8 6.1 %collective-permute-start.20 = (bf16[704,1024]{1,0:T(8,128)(2,1)}, bf16[704,1024]{1,0:T(8,128)(2,1)S(1)}, u32[]{:S(2)}, u32[]{:S(2)}) collective-permute-start(bf16[704,1024]{1,0:T(8,128)(2,1)} %get-tuple-element.194), channel_id=1, source_target_pairs={{0,1},{1,0},{2,3},{3,2},{4,5},{5,4},{6,7},{7,6},{8,9},{9,8},{10,11... | collective-permute-start | bytes 4325384 | tf_op jit(solution)/shard_map/ppermute | solution.py:298
  123.9 21.2 %collective-permute-start.21 = (bf16[128,1024]{1,0:T(8,128)(2,1)S(1)}, bf16[128,1024]{1,0:T(8,128)(2,1)S(1)}, u32[]{:S(2)}, u32[]{:S(2)}) collective-permute-start(bf16[128,1024]{1,0:T(8,128)(2,1)S(1)} %get-tuple-element.274), channel_id=1, source_target_pairs={{0,8},{8,0},{1,9},{9,1},{2,10},{10,2},{3,11},{11,3},{4,12},{12,4},... | collective-permute-start | bytes 786440 | tf_op jit(solution)/shard_map/ppermute | solution.py:298
  126.2 22.5 %collective-permute-start.22 = (bf16[256,1024]{1,0:T(8,128)(2,1)S(1)}, bf16[256,1024]{1,0:T(8,128)(2,1)S(1)}, u32[]{:S(2)}, u32[]{:S(2)}) collective-permute-start(bf16[256,1024]{1,0:T(8,128)(2,1)S(1)} %copy-done.43), channel_id=1, source_target_pairs={{0,2},{2,0},{1,3},{3,1},{4,6},{6,4},{5,7},{7,5},{8,10},{10,8},{9,1... | collective-permute-start | bytes 1572872 | tf_op jit(solution)/shard_map/ppermute | solution.py:298
  127.7 21.0 %collective-permute-start.23 = (bf16[256,768]{1,0:T(8,128)(2,1)S(1)}, bf16[256,768]{1,0:T(8,128)(2,1)S(1)}, u32[]{:S(2)}, u32[]{:S(2)}) collective-permute-start(bf16[256,768]{1,0:T(8,128)(2,1)S(1)} %copy-done.44), channel_id=1, source_target_pairs={{0,2},{2,0},{1,3},{3,1},{4,6},{6,4},{5,7},{7,5},{8,10},{10,8},{9,1... | collective-permute-start | bytes 1179656 | tf_op jit(solution)/shard_map/ppermute | solution.py:298
  128.2 16.9 %collective-permute-start.25 = (bf16[128,1024]{1,0:T(8,128)(2,1)S(1)}, bf16[128,1024]{1,0:T(8,128)(2,1)S(1)}, u32[]{:S(2)}, u32[]{:S(2)}) collective-permute-start(bf16[128,1024]{1,0:T(8,128)(2,1)S(1)} %copy-done.51), channel_id=1, source_target_pairs={{0,0},{1,2},{2,1},{3,3},{8,16},{9,18},{10,17},{11,19},{16,8},{17,1... | collective-permute-start | bytes 786440 | tf_op jit(solution)/shard_map/ppermute | solution.py:1040
  131.1 25.5 %collective-permute-start.24 = (bf16[352,1024]{1,0:T(8,128)(2,1)S(1)}, bf16[352,1024]{1,0:T(8,128)(2,1)S(1)}, u32[]{:S(2)}, u32[]{:S(2)}) collective-permute-start(bf16[352,1024]{1,0:T(8,128)(2,1)S(1)} %pad_maximum_fusion.3), channel_id=1, source_target_pairs={{0,16},{16,0},{1,17},{17,1},{2,18},{18,2},{3,19},{19,3},{4,20},{20... | collective-permute-start | bytes 2162696 | tf_op jit(solution)/shard_map/ppermute | solution.py:298
  145.1 11.5 %copy-start.50 = (bf16[128,1024]{1,0:T(8,128)(2,1)}, bf16[128,1024]{1,0:T(8,128)(2,1)S(1)}, u32[]{:S(2)}) copy-start(bf16[128,1024]{1,0:T(8,128)(2,1)S(1)} %collective-permute-done.21.down_sent) | copy-start | bytes 786436
  145.1 11.5 %copy-start.19 = (bf16[128,1024]{1,0:T(8,128)(2,1)}, bf16[128,1024]{1,0:T(8,128)(2,1)S(1)}, u32[]{:S(2)}) copy-start(bf16[128,1024]{1,0:T(8,128)(2,1)S(1)} %collective-permute-done.25) | copy-start | bytes 786436
  148.7 7.9 %copy-start.28 = (bf16[256,768]{1,0:T(8,128)(2,1)}, bf16[256,768]{1,0:T(8,128)(2,1)S(1)}, u32[]{:S(2)}) copy-start(bf16[256,768]{1,0:T(8,128)(2,1)S(1)} %collective-permute-done.23.joint_away) | copy-start | bytes 1179652
  148.7 7.9 %copy-start.42 = (bf16[256,1024]{1,0:T(8,128)(2,1)}, bf16[256,1024]{1,0:T(8,128)(2,1)S(1)}, u32[]{:S(2)}) copy-start(bf16[256,1024]{1,0:T(8,128)(2,1)S(1)} %collective-permute-done.22.up_away) | copy-start | bytes 1572868
  156.6 5.5 %collective-permute-start.26 = (bf16[704,1024]{1,0:T(8,128)(2,1)}, bf16[704,1024]{1,0:T(8,128)(2,1)S(1)}, u32[]{:S(2)}, u32[]{:S(2)}) collective-permute-start(bf16[704,1024]{1,0:T(8,128)(2,1)} %get-tuple-element.217), channel_id=1, source_target_pairs={{0,1},{1,0},{2,3},{3,2},{4,5},{5,4},{6,7},{7,6},{8,9},{9,8},{10,11... | collective-permute-start | bytes 4325384 | tf_op jit(solution)/shard_map/ppermute | solution.py:298
  157.0 5.1 %collective-permute-start.27 = (f32[16,1024]{1,0:T(8,128)}, f32[16,1024]{1,0:T(8,128)S(1)}, u32[]{:S(2)}, u32[]{:S(2)}) collective-permute-start(f32[16,1024]{1,0:T(8,128)} %get-tuple-element.213), channel_id=1, source_target_pairs={{0,1},{1,0},{2,3},{3,2},{4,5},{5,4},{6,7},{7,6},{8,9},{9,8},{10,11... | collective-permute-start | bytes 196616 | tf_op jit(solution)/shard_map/ppermute | solution.py:298
  164.3 31.4 %collective-permute-start.28 = (bf16[208,1024]{1,0:T(8,128)(2,1)}, bf16[208,1024]{1,0:T(8,128)(2,1)S(1)}, u32[]{:S(2)}, u32[]{:S(2)}) collective-permute-start(bf16[208,1024]{1,0:T(8,128)(2,1)} %get-tuple-element.221), channel_id=1, source_target_pairs={{0,16},{16,0},{1,17},{17,1},{2,18},{18,2},{3,19},{19,3},{4,20},{20... | collective-permute-start | bytes 1277960 | tf_op jit(solution)/shard_map/ppermute | solution.py:298
  166.8 28.9 %collective-permute-start.29 = (bf16[208,1024]{1,0:T(8,128)(2,1)}, bf16[208,1024]{1,0:T(8,128)(2,1)S(1)}, u32[]{:S(2)}, u32[]{:S(2)}) collective-permute-start(bf16[208,1024]{1,0:T(8,128)(2,1)} %get-tuple-element.222), channel_id=1, source_target_pairs={{0,4},{4,0},{1,5},{5,1},{2,6},{6,2},{3,7},{7,3},{8,12},{12,8},{9,1... | collective-permute-start | bytes 1277960 | tf_op jit(solution)/shard_map/ppermute | solution.py:298
  167.4 29.9 %collective-permute-start.30 = (bf16[208,1024]{1,0:T(8,128)(2,1)}, bf16[208,1024]{1,0:T(8,128)(2,1)}, u32[]{:S(2)}, u32[]{:S(2)}) collective-permute-start(bf16[208,1024]{1,0:T(8,128)(2,1)} %get-tuple-element.223), channel_id=1, source_target_pairs={{0,20},{4,16},{16,4},{20,0},{1,21},{5,17},{17,5},{21,1},{2,22},{6,... | collective-permute-start | bytes 1277960 | tf_op jit(solution)/shard_map/ppermute | solution.py:299
  168.3 27.4 %collective-permute-start.32 = (bf16[128,1024]{1,0:T(8,128)(2,1)}, bf16[128,1024]{1,0:T(8,128)(2,1)}, u32[]{:S(2)}, u32[]{:S(2)}) collective-permute-start(bf16[128,1024]{1,0:T(8,128)(2,1)} %get-tuple-element.225), channel_id=1, source_target_pairs={{0,8},{8,0},{1,9},{9,1},{2,10},{10,2},{3,11},{11,3},{4,12},{12,4},... | collective-permute-start | bytes 786440 | tf_op jit(solution)/shard_map/ppermute | solution.py:298
  171.8 23.8 %collective-permute-start.31 = (bf16[128,768]{1,0:T(8,128)(2,1)}, bf16[128,768]{1,0:T(8,128)(2,1)S(1)}, u32[]{:S(2)}, u32[]{:S(2)}) collective-permute-start(bf16[128,768]{1,0:T(8,128)(2,1)} %add_convert_fusion.7), channel_id=1, source_target_pairs={{0,8},{8,0},{1,9},{9,1},{2,10},{10,2},{3,11},{11,3},{4,12},{12,4},... | collective-permute-start | bytes 589832 | tf_op jit(solution)/shard_map/ppermute | solution.py:298
  195.6 8.9 %copy-start.12 = (bf16[208,1024]{1,0:T(8,128)(2,1)}, bf16[208,1024]{1,0:T(8,128)(2,1)S(1)}, u32[]{:S(2)}) copy-start(bf16[208,1024]{1,0:T(8,128)(2,1)S(1)} %collective-permute-done.28) | copy-start | bytes 1277956
  195.7 8.9 %copy-start.13 = (bf16[208,1024]{1,0:T(8,128)(2,1)}, bf16[208,1024]{1,0:T(8,128)(2,1)S(1)}, u32[]{:S(2)}) copy-start(bf16[208,1024]{1,0:T(8,128)(2,1)S(1)} %collective-permute-done.29) | copy-start | bytes 1277956
  200.7 10.9 %copy-start.26 = (bf16[64,1024]{1,0:T(8,128)(2,1)S(1)}, bf16[64,1024]{1,0:T(8,128)(2,1)}, u32[]{:S(2)}) copy-start(bf16[64,1024]{1,0:T(8,128)(2,1)} %dynamic-slice_bitcast_fusion.1) | copy-start | bytes 393220
  200.7 12.3 %copy-start.21 = (bf16[128,1024]{1,0:T(8,128)(2,1)S(1)}, bf16[128,1024]{1,0:T(8,128)(2,1)}, u32[]{:S(2)}) copy-start(bf16[128,1024]{1,0:T(8,128)(2,1)} %copy-done.19) | copy-start | bytes 786436
  200.7 12.3 %copy-start.27 = (bf16[64,896]{1,0:T(8,128)(2,1)S(1)}, bf16[64,896]{1,0:T(8,128)(2,1)}, u32[]{:S(2)}) copy-start(bf16[64,896]{1,0:T(8,128)(2,1)} %get-tuple-element.239) | copy-start | bytes 344068
  200.7 12.2 %collective-permute-start.36 = (bf16[128,1024]{1,0:T(8,128)(2,1)}, bf16[128,1024]{1,0:T(8,128)(2,1)S(1)}, u32[]{:S(2)}, u32[]{:S(2)}) collective-permute-start(bf16[128,1024]{1,0:T(8,128)(2,1)} %get-tuple-element.243), channel_id=1, source_target_pairs={{0,16},{16,0},{1,17},{17,1},{2,18},{18,2},{3,19},{19,3},{4,20},{20... | collective-permute-start | bytes 786440 | tf_op jit(solution)/shard_map/ppermute | solution.py:298
  202.5 9.6 %collective-permute-start.33 = (bf16[64,896]{1,0:T(8,128)(2,1)}, bf16[64,896]{1,0:T(8,128)(2,1)S(1)}, u32[]{:S(2)}, u32[]{:S(2)}) collective-permute-start(bf16[64,896]{1,0:T(8,128)(2,1)} %get-tuple-element.240), channel_id=1, source_target_pairs={{0,1},{1,0},{2,3},{3,2},{4,5},{5,4},{6,7},{7,6},{8,9},{9,8},{10,11... | collective-permute-start | bytes 344072 | tf_op jit(solution)/shard_map/ppermute | solution.py:298
  202.5 9.6 %collective-permute-start.34 = (bf16[64,896]{1,0:T(8,128)(2,1)}, bf16[64,896]{1,0:T(8,128)(2,1)S(1)}, u32[]{:S(2)}, u32[]{:S(2)}) collective-permute-start(bf16[64,896]{1,0:T(8,128)(2,1)} %get-tuple-element.241), channel_id=1, source_target_pairs={{0,4},{4,0},{1,5},{5,1},{2,6},{6,2},{3,7},{7,3},{8,12},{12,8},{9,1... | collective-permute-start | bytes 344072 | tf_op jit(solution)/shard_map/ppermute | solution.py:298
  204.4 7.7 %collective-permute-start.35 = (bf16[64,896]{1,0:T(8,128)(2,1)}, bf16[64,896]{1,0:T(8,128)(2,1)S(1)}, u32[]{:S(2)}, u32[]{:S(2)}) collective-permute-start(bf16[64,896]{1,0:T(8,128)(2,1)} %get-tuple-element.242), channel_id=1, source_target_pairs={{0,5},{1,4},{4,1},{5,0},{2,7},{3,6},{6,3},{7,2},{8,13},{9,12},{12,... | collective-permute-start | bytes 344072 | tf_op jit(solution)/shard_map/ppermute | solution.py:299
  204.6 7.0 %collective-permute-start.37 = (f32[16,1024]{1,0:T(8,128)S(1)}, f32[16,1024]{1,0:T(8,128)S(1)}, u32[]{:S(2)}, u32[]{:S(2)}) collective-permute-start(f32[16,1024]{1,0:T(8,128)S(1)} %add_add_fusion), channel_id=1, source_target_pairs={{0,8},{8,0},{1,9},{9,1},{2,10},{10,2},{3,11},{11,3},{4,12},{12,4},... | collective-permute-start | bytes 196616 | tf_op jit(solution)/shard_map/ppermute | solution.py:298
  207.8 9.5 %copy-start.22 = (bf16[128,1024]{1,0:T(8,128)(2,1)S(1)}, bf16[128,1024]{1,0:T(8,128)(2,1)}, u32[]{:S(2)}) copy-start(bf16[128,1024]{1,0:T(8,128)(2,1)} %get-tuple-element.243) | copy-start | bytes 786436
  211.6 1.3 collective-permute-start.38
  213.1 10.6 %collective-permute-start.42 = (bf16[64,1024]{1,0:T(8,128)(2,1)S(1)}, bf16[64,1024]{1,0:T(8,128)(2,1)S(1)}, u32[]{:S(2)}, u32[]{:S(2)}) collective-permute-start(bf16[64,1024]{1,0:T(8,128)(2,1)S(1)} %fusion.15), channel_id=1, source_target_pairs={{0,16},{16,0},{1,17},{17,1},{2,18},{18,2},{3,19},{19,3},{4,20},{20... | collective-permute-start | bytes 393224 | tf_op jit(solution)/shard_map/ppermute | solution.py:298
  213.4 15.2 %collective-permute-start.41 = (bf16[2,2,64,896]{3,2,1,0:T(8,128)(2,1)S(1)}, bf16[2,2,64,896]{3,2,1,0:T(8,128)(2,1)}, u32[]{:S(2)}, u32[]{:S(2)}) collective-permute-start(bf16[2,2,64,896]{3,2,1,0:T(8,128)(2,1)S(1)} %bitcast.61), channel_id=1, source_target_pairs={{0,16},{16,0},{1,17},{17,1},{2,18},{18,2},{3,19},{19,3},{4,20},{20... | collective-permute-start | bytes 1376264 | tf_op jit(solution)/shard_map/ppermute | solution.py:298
  215.2 4.3 %collective-permute-start.40 = (f32[16,1024]{1,0:T(8,128)S(1)}, f32[16,1024]{1,0:T(8,128)S(1)}, u32[]{:S(2)}, u32[]{:S(2)}) collective-permute-start(f32[16,1024]{1,0:T(8,128)S(1)} %add.261), channel_id=1, source_target_pairs={{0,2},{2,0},{1,3},{3,1},{4,6},{6,4},{5,7},{7,5},{8,10},{10,8},{9,1... | collective-permute-start | bytes 196616 | tf_op jit(solution)/shard_map/ppermute | solution.py:298
  215.2 10.7 %collective-permute-start.39 = (bf16[176,1024]{1,0:T(8,128)(2,1)}, bf16[176,1024]{1,0:T(8,128)(2,1)}, u32[]{:S(2)}, u32[]{:S(2)}) collective-permute-start(bf16[176,1024]{1,0:T(8,128)(2,1)} %add_convert_fusion.4), channel_id=1, source_target_pairs={{0,4},{4,0},{1,5},{5,1},{2,6},{6,2},{3,7},{7,3},{8,12},{12,8},{9,1... | collective-permute-start | bytes 1081352 | tf_op jit(solution)/shard_map/ppermute | solution.py:298
  217.4 8.5 %copy-start.9 = (bf16[352,1024]{1,0:T(8,128)(2,1)S(1)}, bf16[352,1024]{1,0:T(8,128)(2,1)}, u32[]{:S(2)}) copy-start(bf16[352,1024]{1,0:T(8,128)(2,1)} %copy-done.8) | copy-start | bytes 2162692
  217.4 8.5 %copy-start.30 = (f32[1,1024]{1,0:T(1,128)S(1)}, f32[1,1024]{1,0:T(1,128)}, u32[]{:S(2)}) copy-start(f32[1,1024]{1,0:T(1,128)} %get-tuple-element.253) | copy-start | bytes 12292
  (35 other events, 117.2 us)

commit v5 on v4

--- a/solution.py
+++ b/solution.py
@@ -371,20 +371,22 @@
     pairs = []
     for index, piece in enumerate(pieces):
         jo, jq = index // 2, index % 2
-        rows = piece.shape[1] - EXTRA
+        rows = piece.shape[1] if small is None else piece.shape[1] - EXTRA
         for k in range(4):
             jc, jp = k // 2, k % 2
             shard = (((o ^ jo) * 2 + (p ^ jp)) * 2 + (q ^ jq)) * 2 + (c ^ jc)
-            at = pl.multiple_of(shard * rows, rows)
-            pairs.append((piece.at[k, pl.ds(0, rows)], target.at[pl.ds(at, rows)]))
-            at = pl.multiple_of(shard * EXTRA, EXTRA)
-            pairs.append((piece.at[k, pl.ds(rows, EXTRA)], small.at[pl.ds(at, EXTRA)]))
+            if target is not None:
+                at = pl.multiple_of(shard * rows, rows)
+                pairs.append((piece.at[k, pl.ds(0, rows)], target.at[pl.ds(at, rows)]))
+            if small is not None:
+                at = pl.multiple_of(shard * EXTRA, EXTRA)
+                pairs.append((piece.at[k, pl.ds(rows, EXTRA)], small.at[pl.ds(at, EXTRA)]))
     return pairs
 
 
-def vector_of(small, start, size=HEAD):
+def vector_of(small, start, size=HEAD, row=0):
     parts = [
-        wide(small[shard * EXTRA : (shard + 1) * EXTRA, start + at : start + at + HEAD])[:1]
+        wide(small[shard * EXTRA : (shard + 1) * EXTRA, start + at : start + at + HEAD])[row : row + 1]
         for shard in range(16)
         for at in range(0, size, HEAD)
     ]
@@ -418,6 +420,11 @@
     x, o, p, q, c = places_of(ids)
     parts = joint.shape[1] // D
     height = joint.shape[0]
+    first = parts * LANE
+    columns = small.shape[1] - first
+    ours = jnp.concatenate([small[:, :first], small[:, : columns - first]], axis=1)
+    upper = lax.broadcasted_iota(jnp.int32, (EXTRA, columns), 0) < EXTRA // 2
+    vectors = low(jnp.where(upper, wide(small[:, first:]), wide(ours)))
 
     def block(ref, index):
         return ref[:, pl.ds(pl.multiple_of(index * LANE, LANE), LANE)]
@@ -425,7 +432,8 @@
     for jp, target in ((0, keep), (1, send)):
         for jc in (0, 1):
             pp, cc = p ^ jp, c ^ jc
-            target[jc, height:, :] = jnp.broadcast_to(small[...], (EXTRA, small.shape[1]))
+            target[jc, height:, :first] = jnp.broadcast_to(small[:, :first], (EXTRA, first))
+            target[jc, height:, first:] = vectors
             for part in range(parts):
                 target[jc, :height, part * LANE : (part + 1) * LANE] = block(
                     joint, part * 8 + x * 4 + pp * 2 + cc
@@ -479,6 +487,10 @@
     sheet_1,
     sheet_2,
     sheet_3,
+    extra_0,
+    extra_1,
+    extra_2,
+    extra_3,
     output_weight,
     fed,
     cosine,
@@ -508,14 +520,16 @@
     cap = block_0.shape[1]
     finish(
         fetch(
-            sheet_pairs((sheet_0, sheet_1, sheet_2, sheet_3), joint, small, places_of(ids))
+            sheet_pairs((sheet_0, sheet_1, sheet_2, sheet_3), joint, None, places_of(ids))
+            + sheet_pairs((extra_0, extra_1, extra_2, extra_3), None, small, places_of(ids))
             + block_pairs((block_0, block_1, block_2, block_3), tokens, cotangent),
             sems,
         )
     )
-    gain[...] = vector_of(small, 0)
-    shift[...] = vector_of(small, HEAD)
-    offset[...] = vector_of(small, 2 * HEAD, 3 * HEAD)
+    row = EXTRA // 2
+    gain[...] = vector_of(small, 0, row=row)
+    shift[...] = vector_of(small, HEAD, row=row)
+    offset[...] = vector_of(small, 2 * HEAD, 3 * HEAD, row)
     starts = [pl.multiple_of((part * 8 + x * 4 + p * 2 + c) * LANE, LANE) for part in range(3)]
     bias = jnp.concatenate([offset[:, pl.ds(at, LANE)] for at in starts], axis=1)
     total[...] = jnp.zeros_like(total)
@@ -725,8 +739,7 @@
     joint,
     up,
     totals,
-    small_one,
-    small_two,
+    small,
     gain_one,
     gain_two,
     own,
@@ -738,14 +751,14 @@
     finish(
         fetch(
             block_pairs((block_0, block_1, block_2, block_3), tokens, None)
-            + sheet_pairs((join_0, join_1, join_2, join_3), joint, small_one, places)
-            + sheet_pairs((sheet_0, sheet_1, sheet_2, sheet_3), up, small_two, places)
+            + sheet_pairs((join_0, join_1, join_2, join_3), joint, None, places)
+            + sheet_pairs((sheet_0, sheet_1, sheet_2, sheet_3), up, small, places)
             + [(block_0.at[1], own)],
             sems,
         )
     )
-    gain_one[...] = vector_of(small_one, 0)
-    gain_two[...] = vector_of(small_two, 0)
+    gain_one[...] = vector_of(small, 0, row=EXTRA // 2)
+    gain_two[...] = vector_of(small, 0)
     totals[...] = jnp.zeros_like(totals)
 
     def step(pair):
@@ -777,7 +790,6 @@
 def final_kernel(
     up_home,
     up_away,
-    down_sent,
     up_sent,
     joint_home,
     joint_away,
@@ -789,8 +801,9 @@
     down,
 ):
     rows = down.shape[0]
-    down[...] = low(total(up_home[:rows, :], up_away[:rows, :], down_sent[...]))
-    found = low(total(up_home[rows:, :], up_away[rows:, :], up_sent[...]))
+    found = low(total(up_home[...], up_away[...], up_sent[...]))
+    down[...] = found[:rows]
+    found = found[rows:]
     joint = low(total(joint_home[...], joint_away[:rows, :], joint_sent[...]))
     half, width = rows // 2, joint.shape[1] // 2
     hidden = found.shape[1] // 2
@@ -897,12 +910,12 @@
     first, up_own, joint_own, along_p = pin(
         jnp.concatenate([pair, along_x]),
         turned[:, :, 3 * LANE :],
-        turned[:, :, : 3 * LANE],
+        turned[:, :part, : 3 * LANE],
         along_p,
     )
     up_other, up_side = swap(up_own, "o"), swap(up_own, "q")
     grad_along_p, along_both = swap(pin(cotangent, along_p)[0], "p"), swap(along_p, "x")
-    first_came = swap(first, "c")
+    down_corner = swap(down_other, "q")
 
     devices = jnp.stack(
         [
@@ -923,12 +936,12 @@
     sine = jnp.sin(angles)
     sine = jnp.where(place < half_rot, -sine, jnp.where(place < ROT, sine, 0.0))
 
-    cosine, sine, position, up_other, up_side, grad_along_p, along_both, first_came, joint_own, down_other = pin(
-        cosine, sine, position, up_other, up_side, grad_along_p, along_both, first_came, joint_own, down_other
+    cosine, sine, position, up_other, up_side, grad_along_p, along_both, down_corner, joint_own, first = pin(
+        cosine, sine, position, up_other, up_side, grad_along_p, along_both, down_corner, joint_own, first
     )
 
     up_corner, joint_other = swap(up_other, "q"), swap(joint_own, "o")
-    grad_along_both, down_corner = swap(grad_along_p, "x"), swap(down_other, "q")
+    grad_along_both, first_came = swap(grad_along_p, "x"), swap(first, "c")
     turn_over = [
         (((a * 2 + b) * 2 + e) * 2 + f, ((b * 2 + a) * 2 + f) * 2 + e)
         for a in (0, 1)
@@ -937,8 +950,8 @@
         for f in (0, 1)
     ]
     cross = ("x", "o", "q", "c")
-    up_corner, down_corner, joint_other, grad_along_both, output_pair = pin(
-        up_corner, down_corner, joint_other, grad_along_both, join(output_weight, output_came, c)
+    up_corner, first_came, joint_other, grad_along_both, output_pair = pin(
+        up_corner, first_came, joint_other, grad_along_both, join(output_weight, output_came, c)
     )
     second = jnp.stack([along_p, grad_along_p, along_both, grad_along_both])
     second_came = swap(second, "c")
@@ -1005,7 +1018,7 @@
             pltpu.VMEM(tall, bf),
             pltpu.VMEM((rows, LANE), bf),
             pltpu.VMEM((8, 3 * LANE), f32),
-            pltpu.VMEM((16 * EXTRA, 3 * LANE), bf),
+            pltpu.VMEM((16 * EXTRA, hidden), bf),
             pltpu.VMEM((1, D), f32),
             pltpu.VMEM((1, D), f32),
             pltpu.VMEM((1, 3 * D), f32),
@@ -1015,12 +1028,13 @@
         ids,
         *blocks,
         *joint_sheets,
+        *up_sheets,
         output_pair,
         fed,
         cosine,
         sine,
         position,
-        memory="shhhhhhhhvvvvv",
+        memory="shhhhhhhhhhhhvvvvv",
     )
     up_away_1, up_away_0, *found = pin(up_away_1, up_away_0, *found)
     near_part, far_part, grad_joint, joint_home_0, joint_home_1, joint_away, output_grad, joint_sum = found
@@ -1029,8 +1043,7 @@
         at = slice(block * cap, (block + 1) * cap)
         return near[at] + wide(came[at])
 
-    up_sent = low(total(up_home_1, up_away_1))
-    down_sent = swap(up_sent[:unit], "o")
+    up_sent = swap(low(total(up_home_1, up_away_1)), "o")
     joint_away, up_away_0 = swap(joint_away, "q"), swap(up_away_0, "q")
     result_lane = near_part, swap(far_part, "c")
     result_sent, grad_joint = pin(
@@ -1046,7 +1059,6 @@
             pltpu.VMEM((D, 3 * LANE), bf),
             pltpu.VMEM((D, hidden), bf),
             pltpu.VMEM((4, 8, D), f32),
-            pltpu.VMEM((16 * EXTRA, 3 * LANE), bf),
             pltpu.VMEM((16 * EXTRA, hidden), bf),
             pltpu.VMEM((1, D), f32),
             pltpu.VMEM((1, D), f32),
@@ -1064,39 +1076,31 @@
         up_sum,
         memory="shhhhhhhhhhhhvvvv",
     )
-    down_sent, up_away_0, joint_away, result_came, output_part, *found = pin(
-        down_sent, up_away_0, joint_away, result_came, output_part, *found
+    up_sent, up_away_0, joint_away, result_came, output_part, *found = pin(
+        up_sent, up_away_0, joint_away, result_came, output_part, *found
     )
     near_part, far_part, sums = found
     came, sums_came = swap(far_part, "c"), swap(sums, "c")
     output_part = output_part.reshape(2, part, D)
-    result_kept = lane_sum(*result_lane, 0) + wide(result_came[:cap])
-
-    joint_sent, result_sent, output_sent, up_sent, came, sums_came = pin(
+
+    joint_sent, came, sums_came = pin(
         low(total(joint_home_1, joint_away[2 * part :])),
-        low(lane_sum(*result_lane, 2) + wide(result_came[cap:])),
-        take(output_part, 1 - c),
-        up_sent[unit:],
         came,
         sums_came,
     )
 
     lane = near_part, came
-    sums = sums + sums_came
-    top = low(sums)
-    rest = low(sums - wide(top))
-    sums, *sent = pin(
-        wide(top) + wide(rest),
-        *(jnp.concatenate([low(lane_sum(*lane, i)), top, rest]) for i in (1, 2, 3)),
-    )
+    sums, *sent = pin(sums + sums_came, *(low(lane_sum(*lane, i)) for i in (1, 2, 3)))
     side, far_side, corner = swap(sent[0], "x"), swap(sent[1], "p"), swap(sent[2], "x", "p")
-    joint_sent, up_sent = swap(joint_sent, "o"), swap(up_sent, "o")
-    side, far_side, corner, joint_sent, up_sent, output_sent = pin(
-        side, far_side, corner, joint_sent, up_sent, output_sent
-    )
-
-    def rest_of(values):
-        return wide(values[cap : cap + 16]) + wide(values[cap + 16 :])
+    joint_sent = swap(joint_sent, "o")
+    sums = sums + swap(sums, "x")
+    sums = sums + swap(sums, "q")
+    side, far_side, corner, joint_sent, output_part, result_came, sums = pin(
+        side, far_side, corner, joint_sent, output_part, result_came, sums
+    )
+    output_sent = take(output_part, 1 - c)
+    result_kept = lane_sum(*result_lane, 0) + wide(result_came[:cap])
+    result_sent = low(lane_sum(*result_lane, 2) + wide(result_came[cap:]))
 
     *final, down_final = call(
         final_kernel,
@@ -1105,17 +1109,15 @@
         1,
         up_home_0,
         up_away_0,
-        down_sent,
         up_sent,
         joint_home_0,
         joint_away,
         joint_sent,
-        memory="vvvvvvv",
-    )
-    sums = (sums + rest_of(side)) + (rest_of(far_side) + rest_of(corner))
+        memory="vvvvvv",
+    )
     *final, down_final, sums = pin(*final, down_final, sums)
     sent = swap(final[1], "c"), swap(final[2], "p"), swap(final[3], "p", "c")
-    down_came, sums_came, output_sent = swap(down_final, "x"), swap(sums, "o"), swap(output_sent, "c")
+    down_came, sums_came, output_sent = swap(down_final, "x"), swap(sums, "p"), swap(output_sent, "c")
     pulled = lane_sum(*lane, 0) + wide(side[:cap]) + wide(far_side[:cap]) + wide(corner[:cap])
     *sent, down_came, sums_came, output_sent = pin(*sent, down_came, sums_came, output_sent)
 
@@ -1125,11 +1127,9 @@
         low(total(take(output_part, c), output_sent)),
         result_sent,
     )
-    both_came, sums_came, output_came = swap(both, "x"), swap(sums, "q"), swap(output_own, "x")
+    both_came, output_came = swap(both, "x"), swap(output_own, "x")
     result_came = swap(result_sent, "p")
-    own_values = wide(tokens)
-    result = low(own_values + total(result_kept, result_came) + late_offset)
-    sums = sums + sums_came
+    sums = sums + swap(sums, "o")
     shard = ((o * 2 + p) * 2 + q) * 2 + c
 
     def own_part(values):
@@ -1149,6 +1149,7 @@
         memory="svv",
     )
 
+    own_values = wide(tokens)
     own_normed = norm_of(tokens)
     centre = own_values - jnp.mean(own_values, axis=-1, keepdims=True)
     factor = lax.rsqrt(jnp.mean(centre * centre, axis=-1, keepdims=True) + EPSILON)
@@ -1157,6 +1158,8 @@
         - jnp.mean(pulled, axis=-1, keepdims=True)
         - own_normed * jnp.mean(pulled * own_normed, axis=-1, keepdims=True)
     )
+    grad_tokens, result_came = pin(grad_tokens, result_came)
+    result = low(own_values + total(result_kept, result_came) + late_offset)
     norm_grads = [own_part(sums[i]) for i in range(5)]
     return (
         result,

time: 232 us -> 229 us (0.987)
  other arithmetic: 25 us -> 27.9 us
  starting transfers between devices: 53.3 us -> 50.4 us
  local copies, waits for them, and re-layouts: 14.8 us -> 12.2 us
    ppermute x39 -> x40, starting transfers between devices: 50.9 us -> 42.8 us  [swap(): return lax.ppermute(values, axes[0], PAIR)]
    ppermute x2, starting transfers between devices: 1.02 us -> 5.26 us  [swap(): return lax.ppermute(values, axes, [(i, 3 - i) for i in range(4)])]
    convert_element_type x5 -> x6, other arithmetic: 4.67 us -> 8.84 us  [low(): return values.astype(jnp.bfloat16)]
    ppermute x39 -> x40, waiting for transfers between devices: 79.6 us -> 77.5 us  [swap(): return lax.ppermute(values, axes[0], PAIR)]
  transfers between devices with their start and end apart: 43 -> 44, of which waited for: 17 -> 16; matrix products, arithmetic and copies ran while one was open for 12% -> 12% of each run, Pallas kernels for 22% -> 22%
where the time goes in v5:
time: 229 us
  waiting for transfers between devices  80.8 us (35%)
  Pallas kernels  55.9 us (24%)
  starting transfers between devices  50.4 us (22%)
  other arithmetic  27.9 us (12%)
  local copies, waits for them, and re-layouts  12.2 us (5%)
    ppermute x40, waiting for transfers between devices, swap(): return lax.ppermute(values, axes[0], PAIR)  77.5 us
    pallas_call x6, Pallas kernels, call(): pl.pallas_call(kernel, out_shape=tuple(outs), in_specs=[specs[kind] for k...  55.9 us
    ppermute x40, starting transfers between devices, swap(): return lax.ppermute(values, axes[0], PAIR)  42.8 us
    convert_element_type x6, other arithmetic, low(): return values.astype(jnp.bfloat16)  8.84 us
    ppermute x2, starting transfers between devices, swap(): return lax.ppermute(values, axes, [(i, 3 - i) for i in range(4)])  5.26 us
  transfers between devices with their start and end apart: 44, of which 16 were waited for; matrix products, arithmetic and copies ran while one was open for 12% of the time, Pallas kernels for 22%

profile of v5, /device:TPU:0, one launch (start us, length us, event | category | flops | bytes accessed | tf_op | source)
XLA Modules:
  0.0 228.5 jit_solution(4160095338197796481)
XLA Ops:
  0.8 1.2 pad_maximum_fusion.2
  2.0 3.0 %collective-permute-start.3 = (bf16[2,176,1024]{2,1,0:T(8,128)(2,1)S(1)}, bf16[2,176,1024]{2,1,0:T(8,128)(2,1)S(1)}, u32[]{:S(2)}, u32[]{:S(2)}) collective-permute-start(bf16[2,176,1024]{2,1,0:T(8,128)(2,1)S(1)} %pad_maximum_fusion.2), channel_id=1, source_target_pairs={{0,16},{16,0},{1,17},{17,1},{2,18},{18,2},{3,19},{19,3},{4,20},{20... | collective-permute-start | bytes 2162696 | tf_op jit(solution)/shard_map/ppermute | solution.py:298
  5.7 2.6 %collective-permute-start.1 = (bf16[128,1024]{1,0:T(8,128)(2,1)}, bf16[128,1024]{1,0:T(8,128)(2,1)}, u32[]{:S(2)}, u32[]{:S(2)}) collective-permute-start(bf16[128,1024]{1,0:T(8,128)(2,1)} %dynamic-slice_bitcast_fusion.tall_0), channel_id=1, source_target_pairs={{0,8},{8,0},{1,9},{9,1},{2,10},{10,2},{3,11},{11,3},{4,12},{12,4},... | collective-permute-start | bytes 786440 | tf_op jit(solution)/shard_map/ppermute | solution.py:298
  8.3 1.5 collective-permute-start.2
  11.2 2.1 shard_map.263
  13.3 1.6 collective-permute-start
  15.6 1.0 fusion.23
  16.6 3.8 %collective-permute-done.1.tall_2 = bf16[128,1024]{1,0:T(8,128)(2,1)} collective-permute-done((bf16[128,1024]{1,0:T(8,128)(2,1)}, bf16[128,1024]{1,0:T(8,128)(2,1)}, u32[]{:S(2)}, u32[]{:S(2)}) %collective-permute-start.1) | collective-permute-done | bytes 262176 | tf_op jit(solution)/shard_map/ppermute | solution.py:298
  20.4 6.1 %collective-permute-done = bf16[2,80,896]{2,1,0:T(8,128)(2,1)S(1)} collective-permute-done((bf16[2,80,896]{2,1,0:T(8,128)(2,1)}, bf16[2,80,896]{2,1,0:T(8,128)(2,1)S(1)}, u32[]{:S(2)}, u32[]{:S(2)}) %collective-permute-start) | collective-permute-done | bytes 286752 | tf_op jit(solution)/shard_map/ppermute | solution.py:298
  26.5 7.0 %collective-permute-done.4 = bf16[176,1024]{1,0:T(8,128)(2,1)S(1)} collective-permute-done((bf16[176,1024]{1,0:T(8,128)(2,1)S(1)}, bf16[176,1024]{1,0:T(8,128)(2,1)S(1)}, u32[]{:S(2)}, u32[]{:S(2)}) %collective-permute-start.4) | collective-permute-done | bytes 360480 | tf_op jit(solution)/shard_map/ppermute | solution.py:298
  33.5 0.7 copy-done.9
  34.3 0.8 pad_maximum_fusion.7
  36.5 1.3 pad_maximum_fusion.block_0
  37.9 1.1 copy-done.10
  40.0 1.5 collective-permute-start.8
  41.5 2.5 %collective-permute-start.9 = (bf16[176,1024]{1,0:T(8,128)(2,1)S(1)}, bf16[176,1024]{1,0:T(8,128)(2,1)}, u32[]{:S(2)}, u32[]{:S(2)}) collective-permute-start(bf16[176,1024]{1,0:T(8,128)(2,1)S(1)} %copy-done.2), channel_id=1, source_target_pairs={{0,4},{4,0},{1,5},{5,1},{2,6},{6,2},{3,7},{7,3},{8,12},{12,8},{9,1... | collective-permute-start | bytes 1081352 | tf_op jit(solution)/shard_map/ppermute | solution.py:298
  44.0 3.7 %fusion.11 = (f32[1408,128]{1,0:T(8,128)}, f32[1408,128]{1,0:T(8,128)}) fusion(f32[128]{0:T(128)S(1)} %mul.135, f32[1408]{0:T(1024)S(1)} %convert_element_type.113, pred[128]{0:T(512)(128)(4,1)S(1)} %get-tuple-element.287, pred[128]{0:T(512)(128)(4,1)S(1)} %get-tuple-element.288), kind=kLoop, calls=%fused_computation.19 | loop fusion | flops 901120 | bytes 1448192 | tf_op jit(solution)/shard_map/jit(_where)/select_n | solution.py:937
  47.7 9.2 %collective-permute-done.7.sheet_2.extra_2 = bf16[4,80,512]{2,1,0:T(8,128)(2,1)S(1)} collective-permute-done((bf16[4,80,512]{2,1,0:T(8,128)(2,1)S(1)}, bf16[4,80,512]{2,1,0:T(8,128)(2,1)S(1)}, u32[]{:S(2)}, u32[]{:S(2)}) %collective-permute-start.7) | collective-permute-done | bytes 327712 | tf_op jit(solution)/shard_map/ppermute | solution.py:298
  56.8 2.1 collective-permute-done.9
  59.0 0.7 copy-done.12
  59.7 1.1 broadcast_in_dim.75.position
  60.8 1.6 collective-permute-start.15
  63.1 0.9 broadcast_select_fusion.3
  64.1 9.6 %collective-permute-done.14.sheet_2.join_2 = bf16[4,64,384]{2,1,0:T(8,128)(2,1)S(1)} collective-permute-done((bf16[4,64,384]{2,1,0:T(8,128)(2,1)S(1)}, bf16[4,64,384]{2,1,0:T(8,128)(2,1)S(1)}, u32[]{:S(2)}, u32[]{:S(2)}) %collective-permute-start.14) | collective-permute-done | bytes 196640 | tf_op jit(solution)/shard_map/ppermute | solution.py:298
  73.7 1.6 pad_maximum_fusion.1.block_2
  75.4 3.1 %collective-permute-done.16.block_3 = bf16[4,176,1024]{2,1,0:T(8,128)(2,1)S(1)} collective-permute-done((bf16[4,176,1024]{2,1,0:T(8,128)(2,1)S(1)}, bf16[4,176,1024]{2,1,0:T(8,128)(2,1)S(1)}, u32[]{:S(2)}, u32[]{:S(2)}) %collective-permute-start.16) | collective-permute-done | bytes 1441824 | tf_op jit(solution)/shard_map/ppermute | solution.py:298
  78.6 1.5 collective-permute-start.17
  80.7 18.0 %shard_map.264 = (bf16[1408,1024]{1,0:T(8,128)(2,1)}, f32[1,1024]{1,0:T(1,128)}, bf16[1408,512]{1,0:T(8,128)(2,1)}, bf16[256,1024]{1,0:T(8,128)(2,1)}, bf16[256,...) custom-call(s32[5]{0:T(128)} %stack.107.ids, ...), custom_call_target="tpu_custom_call" | custom-call | flops 23000000512 | bytes 14555156 | tf_op jit(solution)/shard_map/pallas_call | solution.py:341
  98.8 0.8 slice_bitcast_fusion
  99.6 2.7 %collective-permute-start.19 = (bf16[256,1024]{1,0:T(8,128)(2,1)}, bf16[256,1024]{1,0:T(8,128)(2,1)S(1)}, u32[]{:S(2)}, u32[]{:S(2)}) collective-permute-start(bf16[256,1024]{1,0:T(8,128)(2,1)} %get-tuple-element.177), channel_id=1, source_target_pairs={{0,2},{2,0},{1,3},{3,1},{4,6},{6,4},{5,7},{7,5},{8,10},{10,8},{9,1... | collective-permute-start | bytes 1572872 | tf_op jit(solution)/shard_map/ppermute | solution.py:298
  102.3 20.6 %shard_map.265 = (f32[704,1024]{1,0:T(8,128)}, bf16[704,1024]{1,0:T(8,128)(2,1)}, bf16[1408,384]{1,0:T(8,128)(2,1)}, bf16[128,768]{1,0:T(8,128)(2,1)}, bf16[128,...) custom-call(s32[5]{0:T(128)} %stack.107.ids, ...), custom_call_target="tpu_custom_call" | custom-call | flops 25300000768 | bytes 19629588 | tf_op jit(solution)/shard_map/pallas_call | solution.py:341
  123.2 2.4 %collective-permute-start.21 = (bf16[256,1024]{1,0:T(8,128)(2,1)S(1)}, bf16[256,1024]{1,0:T(8,128)(2,1)}, u32[]{:S(2)}, u32[]{:S(2)}) collective-permute-start(bf16[256,1024]{1,0:T(8,128)(2,1)S(1)} %add_convert_fusion), channel_id=1, source_target_pairs={{0,8},{8,0},{1,9},{9,1},{2,10},{10,2},{3,11},{11,3},{4,12},{12,4},... | collective-permute-start | bytes 1572872 | tf_op jit(solution)/shard_map/ppermute | solution.py:298
  125.6 1.5 collective-permute-start.22
  127.6 1.6 collective-permute-start.25
  129.2 1.5 add_convert_fusion.6
  130.9 2.4 %collective-permute-start.24 = (bf16[352,1024]{1,0:T(8,128)(2,1)S(1)}, bf16[352,1024]{1,0:T(8,128)(2,1)S(1)}, u32[]{:S(2)}, u32[]{:S(2)}) collective-permute-start(bf16[352,1024]{1,0:T(8,128)(2,1)S(1)} %pad_maximum_fusion.3), channel_id=1, source_target_pairs={{0,16},{16,0},{1,17},{17,1},{2,18},{18,2},{3,19},{19,3},{4,20},{20... | collective-permute-start | bytes 2162696 | tf_op jit(solution)/shard_map/ppermute | solution.py:298
  133.3 10.1 %shard_map.266 = (f32[704,1024]{1,0:T(8,128)}, bf16[704,1024]{1,0:T(8,128)(2,1)}, f32[16,1024]{1,0:T(8,128)}) custom-call(s32[5]{0:T(128)} %stack.107.ids, bf16[4,176,1024]{2,1,0:T(8,128)(2,1)} %copy-done.3, bf16[4,176,1024]{2,1,0:T(8,128)(2,1)} %collective-permute-done.13.block_1, bf16[4,176,1024]{2,1,0:T(8,128)(2,1)} %copy-done.5, ...), custom_call_target="tpu_custom_call" | custom-call | flops 12650000384 | bytes 14781972 | tf_op jit(solution)/shard_map/pallas_call | solution.py:341
  143.4 5.0 %collective-permute-done.23.joint_away = bf16[256,768]{1,0:T(8,128)(2,1)} collective-permute-done((bf16[256,768]{1,0:T(8,128)(2,1)}, bf16[256,768]{1,0:T(8,128)(2,1)}, u32[]{:S(2)}, u32[]{:S(2)}) %collective-permute-start.23) | collective-permute-done | bytes 393248 | tf_op jit(solution)/shard_map/ppermute | solution.py:298
  148.4 6.4 %collective-permute-done.21.up_sent = bf16[256,1024]{1,0:T(8,128)(2,1)} collective-permute-done((bf16[256,1024]{1,0:T(8,128)(2,1)S(1)}, bf16[256,1024]{1,0:T(8,128)(2,1)}, u32[]{:S(2)}, u32[]{:S(2)}) %collective-permute-start.21) | collective-permute-done | bytes 524320 | tf_op jit(solution)/shard_map/ppermute | solution.py:298
  155.5 1.6 add_convert_fusion.7
  157.2 1.2 collective-permute-done.27
  158.3 0.9 add.231
  159.2 2.7 %add_convert_fusion.2 = (bf16[176,1024]{1,0:T(8,128)(2,1)}, bf16[176,1024]{1,0:T(8,128)(2,1)}, bf16[176,1024]{1,0:T(8,128)(2,1)}) fusion(f32[704,1024]{1,0:T(8,128)} %get-tuple-element.214, bf16[704,1024]{1,0:T(8,128)(2,1)S(1)} %collective-permute-done.26), kind=kLoop, calls=%fused_computation.27 | loop fusion | flops 1622016 | bytes 4325376 | tf_op jit(solution)/shard_map/convert_element_type | solution.py:318
  162.0 7.0 %collective-permute-start.32 = (f32[16,1024]{1,0:T(8,128)S(1)}, f32[16,1024]{1,0:T(8,128)S(1)}, u32[]{:S(2)}, u32[]{:S(2)}) collective-permute-start(f32[16,1024]{1,0:T(8,128)S(1)} %add.231), channel_id=1, source_target_pairs={{0,16},{16,0},{1,17},{17,1},{2,18},{18,2},{3,19},{19,3},{4,20},{20... | collective-permute-start | bytes 196616 | tf_op jit(solution)/shard_map/ppermute | solution.py:298
  169.1 3.4 %collective-permute-start.30 = (bf16[176,1024]{1,0:T(8,128)(2,1)}, bf16[176,1024]{1,0:T(8,128)(2,1)}, u32[]{:S(2)}, u32[]{:S(2)}) collective-permute-start(bf16[176,1024]{1,0:T(8,128)(2,1)} %get-tuple-element.218), channel_id=1, source_target_pairs={{0,20},{4,16},{16,4},{20,0},{1,21},{5,17},{17,5},{21,1},{2,22},{6,... | collective-permute-start | bytes 1081352 | tf_op jit(solution)/shard_map/ppermute | solution.py:299
  172.8 1.5 collective-permute-start.33
  174.3 2.8 %collective-permute-done.33 = f32[16,1024]{1,0:T(8,128)S(1)} collective-permute-done((f32[16,1024]{1,0:T(8,128)S(1)}, f32[16,1024]{1,0:T(8,128)S(1)}, u32[]{:S(2)}, u32[]{:S(2)}) %collective-permute-start.33) | collective-permute-done | bytes 65568 | tf_op jit(solution)/shard_map/ppermute | solution.py:298
  177.2 12.1 %collective-permute-done.31.joint_sent = bf16[128,768]{1,0:T(8,128)(2,1)} collective-permute-done((bf16[128,768]{1,0:T(8,128)(2,1)}, bf16[128,768]{1,0:T(8,128)(2,1)}, u32[]{:S(2)}, u32[]{:S(2)}) %collective-permute-start.31) | collective-permute-done | bytes 196640 | tf_op jit(solution)/shard_map/ppermute | solution.py:298
  189.3 3.3 %collective-permute-done.30 = bf16[176,1024]{1,0:T(8,128)(2,1)} collective-permute-done((bf16[176,1024]{1,0:T(8,128)(2,1)}, bf16[176,1024]{1,0:T(8,128)(2,1)}, u32[]{:S(2)}, u32[]{:S(2)}) %collective-permute-start.30) | collective-permute-done | bytes 360480 | tf_op jit(solution)/shard_map/ppermute | solution.py:299
  192.6 2.5 %shard_map.267 = (bf16[64,896]{1,0:T(8,128)(2,1)}, bf16[64,896]{1,0:T(8,128)(2,1)}, bf16[64,896]{1,0:T(8,128)(2,1)}, bf16[64,896]{1,0:T(8,128)(2,1)}, bf16[128,1024]{1,0:T(8,128)(2,1)}) custom-call(bf16[256,1024]{1,0:T(8,128)(2,1)} %get-tuple-element.227.up_home, bf16[256,1024]{1,0:T(8,128)(2,1)} %collective-permute-done.22.up_away, ...), custom_call_target="tpu_custom_call" | custom-call | flops 1150000000 | bytes 3080192 | tf_op jit(solution)/shard_map/pallas_call | solution.py:341
  195.5 1.9 collective-permute-start.36
  197.7 2.0 fusion.22
  199.7 1.2 fusion.9
  200.9 4.3 %collective-permute-done.38 = f32[16,1024]{1,0:T(8,128)S(1)} collective-permute-done((f32[16,1024]{1,0:T(8,128)S(1)}, f32[16,1024]{1,0:T(8,128)S(1)}, u32[]{:S(2)}, u32[]{:S(2)}) %collective-permute-start.38) | collective-permute-done | bytes 65568 | tf_op jit(solution)/shard_map/ppermute | solution.py:298
  205.1 2.0 add_convert_fusion.1
  207.2 0.8 pad_maximum_fusion.5
  208.1 1.7 collective-permute-start.43
  210.1 1.4 collective-permute-start.41
  211.5 1.3 collective-permute-start.40
  212.9 1.1 maximum_convert_fusion
  214.0 2.2 collective-permute-done.41
  220.6 2.5 %collective-permute-done.40 = bf16[176,1024]{1,0:T(8,128)(2,1)} collective-permute-done((bf16[176,1024]{1,0:T(8,128)(2,1)}, bf16[176,1024]{1,0:T(8,128)(2,1)}, u32[]{:S(2)}, u32[]{:S(2)}) %collective-permute-start.40) | collective-permute-done | bytes 360480 | tf_op jit(solution)/shard_map/ppermute | solution.py:298
  223.2 2.2 fusion.14
  225.4 2.6 %shard_map.268 = (f32[64,3072]{1,0:T(8,128)}, f32[64,4096]{1,0:T(8,128)}) custom-call(s32[5]{0:T(128)} %stack.107.ids, bf16[2,2,64,896]{3,2,1,0:T(8,128)(2,1)} %bitcast.31.own, bf16[2,2,64,896]{3,2,1,0:T(8,128)(2,1)} %collective-permute-done.42.other), custom_call_target="tpu_custom_call" | custom-call | flops 1150000000 | bytes 2752532 | tf_op jit(solution)/shard_map/pallas_call | solution.py:341
  (178 shorter events, 15.1 us)
Async XLA Ops:
  0.7 9.2 %copy-start.24 = (bf16[64]{0:T(256)(128)(2,1)S(1)}, bf16[64]{0:T(256)(128)(2,1)}, u32[]{:S(2)}) copy-start(bf16[64]{0:T(256)(128)(2,1)} %param.20) | copy-start | bytes 388
  0.7 9.2 %copy-start.25 = (bf16[64]{0:T(256)(128)(2,1)S(1)}, bf16[64]{0:T(256)(128)(2,1)}, u32[]{:S(2)}) copy-start(bf16[64]{0:T(256)(128)(2,1)} %param.21) | copy-start | bytes 388
  0.7 9.2 %copy-start.26 = (bf16[192]{0:T(256)(128)(2,1)S(1)}, bf16[192]{0:T(256)(128)(2,1)}, u32[]{:S(2)}) copy-start(bf16[192]{0:T(256)(128)(2,1)} %param.23) | copy-start | bytes 1156
  0.7 9.2 %copy-start.30 = (bf16[64]{0:T(256)(128)(2,1)S(1)}, bf16[64]{0:T(256)(128)(2,1)}, u32[]{:S(2)}) copy-start(bf16[64]{0:T(256)(128)(2,1)} %param.25) | copy-start | bytes 388
  0.7 14.2 %copy-start.1 = (bf16[176,1024]{1,0:T(8,128)(2,1)S(1)}, bf16[176,1024]{1,0:T(8,128)(2,1)}, u32[]{:S(2)}) copy-start(bf16[176,1024]{1,0:T(8,128)(2,1)} %param.16) | copy-start | bytes 1081348
  2.0 32.2 %collective-permute-start.3 = (bf16[2,176,1024]{2,1,0:T(8,128)(2,1)S(1)}, bf16[2,176,1024]{2,1,0:T(8,128)(2,1)S(1)}, u32[]{:S(2)}, u32[]{:S(2)}) collective-permute-start(bf16[2,176,1024]{2,1,0:T(8,128)(2,1)S(1)} %pad_maximum_fusion.2), channel_id=1, source_target_pairs={{0,16},{16,0},{1,17},{17,1},{2,18},{18,2},{3,19},{19,3},{4,20},{20... | collective-permute-start | bytes 2162696 | tf_op jit(solution)/shard_map/ppermute | solution.py:298
  5.7 29.4 %copy-start.22 = (s32[64]{0:T(128)S(1)}, s32[64]{0:T(128)}, u32[]{:S(2)}) copy-start(s32[64]{0:T(128)} %param.18) | copy-start | bytes 772
  5.7 29.4 %copy-start.23 = (s32[64]{0:T(128)S(1)}, s32[64]{0:T(128)}, u32[]{:S(2)}) copy-start(s32[64]{0:T(128)} %param.19) | copy-start | bytes 772
  5.7 30.7 %copy-start.2 = (bf16[176,1024]{1,0:T(8,128)(2,1)S(1)}, bf16[176,1024]{1,0:T(8,128)(2,1)}, u32[]{:S(2)}) copy-start(bf16[176,1024]{1,0:T(8,128)(2,1)} %param.17) | copy-start | bytes 1081348
  5.7 14.7 %collective-permute-start.1 = (bf16[128,1024]{1,0:T(8,128)(2,1)}, bf16[128,1024]{1,0:T(8,128)(2,1)}, u32[]{:S(2)}, u32[]{:S(2)}) collective-permute-start(bf16[128,1024]{1,0:T(8,128)(2,1)} %dynamic-slice_bitcast_fusion.tall_0), channel_id=1, source_target_pairs={{0,8},{8,0},{1,9},{9,1},{2,10},{10,2},{3,11},{11,3},{4,12},{12,4},... | collective-permute-start | bytes 786440 | tf_op jit(solution)/shard_map/ppermute | solution.py:298
  8.3 12.1 %collective-permute-start.2 = (bf16[128,1024]{1,0:T(8,128)(2,1)}, bf16[128,1024]{1,0:T(8,128)(2,1)}, u32[]{:S(2)}, u32[]{:S(2)}) collective-permute-start(bf16[128,1024]{1,0:T(8,128)(2,1)} %dynamic-slice_bitcast_fusion.tall_0), channel_id=1, source_target_pairs={{0,2},{2,0},{1,3},{3,1},{4,6},{6,4},{5,7},{7,5},{8,10},{10,8},{9,1... | collective-permute-start | bytes 786440 | tf_op jit(solution)/shard_map/ppermute | solution.py:298
  13.3 13.2 %collective-permute-start = (bf16[2,80,896]{2,1,0:T(8,128)(2,1)}, bf16[2,80,896]{2,1,0:T(8,128)(2,1)S(1)}, u32[]{:S(2)}, u32[]{:S(2)}) collective-permute-start(bf16[2,80,896]{2,1,0:T(8,128)(2,1)} %get-tuple-element.137), channel_id=1, source_target_pairs={{0,4},{4,0},{1,5},{5,1},{2,6},{6,2},{3,7},{7,3},{8,12},{12,8},{9,1... | collective-permute-start | bytes 860168 | tf_op jit(solution)/shard_map/ppermute | solution.py:298
  14.9 18.6 %collective-permute-start.4 = (bf16[176,1024]{1,0:T(8,128)(2,1)S(1)}, bf16[176,1024]{1,0:T(8,128)(2,1)S(1)}, u32[]{:S(2)}, u32[]{:S(2)}) collective-permute-start(bf16[176,1024]{1,0:T(8,128)(2,1)S(1)} %copy-done.1), channel_id=1, source_target_pairs={{0,4},{4,0},{1,5},{5,1},{2,6},{6,2},{3,7},{7,3},{8,12},{12,8},{9,1... | collective-permute-start | bytes 1081352 | tf_op jit(solution)/shard_map/ppermute | solution.py:298
  20.4 17.3 %collective-permute-start.6 = (bf16[64,1024]{1,0:T(8,128)(2,1)}, bf16[64,1024]{1,0:T(8,128)(2,1)}, u32[]{:S(2)}, u32[]{:S(2)}) collective-permute-start(bf16[64,1024]{1,0:T(8,128)(2,1)} %param.24), channel_id=1, source_target_pairs={{0,1},{1,0},{2,3},{3,2},{4,5},{5,4},{6,7},{7,6},{8,9},{9,8},{10,11... | collective-permute-start | bytes 393224 | tf_op jit(solution)/shard_map/ppermute | solution.py:298
  35.1 2.7 %collective-permute-start.5 = (bf16[2,80,896]{2,1,0:T(8,128)(2,1)}, bf16[2,80,896]{2,1,0:T(8,128)(2,1)S(1)}, u32[]{:S(2)}, u32[]{:S(2)}) collective-permute-start(bf16[2,80,896]{2,1,0:T(8,128)(2,1)} %pad_maximum_fusion.7), channel_id=1, source_target_pairs={{0,1},{1,0},{2,3},{3,2},{4,5},{5,4},{6,7},{7,6},{8,9},{9,8},{10,11... | collective-permute-start | bytes 860168 | tf_op jit(solution)/shard_map/ppermute | solution.py:298
  35.9 11.8 %collective-permute-start.11 = (bf16[128,1024]{1,0:T(8,128)(2,1)}, bf16[128,1024]{1,0:T(8,128)(2,1)S(1)}, u32[]{:S(2)}, u32[]{:S(2)}) collective-permute-start(bf16[128,1024]{1,0:T(8,128)(2,1)} %collective-permute-done.1.tall_2), channel_id=1, source_target_pairs={{0,2},{2,0},{1,3},{3,1},{4,6},{6,4},{5,7},{7,5},{8,10},{10,8},{9,1... | collective-permute-start | bytes 786440 | tf_op jit(solution)/shard_map/ppermute | solution.py:298
  37.7 23.1 %copy-start.3 = (bf16[4,176,1024]{2,1,0:T(8,128)(2,1)}, bf16[4,176,1024]{2,1,0:T(8,128)(2,1)S(1)}, u32[]{:S(2)}) copy-start(bf16[4,176,1024]{2,1,0:T(8,128)(2,1)S(1)} %pad_maximum_fusion.block_0) | copy-start | bytes 4325380
  37.8 37.6 %copy-start.6 = (bf16[4,64,384]{2,1,0:T(8,128)(2,1)}, bf16[4,64,384]{2,1,0:T(8,128)(2,1)S(1)}, u32[]{:S(2)}) copy-start(bf16[4,64,384]{2,1,0:T(8,128)(2,1)S(1)} %pad_maximum_fusion.9.sheet_0.join_0) | copy-start | bytes 589828
  37.9 25.2 %copy-start.19 = (bf16[64,1024]{1,0:T(8,128)(2,1)S(1)}, bf16[64,1024]{1,0:T(8,128)(2,1)}, u32[]{:S(2)}) copy-start(bf16[64,1024]{1,0:T(8,128)(2,1)} %param.24) | copy-start | bytes 393220
  39.0 21.9 %copy-start.13 = (bf16[4,80,512]{2,1,0:T(8,128)(2,1)}, bf16[4,80,512]{2,1,0:T(8,128)(2,1)S(1)}, u32[]{:S(2)}) copy-start(bf16[4,80,512]{2,1,0:T(8,128)(2,1)S(1)} %slice.136.sheet_0.extra_0) | copy-start | bytes 983044
  39.0 20.0 %collective-permute-start.10 = (bf16[176,1024]{1,0:T(8,128)(2,1)S(1)}, bf16[176,1024]{1,0:T(8,128)(2,1)S(1)}, u32[]{:S(2)}, u32[]{:S(2)}) collective-permute-start(bf16[176,1024]{1,0:T(8,128)(2,1)S(1)} %copy-done.10), channel_id=1, source_target_pairs={{0,16},{16,0},{1,17},{17,1},{2,18},{18,2},{3,19},{19,3},{4,20},{20... | collective-permute-start | bytes 1081352 | tf_op jit(solution)/shard_map/ppermute | solution.py:298
  39.5 17.3 %collective-permute-start.7 = (bf16[4,80,512]{2,1,0:T(8,128)(2,1)S(1)}, bf16[4,80,512]{2,1,0:T(8,128)(2,1)S(1)}, u32[]{:S(2)}, u32[]{:S(2)}) collective-permute-start(bf16[4,80,512]{2,1,0:T(8,128)(2,1)S(1)} %slice.136.sheet_0.extra_0), channel_id=1, source_target_pairs={{0,8},{8,0},{1,9},{9,1},{2,10},{10,2},{3,11},{11,3},{4,12},{12,4},... | collective-permute-start | bytes 983048 | tf_op jit(solution)/shard_map/ppermute | solution.py:298
  40.0 16.9 %collective-permute-start.8 = (bf16[4,80,512]{2,1,0:T(8,128)(2,1)S(1)}, bf16[4,80,512]{2,1,0:T(8,128)(2,1)S(1)}, u32[]{:S(2)}, u32[]{:S(2)}) collective-permute-start(bf16[4,80,512]{2,1,0:T(8,128)(2,1)S(1)} %slice.136.sheet_0.extra_0), channel_id=1, source_target_pairs={{0,2},{2,0},{1,3},{3,1},{4,6},{6,4},{5,7},{7,5},{8,10},{10,8},{9,1... | collective-permute-start | bytes 983048 | tf_op jit(solution)/shard_map/ppermute | solution.py:298
  41.5 17.5 %collective-permute-start.9 = (bf16[176,1024]{1,0:T(8,128)(2,1)S(1)}, bf16[176,1024]{1,0:T(8,128)(2,1)}, u32[]{:S(2)}, u32[]{:S(2)}) collective-permute-start(bf16[176,1024]{1,0:T(8,128)(2,1)S(1)} %copy-done.2), channel_id=1, source_target_pairs={{0,4},{4,0},{1,5},{5,1},{2,6},{6,2},{3,7},{7,3},{8,12},{12,8},{9,1... | collective-permute-start | bytes 1081352 | tf_op jit(solution)/shard_map/ppermute | solution.py:298
  44.0 29.7 %copy-start.11 = (bf16[176,1024]{1,0:T(8,128)(2,1)S(1)}, bf16[176,1024]{1,0:T(8,128)(2,1)}, u32[]{:S(2)}) copy-start(bf16[176,1024]{1,0:T(8,128)(2,1)} %copy-done.9) | copy-start | bytes 1081348
  47.7 13.2 %copy-start.36 = (bf16[128,1024]{1,0:T(8,128)(2,1)}, bf16[128,1024]{1,0:T(8,128)(2,1)S(1)}, u32[]{:S(2)}) copy-start(bf16[128,1024]{1,0:T(8,128)(2,1)S(1)} %collective-permute-done.11.tall_3) | copy-start | bytes 786436
  60.8 12.9 %collective-permute-start.13 = (bf16[4,176,1024]{2,1,0:T(8,128)(2,1)S(1)}, bf16[4,176,1024]{2,1,0:T(8,128)(2,1)}, u32[]{:S(2)}, u32[]{:S(2)}) collective-permute-start(bf16[4,176,1024]{2,1,0:T(8,128)(2,1)S(1)} %pad_maximum_fusion.block_0), channel_id=1, source_target_pairs={{0,1},{1,0},{2,3},{3,2},{4,5},{5,4},{6,7},{7,6},{8,9},{9,8},{10,11... | collective-permute-start | bytes 4325384 | tf_op jit(solution)/shard_map/ppermute | solution.py:298
  60.8 12.8 %collective-permute-start.15 = (bf16[176,1024]{1,0:T(8,128)(2,1)}, bf16[176,1024]{1,0:T(8,128)(2,1)}, u32[]{:S(2)}, u32[]{:S(2)}) collective-permute-start(bf16[176,1024]{1,0:T(8,128)(2,1)} %collective-permute-done.9), channel_id=1, source_target_pairs={{0,16},{16,0},{1,17},{17,1},{2,18},{18,2},{3,19},{19,3},{4,20},{20... | collective-permute-start | bytes 1081352 | tf_op jit(solution)/shard_map/ppermute | solution.py:298
  62.4 11.3 %collective-permute-start.12 = (bf16[4,80,512]{2,1,0:T(8,128)(2,1)}, bf16[4,80,512]{2,1,0:T(8,128)(2,1)S(1)}, u32[]{:S(2)}, u32[]{:S(2)}) collective-permute-start(bf16[4,80,512]{2,1,0:T(8,128)(2,1)} %copy-done.33), channel_id=1, source_target_pairs={{0,2},{2,0},{1,3},{3,1},{4,6},{6,4},{5,7},{7,5},{8,10},{10,8},{9,1... | collective-permute-start | bytes 983048 | tf_op jit(solution)/shard_map/ppermute | solution.py:298
  63.0 10.7 %collective-permute-start.14 = (bf16[4,64,384]{2,1,0:T(8,128)(2,1)S(1)}, bf16[4,64,384]{2,1,0:T(8,128)(2,1)S(1)}, u32[]{:S(2)}, u32[]{:S(2)}) collective-permute-start(bf16[4,64,384]{2,1,0:T(8,128)(2,1)S(1)} %pad_maximum_fusion.9.sheet_0.join_0), channel_id=1, source_target_pairs={{0,8},{8,0},{1,9},{9,1},{2,10},{10,2},{3,11},{11,3},{4,12},{12,4},... | collective-permute-start | bytes 589832 | tf_op jit(solution)/shard_map/ppermute | solution.py:298
  75.3 3.3 %collective-permute-start.16 = (bf16[4,176,1024]{2,1,0:T(8,128)(2,1)S(1)}, bf16[4,176,1024]{2,1,0:T(8,128)(2,1)S(1)}, u32[]{:S(2)}, u32[]{:S(2)}) collective-permute-start(bf16[4,176,1024]{2,1,0:T(8,128)(2,1)S(1)} %pad_maximum_fusion.1.block_2), channel_id=1, source_target_pairs={{0,1},{1,0},{2,3},{3,2},{4,5},{5,4},{6,7},{7,6},{8,9},{9,8},{10,11... | collective-permute-start | bytes 4325384 | tf_op jit(solution)/shard_map/ppermute | solution.py:298
  78.6 20.2 %collective-permute-start.17 = (bf16[2,4,64,384]{3,2,1,0:T(8,128)(2,1)S(1)}, bf16[2,4,64,384]{3,2,1,0:T(8,128)(2,1)S(1)}, u32[]{:S(2)}, u32[]{:S(2)}) collective-permute-start(bf16[2,4,64,384]{3,2,1,0:T(8,128)(2,1)S(1)} %pad_maximum_fusion.6), channel_id=1, source_target_pairs={{0,2},{2,0},{1,3},{3,1},{4,6},{6,4},{5,7},{7,5},{8,10},{10,8},{9,1... | collective-permute-start | bytes 1179656 | tf_op jit(solution)/shard_map/ppermute | solution.py:298
  80.0 18.7 %collective-permute-start.18 = (bf16[128,1024]{1,0:T(8,128)(2,1)S(1)}, bf16[128,1024]{1,0:T(8,128)(2,1)S(1)}, u32[]{:S(2)}, u32[]{:S(2)}) collective-permute-start(bf16[128,1024]{1,0:T(8,128)(2,1)S(1)} %pad_maximum_fusion.8), channel_id=1, source_target_pairs={{0,0},{1,2},{2,1},{3,3},{8,16},{9,18},{10,17},{11,19},{16,8},{17,1... | collective-permute-start | bytes 786440 | tf_op jit(solution)/shard_map/ppermute | solution.py:965
  99.6 23.3 %collective-permute-start.19 = (bf16[256,1024]{1,0:T(8,128)(2,1)}, bf16[256,1024]{1,0:T(8,128)(2,1)S(1)}, u32[]{:S(2)}, u32[]{:S(2)}) collective-permute-start(bf16[256,1024]{1,0:T(8,128)(2,1)} %get-tuple-element.177), channel_id=1, source_target_pairs={{0,2},{2,0},{1,3},{3,1},{4,6},{6,4},{5,7},{7,5},{8,10},{10,8},{9,1... | collective-permute-start | bytes 1572872 | tf_op jit(solution)/shard_map/ppermute | solution.py:298
  102.3 20.7 %copy-start.8 = (bf16[256,1024]{1,0:T(8,128)(2,1)S(1)}, bf16[256,1024]{1,0:T(8,128)(2,1)}, u32[]{:S(2)}) copy-start(bf16[256,1024]{1,0:T(8,128)(2,1)} %get-tuple-element.195) | copy-start | bytes 1572868
  122.9 6.3 %collective-permute-start.20 = (bf16[704,1024]{1,0:T(8,128)(2,1)}, bf16[704,1024]{1,0:T(8,128)(2,1)S(1)}, u32[]{:S(2)}, u32[]{:S(2)}) collective-permute-start(bf16[704,1024]{1,0:T(8,128)(2,1)} %get-tuple-element.194), channel_id=1, source_target_pairs={{0,1},{1,0},{2,3},{3,2},{4,5},{5,4},{6,7},{7,6},{8,9},{9,8},{10,11... | collective-permute-start | bytes 4325384 | tf_op jit(solution)/shard_map/ppermute | solution.py:298
  123.2 31.6 %collective-permute-start.21 = (bf16[256,1024]{1,0:T(8,128)(2,1)S(1)}, bf16[256,1024]{1,0:T(8,128)(2,1)}, u32[]{:S(2)}, u32[]{:S(2)}) collective-permute-start(bf16[256,1024]{1,0:T(8,128)(2,1)S(1)} %add_convert_fusion), channel_id=1, source_target_pairs={{0,8},{8,0},{1,9},{9,1},{2,10},{10,2},{3,11},{11,3},{4,12},{12,4},... | collective-permute-start | bytes 1572872 | tf_op jit(solution)/shard_map/ppermute | solution.py:298
  125.6 29.2 %collective-permute-start.22 = (bf16[256,1024]{1,0:T(8,128)(2,1)}, bf16[256,1024]{1,0:T(8,128)(2,1)}, u32[]{:S(2)}, u32[]{:S(2)}) collective-permute-start(bf16[256,1024]{1,0:T(8,128)(2,1)} %get-tuple-element.197), channel_id=1, source_target_pairs={{0,2},{2,0},{1,3},{3,1},{4,6},{6,4},{5,7},{7,5},{8,10},{10,8},{9,1... | collective-permute-start | bytes 1572872 | tf_op jit(solution)/shard_map/ppermute | solution.py:298
  127.1 21.3 %collective-permute-start.23 = (bf16[256,768]{1,0:T(8,128)(2,1)}, bf16[256,768]{1,0:T(8,128)(2,1)}, u32[]{:S(2)}, u32[]{:S(2)}) collective-permute-start(bf16[256,768]{1,0:T(8,128)(2,1)} %get-tuple-element.198), channel_id=1, source_target_pairs={{0,2},{2,0},{1,3},{3,1},{4,6},{6,4},{5,7},{7,5},{8,10},{10,8},{9,1... | collective-permute-start | bytes 1179656 | tf_op jit(solution)/shard_map/ppermute | solution.py:298
  127.6 15.7 %collective-permute-start.25 = (bf16[128,1024]{1,0:T(8,128)(2,1)}, bf16[128,1024]{1,0:T(8,128)(2,1)S(1)}, u32[]{:S(2)}, u32[]{:S(2)}) collective-permute-start(bf16[128,1024]{1,0:T(8,128)(2,1)} %get-tuple-element.201), channel_id=1, source_target_pairs={{0,0},{1,2},{2,1},{3,3},{8,16},{9,18},{10,17},{11,19},{16,8},{17,1... | collective-permute-start | bytes 786440 | tf_op jit(solution)/shard_map/ppermute | solution.py:1053
  130.8 24.7 %copy-start.18 = (bf16[128,768]{1,0:T(8,128)(2,1)S(1)}, bf16[128,768]{1,0:T(8,128)(2,1)}, u32[]{:S(2)}) copy-start(bf16[128,768]{1,0:T(8,128)(2,1)} %get-tuple-element.210) | copy-start | bytes 589828
  130.9 24.0 %collective-permute-start.24 = (bf16[352,1024]{1,0:T(8,128)(2,1)S(1)}, bf16[352,1024]{1,0:T(8,128)(2,1)S(1)}, u32[]{:S(2)}, u32[]{:S(2)}) collective-permute-start(bf16[352,1024]{1,0:T(8,128)(2,1)S(1)} %pad_maximum_fusion.3), channel_id=1, source_target_pairs={{0,16},{16,0},{1,17},{17,1},{2,18},{18,2},{3,19},{19,3},{4,20},{20... | collective-permute-start | bytes 2162696 | tf_op jit(solution)/shard_map/ppermute | solution.py:298
  143.3 18.6 %copy-start.14 = (bf16[128,1024]{1,0:T(8,128)(2,1)}, bf16[128,1024]{1,0:T(8,128)(2,1)S(1)}, u32[]{:S(2)}) copy-start(bf16[128,1024]{1,0:T(8,128)(2,1)S(1)} %collective-permute-done.25) | copy-start | bytes 786436
  154.8 3.5 %collective-permute-start.26 = (bf16[704,1024]{1,0:T(8,128)(2,1)}, bf16[704,1024]{1,0:T(8,128)(2,1)S(1)}, u32[]{:S(2)}, u32[]{:S(2)}) collective-permute-start(bf16[704,1024]{1,0:T(8,128)(2,1)} %get-tuple-element.212), channel_id=1, source_target_pairs={{0,1},{1,0},{2,3},{3,2},{4,5},{5,4},{6,7},{7,6},{8,9},{9,8},{10,11... | collective-permute-start | bytes 4325384 | tf_op jit(solution)/shard_map/ppermute | solution.py:298
  155.0 3.4 %collective-permute-start.27 = (f32[16,1024]{1,0:T(8,128)}, f32[16,1024]{1,0:T(8,128)S(1)}, u32[]{:S(2)}, u32[]{:S(2)}) collective-permute-start(f32[16,1024]{1,0:T(8,128)} %get-tuple-element.209), channel_id=1, source_target_pairs={{0,1},{1,0},{2,3},{3,2},{4,5},{5,4},{6,7},{7,6},{8,9},{9,8},{10,11... | collective-permute-start | bytes 196616 | tf_op jit(solution)/shard_map/ppermute | solution.py:298
  162.0 10.8 %collective-permute-start.32 = (f32[16,1024]{1,0:T(8,128)S(1)}, f32[16,1024]{1,0:T(8,128)S(1)}, u32[]{:S(2)}, u32[]{:S(2)}) collective-permute-start(f32[16,1024]{1,0:T(8,128)S(1)} %add.231), channel_id=1, source_target_pairs={{0,16},{16,0},{1,17},{17,1},{2,18},{18,2},{3,19},{19,3},{4,20},{20... | collective-permute-start | bytes 196616 | tf_op jit(solution)/shard_map/ppermute | solution.py:298
  169.0 20.3 %collective-permute-start.28 = (bf16[176,1024]{1,0:T(8,128)(2,1)}, bf16[176,1024]{1,0:T(8,128)(2,1)}, u32[]{:S(2)}, u32[]{:S(2)}) collective-permute-start(bf16[176,1024]{1,0:T(8,128)(2,1)} %get-tuple-element.216), channel_id=1, source_target_pairs={{0,16},{16,0},{1,17},{17,1},{2,18},{18,2},{3,19},{19,3},{4,20},{20... | collective-permute-start | bytes 1081352 | tf_op jit(solution)/shard_map/ppermute | solution.py:298
  169.1 20.2 %collective-permute-start.29 = (bf16[176,1024]{1,0:T(8,128)(2,1)}, bf16[176,1024]{1,0:T(8,128)(2,1)}, u32[]{:S(2)}, u32[]{:S(2)}) collective-permute-start(bf16[176,1024]{1,0:T(8,128)(2,1)} %get-tuple-element.217), channel_id=1, source_target_pairs={{0,4},{4,0},{1,5},{5,1},{2,6},{6,2},{3,7},{7,3},{8,12},{12,8},{9,1... | collective-permute-start | bytes 1081352 | tf_op jit(solution)/shard_map/ppermute | solution.py:298
  169.1 23.5 %collective-permute-start.30 = (bf16[176,1024]{1,0:T(8,128)(2,1)}, bf16[176,1024]{1,0:T(8,128)(2,1)}, u32[]{:S(2)}, u32[]{:S(2)}) collective-permute-start(bf16[176,1024]{1,0:T(8,128)(2,1)} %get-tuple-element.218), channel_id=1, source_target_pairs={{0,20},{4,16},{16,4},{20,0},{1,21},{5,17},{17,5},{21,1},{2,22},{6,... | collective-permute-start | bytes 1081352 | tf_op jit(solution)/shard_map/ppermute | solution.py:299
  172.7 16.6 %collective-permute-start.31 = (bf16[128,768]{1,0:T(8,128)(2,1)}, bf16[128,768]{1,0:T(8,128)(2,1)}, u32[]{:S(2)}, u32[]{:S(2)}) collective-permute-start(bf16[128,768]{1,0:T(8,128)(2,1)} %add_convert_fusion.7), channel_id=1, source_target_pairs={{0,8},{8,0},{1,9},{9,1},{2,10},{10,2},{3,11},{11,3},{4,12},{12,4},... | collective-permute-start | bytes 589832 | tf_op jit(solution)/shard_map/ppermute | solution.py:298
  172.8 4.3 %collective-permute-start.33 = (f32[16,1024]{1,0:T(8,128)S(1)}, f32[16,1024]{1,0:T(8,128)S(1)}, u32[]{:S(2)}, u32[]{:S(2)}) collective-permute-start(f32[16,1024]{1,0:T(8,128)S(1)} %add.235), channel_id=1, source_target_pairs={{0,2},{2,0},{1,3},{3,1},{4,6},{6,4},{5,7},{7,5},{8,10},{10,8},{9,1... | collective-permute-start | bytes 196616 | tf_op jit(solution)/shard_map/ppermute | solution.py:298
  195.1 12.0 %collective-permute-start.37 = (bf16[128,1024]{1,0:T(8,128)(2,1)}, bf16[128,1024]{1,0:T(8,128)(2,1)S(1)}, u32[]{:S(2)}, u32[]{:S(2)}) collective-permute-start(bf16[128,1024]{1,0:T(8,128)(2,1)} %get-tuple-element.242), channel_id=1, source_target_pairs={{0,16},{16,0},{1,17},{17,1},{2,18},{18,2},{3,19},{19,3},{4,20},{20... | collective-permute-start | bytes 786440 | tf_op jit(solution)/shard_map/ppermute | solution.py:298
  195.5 11.6 %collective-permute-start.34 = (bf16[64,896]{1,0:T(8,128)(2,1)}, bf16[64,896]{1,0:T(8,128)(2,1)S(1)}, u32[]{:S(2)}, u32[]{:S(2)}) collective-permute-start(bf16[64,896]{1,0:T(8,128)(2,1)} %get-tuple-element.239), channel_id=1, source_target_pairs={{0,1},{1,0},{2,3},{3,2},{4,5},{5,4},{6,7},{7,6},{8,9},{9,8},{10,11... | collective-permute-start | bytes 344072 | tf_op jit(solution)/shard_map/ppermute | solution.py:298
  195.5 11.6 %collective-permute-start.35 = (bf16[64,896]{1,0:T(8,128)(2,1)}, bf16[64,896]{1,0:T(8,128)(2,1)S(1)}, u32[]{:S(2)}, u32[]{:S(2)}) collective-permute-start(bf16[64,896]{1,0:T(8,128)(2,1)} %get-tuple-element.240), channel_id=1, source_target_pairs={{0,4},{4,0},{1,5},{5,1},{2,6},{6,2},{3,7},{7,3},{8,12},{12,8},{9,1... | collective-permute-start | bytes 344072 | tf_op jit(solution)/shard_map/ppermute | solution.py:298
  195.5 11.6 %collective-permute-start.36 = (bf16[64,896]{1,0:T(8,128)(2,1)}, bf16[64,896]{1,0:T(8,128)(2,1)S(1)}, u32[]{:S(2)}, u32[]{:S(2)}) collective-permute-start(bf16[64,896]{1,0:T(8,128)(2,1)} %get-tuple-element.241), channel_id=1, source_target_pairs={{0,5},{1,4},{4,1},{5,0},{2,7},{3,6},{6,3},{7,2},{8,13},{9,12},{12,... | collective-permute-start | bytes 344072 | tf_op jit(solution)/shard_map/ppermute | solution.py:299
  197.4 7.8 %collective-permute-start.38 = (f32[16,1024]{1,0:T(8,128)S(1)}, f32[16,1024]{1,0:T(8,128)S(1)}, u32[]{:S(2)}, u32[]{:S(2)}) collective-permute-start(f32[16,1024]{1,0:T(8,128)S(1)} %add.236), channel_id=1, source_target_pairs={{0,4},{4,0},{1,5},{5,1},{2,6},{6,2},{3,7},{7,3},{8,12},{12,8},{9,1... | collective-permute-start | bytes 196616 | tf_op jit(solution)/shard_map/ppermute | solution.py:298
  200.9 12.0 %copy-start.16 = (bf16[128,1024]{1,0:T(8,128)(2,1)S(1)}, bf16[128,1024]{1,0:T(8,128)(2,1)}, u32[]{:S(2)}) copy-start(bf16[128,1024]{1,0:T(8,128)(2,1)} %get-tuple-element.242) | copy-start | bytes 786436
  205.1 2.0 collective-permute-start.39
  208.1 11.8 %collective-permute-start.43 = (bf16[64,1024]{1,0:T(8,128)(2,1)S(1)}, bf16[64,1024]{1,0:T(8,128)(2,1)S(1)}, u32[]{:S(2)}, u32[]{:S(2)}) collective-permute-start(bf16[64,1024]{1,0:T(8,128)(2,1)S(1)} %fusion.15), channel_id=1, source_target_pairs={{0,16},{16,0},{1,17},{17,1},{2,18},{18,2},{3,19},{19,3},{4,20},{20... | collective-permute-start | bytes 393224 | tf_op jit(solution)/shard_map/ppermute | solution.py:298
  209.7 15.7 %collective-permute-start.42 = (bf16[2,2,64,896]{3,2,1,0:T(8,128)(2,1)}, bf16[2,2,64,896]{3,2,1,0:T(8,128)(2,1)}, u32[]{:S(2)}, u32[]{:S(2)}) collective-permute-start(bf16[2,2,64,896]{3,2,1,0:T(8,128)(2,1)} %bitcast.31.own), channel_id=1, source_target_pairs={{0,16},{16,0},{1,17},{17,1},{2,18},{18,2},{3,19},{19,3},{4,20},{20... | collective-permute-start | bytes 1376264 | tf_op jit(solution)/shard_map/ppermute | solution.py:298
  210.1 6.0 %collective-permute-start.41 = (f32[16,1024]{1,0:T(8,128)S(1)}, f32[16,1024]{1,0:T(8,128)S(1)}, u32[]{:S(2)}, u32[]{:S(2)}) collective-permute-start(f32[16,1024]{1,0:T(8,128)S(1)} %add.245), channel_id=1, source_target_pairs={{0,8},{8,0},{1,9},{9,1},{2,10},{10,2},{3,11},{11,3},{4,12},{12,4},... | collective-permute-start | bytes 196616 | tf_op jit(solution)/shard_map/ppermute | solution.py:298
  211.5 11.7 %collective-permute-start.40 = (bf16[176,1024]{1,0:T(8,128)(2,1)}, bf16[176,1024]{1,0:T(8,128)(2,1)}, u32[]{:S(2)}, u32[]{:S(2)}) collective-permute-start(bf16[176,1024]{1,0:T(8,128)(2,1)} %add_convert_fusion.1), channel_id=1, source_target_pairs={{0,4},{4,0},{1,5},{5,1},{2,6},{6,2},{3,7},{7,3},{8,12},{12,8},{9,1... | collective-permute-start | bytes 1081352 | tf_op jit(solution)/shard_map/ppermute | solution.py:298
  212.9 10.3 %copy-start.21 = (f32[1,1024]{1,0:T(1,128)S(1)}, f32[1,1024]{1,0:T(1,128)}, u32[]{:S(2)}) copy-start(f32[1,1024]{1,0:T(1,128)} %get-tuple-element.252) | copy-start | bytes 12292
  216.3 11.7 %copy-start.38 = (f32[64]{0:T(128)}, f32[64]{0:T(128)S(1)}, u32[]{:S(2)}) copy-start(f32[64]{0:T(128)S(1)} %fusion.18) | copy-start | bytes 772
  (19 other events, 76.0 us)

commit v6 on v5

--- a/solution.py
+++ b/solution.py
@@ -290,7 +290,7 @@
 LANE = 128
 EXTRA = 16
 GROUP = ("o", "p", "q", "c")
-VMEM_BYTES = 58 * 1024 * 1024
+VMEM_BYTES = 48 * 1024 * 1024
 
 
 def swap(values, *axes):

time: 229 us -> 224 us (0.978)
  Pallas kernels: 55.9 us -> 52.1 us
  waiting for transfers between devices: 80.8 us -> 78.2 us
    unnamed x81 -> x101, local copies, waits for them, and re-layouts: 3.2 us -> 7.15 us
    pallas_call x6, Pallas kernels: 55.9 us -> 52.1 us  [call(): pl.pallas_call(kernel, out_shape=tuple(outs), in_specs=[specs[kind] for k...]
    ppermute x40, waiting for transfers between devices: 77.5 us -> 74.9 us  [swap(): return lax.ppermute(values, axes[0], PAIR)]
  transfers between devices with their start and end apart: 44 -> 44, of which waited for: 16 -> 16; matrix products, arithmetic and copies ran while one was open for 12% -> 11% of each run, Pallas kernels for 22% -> 22%
where the time goes in v6:
time: 224 us; the launch traced here: 223 us
  waiting for transfers between devices  78.2 us (35%)
  Pallas kernels  52.1 us (23%)
  starting transfers between devices  50.6 us (23%)
  other arithmetic  28 us (12%)
  local copies, waits for them, and re-layouts  12.6 us (6%)
    ppermute x40, waiting for transfers between devices, swap(): return lax.ppermute(values, axes[0], PAIR)  74.9 us
    pallas_call x6, Pallas kernels, call(): pl.pallas_call(kernel, out_shape=tuple(outs), in_specs=[specs[kind] for k...  52.1 us
    ppermute x40, starting transfers between devices, swap(): return lax.ppermute(values, axes[0], PAIR)  44.1 us
    convert_element_type x6, other arithmetic, low(): return values.astype(jnp.bfloat16)  7.89 us
    unnamed x101, local copies, waits for them, and re-layouts  7.15 us
    ppermute x2, starting transfers between devices, swap(): return lax.ppermute(values, axes, [(i, 3 - i) for i in range(4)])  5.26 us
  transfers between devices with their start and end apart: 44, of which 16 were waited for; matrix products, arithmetic and copies ran while one was open for 11% of the time, Pallas kernels for 22%

profile of v6, /device:TPU:0, one launch (start us, length us, event | category | flops | bytes accessed | tf_op | source)
XLA Modules:
  0.0 223.0 jit_solution(6942280690304079072)
XLA Ops:
  0.8 2.2 pad_maximum_fusion.2
  3.0 2.9 %collective-permute-start.3 = (bf16[2,176,1024]{2,1,0:T(8,128)(2,1)}, bf16[2,176,1024]{2,1,0:T(8,128)(2,1)}, u32[]{:S(2)}, u32[]{:S(2)}) collective-permute-start(bf16[2,176,1024]{2,1,0:T(8,128)(2,1)} %pad_maximum_fusion.2), channel_id=1, source_target_pairs={{0,16},{16,0},{1,17},{17,1},{2,18},{18,2},{3,19},{19,3},{4,20},{20... | collective-permute-start | bytes 2162696 | tf_op jit(solution)/shard_map/ppermute | solution.py:298
  6.0 2.7 %collective-permute-start.1 = (bf16[128,1024]{1,0:T(8,128)(2,1)S(1)}, bf16[128,1024]{1,0:T(8,128)(2,1)}, u32[]{:S(2)}, u32[]{:S(2)}) collective-permute-start(bf16[128,1024]{1,0:T(8,128)(2,1)S(1)} %dynamic-slice_bitcast_fusion.tall_0), channel_id=1, source_target_pairs={{0,8},{8,0},{1,9},{9,1},{2,10},{10,2},{3,11},{11,3},{4,12},{12,4},... | collective-permute-start | bytes 786440 | tf_op jit(solution)/shard_map/ppermute | solution.py:298
  8.6 1.5 collective-permute-start.2
  10.4 0.7 shard_map.263
  11.1 1.6 collective-permute-start
  13.4 7.1 %collective-permute-done.1.tall_2 = bf16[128,1024]{1,0:T(8,128)(2,1)} collective-permute-done((bf16[128,1024]{1,0:T(8,128)(2,1)S(1)}, bf16[128,1024]{1,0:T(8,128)(2,1)}, u32[]{:S(2)}, u32[]{:S(2)}) %collective-permute-start.1) | collective-permute-done | bytes 262176 | tf_op jit(solution)/shard_map/ppermute | solution.py:298
  20.5 4.7 %collective-permute-done = bf16[2,80,896]{2,1,0:T(8,128)(2,1)S(1)} collective-permute-done((bf16[2,80,896]{2,1,0:T(8,128)(2,1)S(1)}, bf16[2,80,896]{2,1,0:T(8,128)(2,1)S(1)}, u32[]{:S(2)}, u32[]{:S(2)}) %collective-permute-start) | collective-permute-done | bytes 286752 | tf_op jit(solution)/shard_map/ppermute | solution.py:298
  25.3 5.8 %collective-permute-done.4 = bf16[176,1024]{1,0:T(8,128)(2,1)S(1)} collective-permute-done((bf16[176,1024]{1,0:T(8,128)(2,1)S(1)}, bf16[176,1024]{1,0:T(8,128)(2,1)S(1)}, u32[]{:S(2)}, u32[]{:S(2)}) %collective-permute-start.4) | collective-permute-done | bytes 360480 | tf_op jit(solution)/shard_map/ppermute | solution.py:298
  31.1 0.7 copy-done.31
  33.3 1.5 pad_maximum_fusion.block_0
  35.6 1.1 pad_maximum_fusion.4
  37.9 1.5 collective-permute-start.8
  39.3 2.5 %collective-permute-start.9 = (bf16[176,1024]{1,0:T(8,128)(2,1)S(1)}, bf16[176,1024]{1,0:T(8,128)(2,1)}, u32[]{:S(2)}, u32[]{:S(2)}) collective-permute-start(bf16[176,1024]{1,0:T(8,128)(2,1)S(1)} %copy-done.23), channel_id=1, source_target_pairs={{0,4},{4,0},{1,5},{5,1},{2,6},{6,2},{3,7},{7,3},{8,12},{12,8},{9,1... | collective-permute-start | bytes 1081352 | tf_op jit(solution)/shard_map/ppermute | solution.py:298
  41.8 3.6 %fusion.11 = (f32[1408,128]{1,0:T(8,128)S(1)}, f32[1408,128]{1,0:T(8,128)}) fusion(f32[128]{0:T(128)S(1)} %mul.135, f32[1408]{0:T(1024)S(1)} %convert_element_type.113, pred[128]{0:T(512)(128)(4,1)S(1)} %get-tuple-element.287, pred[128]{0:T(512)(128)(4,1)S(1)} %get-tuple-element.288), kind=kLoop, calls=%fused_computation.19 | loop fusion | flops 901120 | bytes 1448192 | tf_op jit(solution)/shard_map/jit(_where)/select_n | solution.py:937
  45.4 0.7 copy-done.17
  46.2 8.5 %collective-permute-done.7.sheet_2.extra_2 = bf16[4,80,512]{2,1,0:T(8,128)(2,1)S(1)} collective-permute-done((bf16[4,80,512]{2,1,0:T(8,128)(2,1)S(1)}, bf16[4,80,512]{2,1,0:T(8,128)(2,1)S(1)}, u32[]{:S(2)}, u32[]{:S(2)}) %collective-permute-start.7) | collective-permute-done | bytes 327712 | tf_op jit(solution)/shard_map/ppermute | solution.py:298
  54.7 0.7 copy-done.11
  55.4 0.7 copy-done.13
  56.8 0.7 copy-done.33
  57.5 1.1 broadcast_in_dim.75.position
  58.6 1.5 collective-permute-start.15
  60.1 0.9 collective-permute-start.12
  61.0 1.0 broadcast_select_fusion.3
  62.0 9.8 %collective-permute-done.14.sheet_2.join_2 = bf16[4,64,384]{2,1,0:T(8,128)(2,1)S(1)} collective-permute-done((bf16[4,64,384]{2,1,0:T(8,128)(2,1)S(1)}, bf16[4,64,384]{2,1,0:T(8,128)(2,1)S(1)}, u32[]{:S(2)}, u32[]{:S(2)}) %collective-permute-start.14) | collective-permute-done | bytes 196640 | tf_op jit(solution)/shard_map/ppermute | solution.py:298
  71.9 1.6 pad_maximum_fusion.1.block_2
  73.6 3.1 %collective-permute-done.16.block_3 = bf16[4,176,1024]{2,1,0:T(8,128)(2,1)S(1)} collective-permute-done((bf16[4,176,1024]{2,1,0:T(8,128)(2,1)S(1)}, bf16[4,176,1024]{2,1,0:T(8,128)(2,1)S(1)}, u32[]{:S(2)}, u32[]{:S(2)}) %collective-permute-start.16) | collective-permute-done | bytes 1441824 | tf_op jit(solution)/shard_map/ppermute | solution.py:298
  76.8 1.1 collective-permute-start.17
  78.6 18.0 %shard_map.264 = (bf16[1408,1024]{1,0:T(8,128)(2,1)}, f32[1,1024]{1,0:T(1,128)S(1)}, bf16[1408,512]{1,0:T(8,128)(2,1)S(1)}, bf16[256,1024]{1,0:T(8,128)(2,1)S(1)...) custom-call(s32[5]{0:T(128)S(1)} %stack.107.ids, ...), custom_call_target="tpu_custom_call" | custom-call | flops 23000000512 | bytes 14555156 | tf_op jit(solution)/shard_map/pallas_call | solution.py:341
  96.6 2.8 %collective-permute-start.19 = (bf16[256,1024]{1,0:T(8,128)(2,1)S(1)}, bf16[256,1024]{1,0:T(8,128)(2,1)S(1)}, u32[]{:S(2)}, u32[]{:S(2)}) collective-permute-start(bf16[256,1024]{1,0:T(8,128)(2,1)S(1)} %get-tuple-element.177), channel_id=1, source_target_pairs={{0,2},{2,0},{1,3},{3,1},{4,6},{6,4},{5,7},{7,5},{8,10},{10,8},{9,1... | collective-permute-start | bytes 1572872 | tf_op jit(solution)/shard_map/ppermute | solution.py:298
  99.4 21.0 %shard_map.265 = (f32[704,1024]{1,0:T(8,128)}, bf16[704,1024]{1,0:T(8,128)(2,1)}, bf16[1408,384]{1,0:T(8,128)(2,1)}, bf16[128,768]{1,0:T(8,128)(2,1)S(1)}, bf16[...) custom-call(s32[5]{0:T(128)S(1)} %stack.107.ids, ...), custom_call_target="tpu_custom_call" | custom-call | flops 25300000768 | bytes 19629588 | tf_op jit(solution)/shard_map/pallas_call | solution.py:341
  120.7 2.4 %collective-permute-start.21 = (bf16[256,1024]{1,0:T(8,128)(2,1)S(1)}, bf16[256,1024]{1,0:T(8,128)(2,1)S(1)}, u32[]{:S(2)}, u32[]{:S(2)}) collective-permute-start(bf16[256,1024]{1,0:T(8,128)(2,1)S(1)} %add_convert_fusion), channel_id=1, source_target_pairs={{0,8},{8,0},{1,9},{9,1},{2,10},{10,2},{3,11},{11,3},{4,12},{12,4},... | collective-permute-start | bytes 1572872 | tf_op jit(solution)/shard_map/ppermute | solution.py:298
  123.1 1.3 collective-permute-start.22
  124.4 0.7 collective-permute-start.23
  125.8 2.1 add_convert_fusion.6
  128.0 3.3 %collective-permute-start.24 = (bf16[352,1024]{1,0:T(8,128)(2,1)S(1)}, bf16[352,1024]{1,0:T(8,128)(2,1)S(1)}, u32[]{:S(2)}, u32[]{:S(2)}) collective-permute-start(bf16[352,1024]{1,0:T(8,128)(2,1)S(1)} %pad_maximum_fusion.3), channel_id=1, source_target_pairs={{0,16},{16,0},{1,17},{17,1},{2,18},{18,2},{3,19},{19,3},{4,20},{20... | collective-permute-start | bytes 2162696 | tf_op jit(solution)/shard_map/ppermute | solution.py:298
  131.4 10.2 %shard_map.266 = (f32[704,1024]{1,0:T(8,128)}, bf16[704,1024]{1,0:T(8,128)(2,1)S(1)}, f32[16,1024]{1,0:T(8,128)S(1)}) custom-call(s32[5]{0:T(128)S(1)} %stack.107.ids, bf16[4,176,1024]{2,1,0:T(8,128)(2,1)S(1)} %copy-done.2, bf16[4,176,1024]{2,1,0:T(8,128)(2,1)} %collective-permute-done.13.block_1, bf16[4,176,1024]{2,1,0:T(8,128)(2,1)} %copy-done.27, ...), custom_call_target="tpu_custom_call" | custom-call | flops 12650000384 | bytes 14781972 | tf_op jit(solution)/shard_map/pallas_call | solution.py:341
  141.6 3.9 %collective-permute-done.23.joint_away = bf16[256,768]{1,0:T(8,128)(2,1)S(1)} collective-permute-done((bf16[256,768]{1,0:T(8,128)(2,1)S(1)}, bf16[256,768]{1,0:T(8,128)(2,1)S(1)}, u32[]{:S(2)}, u32[]{:S(2)}) %collective-permute-start.23) | collective-permute-done | bytes 393248 | tf_op jit(solution)/shard_map/ppermute | solution.py:298
  145.6 6.3 %collective-permute-done.21.up_sent = bf16[256,1024]{1,0:T(8,128)(2,1)S(1)} collective-permute-done((bf16[256,1024]{1,0:T(8,128)(2,1)S(1)}, bf16[256,1024]{1,0:T(8,128)(2,1)S(1)}, u32[]{:S(2)}, u32[]{:S(2)}) %collective-permute-start.21) | collective-permute-done | bytes 524320 | tf_op jit(solution)/shard_map/ppermute | solution.py:298
  152.7 0.7 add_convert_fusion.7
  153.4 1.9 collective-permute-done.27
  155.3 3.3 %add_convert_fusion.2 = (bf16[176,1024]{1,0:T(8,128)(2,1)}, bf16[176,1024]{1,0:T(8,128)(2,1)}, bf16[176,1024]{1,0:T(8,128)(2,1)}) fusion(f32[704,1024]{1,0:T(8,128)} %get-tuple-element.214, bf16[704,1024]{1,0:T(8,128)(2,1)S(1)} %collective-permute-done.26), kind=kLoop, calls=%fused_computation.27 | loop fusion | flops 1622016 | bytes 4325376 | tf_op jit(solution)/shard_map/convert_element_type | solution.py:318
  158.7 7.2 %collective-permute-start.32 = (f32[16,1024]{1,0:T(8,128)S(1)}, f32[16,1024]{1,0:T(8,128)S(1)}, u32[]{:S(2)}, u32[]{:S(2)}) collective-permute-start(f32[16,1024]{1,0:T(8,128)S(1)} %add.231), channel_id=1, source_target_pairs={{0,16},{16,0},{1,17},{17,1},{2,18},{18,2},{3,19},{19,3},{4,20},{20... | collective-permute-start | bytes 196616 | tf_op jit(solution)/shard_map/ppermute | solution.py:298
  166.0 3.4 %collective-permute-start.30 = (bf16[176,1024]{1,0:T(8,128)(2,1)}, bf16[176,1024]{1,0:T(8,128)(2,1)}, u32[]{:S(2)}, u32[]{:S(2)}) collective-permute-start(bf16[176,1024]{1,0:T(8,128)(2,1)} %get-tuple-element.218), channel_id=1, source_target_pairs={{0,20},{4,16},{16,4},{20,0},{1,21},{5,17},{17,5},{21,1},{2,22},{6,... | collective-permute-start | bytes 1081352 | tf_op jit(solution)/shard_map/ppermute | solution.py:299
  169.7 1.4 collective-permute-start.33
  171.1 2.9 %collective-permute-done.33 = f32[16,1024]{1,0:T(8,128)S(1)} collective-permute-done((f32[16,1024]{1,0:T(8,128)S(1)}, f32[16,1024]{1,0:T(8,128)S(1)}, u32[]{:S(2)}, u32[]{:S(2)}) %collective-permute-start.33) | collective-permute-done | bytes 65568 | tf_op jit(solution)/shard_map/ppermute | solution.py:298
  174.1 12.3 %collective-permute-done.31.joint_sent = bf16[128,768]{1,0:T(8,128)(2,1)S(1)} collective-permute-done((bf16[128,768]{1,0:T(8,128)(2,1)}, bf16[128,768]{1,0:T(8,128)(2,1)S(1)}, u32[]{:S(2)}, u32[]{:S(2)}) %collective-permute-start.31) | collective-permute-done | bytes 196640 | tf_op jit(solution)/shard_map/ppermute | solution.py:298
  186.4 3.3 %collective-permute-done.30 = bf16[176,1024]{1,0:T(8,128)(2,1)} collective-permute-done((bf16[176,1024]{1,0:T(8,128)(2,1)}, bf16[176,1024]{1,0:T(8,128)(2,1)}, u32[]{:S(2)}, u32[]{:S(2)}) %collective-permute-start.30) | collective-permute-done | bytes 360480 | tf_op jit(solution)/shard_map/ppermute | solution.py:299
  189.7 1.0 copy-done.8
  190.8 1.0 copy-done.10
  192.5 1.9 collective-permute-start.36
  194.7 1.8 fusion.22
  196.5 1.2 fusion.9
  197.7 4.2 %collective-permute-done.38 = f32[16,1024]{1,0:T(8,128)S(1)} collective-permute-done((f32[16,1024]{1,0:T(8,128)S(1)}, f32[16,1024]{1,0:T(8,128)S(1)}, u32[]{:S(2)}, u32[]{:S(2)}) %collective-permute-start.38) | collective-permute-done | bytes 65568 | tf_op jit(solution)/shard_map/ppermute | solution.py:298
  201.9 1.3 add_convert_fusion.1
  203.5 1.7 collective-permute-start.43
  205.6 1.3 collective-permute-start.41
  206.9 1.4 collective-permute-start.40
  208.3 1.1 maximum_convert_fusion
  209.4 2.2 collective-permute-done.41
  215.4 1.6 convert_add_fusion.3
  217.0 1.2 collective-permute-done.40
  218.2 2.3 %fusion.14 = bf16[176,1024]{1,0:T(8,128)(2,1)} fusion(bf16[176,1024]{1,0:T(8,128)(2,1)S(1)} %copy-done.22, bf16[176,1024]{1,0:T(8,128)(2,1)S(1)} %collective-permute-done.40, f32[704,1024]{1,0:T(8,128)} %get-tuple-element.193, bf16[704,1024]{1,0:T(8,128)(2,1)} %copy-done.25, f32[1024]{0:T(1024)S(1)} %bitcast.61, bf16[352,1024]{1,0:T(8,128)(2,1)} %copy-done.29), kind=kLoop, calls=%fused_computation.22 | loop fusion | flops 1802240 | bytes 2527232 | tf_op jit(solution)/shard_map/convert_element_type | solution.py:318
  220.5 2.0 shard_map.268
  (198 shorter events, 13.9 us)
Async XLA Ops:
  0.7 9.5 %copy-start.39 = (bf16[64]{0:T(256)(128)(2,1)S(1)}, bf16[64]{0:T(256)(128)(2,1)}, u32[]{:S(2)}) copy-start(bf16[64]{0:T(256)(128)(2,1)} %param.20) | copy-start | bytes 388
  0.7 9.5 %copy-start.40 = (bf16[64]{0:T(256)(128)(2,1)S(1)}, bf16[64]{0:T(256)(128)(2,1)}, u32[]{:S(2)}) copy-start(bf16[64]{0:T(256)(128)(2,1)} %param.21) | copy-start | bytes 388
  0.7 9.5 %copy-start.41 = (bf16[192]{0:T(256)(128)(2,1)S(1)}, bf16[192]{0:T(256)(128)(2,1)}, u32[]{:S(2)}) copy-start(bf16[192]{0:T(256)(128)(2,1)} %param.23) | copy-start | bytes 1156
  0.7 9.5 %copy-start.45 = (bf16[64]{0:T(256)(128)(2,1)S(1)}, bf16[64]{0:T(256)(128)(2,1)}, u32[]{:S(2)}) copy-start(bf16[64]{0:T(256)(128)(2,1)} %param.25) | copy-start | bytes 388
  0.7 9.5 %copy-start.42 = (bf16[64]{0:T(256)(128)(2,1)S(1)}, bf16[64]{0:T(256)(128)(2,1)}, u32[]{:S(2)}) copy-start(bf16[64]{0:T(256)(128)(2,1)} %param.26) | copy-start | bytes 388
  0.7 9.5 %copy-start.43 = (bf16[64]{0:T(256)(128)(2,1)S(1)}, bf16[64]{0:T(256)(128)(2,1)}, u32[]{:S(2)}) copy-start(bf16[64]{0:T(256)(128)(2,1)} %param.27) | copy-start | bytes 388
  0.7 9.5 %copy-start.44 = (bf16[256]{0:T(256)(128)(2,1)S(1)}, bf16[256]{0:T(256)(128)(2,1)}, u32[]{:S(2)}) copy-start(bf16[256]{0:T(256)(128)(2,1)} %param.29) | copy-start | bytes 1540
  0.7 9.6 %copy-start.6 = (bf16[64,3072]{1,0:T(8,128)(2,1)S(1)}, bf16[64,3072]{1,0:T(8,128)(2,1)}, u32[]{:S(2)}) copy-start(bf16[64,3072]{1,0:T(8,128)(2,1)} %joint.1) | copy-start | bytes 1179652
  0.8 9.6 %copy-start.5 = (bf16[64,4096]{1,0:T(8,128)(2,1)S(1)}, bf16[64,4096]{1,0:T(8,128)(2,1)}, u32[]{:S(2)}) copy-start(bf16[64,4096]{1,0:T(8,128)(2,1)} %up.1) | copy-start | bytes 1572868
  0.8 12.0 %copy-start.21 = (bf16[176,1024]{1,0:T(8,128)(2,1)S(1)}, bf16[176,1024]{1,0:T(8,128)(2,1)}, u32[]{:S(2)}) copy-start(bf16[176,1024]{1,0:T(8,128)(2,1)} %param.16) | copy-start | bytes 1081348
  3.0 28.1 %collective-permute-start.3 = (bf16[2,176,1024]{2,1,0:T(8,128)(2,1)}, bf16[2,176,1024]{2,1,0:T(8,128)(2,1)}, u32[]{:S(2)}, u32[]{:S(2)}) collective-permute-start(bf16[2,176,1024]{2,1,0:T(8,128)(2,1)} %pad_maximum_fusion.2), channel_id=1, source_target_pairs={{0,16},{16,0},{1,17},{17,1},{2,18},{18,2},{3,19},{19,3},{4,20},{20... | collective-permute-start | bytes 2162696 | tf_op jit(solution)/shard_map/ppermute | solution.py:298
  5.9 26.0 %copy-start.37 = (s32[64]{0:T(128)S(1)}, s32[64]{0:T(128)}, u32[]{:S(2)}) copy-start(s32[64]{0:T(128)} %param.18) | copy-start | bytes 772
  5.9 26.0 %copy-start.38 = (s32[64]{0:T(128)S(1)}, s32[64]{0:T(128)}, u32[]{:S(2)}) copy-start(s32[64]{0:T(128)} %param.19) | copy-start | bytes 772
  6.0 14.6 %collective-permute-start.1 = (bf16[128,1024]{1,0:T(8,128)(2,1)S(1)}, bf16[128,1024]{1,0:T(8,128)(2,1)}, u32[]{:S(2)}, u32[]{:S(2)}) collective-permute-start(bf16[128,1024]{1,0:T(8,128)(2,1)S(1)} %dynamic-slice_bitcast_fusion.tall_0), channel_id=1, source_target_pairs={{0,8},{8,0},{1,9},{9,1},{2,10},{10,2},{3,11},{11,3},{4,12},{12,4},... | collective-permute-start | bytes 786440 | tf_op jit(solution)/shard_map/ppermute | solution.py:298
  8.6 11.9 %collective-permute-start.2 = (bf16[128,1024]{1,0:T(8,128)(2,1)S(1)}, bf16[128,1024]{1,0:T(8,128)(2,1)S(1)}, u32[]{:S(2)}, u32[]{:S(2)}) collective-permute-start(bf16[128,1024]{1,0:T(8,128)(2,1)S(1)} %dynamic-slice_bitcast_fusion.tall_0), channel_id=1, source_target_pairs={{0,2},{2,0},{1,3},{3,1},{4,6},{6,4},{5,7},{7,5},{8,10},{10,8},{9,1... | collective-permute-start | bytes 786440 | tf_op jit(solution)/shard_map/ppermute | solution.py:298
  11.1 14.2 %collective-permute-start = (bf16[2,80,896]{2,1,0:T(8,128)(2,1)S(1)}, bf16[2,80,896]{2,1,0:T(8,128)(2,1)S(1)}, u32[]{:S(2)}, u32[]{:S(2)}) collective-permute-start(bf16[2,80,896]{2,1,0:T(8,128)(2,1)S(1)} %get-tuple-element.137), channel_id=1, source_target_pairs={{0,4},{4,0},{1,5},{5,1},{2,6},{6,2},{3,7},{7,3},{8,12},{12,8},{9,1... | collective-permute-start | bytes 860168 | tf_op jit(solution)/shard_map/ppermute | solution.py:298
  12.7 18.4 %collective-permute-start.4 = (bf16[176,1024]{1,0:T(8,128)(2,1)S(1)}, bf16[176,1024]{1,0:T(8,128)(2,1)S(1)}, u32[]{:S(2)}, u32[]{:S(2)}) collective-permute-start(bf16[176,1024]{1,0:T(8,128)(2,1)S(1)} %copy-done.21), channel_id=1, source_target_pairs={{0,4},{4,0},{1,5},{5,1},{2,6},{6,2},{3,7},{7,3},{8,12},{12,8},{9,1... | collective-permute-start | bytes 1081352 | tf_op jit(solution)/shard_map/ppermute | solution.py:298
  20.5 14.3 %collective-permute-start.6 = (bf16[64,1024]{1,0:T(8,128)(2,1)}, bf16[64,1024]{1,0:T(8,128)(2,1)S(1)}, u32[]{:S(2)}, u32[]{:S(2)}) collective-permute-start(bf16[64,1024]{1,0:T(8,128)(2,1)} %param.24), channel_id=1, source_target_pairs={{0,1},{1,0},{2,3},{3,2},{4,5},{5,4},{6,7},{7,6},{8,9},{9,8},{10,11... | collective-permute-start | bytes 393224 | tf_op jit(solution)/shard_map/ppermute | solution.py:298
  20.5 12.2 %copy-start.15 = (bf16[128,1024]{1,0:T(8,128)(2,1)}, bf16[128,1024]{1,0:T(8,128)(2,1)S(1)}, u32[]{:S(2)}) copy-start(bf16[128,1024]{1,0:T(8,128)(2,1)S(1)} %collective-permute-done.2.tall_1) | copy-start | bytes 786436
  31.9 2.9 %collective-permute-start.5 = (bf16[2,80,896]{2,1,0:T(8,128)(2,1)S(1)}, bf16[2,80,896]{2,1,0:T(8,128)(2,1)S(1)}, u32[]{:S(2)}, u32[]{:S(2)}) collective-permute-start(bf16[2,80,896]{2,1,0:T(8,128)(2,1)S(1)} %pad_maximum_fusion.7), channel_id=1, source_target_pairs={{0,1},{1,0},{2,3},{3,2},{4,5},{5,4},{6,7},{7,6},{8,9},{9,8},{10,11... | collective-permute-start | bytes 860168 | tf_op jit(solution)/shard_map/ppermute | solution.py:298
  32.7 12.7 %collective-permute-start.11 = (bf16[128,1024]{1,0:T(8,128)(2,1)}, bf16[128,1024]{1,0:T(8,128)(2,1)S(1)}, u32[]{:S(2)}, u32[]{:S(2)}) collective-permute-start(bf16[128,1024]{1,0:T(8,128)(2,1)} %collective-permute-done.1.tall_2), channel_id=1, source_target_pairs={{0,2},{2,0},{1,3},{3,1},{4,6},{6,4},{5,7},{7,5},{8,10},{10,8},{9,1... | collective-permute-start | bytes 786440 | tf_op jit(solution)/shard_map/ppermute | solution.py:298
  34.8 23.9 %copy-start.1 = (bf16[4,176,1024]{2,1,0:T(8,128)(2,1)}, bf16[4,176,1024]{2,1,0:T(8,128)(2,1)S(1)}, u32[]{:S(2)}) copy-start(bf16[4,176,1024]{2,1,0:T(8,128)(2,1)S(1)} %pad_maximum_fusion.block_0) | copy-start | bytes 4325380
  36.7 20.0 %collective-permute-start.10 = (bf16[176,1024]{1,0:T(8,128)(2,1)S(1)}, bf16[176,1024]{1,0:T(8,128)(2,1)S(1)}, u32[]{:S(2)}, u32[]{:S(2)}) collective-permute-start(bf16[176,1024]{1,0:T(8,128)(2,1)S(1)} %copy-done.32), channel_id=1, source_target_pairs={{0,16},{16,0},{1,17},{17,1},{2,18},{18,2},{3,19},{19,3},{4,20},{20... | collective-permute-start | bytes 1081352 | tf_op jit(solution)/shard_map/ppermute | solution.py:298
  37.3 17.4 %collective-permute-start.7 = (bf16[4,80,512]{2,1,0:T(8,128)(2,1)S(1)}, bf16[4,80,512]{2,1,0:T(8,128)(2,1)S(1)}, u32[]{:S(2)}, u32[]{:S(2)}) collective-permute-start(bf16[4,80,512]{2,1,0:T(8,128)(2,1)S(1)} %slice.136.sheet_0.extra_0), channel_id=1, source_target_pairs={{0,8},{8,0},{1,9},{9,1},{2,10},{10,2},{3,11},{11,3},{4,12},{12,4},... | collective-permute-start | bytes 983048 | tf_op jit(solution)/shard_map/ppermute | solution.py:298
  37.9 16.8 %collective-permute-start.8 = (bf16[4,80,512]{2,1,0:T(8,128)(2,1)S(1)}, bf16[4,80,512]{2,1,0:T(8,128)(2,1)S(1)}, u32[]{:S(2)}, u32[]{:S(2)}) collective-permute-start(bf16[4,80,512]{2,1,0:T(8,128)(2,1)S(1)} %slice.136.sheet_0.extra_0), channel_id=1, source_target_pairs={{0,2},{2,0},{1,3},{3,1},{4,6},{6,4},{5,7},{7,5},{8,10},{10,8},{9,1... | collective-permute-start | bytes 983048 | tf_op jit(solution)/shard_map/ppermute | solution.py:298
  39.3 17.4 %collective-permute-start.9 = (bf16[176,1024]{1,0:T(8,128)(2,1)S(1)}, bf16[176,1024]{1,0:T(8,128)(2,1)}, u32[]{:S(2)}, u32[]{:S(2)}) collective-permute-start(bf16[176,1024]{1,0:T(8,128)(2,1)S(1)} %copy-done.23), channel_id=1, source_target_pairs={{0,4},{4,0},{1,5},{5,1},{2,6},{6,2},{3,7},{7,3},{8,12},{12,8},{9,1... | collective-permute-start | bytes 1081352 | tf_op jit(solution)/shard_map/ppermute | solution.py:298
  58.6 13.2 %collective-permute-start.13 = (bf16[4,176,1024]{2,1,0:T(8,128)(2,1)S(1)}, bf16[4,176,1024]{2,1,0:T(8,128)(2,1)}, u32[]{:S(2)}, u32[]{:S(2)}) collective-permute-start(bf16[4,176,1024]{2,1,0:T(8,128)(2,1)S(1)} %pad_maximum_fusion.block_0), channel_id=1, source_target_pairs={{0,1},{1,0},{2,3},{3,2},{4,5},{5,4},{6,7},{7,6},{8,9},{9,8},{10,11... | collective-permute-start | bytes 4325384 | tf_op jit(solution)/shard_map/ppermute | solution.py:298
  58.6 13.2 %collective-permute-start.15 = (bf16[176,1024]{1,0:T(8,128)(2,1)}, bf16[176,1024]{1,0:T(8,128)(2,1)}, u32[]{:S(2)}, u32[]{:S(2)}) collective-permute-start(bf16[176,1024]{1,0:T(8,128)(2,1)} %collective-permute-done.9), channel_id=1, source_target_pairs={{0,16},{16,0},{1,17},{17,1},{2,18},{18,2},{3,19},{19,3},{4,20},{20... | collective-permute-start | bytes 1081352 | tf_op jit(solution)/shard_map/ppermute | solution.py:298
  60.1 11.7 %collective-permute-start.12 = (bf16[4,80,512]{2,1,0:T(8,128)(2,1)}, bf16[4,80,512]{2,1,0:T(8,128)(2,1)S(1)}, u32[]{:S(2)}, u32[]{:S(2)}) collective-permute-start(bf16[4,80,512]{2,1,0:T(8,128)(2,1)} %copy-done.11), channel_id=1, source_target_pairs={{0,2},{2,0},{1,3},{3,1},{4,6},{6,4},{5,7},{7,5},{8,10},{10,8},{9,1... | collective-permute-start | bytes 983048 | tf_op jit(solution)/shard_map/ppermute | solution.py:298
  61.0 10.8 %collective-permute-start.14 = (bf16[4,64,384]{2,1,0:T(8,128)(2,1)S(1)}, bf16[4,64,384]{2,1,0:T(8,128)(2,1)S(1)}, u32[]{:S(2)}, u32[]{:S(2)}) collective-permute-start(bf16[4,64,384]{2,1,0:T(8,128)(2,1)S(1)} %pad_maximum_fusion.9.sheet_0.join_0), channel_id=1, source_target_pairs={{0,8},{8,0},{1,9},{9,1},{2,10},{10,2},{3,11},{11,3},{4,12},{12,4},... | collective-permute-start | bytes 589832 | tf_op jit(solution)/shard_map/ppermute | solution.py:298
  73.5 3.3 %collective-permute-start.16 = (bf16[4,176,1024]{2,1,0:T(8,128)(2,1)S(1)}, bf16[4,176,1024]{2,1,0:T(8,128)(2,1)S(1)}, u32[]{:S(2)}, u32[]{:S(2)}) collective-permute-start(bf16[4,176,1024]{2,1,0:T(8,128)(2,1)S(1)} %pad_maximum_fusion.1.block_2), channel_id=1, source_target_pairs={{0,1},{1,0},{2,3},{3,2},{4,5},{5,4},{6,7},{7,6},{8,9},{9,8},{10,11... | collective-permute-start | bytes 4325384 | tf_op jit(solution)/shard_map/ppermute | solution.py:298
  73.6 25.8 %copy-start.3 = (f32[1408,128]{1,0:T(8,128)S(1)}, f32[1408,128]{1,0:T(8,128)}, u32[]{:S(2)}) copy-start(f32[1408,128]{1,0:T(8,128)} %get-tuple-element.182.cosine) | copy-start | bytes 2162692
  73.6 25.8 %copy-start.4 = (s32[1408,128]{1,0:T(8,128)S(1)}, s32[1408,128]{1,0:T(8,128)}, u32[]{:S(2)}) copy-start(s32[1408,128]{1,0:T(8,128)} %broadcast_in_dim.75.position) | copy-start | bytes 2162692
  76.8 19.8 %collective-permute-start.17 = (bf16[2,4,64,384]{3,2,1,0:T(8,128)(2,1)S(1)}, bf16[2,4,64,384]{3,2,1,0:T(8,128)(2,1)S(1)}, u32[]{:S(2)}, u32[]{:S(2)}) collective-permute-start(bf16[2,4,64,384]{3,2,1,0:T(8,128)(2,1)S(1)} %pad_maximum_fusion.6), channel_id=1, source_target_pairs={{0,2},{2,0},{1,3},{3,1},{4,6},{6,4},{5,7},{7,5},{8,10},{10,8},{9,1... | collective-permute-start | bytes 1179656 | tf_op jit(solution)/shard_map/ppermute | solution.py:298
  77.8 18.7 %collective-permute-start.18 = (bf16[128,1024]{1,0:T(8,128)(2,1)S(1)}, bf16[128,1024]{1,0:T(8,128)(2,1)S(1)}, u32[]{:S(2)}, u32[]{:S(2)}) collective-permute-start(bf16[128,1024]{1,0:T(8,128)(2,1)S(1)} %pad_maximum_fusion.8), channel_id=1, source_target_pairs={{0,0},{1,2},{2,1},{3,3},{8,16},{9,18},{10,17},{11,19},{16,8},{17,1... | collective-permute-start | bytes 786440 | tf_op jit(solution)/shard_map/ppermute | solution.py:965
  96.5 23.8 %copy-start.19 = (bf16[1408,512]{1,0:T(8,128)(2,1)}, bf16[1408,512]{1,0:T(8,128)(2,1)S(1)}, u32[]{:S(2)}) copy-start(bf16[1408,512]{1,0:T(8,128)(2,1)S(1)} %get-tuple-element.203.grad_before) | copy-start | bytes 4325380
  96.6 23.8 %collective-permute-start.19 = (bf16[256,1024]{1,0:T(8,128)(2,1)S(1)}, bf16[256,1024]{1,0:T(8,128)(2,1)S(1)}, u32[]{:S(2)}, u32[]{:S(2)}) collective-permute-start(bf16[256,1024]{1,0:T(8,128)(2,1)S(1)} %get-tuple-element.177), channel_id=1, source_target_pairs={{0,2},{2,0},{1,3},{3,1},{4,6},{6,4},{5,7},{7,5},{8,10},{10,8},{9,1... | collective-permute-start | bytes 1572872 | tf_op jit(solution)/shard_map/ppermute | solution.py:298
  120.4 5.4 %collective-permute-start.20 = (bf16[704,1024]{1,0:T(8,128)(2,1)}, bf16[704,1024]{1,0:T(8,128)(2,1)S(1)}, u32[]{:S(2)}, u32[]{:S(2)}) collective-permute-start(bf16[704,1024]{1,0:T(8,128)(2,1)} %get-tuple-element.194), channel_id=1, source_target_pairs={{0,1},{1,0},{2,3},{3,2},{4,5},{5,4},{6,7},{7,6},{8,9},{9,8},{10,11... | collective-permute-start | bytes 4325384 | tf_op jit(solution)/shard_map/ppermute | solution.py:298
  120.7 31.2 %collective-permute-start.21 = (bf16[256,1024]{1,0:T(8,128)(2,1)S(1)}, bf16[256,1024]{1,0:T(8,128)(2,1)S(1)}, u32[]{:S(2)}, u32[]{:S(2)}) collective-permute-start(bf16[256,1024]{1,0:T(8,128)(2,1)S(1)} %add_convert_fusion), channel_id=1, source_target_pairs={{0,8},{8,0},{1,9},{9,1},{2,10},{10,2},{3,11},{11,3},{4,12},{12,4},... | collective-permute-start | bytes 1572872 | tf_op jit(solution)/shard_map/ppermute | solution.py:298
  123.1 28.8 %collective-permute-start.22 = (bf16[256,1024]{1,0:T(8,128)(2,1)S(1)}, bf16[256,1024]{1,0:T(8,128)(2,1)S(1)}, u32[]{:S(2)}, u32[]{:S(2)}) collective-permute-start(bf16[256,1024]{1,0:T(8,128)(2,1)S(1)} %get-tuple-element.197), channel_id=1, source_target_pairs={{0,2},{2,0},{1,3},{3,1},{4,6},{6,4},{5,7},{7,5},{8,10},{10,8},{9,1... | collective-permute-start | bytes 1572872 | tf_op jit(solution)/shard_map/ppermute | solution.py:298
  124.4 21.2 %collective-permute-start.23 = (bf16[256,768]{1,0:T(8,128)(2,1)S(1)}, bf16[256,768]{1,0:T(8,128)(2,1)S(1)}, u32[]{:S(2)}, u32[]{:S(2)}) collective-permute-start(bf16[256,768]{1,0:T(8,128)(2,1)S(1)} %get-tuple-element.198), channel_id=1, source_target_pairs={{0,2},{2,0},{1,3},{3,1},{4,6},{6,4},{5,7},{7,5},{8,10},{10,8},{9,1... | collective-permute-start | bytes 1179656 | tf_op jit(solution)/shard_map/ppermute | solution.py:298
  125.1 16.5 %collective-permute-start.25 = (bf16[128,1024]{1,0:T(8,128)(2,1)S(1)}, bf16[128,1024]{1,0:T(8,128)(2,1)S(1)}, u32[]{:S(2)}, u32[]{:S(2)}) collective-permute-start(bf16[128,1024]{1,0:T(8,128)(2,1)S(1)} %get-tuple-element.201), channel_id=1, source_target_pairs={{0,0},{1,2},{2,1},{3,3},{8,16},{9,18},{10,17},{11,19},{16,8},{17,1... | collective-permute-start | bytes 786440 | tf_op jit(solution)/shard_map/ppermute | solution.py:1053
  128.0 24.0 %copy-start.22 = (bf16[176,1024]{1,0:T(8,128)(2,1)S(1)}, bf16[176,1024]{1,0:T(8,128)(2,1)}, u32[]{:S(2)}) copy-start(bf16[176,1024]{1,0:T(8,128)(2,1)} %param.16) | copy-start | bytes 1081348
  128.0 23.9 %collective-permute-start.24 = (bf16[352,1024]{1,0:T(8,128)(2,1)S(1)}, bf16[352,1024]{1,0:T(8,128)(2,1)S(1)}, u32[]{:S(2)}, u32[]{:S(2)}) collective-permute-start(bf16[352,1024]{1,0:T(8,128)(2,1)S(1)} %pad_maximum_fusion.3), channel_id=1, source_target_pairs={{0,16},{16,0},{1,17},{17,1},{2,18},{18,2},{3,19},{19,3},{4,20},{20... | collective-permute-start | bytes 2162696 | tf_op jit(solution)/shard_map/ppermute | solution.py:298
  141.6 17.0 %copy-start.34 = (bf16[128,1024]{1,0:T(8,128)(2,1)}, bf16[128,1024]{1,0:T(8,128)(2,1)S(1)}, u32[]{:S(2)}) copy-start(bf16[128,1024]{1,0:T(8,128)(2,1)S(1)} %collective-permute-done.25) | copy-start | bytes 786436
  151.9 3.4 %collective-permute-start.26 = (bf16[704,1024]{1,0:T(8,128)(2,1)S(1)}, bf16[704,1024]{1,0:T(8,128)(2,1)S(1)}, u32[]{:S(2)}, u32[]{:S(2)}) collective-permute-start(bf16[704,1024]{1,0:T(8,128)(2,1)S(1)} %get-tuple-element.212), channel_id=1, source_target_pairs={{0,1},{1,0},{2,3},{3,2},{4,5},{5,4},{6,7},{7,6},{8,9},{9,8},{10,11... | collective-permute-start | bytes 4325384 | tf_op jit(solution)/shard_map/ppermute | solution.py:298
  152.2 3.1 %collective-permute-start.27 = (f32[16,1024]{1,0:T(8,128)S(1)}, f32[16,1024]{1,0:T(8,128)S(1)}, u32[]{:S(2)}, u32[]{:S(2)}) collective-permute-start(f32[16,1024]{1,0:T(8,128)S(1)} %get-tuple-element.209), channel_id=1, source_target_pairs={{0,1},{1,0},{2,3},{3,2},{4,5},{5,4},{6,7},{7,6},{8,9},{9,8},{10,11... | collective-permute-start | bytes 196616 | tf_op jit(solution)/shard_map/ppermute | solution.py:298
  158.7 11.0 %collective-permute-start.32 = (f32[16,1024]{1,0:T(8,128)S(1)}, f32[16,1024]{1,0:T(8,128)S(1)}, u32[]{:S(2)}, u32[]{:S(2)}) collective-permute-start(f32[16,1024]{1,0:T(8,128)S(1)} %add.231), channel_id=1, source_target_pairs={{0,16},{16,0},{1,17},{17,1},{2,18},{18,2},{3,19},{19,3},{4,20},{20... | collective-permute-start | bytes 196616 | tf_op jit(solution)/shard_map/ppermute | solution.py:298
  165.9 20.5 %collective-permute-start.28 = (bf16[176,1024]{1,0:T(8,128)(2,1)}, bf16[176,1024]{1,0:T(8,128)(2,1)S(1)}, u32[]{:S(2)}, u32[]{:S(2)}) collective-permute-start(bf16[176,1024]{1,0:T(8,128)(2,1)} %get-tuple-element.216), channel_id=1, source_target_pairs={{0,16},{16,0},{1,17},{17,1},{2,18},{18,2},{3,19},{19,3},{4,20},{20... | collective-permute-start | bytes 1081352 | tf_op jit(solution)/shard_map/ppermute | solution.py:298
  166.0 20.5 %collective-permute-start.29 = (bf16[176,1024]{1,0:T(8,128)(2,1)}, bf16[176,1024]{1,0:T(8,128)(2,1)S(1)}, u32[]{:S(2)}, u32[]{:S(2)}) collective-permute-start(bf16[176,1024]{1,0:T(8,128)(2,1)} %get-tuple-element.217), channel_id=1, source_target_pairs={{0,4},{4,0},{1,5},{5,1},{2,6},{6,2},{3,7},{7,3},{8,12},{12,8},{9,1... | collective-permute-start | bytes 1081352 | tf_op jit(solution)/shard_map/ppermute | solution.py:298
  166.0 23.8 %collective-permute-start.30 = (bf16[176,1024]{1,0:T(8,128)(2,1)}, bf16[176,1024]{1,0:T(8,128)(2,1)}, u32[]{:S(2)}, u32[]{:S(2)}) collective-permute-start(bf16[176,1024]{1,0:T(8,128)(2,1)} %get-tuple-element.218), channel_id=1, source_target_pairs={{0,20},{4,16},{16,4},{20,0},{1,21},{5,17},{17,5},{21,1},{2,22},{6,... | collective-permute-start | bytes 1081352 | tf_op jit(solution)/shard_map/ppermute | solution.py:299
  169.6 16.8 %collective-permute-start.31 = (bf16[128,768]{1,0:T(8,128)(2,1)}, bf16[128,768]{1,0:T(8,128)(2,1)S(1)}, u32[]{:S(2)}, u32[]{:S(2)}) collective-permute-start(bf16[128,768]{1,0:T(8,128)(2,1)} %add_convert_fusion.7), channel_id=1, source_target_pairs={{0,8},{8,0},{1,9},{9,1},{2,10},{10,2},{3,11},{11,3},{4,12},{12,4},... | collective-permute-start | bytes 589832 | tf_op jit(solution)/shard_map/ppermute | solution.py:298
  169.7 4.3 %collective-permute-start.33 = (f32[16,1024]{1,0:T(8,128)S(1)}, f32[16,1024]{1,0:T(8,128)S(1)}, u32[]{:S(2)}, u32[]{:S(2)}) collective-permute-start(f32[16,1024]{1,0:T(8,128)S(1)} %add.235), channel_id=1, source_target_pairs={{0,2},{2,0},{1,3},{3,1},{4,6},{6,4},{5,7},{7,5},{8,10},{10,8},{9,1... | collective-permute-start | bytes 196616 | tf_op jit(solution)/shard_map/ppermute | solution.py:298
  192.1 11.2 %collective-permute-start.37 = (bf16[128,1024]{1,0:T(8,128)(2,1)S(1)}, bf16[128,1024]{1,0:T(8,128)(2,1)S(1)}, u32[]{:S(2)}, u32[]{:S(2)}) collective-permute-start(bf16[128,1024]{1,0:T(8,128)(2,1)S(1)} %get-tuple-element.242), channel_id=1, source_target_pairs={{0,16},{16,0},{1,17},{17,1},{2,18},{18,2},{3,19},{19,3},{4,20},{20... | collective-permute-start | bytes 786440 | tf_op jit(solution)/shard_map/ppermute | solution.py:298
  192.5 10.8 %collective-permute-start.34 = (bf16[64,896]{1,0:T(8,128)(2,1)S(1)}, bf16[64,896]{1,0:T(8,128)(2,1)S(1)}, u32[]{:S(2)}, u32[]{:S(2)}) collective-permute-start(bf16[64,896]{1,0:T(8,128)(2,1)S(1)} %get-tuple-element.239), channel_id=1, source_target_pairs={{0,1},{1,0},{2,3},{3,2},{4,5},{5,4},{6,7},{7,6},{8,9},{9,8},{10,11... | collective-permute-start | bytes 344072 | tf_op jit(solution)/shard_map/ppermute | solution.py:298
  192.5 10.8 %collective-permute-start.35 = (bf16[64,896]{1,0:T(8,128)(2,1)S(1)}, bf16[64,896]{1,0:T(8,128)(2,1)S(1)}, u32[]{:S(2)}, u32[]{:S(2)}) collective-permute-start(bf16[64,896]{1,0:T(8,128)(2,1)S(1)} %get-tuple-element.240), channel_id=1, source_target_pairs={{0,4},{4,0},{1,5},{5,1},{2,6},{6,2},{3,7},{7,3},{8,12},{12,8},{9,1... | collective-permute-start | bytes 344072 | tf_op jit(solution)/shard_map/ppermute | solution.py:298
  192.5 10.8 %collective-permute-start.36 = (bf16[64,896]{1,0:T(8,128)(2,1)S(1)}, bf16[64,896]{1,0:T(8,128)(2,1)S(1)}, u32[]{:S(2)}, u32[]{:S(2)}) collective-permute-start(bf16[64,896]{1,0:T(8,128)(2,1)S(1)} %get-tuple-element.241), channel_id=1, source_target_pairs={{0,5},{1,4},{4,1},{5,0},{2,7},{3,6},{6,3},{7,2},{8,13},{9,12},{12,... | collective-permute-start | bytes 344072 | tf_op jit(solution)/shard_map/ppermute | solution.py:299
  194.4 7.6 %collective-permute-start.38 = (f32[16,1024]{1,0:T(8,128)S(1)}, f32[16,1024]{1,0:T(8,128)S(1)}, u32[]{:S(2)}, u32[]{:S(2)}) collective-permute-start(f32[16,1024]{1,0:T(8,128)S(1)} %add.236), channel_id=1, source_target_pairs={{0,4},{4,0},{1,5},{5,1},{2,6},{6,2},{3,7},{7,3},{8,12},{12,8},{9,1... | collective-permute-start | bytes 196616 | tf_op jit(solution)/shard_map/ppermute | solution.py:298
  201.9 1.4 collective-permute-start.39
  203.5 11.9 %collective-permute-start.43 = (bf16[64,1024]{1,0:T(8,128)(2,1)S(1)}, bf16[64,1024]{1,0:T(8,128)(2,1)}, u32[]{:S(2)}, u32[]{:S(2)}) collective-permute-start(bf16[64,1024]{1,0:T(8,128)(2,1)S(1)} %fusion.15), channel_id=1, source_target_pairs={{0,16},{16,0},{1,17},{17,1},{2,18},{18,2},{3,19},{19,3},{4,20},{20... | collective-permute-start | bytes 393224 | tf_op jit(solution)/shard_map/ppermute | solution.py:298
  205.2 15.3 %collective-permute-start.42 = (bf16[2,2,64,896]{3,2,1,0:T(8,128)(2,1)S(1)}, bf16[2,2,64,896]{3,2,1,0:T(8,128)(2,1)S(1)}, u32[]{:S(2)}, u32[]{:S(2)}) collective-permute-start(bf16[2,2,64,896]{3,2,1,0:T(8,128)(2,1)S(1)} %bitcast.57), channel_id=1, source_target_pairs={{0,16},{16,0},{1,17},{17,1},{2,18},{18,2},{3,19},{19,3},{4,20},{20... | collective-permute-start | bytes 1376264 | tf_op jit(solution)/shard_map/ppermute | solution.py:298
  205.6 6.0 %collective-permute-start.41 = (f32[16,1024]{1,0:T(8,128)S(1)}, f32[16,1024]{1,0:T(8,128)S(1)}, u32[]{:S(2)}, u32[]{:S(2)}) collective-permute-start(f32[16,1024]{1,0:T(8,128)S(1)} %add.245), channel_id=1, source_target_pairs={{0,8},{8,0},{1,9},{9,1},{2,10},{10,2},{3,11},{11,3},{4,12},{12,4},... | collective-permute-start | bytes 196616 | tf_op jit(solution)/shard_map/ppermute | solution.py:298
  206.9 11.4 %collective-permute-start.40 = (bf16[176,1024]{1,0:T(8,128)(2,1)S(1)}, bf16[176,1024]{1,0:T(8,128)(2,1)S(1)}, u32[]{:S(2)}, u32[]{:S(2)}) collective-permute-start(bf16[176,1024]{1,0:T(8,128)(2,1)S(1)} %add_convert_fusion.1), channel_id=1, source_target_pairs={{0,4},{4,0},{1,5},{5,1},{2,6},{6,2},{3,7},{7,3},{8,12},{12,8},{9,1... | collective-permute-start | bytes 1081352 | tf_op jit(solution)/shard_map/ppermute | solution.py:298
  211.7 10.8 %copy-start.48 = (f32[64]{0:T(128)}, f32[64]{0:T(128)S(1)}, u32[]{:S(2)}) copy-start(f32[64]{0:T(128)S(1)} %fusion.18) | copy-start | bytes 772
  (29 other events, 107.8 us)
